TPU v7x, 32 devices: a whole 2x2x4 slice. The times are simulated.
32 devices in a mesh: pr: 8 (over z, y), tp: 4 (over x, core).
Axes of the slice: x: 2, y: 2, z: 4, core: 2. Of those that a mesh axis runs over, the one named last changes fastest.
Arguments:
- tokens: bfloat16 [2048, 896], P('pr'), may hold values from -18 to 18
- prompt_lengths: int32 [8, 2], P('pr'), may hold values from 1 to 160, 256 in all within a row
- query_weight: bfloat16 [896, 1024], P(None, 'tp'), may hold values from -0.1875 to 0.1875
- key_weight: bfloat16 [896, 256], P(None, 'tp'), may hold values from -0.1875 to 0.1875
- value_weight: bfloat16 [896, 256], P(None, 'tp'), may hold values from -1.5 to 1.5
- attention_gain: float32 [1024], P('tp'), may hold values from 0.1 to 1.9
- inner_weight: bfloat16 [896, 2, 2048], P(None, None, 'tp'), may hold values from -0.1875 to 0.1875
- conv_weight: float32 [4, 2048], P(None, 'tp'), may hold values from -3 to 3
- scan_weight: bfloat16 [2048, 96], P('tp'), may hold values from -0.125 to 0.125
- step_weight: bfloat16 [64, 2048], P(None, 'tp'), may hold values from -0.75 to 0.75
- step_bias: float32 [2048], P('tp'), may hold values from -4 to -1
- mamba_rate: float32 [16, 2048], P(None, 'tp'), may hold values from 0.05 to 1
- mamba_skip: float32 [2048], P('tp'), may hold values from 0.3 to 2.7
- mamba_gain: float32 [2048], P('tp'), may hold values from 0.1 to 1.9
- request_prompt: int32 [448], P('pr'), may hold values from 0 to 1, as said below
- request_owner: int32 [448], P('pr'), may hold values from 0 to 7, as said below
- request_slot: int32 [448], P('pr'), may hold values from 0 to 55, as said below
Outputs:
- attention_out: bfloat16 [2048, 1024], P('pr', 'tp')
- mamba_out: bfloat16 [2048, 2048], P('pr', 'tp')
- cache_keyval: bfloat16 [448, 2, 32, 256], P('pr', None, None, 'tp')
- cache_state: bfloat16 [448, 16, 2048], P('pr', None, 'tp')
- cache_conv: bfloat16 [448, 3, 2048], P('pr', None, 'tp')
Inputs may be any that keep to these rules, and one draw needn't show every extreme that they name: `request_prompt`: in each group one prompt has 29 requests and the other 27. `request_owner`: every owner receives exactly 56 requests; the requests of one group that name an owner name it exactly 7 times. `request_slot`: the requests of one owner have distinct slots.
All inputs are finite; a program needn't handle non-finite values.
Results may differ from a plain program's by a relative error of at most 0.012.
The roundings to bfloat16 on the way count: a program that leaves them out, or rounds other values in their place, can miss the bound.
Values may be sent and summed in bfloat16 or wider, within the bound.
No kernel may reach another device: no remote copies, remote signals or barrier semaphores. Data moves between devices by JAX's collectives and lax.ppermute only.
A program may use at most 64 MiB of HBM per device.

v0:
```python
import jax
import jax.numpy as jnp
from jax import lax
from jax.sharding import PartitionSpec as P

HEADS = 16
KV_HEADS = 4
HEAD_DIM = 64
INNER = 2048
STATE = 16
DT_RANK = 64
CONV = 4
WINDOW = 32


EPSILON = 1e-06
ROWS_BLOCK = 8


def prompt_layout(lengths, total_rows):
    prompt_ends = jnp.cumsum(lengths)
    starts = prompt_ends - lengths
    position = jnp.arange(total_rows, dtype=jnp.int32)
    member = (position[:, None] >= starts[None, :]) & (position[:, None] < prompt_ends[None, :])
    segment = jnp.sum((position[:, None] >= prompt_ends[None, :]).astype(jnp.int32), axis=1)
    first_pos = jnp.sum(jnp.where(member, starts[None, :], 0), axis=1)
    return (starts, prompt_ends, segment, position - first_pos)


def tail_rows(values, starts, prompt_ends, tail_depth):
    offsets = jnp.arange(tail_depth, dtype=jnp.int32)
    wanted = prompt_ends[:, None] - tail_depth + offsets[None, :]
    inside_prompt = wanted >= starts[:, None]
    picked = jnp.take(values, jnp.clip(wanted, 0, values.shape[0] - 1), axis=0)
    return jnp.where(inside_prompt[:, :, None], picked, jnp.zeros((), values.dtype))


def on_device(
    tokens,
    prompt_lengths,
    query_weight,
    key_weight,
    value_weight,
    attention_gain,
    inner_weight,
    conv_weight,
    scan_weight,
    step_weight,
    step_bias,
    mamba_rate,
    mamba_skip,
    mamba_gain,
    request_prompt,
    request_owner,
    request_slot,
):
    total_rows = tokens.shape[0]
    starts, prompt_ends, segment, offset = prompt_layout(prompt_lengths[0], total_rows)
    queries = jnp.dot(tokens, query_weight, preferred_element_type=jnp.float32).astype(jnp.bfloat16)
    keys_bf = jnp.dot(tokens, key_weight, preferred_element_type=jnp.float32).astype(jnp.bfloat16)
    values_bf = jnp.dot(tokens, value_weight, preferred_element_type=jnp.float32).astype(
        jnp.bfloat16
    )
    local_kv = key_weight.shape[1] // HEAD_DIM
    group_size = HEADS // KV_HEADS
    query_heads = queries.reshape(total_rows, local_kv, group_size, HEAD_DIM)
    key_heads = keys_bf.reshape(total_rows, local_kv, HEAD_DIM)
    value_heads = values_bf.reshape(total_rows, local_kv, HEAD_DIM)
    scores = jnp.einsum(
        "tkgd,ukd->kgtu", query_heads, key_heads, preferred_element_type=jnp.float32
    ) * HEAD_DIM ** (-0.5)
    position = jnp.arange(total_rows, dtype=jnp.int32)
    distance = position[:, None] - position[None, :]
    allowed = (segment[:, None] == segment[None, :]) & (distance >= 0) & (distance < WINDOW)
    masked = jnp.where(allowed[None, None], scores, -1e30)
    row_max = jnp.max(masked, axis=3, keepdims=True)
    expons = jnp.where(allowed[None, None], jnp.exp(masked - row_max), 0.0)
    weights = (expons / jnp.sum(expons, axis=3, keepdims=True)).astype(jnp.bfloat16)
    attended = jnp.einsum(
        "kgtu,ukd->tkgd", weights, value_heads, preferred_element_type=jnp.float32
    ).reshape(total_rows, -1)
    local_inner = inner_weight.shape[2]
    inner_proj = jnp.dot(
        tokens,
        inner_weight.reshape(tokens.shape[1], 2 * local_inner),
        preferred_element_type=jnp.float32,
    )
    inner_proj = inner_proj.astype(jnp.bfloat16).reshape(total_rows, 2, local_inner)
    raw_inner = inner_proj[:, 0]
    gate_inner = inner_proj[:, 1]
    conv_sum = jnp.zeros((total_rows, local_inner), jnp.float32)
    for tap_index in range(CONV):
        lag_rows = CONV - 1 - tap_index
        shifted = jnp.pad(raw_inner, ((lag_rows, 0), (0, 0)))[:total_rows].astype(jnp.float32)
        shifted = jnp.where((offset >= lag_rows)[:, None], shifted, 0.0)
        conv_sum = conv_sum + shifted * conv_weight[tap_index]
    mixed_inner = jax.nn.silu(conv_sum).astype(jnp.bfloat16)
    partial_proj = jnp.dot(mixed_inner, scan_weight, preferred_element_type=jnp.float32)
    projected = lax.psum(partial_proj, "tp")
    low_rank = projected[:, :DT_RANK].astype(jnp.bfloat16)
    input_map = projected[:, DT_RANK : DT_RANK + STATE]
    output_map = projected[:, DT_RANK + STATE :]
    step_size = jax.nn.softplus(
        jnp.dot(low_rank, step_weight, preferred_element_type=jnp.float32) + step_bias
    )
    mixed_float = mixed_inner.astype(jnp.float32)
    keep_state = jnp.where(offset == 0, 0.0, 1.0).astype(jnp.float32)
    prompts_here = prompt_ends.shape[0]
    is_last = position[:, None] == (prompt_ends - 1)[None, :]
    block_total = total_rows // ROWS_BLOCK

    def to_blocks(matrix):
        return matrix.reshape((block_total, ROWS_BLOCK) + matrix.shape[1:])

    def scan_block(carried, block_item):
        state_now, finals = carried
        step_rows, input_rows, output_rows, mixed_rows, keep_rows, last_rows = block_item
        out_rows = []
        for row_index in range(ROWS_BLOCK):
            decay_rate = jnp.exp(-step_rows[row_index][None, :] * mamba_rate)
            state_now = (
                state_now * decay_rate * keep_rows[row_index]
                + input_rows[row_index][:, None]
                * (step_rows[row_index] * mixed_rows[row_index])[None, :]
            )
            out_rows.append(jnp.sum(output_rows[row_index][:, None] * state_now, axis=0))
            finals = jnp.where(last_rows[row_index][:, None, None], state_now[None], finals)
        return ((state_now, finals), jnp.stack(out_rows, axis=0))

    start_state = jnp.zeros((STATE, local_inner), jnp.float32)
    start_finals = jnp.zeros((prompts_here, STATE, local_inner), jnp.float32)
    (_, last_states), scan_out = lax.scan(
        scan_block,
        (start_state, start_finals),
        (
            to_blocks(step_size),
            to_blocks(input_map),
            to_blocks(output_map),
            to_blocks(mixed_float),
            to_blocks(keep_state),
            to_blocks(is_last),
        ),
    )
    scanned = scan_out.reshape(total_rows, local_inner)
    final_state = last_states.astype(jnp.bfloat16)
    gated_out = (scanned + mamba_skip * mixed_float) * jax.nn.silu(gate_inner.astype(jnp.float32))
    attn_total, mamba_total = lax.psum(
        (jnp.sum(attended * attended, axis=1), jnp.sum(gated_out * gated_out, axis=1)), "tp"
    )
    norm_attn = jnp.sqrt(attn_total / (HEADS * HEAD_DIM) + EPSILON)
    norm_mamba = jnp.sqrt(mamba_total / INNER + EPSILON)
    attention_out = (attended / norm_attn[:, None] * attention_gain).astype(jnp.bfloat16)
    mamba_out = (gated_out / norm_mamba[:, None] * mamba_gain).astype(jnp.bfloat16)
    keyval = jnp.stack(
        [
            tail_rows(keys_bf, starts, prompt_ends, WINDOW),
            tail_rows(values_bf, starts, prompt_ends, WINDOW),
        ],
        axis=1,
    )
    conv_tail = tail_rows(raw_inner, starts, prompt_ends, CONV - 1)
    slots_here = request_owner.shape[0]
    my_index = lax.axis_index("pr")
    owners, slot_list, prompt_list = (
        lax.all_gather(request_owner, "pr", axis=0, tiled=True),
        lax.all_gather(request_slot, "pr", axis=0, tiled=True),
        lax.all_gather(request_prompt, "pr", axis=0, tiled=True),
    )
    all_requests = owners.shape[0]
    source = jnp.arange(all_requests, dtype=jnp.int32) // slots_here
    wanted = source * prompts_here + prompt_list
    slot_ids = jnp.arange(slots_here, dtype=jnp.int32)
    matched = (owners[None, :] == my_index) & (slot_list[None, :] == slot_ids[:, None])
    source_prompt = jnp.sum(jnp.where(matched, wanted[None, :], 0), axis=1)
    all_keyval, all_state, all_conv = (
        lax.all_gather(keyval, "pr", axis=0, tiled=True),
        lax.all_gather(final_state, "pr", axis=0, tiled=True),
        lax.all_gather(conv_tail, "pr", axis=0, tiled=True),
    )
    cache_keyval = jnp.take(all_keyval, source_prompt, axis=0)
    cache_state = jnp.take(all_state, source_prompt, axis=0)
    cache_conv = jnp.take(all_conv, source_prompt, axis=0)
    return (attention_out, mamba_out, cache_keyval, cache_state, cache_conv)


def solution(mesh):
    return jax.shard_map(
        on_device,
        mesh=mesh,
        in_specs=(
            P("pr", None),
            P("pr", None),
            P(None, "tp"),
            P(None, "tp"),
            P(None, "tp"),
            P("tp"),
            P(None, None, "tp"),
            P(None, "tp"),
            P("tp", None),
            P(None, "tp"),
            P("tp"),
            P(None, "tp"),
            P("tp"),
            P("tp"),
            P("pr"),
            P("pr"),
            P("pr"),
        ),
        out_specs=(
            P("pr", "tp"),
            P("pr", "tp"),
            P("pr", None, None, "tp"),
            P("pr", None, "tp"),
            P("pr", None, "tp"),
        ),
        check_vma=False,
    )
```

profile of v0, /device:TPU:0, one launch (start us, length us, event | category | flops | bytes accessed | tf_op | source)
XLA Modules:
  0.0 415.9 jit_solution(6443218835417818729)
XLA Ops:
  17.2 13.2 %all-reduce.6 = (s32[448]{0:T(512)S(1)}, s32[448]{0:T(512)S(1)}, s32[448]{0:T(512)S(1)}) all-reduce(s32[448]{0:T(512)S(1)} %dynamic-update-slice.2, s32[448]{0:T(512)S(1)} %dynamic-update-slice.1, s32[448]{0:T(512)S(1)} %dynamic-update-slice), channel_id=1, replica_groups=mesh['pr'=8,'tp'=4] {'pr'}, use_global_device_ids=true, to_apply=%add.5 | all-reduce | flops 1344 | bytes 10752
  34.6 30.8 %all_gather.21 = bf16[16,2,32,64]{3,2,1,0:T(8,128)(2,1)S(1)} all-gather(bf16[2,2,32,64]{3,2,1,0:T(8,128)(2,1)S(1)} %pad_maximum_fusion), channel_id=1, replica_groups=mesh['pr'=8,'tp'=4] {'pr'}, dimensions={0}, use_global_device_ids=true | all-gather | bytes 147456 | tf_op jit(solution)/shard_map/all_gather | solution.py:176
  66.2 30.5 %all_gather.23 = bf16[16,3,512]{2,1,0:T(4,128)(2,1)S(1)} all-gather(bf16[2,3,512]{2,1,0:T(4,128)(2,1)S(1)} %select_select_fusion.3), channel_id=1, replica_groups=mesh['pr'=8,'tp'=4] {'pr'}, dimensions={0}, use_global_device_ids=true | all-gather | bytes 55296 | tf_op jit(solution)/shard_map/all_gather | solution.py:178
  103.5 265.4 %while.15 = (s32[]{:T(128)}, f32[16,512]{1,0:T(8,128)S(1)}, bf16[2,16,512]{2,1,0:T(8,128)(2,1)S(1)}, f32[32,8,512]{2,1,0:T(8,128)}, f32[32,8,512]{2,1,0:T(8,128)...) while((s32[]{:T(128)}, f32[16,512]{1,0:T(8,128)S(1)}, ...), condition=%wide.region_17.18_spmd.clone, body=%wide.region_8.17_spmd.clone.sunk | while | flops 618506 | bytes 1071152 | solution.py:132
  105.4 5.1 %multiply_reduce_fusion.17 = (f32[512]{0:T(512)S(1)}, f32[16,512]{1,0:T(8,128)S(1)}, f32[16,512]{1,0:T(8,128)S(1)}, f32[16,512]{1,0:T(8,128)S(1)}, f32[16,512]{1...) fusion(f32[16]{0:T(128)S(1)} %get-tuple-element.408, ...), kind=kLoop, calls=%fused_computation.17.clone.1 | loop fusion | flops 351744 | bytes 363105 | tf_op jit(solution)/shard_map/while/body/eval_jaxpr/reduce_sum | solution.py:126
  113.7 5.1 %multiply_reduce_fusion.17 = (f32[512]{0:T(512)S(1)}, f32[16,512]{1,0:T(8,128)S(1)}, f32[16,512]{1,0:T(8,128)S(1)}, f32[16,512]{1,0:T(8,128)S(1)}, f32[16,512]{1...) fusion(f32[16]{0:T(128)S(1)} %get-tuple-element.408, ...), kind=kLoop, calls=%fused_computation.17.clone.1 | loop fusion | flops 351744 | bytes 363105 | tf_op jit(solution)/shard_map/while/body/eval_jaxpr/reduce_sum | solution.py:126
  122.0 5.1 %multiply_reduce_fusion.17 = (f32[512]{0:T(512)S(1)}, f32[16,512]{1,0:T(8,128)S(1)}, f32[16,512]{1,0:T(8,128)S(1)}, f32[16,512]{1,0:T(8,128)S(1)}, f32[16,512]{1...) fusion(f32[16]{0:T(128)S(1)} %get-tuple-element.408, ...), kind=kLoop, calls=%fused_computation.17.clone.1 | loop fusion | flops 351744 | bytes 363105 | tf_op jit(solution)/shard_map/while/body/eval_jaxpr/reduce_sum | solution.py:126
  130.3 5.1 %multiply_reduce_fusion.17 = (f32[512]{0:T(512)S(1)}, f32[16,512]{1,0:T(8,128)S(1)}, f32[16,512]{1,0:T(8,128)S(1)}, f32[16,512]{1,0:T(8,128)S(1)}, f32[16,512]{1...) fusion(f32[16]{0:T(128)S(1)} %get-tuple-element.408, ...), kind=kLoop, calls=%fused_computation.17.clone.1 | loop fusion | flops 351744 | bytes 363105 | tf_op jit(solution)/shard_map/while/body/eval_jaxpr/reduce_sum | solution.py:126
  138.6 5.1 %multiply_reduce_fusion.17 = (f32[512]{0:T(512)S(1)}, f32[16,512]{1,0:T(8,128)S(1)}, f32[16,512]{1,0:T(8,128)S(1)}, f32[16,512]{1,0:T(8,128)S(1)}, f32[16,512]{1...) fusion(f32[16]{0:T(128)S(1)} %get-tuple-element.408, ...), kind=kLoop, calls=%fused_computation.17.clone.1 | loop fusion | flops 351744 | bytes 363105 | tf_op jit(solution)/shard_map/while/body/eval_jaxpr/reduce_sum | solution.py:126
  146.9 5.1 %multiply_reduce_fusion.17 = (f32[512]{0:T(512)S(1)}, f32[16,512]{1,0:T(8,128)S(1)}, f32[16,512]{1,0:T(8,128)S(1)}, f32[16,512]{1,0:T(8,128)S(1)}, f32[16,512]{1...) fusion(f32[16]{0:T(128)S(1)} %get-tuple-element.408, ...), kind=kLoop, calls=%fused_computation.17.clone.1 | loop fusion | flops 351744 | bytes 363105 | tf_op jit(solution)/shard_map/while/body/eval_jaxpr/reduce_sum | solution.py:126
  155.2 5.1 %multiply_reduce_fusion.17 = (f32[512]{0:T(512)S(1)}, f32[16,512]{1,0:T(8,128)S(1)}, f32[16,512]{1,0:T(8,128)S(1)}, f32[16,512]{1,0:T(8,128)S(1)}, f32[16,512]{1...) fusion(f32[16]{0:T(128)S(1)} %get-tuple-element.408, ...), kind=kLoop, calls=%fused_computation.17.clone.1 | loop fusion | flops 351744 | bytes 363105 | tf_op jit(solution)/shard_map/while/body/eval_jaxpr/reduce_sum | solution.py:126
  171.7 5.1 %multiply_reduce_fusion.17 = (f32[512]{0:T(512)S(1)}, f32[16,512]{1,0:T(8,128)S(1)}, f32[16,512]{1,0:T(8,128)S(1)}, f32[16,512]{1,0:T(8,128)S(1)}, f32[16,512]{1...) fusion(f32[16]{0:T(128)S(1)} %get-tuple-element.408, ...), kind=kLoop, calls=%fused_computation.17.clone.1 | loop fusion | flops 351744 | bytes 363105 | tf_op jit(solution)/shard_map/while/body/eval_jaxpr/reduce_sum | solution.py:126
  180.0 5.1 %multiply_reduce_fusion.17 = (f32[512]{0:T(512)S(1)}, f32[16,512]{1,0:T(8,128)S(1)}, f32[16,512]{1,0:T(8,128)S(1)}, f32[16,512]{1,0:T(8,128)S(1)}, f32[16,512]{1...) fusion(f32[16]{0:T(128)S(1)} %get-tuple-element.408, ...), kind=kLoop, calls=%fused_computation.17.clone.1 | loop fusion | flops 351744 | bytes 363105 | tf_op jit(solution)/shard_map/while/body/eval_jaxpr/reduce_sum | solution.py:126
  196.6 5.1 %multiply_reduce_fusion.17 = (f32[512]{0:T(512)S(1)}, f32[16,512]{1,0:T(8,128)S(1)}, f32[16,512]{1,0:T(8,128)S(1)}, f32[16,512]{1,0:T(8,128)S(1)}, f32[16,512]{1...) fusion(f32[16]{0:T(128)S(1)} %get-tuple-element.408, ...), kind=kLoop, calls=%fused_computation.17.clone.1 | loop fusion | flops 351744 | bytes 363105 | tf_op jit(solution)/shard_map/while/body/eval_jaxpr/reduce_sum | solution.py:126
  204.9 5.1 %multiply_reduce_fusion.17 = (f32[512]{0:T(512)S(1)}, f32[16,512]{1,0:T(8,128)S(1)}, f32[16,512]{1,0:T(8,128)S(1)}, f32[16,512]{1,0:T(8,128)S(1)}, f32[16,512]{1...) fusion(f32[16]{0:T(128)S(1)} %get-tuple-element.408, ...), kind=kLoop, calls=%fused_computation.17.clone.1 | loop fusion | flops 351744 | bytes 363105 | tf_op jit(solution)/shard_map/while/body/eval_jaxpr/reduce_sum | solution.py:126
  213.2 5.1 %multiply_reduce_fusion.17 = (f32[512]{0:T(512)S(1)}, f32[16,512]{1,0:T(8,128)S(1)}, f32[16,512]{1,0:T(8,128)S(1)}, f32[16,512]{1,0:T(8,128)S(1)}, f32[16,512]{1...) fusion(f32[16]{0:T(128)S(1)} %get-tuple-element.408, ...), kind=kLoop, calls=%fused_computation.17.clone.1 | loop fusion | flops 351744 | bytes 363105 | tf_op jit(solution)/shard_map/while/body/eval_jaxpr/reduce_sum | solution.py:126
  221.5 5.1 %multiply_reduce_fusion.17 = (f32[512]{0:T(512)S(1)}, f32[16,512]{1,0:T(8,128)S(1)}, f32[16,512]{1,0:T(8,128)S(1)}, f32[16,512]{1,0:T(8,128)S(1)}, f32[16,512]{1...) fusion(f32[16]{0:T(128)S(1)} %get-tuple-element.408, ...), kind=kLoop, calls=%fused_computation.17.clone.1 | loop fusion | flops 351744 | bytes 363105 | tf_op jit(solution)/shard_map/while/body/eval_jaxpr/reduce_sum | solution.py:126
  238.1 5.1 %multiply_reduce_fusion.17 = (f32[512]{0:T(512)S(1)}, f32[16,512]{1,0:T(8,128)S(1)}, f32[16,512]{1,0:T(8,128)S(1)}, f32[16,512]{1,0:T(8,128)S(1)}, f32[16,512]{1...) fusion(f32[16]{0:T(128)S(1)} %get-tuple-element.408, ...), kind=kLoop, calls=%fused_computation.17.clone.1 | loop fusion | flops 351744 | bytes 363105 | tf_op jit(solution)/shard_map/while/body/eval_jaxpr/reduce_sum | solution.py:126
  246.4 5.1 %multiply_reduce_fusion.17 = (f32[512]{0:T(512)S(1)}, f32[16,512]{1,0:T(8,128)S(1)}, f32[16,512]{1,0:T(8,128)S(1)}, f32[16,512]{1,0:T(8,128)S(1)}, f32[16,512]{1...) fusion(f32[16]{0:T(128)S(1)} %get-tuple-element.408, ...), kind=kLoop, calls=%fused_computation.17.clone.1 | loop fusion | flops 351744 | bytes 363105 | tf_op jit(solution)/shard_map/while/body/eval_jaxpr/reduce_sum | solution.py:126
  254.7 5.1 %multiply_reduce_fusion.17 = (f32[512]{0:T(512)S(1)}, f32[16,512]{1,0:T(8,128)S(1)}, f32[16,512]{1,0:T(8,128)S(1)}, f32[16,512]{1,0:T(8,128)S(1)}, f32[16,512]{1...) fusion(f32[16]{0:T(128)S(1)} %get-tuple-element.408, ...), kind=kLoop, calls=%fused_computation.17.clone.1 | loop fusion | flops 351744 | bytes 363105 | tf_op jit(solution)/shard_map/while/body/eval_jaxpr/reduce_sum | solution.py:126
  263.0 5.1 %multiply_reduce_fusion.17 = (f32[512]{0:T(512)S(1)}, f32[16,512]{1,0:T(8,128)S(1)}, f32[16,512]{1,0:T(8,128)S(1)}, f32[16,512]{1,0:T(8,128)S(1)}, f32[16,512]{1...) fusion(f32[16]{0:T(128)S(1)} %get-tuple-element.408, ...), kind=kLoop, calls=%fused_computation.17.clone.1 | loop fusion | flops 351744 | bytes 363105 | tf_op jit(solution)/shard_map/while/body/eval_jaxpr/reduce_sum | solution.py:126
  271.3 5.1 %multiply_reduce_fusion.17 = (f32[512]{0:T(512)S(1)}, f32[16,512]{1,0:T(8,128)S(1)}, f32[16,512]{1,0:T(8,128)S(1)}, f32[16,512]{1,0:T(8,128)S(1)}, f32[16,512]{1...) fusion(f32[16]{0:T(128)S(1)} %get-tuple-element.408, ...), kind=kLoop, calls=%fused_computation.17.clone.1 | loop fusion | flops 351744 | bytes 363105 | tf_op jit(solution)/shard_map/while/body/eval_jaxpr/reduce_sum | solution.py:126
  368.9 30.8 %all_gather.22 = bf16[16,16,512]{2,1,0:T(8,128)(2,1)S(1)} all-gather(bf16[2,16,512]{2,1,0:T(8,128)(2,1)S(1)} %get-tuple-element.65), channel_id=1, replica_groups=mesh['pr'=8,'tp'=4] {'pr'}, dimensions={0}, use_global_device_ids=true | all-gather | bytes 294912 | tf_op jit(solution)/shard_map/all_gather | solution.py:177
  401.7 5.7 %all-reduce.7 = (f32[256]{0:T(256)S(1)}, f32[256]{0:T(256)S(1)}) all-reduce(f32[256]{0:T(256)S(1)} %get-tuple-element.277, f32[256]{0:T(256)S(1)} %get-tuple-element.199), channel_id=1, replica_groups=mesh['pr'=8,'tp'=4] {'tp'}, use_global_device_ids=true, to_apply=%region_5.6 | all-reduce | flops 512 | bytes 4096 | tf_op jit(solution)/shard_map/psum | solution.py:147
  (700 shorter events, 196.1 us)
Async XLA Ops:
  7.2 4.6 %copy-start = (bf16[256,896]{1,0:T(8,128)(2,1)S(1)}, bf16[256,896]{1,0:T(8,128)(2,1)}, u32[]{:S(2)}) copy-start(bf16[256,896]{1,0:T(8,128)(2,1)} %param.21) | copy-start | bytes 1376260
  7.2 93.3 %all-reduce.10.cloned.1.call-start = ((), (), s32[]{:S(2)}) async-start(), calls=%async_computation | async-start | bytes 196608 | tf_op jit(solution)/shard_map/psum | solution.py:99
  12.8 1.4 copy-start.6
  12.8 2.4 copy-start.10
  12.9 2.4 copy-start.16
  12.9 3.6 copy-start.13
  12.9 3.9 copy-start.14
  12.9 4.1 copy-start.15
  12.9 18.1 %copy-start.4 = (bf16[896,64]{0,1:T(8,128)(2,1)S(1)}, bf16[896,64]{0,1:T(8,128)(2,1)}, u32[]{:S(2)}) copy-start(bf16[896,64]{0,1:T(8,128)(2,1)} %param.24) | copy-start | bytes 344068
  13.7 17.7 %copy-start.3 = (bf16[896,256]{1,0:T(8,128)(2,1)S(1)}, bf16[896,256]{1,0:T(8,128)(2,1)}, u32[]{:S(2)}) copy-start(bf16[896,256]{1,0:T(8,128)(2,1)} %param.23) | copy-start | bytes 1376260
  13.7 18.0 %copy-start.5 = (bf16[896,64]{0,1:T(8,128)(2,1)S(1)}, bf16[896,64]{0,1:T(8,128)(2,1)}, u32[]{:S(2)}) copy-start(bf16[896,64]{0,1:T(8,128)(2,1)} %param.25) | copy-start | bytes 344068
  99.2 2.1 copy-start.11
  99.3 2.1 copy-start.12
  99.3 4.3 %copy-start.1 = (f32[16,512]{1,0:T(8,128)S(1)}, f32[16,512]{1,0:T(8,128)}, u32[]{:S(2)}) copy-start(f32[16,512]{1,0:T(8,128)} %param.32) | copy-start | bytes 98308
  399.7 1.7 copy-start.2
  399.7 1.7 copy-start.8
  400.3 7.1 %copy-start.7 = (f32[512]{0:T(512)S(1)}, f32[512]{0:T(512)}, u32[]{:S(2)}) copy-start(f32[512]{0:T(512)} %param.34) | copy-start | bytes 6148
  400.4 7.9 %copy-start.9 = (f32[256]{0:T(256)S(1)}, f32[256]{0:T(256)}, u32[]{:S(2)}) copy-start(f32[256]{0:T(256)} %param.26) | copy-start | bytes 3076
Sparse Core Ops, SparseCore 0:
  15.2 34.0 all-reduce.9
where the time goes:
time: 421 us; the launch traced here: 416 us
  other arithmetic  227 us (54%)
  blocking collectives  111 us (26%)
  local copies, waits for them, and re-layouts  55.3 us (13%)
  between operations  15.1 us (4%)
  matrix products  5.32 us (1%)
    reduce_sum x256, other arithmetic, scan_block(): jnp.sum(output_rows[row_index][:, None] * state_now, axis=0)  183 us
    mul x32, other arithmetic, scan_block(): step_rows[row_index] * mixed_rows[row_index]  34 us
    all_gather x1, blocking collectives, on_device(): lax.all_gather(keyval, 'pr', axis=0, tiled=True)  30.8 us
    all_gather x1, blocking collectives, on_device(): lax.all_gather(final_state, 'pr', axis=0, tiled=True)  30.8 us
    all_gather x1, blocking collectives, on_device(): lax.all_gather(conv_tail, 'pr', axis=0, tiled=True)  30.5 us
    slice x32, local copies, waits for them, and re-layouts, scan_block(): keep_rows[row_index]  21.5 us
    dynamic_update_slice x32, local copies, waits for them, and re-layouts, on_device(): lax.scan(scan_block, (start_state, start_finals), (to_blocks(step_size),...  19.4 us
    unnamed x1, blocking collectives  13.2 us
  transfers between devices with their start and end apart: 1, of which 0 were waited for; matrix products, arithmetic and copies ran while one was open for 2% of the time, Pallas kernels for 0%

commit v1 on v0

v1 whole, which is shorter than its diff:
```python
import functools
import math

import jax
import jax.numpy as jnp
from jax import lax
from jax.experimental import pallas as pl
from jax.experimental.pallas import tpu as pltpu
from jax.sharding import PartitionSpec as P

HEADS = 16
KV_HEADS = 4
HEAD_DIM = 64
INNER = 2048
STATE = 16
DT_RANK = 64
CONV = 4
WINDOW = 32
EPSILON = 1e-06
LANES = 128
BLOCK = 16
RESET = 1e30

F32 = jnp.float32
BF16 = jnp.bfloat16
VMEM = pl.BlockSpec(memory_space=pltpu.VMEM)
SMEM = pl.BlockSpec(memory_space=pltpu.SMEM)
ANY = pl.BlockSpec(memory_space=pl.ANY)


def params(mib):
    return pltpu.CompilerParams(vmem_limit_bytes=mib << 20)


def dot_nt(a, b):
    return lax.dot_general(a, b, (((1,), (1,)), ((), ())), preferred_element_type=F32)


def bounds(len_ref, prompts):
    starts, ends = [], []
    at = 0
    for p in range(prompts):
        starts.append(at)
        at = at + len_ref[0, p]
        ends.append(at)
    return starts, ends


def first_row_of(position, starts, prompts):
    first = jnp.zeros_like(position)
    for p in range(1, prompts):
        first = jnp.where(position >= starts[p], starts[p], first)
    return first


def interleave(tokens, which):
    out = []
    for at in range(0, tokens.shape[1], LANES):
        wide = min(LANES, tokens.shape[1] - at)
        row = lax.broadcasted_iota(jnp.int32, (wide, 2 * wide), 0)
        column = lax.broadcasted_iota(jnp.int32, (wide, 2 * wide), 1)
        pick = jnp.where(column == 2 * row + which, 1.0, 0.0).astype(BF16)
        out.append(
            jnp.dot(tokens[:, at : at + wide], pick, preferred_element_type=F32).astype(BF16)
        )
    return jnp.concatenate(out, axis=1)


def last_rows(shape, depth, starts, ends):
    row = lax.broadcasted_iota(jnp.int32, shape, 0)
    position = lax.broadcasted_iota(jnp.int32, shape, 1)
    hit = jnp.zeros(shape, F32)
    for p in range(len(starts)):
        here = (row >= p * depth) & (row < (p + 1) * depth) & (position >= starts[p])
        hit = jnp.where(here & (position - row == ends[p] - (p + 1) * depth), 1.0, hit)
    return hit.astype(BF16)


def sigmoid(x):
    return 0.5 * jnp.tanh(0.5 * x) + 0.5


def mix_kernel(
    prompts,
    len_ref,
    tokens_hbm,
    inner_hbm,
    conv_ref,
    scan_ref,
    partial_ref,
    mixed_ref,
    tail_ref,
    tokens_ref,
    inner_ref,
    raw_ref,
    sems,
):
    tokens_copy = pltpu.make_async_copy(tokens_hbm, tokens_ref, sems.at[0])
    inner_copy = pltpu.make_async_copy(inner_hbm, inner_ref, sems.at[1])
    tokens_copy.start()
    inner_copy.start()
    rows, width = tokens_ref.shape
    channels = inner_ref.shape[2]
    starts, ends = bounds(len_ref, prompts)
    tokens_copy.wait()
    spread = interleave(tokens_ref[...], 0)
    inner_copy.wait()
    weight = inner_ref[...].reshape(2 * width, channels)
    raw = jnp.dot(spread, weight, preferred_element_type=F32).astype(BF16).astype(F32)
    raw_ref[pl.ds(0, 8), :] = jnp.zeros((8, channels), F32)
    raw_ref[pl.ds(8, rows), :] = raw
    position = lax.broadcasted_iota(jnp.int32, (rows, 1), 0)
    offset = position - first_row_of(position, starts, prompts)
    total = raw * conv_ref[CONV - 1 : CONV, :]
    for lag in range(1, CONV):
        shifted = raw_ref[pl.ds(8 - lag, rows), :]
        shifted = jnp.where(offset >= lag, shifted, 0.0)
        total = total + shifted * conv_ref[CONV - 1 - lag : CONV - lag, :]
    mixed = (total * sigmoid(total)).astype(BF16)
    mixed_ref[...] = mixed
    partial_ref[...] = dot_nt(scan_ref[...], mixed)
    pick = last_rows((8, rows), CONV - 1, starts, ends)
    tail_ref[...] = jnp.dot(pick, raw.astype(BF16), preferred_element_type=F32)


def attend_kernel(
    prompts,
    len_ref,
    tokens_ref,
    query_ref,
    key_ref,
    value_ref,
    inner_hbm,
    tail_ref,
    prompt_ref,
    owner_ref,
    slot_ref,
    attended_ref,
    square_ref,
    gate_ref,
    packed_ref,
    inner_ref,
    request_ref,
    sem,
):
    inner_copy = pltpu.make_async_copy(inner_hbm, inner_ref, sem)
    inner_copy.start()
    rows, width = tokens_ref.shape
    channels = inner_ref.shape[2]
    features = query_ref.shape[1]
    group = features // HEAD_DIM
    starts, ends = bounds(len_ref, prompts)
    tokens = tokens_ref[...]
    queries = jnp.dot(tokens, query_ref[...], preferred_element_type=F32).astype(BF16)
    keys = dot_nt(tokens, jnp.concatenate([key_ref[...]] * group, axis=0)).astype(BF16)
    values = dot_nt(tokens, jnp.concatenate([value_ref[...]] * group, axis=0)).astype(BF16)
    at_row = lax.broadcasted_iota(jnp.int32, (rows, rows), 0)
    at_column = lax.broadcasted_iota(jnp.int32, (rows, rows), 1)
    row_first = first_row_of(at_row, starts, prompts)
    allowed = (at_column <= at_row) & (at_row - at_column < WINDOW) & (at_column >= row_first)
    head_of = lax.broadcasted_iota(jnp.int32, (rows, features), 1) // HEAD_DIM
    zero = jnp.zeros((), BF16)
    attended = jnp.zeros((rows, features), F32)
    for head in range(group):
        mine = head_of == head
        scores = dot_nt(queries, jnp.where(mine, keys, zero)) * HEAD_DIM ** (-0.5)
        scores = jnp.where(allowed, scores, -1e30)
        top = jnp.max(scores, axis=1, keepdims=True)
        expons = jnp.exp(scores - top)
        weights = expons * (1.0 / jnp.sum(expons, axis=1, keepdims=True))
        attended = attended + jnp.dot(
            weights.astype(BF16), jnp.where(mine, values, zero), preferred_element_type=F32
        )
    attended_ref[...] = attended
    ones = jnp.ones((8, features), BF16)
    square_ref[...] = dot_nt(ones, (attended * attended).astype(BF16))
    lane = lax.broadcasted_iota(jnp.int32, (rows, LANES), 1)
    both = jnp.where(lane < HEAD_DIM, keys[:, :LANES], values[:, :LANES])
    pick = last_rows((prompts * WINDOW, rows), WINDOW, starts, ends)
    packed_ref[: prompts * WINDOW, :] = jnp.dot(pick, both, preferred_element_type=F32).astype(
        BF16
    )
    request_ref[...] = jnp.zeros(request_ref.shape, F32)
    requests = owner_ref.shape[1]
    request_ref[0:1, 0:requests] = owner_ref[...].astype(F32)
    request_ref[1:2, 0:requests] = slot_ref[...].astype(F32)
    request_ref[2:3, 0:requests] = prompt_ref[...].astype(F32)
    base = prompts * WINDOW
    for tile in range(channels // LANES):
        tail = tail_ref[:, tile * LANES : (tile + 1) * LANES]
        extra = request_ref[...] if tile == 0 else jnp.zeros((8, LANES), F32)
        packed_ref[base + 16 * tile : base + 16 * (tile + 1), :] = jnp.concatenate(
            [tail, extra], axis=0
        ).astype(BF16)
    inner_copy.wait()
    spread = interleave(tokens, 1)
    gate_ref[...] = jnp.dot(
        spread, inner_ref[...].reshape(2 * width, channels), preferred_element_type=F32
    ).astype(BF16)


def scan_kernel(
    prompts,
    len_ref,
    own_ref,
    other_ref,
    mixed_ref,
    gate_ref,
    step_weight_ref,
    step_bias_ref,
    rate_ref,
    skip_ref,
    early_ref,
    square_ref,
    gated_ref,
    sums_ref,
    payload_ref,
    decay_ref,
    input_ref,
    partial_ref,
    in_map_ref,
    out_map_ref,
    begin_ref,
    final_ref,
):
    rows, channels = mixed_ref.shape
    blocks = rows // BLOCK
    starts, ends = bounds(len_ref, prompts)
    projected = own_ref[...] + other_ref[...]
    low = projected[:DT_RANK, :].T.astype(BF16)
    pre = jnp.dot(low, step_weight_ref[...], preferred_element_type=F32) + step_bias_ref[...]
    step = jnp.maximum(pre, 0.0) + jnp.log1p(jnp.exp(-jnp.abs(pre)))
    position = lax.broadcasted_iota(jnp.int32, (rows, 1), 0)
    is_first = position == 0
    for p in range(1, prompts):
        is_first = is_first | (position == starts[p])
    decay_ref[...] = jnp.where(is_first, RESET, step)
    input_ref[...] = step * mixed_ref[...].astype(F32)
    for block in range(blocks):
        columns = slice(block * BLOCK, (block + 1) * BLOCK)
        in_map_ref[block, :, 0:BLOCK] = projected[DT_RANK : DT_RANK + STATE, columns]
        out_map_ref[block, :, 0:BLOCK] = projected[DT_RANK + STATE :, columns]
    rate = rate_ref[...] * (-math.log2(math.e))

    def advance(state, block, index):
        at = pl.multiple_of(block * BLOCK, BLOCK) + index
        decay = jnp.exp2(decay_ref[pl.ds(at, 1), :] * rate)
        entering = in_map_ref[block, :, index : index + 1] * input_ref[pl.ds(at, 1), :]
        return state * decay + entering

    def step_block(block, state):
        begin_ref[block] = state
        for index in range(BLOCK):
            state = advance(state, block, index)
            leaving = out_map_ref[block, :, index : index + 1] * state
            at = pl.multiple_of(block * BLOCK * 8, BLOCK * 8) + 8 * index
            half = leaving[:8, :] + leaving[8:, :]
            for tile in range(channels // LANES):
                partial_ref[tile, pl.ds(at, 8), :] = half[:, tile * LANES : (tile + 1) * LANES]
        return state

    state = lax.fori_loop(0, blocks, step_block, jnp.zeros((STATE, channels), F32))
    for p in range(prompts):
        if p < prompts - 1:
            last = ends[p] - 1
            block = last // BLOCK
            final_ref[...] = begin_ref[block]

            def again(index, _, block=block):
                at = block * BLOCK + index
                decay = jnp.exp2(decay_ref[pl.ds(at, 1), :] * rate)
                lane = lax.broadcasted_iota(jnp.int32, (STATE, LANES), 1)
                column = jnp.sum(
                    jnp.where(lane == index, in_map_ref[block], 0.0), axis=1, keepdims=True
                )
                entering = column * input_ref[pl.ds(at, 1), :]
                final_ref[...] = final_ref[...] * decay + entering
                return 0

            lax.fori_loop(0, last - block * BLOCK + 1, again, 0)
            final = final_ref[...].astype(BF16)
        else:
            final = state.astype(BF16)
        for tile in range(channels // LANES):
            at = (p * (channels // LANES) + tile) * STATE
            payload_ref[at : at + STATE, :] = final[:, tile * LANES : (tile + 1) * LANES]
    base = prompts * channels // LANES * STATE
    payload_ref[base:, :] = early_ref[...]
    scanned = []
    for tile in range(channels // LANES):
        total = partial_ref[tile, pl.ds(0, rows, stride=8), :]
        for index in range(1, 8):
            total = total + partial_ref[tile, pl.ds(index, rows, stride=8), :]
        scanned.append(total)
    scanned = jnp.concatenate(scanned, axis=1)
    gate = gate_ref[...].astype(F32)
    gated = (scanned + skip_ref[...] * mixed_ref[...].astype(F32)) * (gate * sigmoid(gate))
    gated_ref[...] = gated
    ones = jnp.ones((8, channels), BF16)
    sums_ref[0:1, :] = square_ref[0:1, :]
    sums_ref[1:2, :] = dot_nt(ones, (gated * gated).astype(BF16))[0:1, :]


def finish_kernel(
    prompts,
    pieces,
    order,
    me_ref,
    attended_ref,
    gated_ref,
    own_ref,
    other_ref,
    attention_gain_ref,
    mamba_gain_ref,
    *refs,
):
    piece_refs = refs[:pieces]
    (
        attention_ref,
        mamba_ref,
        keyval_ref,
        state_ref,
        conv_ref,
        window_ref,
        tail_ref,
        pick_vmem,
        pick_smem,
        sem,
    ) = refs[pieces:]
    me = me_ref[0]
    slots = keyval_ref.shape[0]
    channels = state_ref.shape[2]
    tiles = channels // LANES
    state_rows = prompts * tiles * STATE
    early = state_rows + prompts * WINDOW
    where = []
    for piece in range(pieces):
        for block in range(piece_refs[piece].shape[0]):
            where.append((piece, block))
    sources = len(where)

    key_rows, value_rows = [], []
    for index, (piece, block) in enumerate(where):
        request = piece_refs[piece][block, early : early + 16, :].astype(F32)
        mine = request[8:9, :] == me.astype(F32)
        key_rows.append(jnp.where(mine, request[9:10, :], -1.0))
        value_rows.append(request[10:11, :] + float(index * prompts))
    keys = jnp.concatenate(key_rows, axis=0).T
    values = jnp.concatenate(value_rows, axis=0).T
    lane = lax.broadcasted_iota(jnp.int32, (LANES, LANES), 1).astype(F32)
    total = jnp.zeros((LANES, LANES), F32)
    requests = LANES
    lane_ok = lax.broadcasted_iota(jnp.int32, (LANES, LANES), 0) < slots
    for index in range(sources):
        hit = (keys[:, index : index + 1] == lane) & lane_ok
        total = total + jnp.where(hit, values[:, index : index + 1], 0.0)
    pick = jnp.sum(total, axis=0, keepdims=True).astype(jnp.int32)
    pick_vmem[...] = pick
    pick_copy = pltpu.make_async_copy(pick_vmem, pick_smem, sem)
    pick_copy.start()

    for index, (piece, block) in enumerate(where):
        rows = piece_refs[piece]
        for p in range(prompts):
            at = state_rows + p * WINDOW
            pair = rows[block, at : at + WINDOW, :]
            window_ref[index * prompts + p, 0] = pair[:, :HEAD_DIM]
            window_ref[index * prompts + p, 1] = pair[:, HEAD_DIM:]
        for tile in range(tiles):
            tail_ref[index * 16 : (index + 1) * 16, tile * LANES : (tile + 1) * LANES] = rows[
                block, early + 16 * tile : early + 16 * (tile + 1), :
            ]

    sums = (own_ref[...] + other_ref[...])
    sums = jnp.concatenate([sums, jnp.zeros((6, sums.shape[1]), F32)], axis=0).T
    attention_scale = lax.rsqrt(sums[:, 0:1] / (HEADS * HEAD_DIM) + EPSILON)
    attention_ref[...] = (attended_ref[...] * attention_scale * attention_gain_ref[...]).astype(
        BF16
    )
    mamba_scale = lax.rsqrt(sums[:, 1:2] / INNER + EPSILON)
    mamba_ref[...] = (gated_ref[...] * mamba_scale * mamba_gain_ref[...]).astype(BF16)

    row = lax.broadcasted_iota(jnp.int32, (sources * 16, LANES), 0)
    depth = CONV - 1
    first = (pick // prompts) * 16 + (pick % prompts) * depth
    for tap in range(depth):
        hot = jnp.where(row == first + tap, 1.0, 0.0).T.astype(BF16)
        conv_ref[tap] = jnp.dot(hot[:slots, :], tail_ref[...], preferred_element_type=F32).astype(
            BF16
        )

    pick_copy.wait()

    def deliver(slot, _):
        wanted = pick_smem[0, slot]
        keyval_ref[slot] = window_ref[wanted]
        index = wanted // prompts
        p = wanted - index * prompts
        at = 0
        for piece in range(pieces):
            count = piece_refs[piece].shape[0]

            @pl.when((index >= at) & (index < at + count))
            def _(piece=piece, at=at):
                for tile in range(tiles):
                    start = pl.multiple_of((p * tiles + tile) * STATE, STATE)
                    state_ref[slot, :, tile * LANES : (tile + 1) * LANES] = piece_refs[piece][
                        index - at, pl.ds(start, STATE), :
                    ]

            at += count
        return 0

    lax.fori_loop(0, slots, deliver, 0)


def on_device(
    pr_size,
    tp_size,
    tokens,
    prompt_lengths,
    query_weight,
    key_weight,
    value_weight,
    attention_gain,
    inner_weight,
    conv_weight,
    scan_weight,
    step_weight,
    step_bias,
    mamba_rate,
    mamba_skip,
    mamba_gain,
    request_prompt,
    request_owner,
    request_slot,
):
    rows, width = tokens.shape
    prompts = prompt_lengths.shape[1]
    channels = inner_weight.shape[2]
    features = query_weight.shape[1]
    slots = request_owner.shape[0]
    tiles = channels // LANES

    def shape(dims, dtype=F32):
        return jax.ShapeDtypeStruct(dims, dtype)

    partial, mixed, tail = pl.pallas_call(
        functools.partial(mix_kernel, prompts),
        out_shape=(
            shape((DT_RANK + 2 * STATE, rows)),
            shape((rows, channels), BF16),
            shape((8, channels)),
        ),
        in_specs=[SMEM, ANY, ANY, VMEM, VMEM],
        out_specs=(VMEM, VMEM, VMEM),
        scratch_shapes=[
            pltpu.VMEM((rows, width), BF16),
            pltpu.VMEM((width, 2, channels), BF16),
            pltpu.VMEM((rows + 8, channels), F32),
            pltpu.SemaphoreType.DMA((2,)),
        ],
        compiler_params=params(32),
        name="mix",
    )(prompt_lengths, tokens, inner_weight, conv_weight, scan_weight.T)

    def swap(x, axis, size, bit):
        return lax.ppermute(x, axis, [(i, i ^ bit) for i in range(size)])

    near = swap(partial, "tp", tp_size, 1)
    early_rows = prompts * WINDOW + 16 * tiles
    attended, square, gate, early = pl.pallas_call(
        functools.partial(attend_kernel, prompts),
        out_shape=(
            shape((rows, features)),
            shape((8, rows)),
            shape((rows, channels), BF16),
            shape((early_rows, LANES), BF16),
        ),
        in_specs=[SMEM, VMEM, VMEM, VMEM, VMEM, ANY, VMEM, VMEM, VMEM, VMEM],
        out_specs=(VMEM, VMEM, VMEM, VMEM),
        scratch_shapes=[
            pltpu.VMEM((width, 2, channels), BF16),
            pltpu.VMEM((8, LANES), F32),
            pltpu.SemaphoreType.DMA,
        ],
        compiler_params=params(32),
        cost_estimate=pl.CostEstimate(
            flops=2 * rows * width * (features + channels), bytes_accessed=4 << 20, transcendentals=0
        ),
        name="attend",
    )(
        prompt_lengths,
        tokens,
        query_weight,
        key_weight.T,
        value_weight.T,
        inner_weight,
        tail,
        request_prompt[None],
        request_owner[None],
        request_slot[None],
    )
    pair = partial + near
    bit = 2
    while bit < tp_size // 2:
        pair = pair + swap(pair, "tp", tp_size, bit)
        bit *= 2
    far = swap(pair, "tp", tp_size, bit)

    payload_rows = prompts * tiles * STATE + early_rows
    gated, sums, payload = pl.pallas_call(
        functools.partial(scan_kernel, prompts),
        out_shape=(
            shape((rows, channels)),
            shape((2, rows)),
            shape((payload_rows, LANES), BF16),
        ),
        in_specs=[SMEM] + [VMEM] * 10,
        out_specs=(VMEM, VMEM, VMEM),
        scratch_shapes=[
            pltpu.VMEM((rows, channels), F32),
            pltpu.VMEM((rows, channels), F32),
            pltpu.VMEM((tiles, rows * 8, LANES), F32),
            pltpu.VMEM((rows // BLOCK, STATE, LANES), F32),
            pltpu.VMEM((rows // BLOCK, STATE, LANES), F32),
            pltpu.VMEM((rows // BLOCK, STATE, channels), F32),
            pltpu.VMEM((STATE, channels), F32),
        ],
        compiler_params=params(32),
        name="scan",
    )(
        prompt_lengths,
        pair,
        far,
        mixed,
        gate,
        step_weight,
        step_bias[None],
        mamba_rate,
        mamba_skip[None],
        early,
        square,
    )

    me = lax.axis_index("pr").astype(jnp.int32)
    pieces = [payload[None]]
    order = []
    bit = pr_size // 2
    while bit:
        held = pieces[0] if len(pieces) == 1 else jnp.concatenate(pieces, axis=0)
        pieces.append(swap(held, "pr", pr_size, bit))
        order.append(bit)
        bit //= 2
    bit = 1
    while bit < tp_size // 2:
        sums = sums + swap(sums, "tp", tp_size, bit)
        bit *= 2
    sums_far = swap(sums, "tp", tp_size, bit)

    attention_out, mamba_out, keyval, state, conv = pl.pallas_call(
        functools.partial(finish_kernel, prompts, len(pieces), tuple(order)),
        out_shape=(
            shape((rows, features), BF16),
            shape((rows, channels), BF16),
            shape((slots, 2, WINDOW, HEAD_DIM), BF16),
            shape((slots, STATE, channels), BF16),
            shape((CONV - 1, slots, channels), BF16),
        ),
        in_specs=[SMEM] + [VMEM] * (6 + len(pieces)),
        out_specs=(VMEM,) * 5,
        scratch_shapes=[
            pltpu.VMEM((pr_size * prompts, 2, WINDOW, HEAD_DIM), BF16),
            pltpu.VMEM((pr_size * 16, channels), BF16),
            pltpu.VMEM((1, LANES), jnp.int32),
            pltpu.SMEM((1, LANES), jnp.int32),
            pltpu.SemaphoreType.DMA,
        ],
        compiler_params=params(32),
        name="finish",
    )(
        me[None],
        attended,
        gated,
        sums,
        sums_far,
        attention_gain[None],
        mamba_gain[None],
        *pieces,
    )
    return (attention_out, mamba_out, keyval, state, conv.transpose(1, 0, 2))


def solution(mesh):
    return jax.shard_map(
        functools.partial(on_device, mesh.shape["pr"], mesh.shape["tp"]),
        mesh=mesh,
        in_specs=(
            P("pr", None),
            P("pr", None),
            P(None, "tp"),
            P(None, "tp"),
            P(None, "tp"),
            P("tp"),
            P(None, None, "tp"),
            P(None, "tp"),
            P("tp", None),
            P(None, "tp"),
            P("tp"),
            P(None, "tp"),
            P("tp"),
            P("tp"),
            P("pr"),
            P("pr"),
            P("pr"),
        ),
        out_specs=(
            P("pr", "tp"),
            P("pr", "tp"),
            P("pr", None, None, "tp"),
            P("pr", None, "tp"),
            P("pr", None, "tp"),
        ),
        check_vma=False,
    )
```

time: 421 us -> 44.3 us (0.11); the launches traced: 416 us -> 43.7 us
  other arithmetic: 227 us -> 0.06 us
  blocking collectives: 111 us -> 0 us
  local copies, waits for them, and re-layouts: 55.3 us -> 4.83 us
  Pallas kernels: 0 us -> 15.7 us
  between operations: 15.1 us -> 0.82 us
  starting transfers between devices: 0.04 us -> 11.6 us
  waiting for transfers between devices: 0.02 us -> 10.6 us
  matrix products: 5.32 us -> 0 us
    reduce_sum x260 -> x0, other arithmetic: 183 us -> none  [the longest x256 183 us: scan_block(): jnp.sum(output_rows[row_index][:, None] * state_now, axis=0)]
    all_gather x3 -> x0, blocking collectives: 92 us -> none  [the longest x1 30.8 us: on_device(): lax.all_gather(keyval, 'pr', axis=0, tiled=True)]
    mul x32 -> x0, other arithmetic: 34 us -> none  [scan_block(): step_rows[row_index] * mixed_rows[row_index]]
    slice x37 -> x0, local copies, waits for them, and re-layouts: 24 us -> none  [the longest x32 21.5 us: scan_block(): keep_rows[row_index]]
    dynamic_update_slice x32 -> x0, local copies, waits for them, and re-layouts: 19.4 us -> none  [on_device(): lax.scan(scan_block, (start_state, start_finals), (to_blocks(step_size),...]
    pallas_call x0 -> x4, Pallas kernels: none -> 15.7 us  [the longest x1 5.32 us: on_device(): pl.pallas_call(functools.partial(scan_kernel, prompts), out_shape=(shape(...]
    unnamed x1 -> x0, blocking collectives: 13.2 us -> none
    ppermute x0 -> x7, starting transfers between devices: none -> 11.6 us  [swap(): return lax.ppermute(x, axis, [(i, i ^ bit) for i in range(size)])]
  transfers between devices with their start and end apart: 1 -> 7, of which waited for: 0 -> 5; matrix products, arithmetic and copies ran while one was open for 2% -> 0% of each run, Pallas kernels for 0% -> 7%
where the time goes in v1:
time: 44.3 us; the launch traced here: 43.7 us
  Pallas kernels  15.7 us (35%)
  starting transfers between devices  11.6 us (26%)
  waiting for transfers between devices  10.6 us (24%)
  local copies, waits for them, and re-layouts  4.83 us (11%)
  between operations  0.82 us (2%)
    ppermute x7, starting transfers between devices, swap(): return lax.ppermute(x, axis, [(i, i ^ bit) for i in range(size)])  11.6 us
    ppermute x7, waiting for transfers between devices, swap(): return lax.ppermute(x, axis, [(i, i ^ bit) for i in range(size)])  10.6 us
    pallas_call x1, Pallas kernels, on_device(): pl.pallas_call(functools.partial(scan_kernel, prompts), out_shape=(shape(...  5.32 us
    unnamed x34, local copies, waits for them, and re-layouts  4.83 us
    pallas_call x1, Pallas kernels, on_device(): pl.pallas_call(functools.partial(finish_kernel, prompts, len(pieces), tup...  4.67 us
    pallas_call x1, Pallas kernels, on_device(): pl.pallas_call(functools.partial(attend_kernel, prompts), out_shape=(shap...  3.16 us
    pallas_call x1, Pallas kernels, on_device(): pl.pallas_call(functools.partial(mix_kernel, prompts), out_shape=(shape((...  2.58 us
  transfers between devices with their start and end apart: 7, of which 5 were waited for; matrix products, arithmetic and copies ran while one was open for 0% of the time, Pallas kernels for 7%

profile of v1, /device:TPU:0, one launch (start us, length us, event | category | flops | bytes accessed | tf_op | source)
XLA Modules:
  0.0 43.7 jit_solution(13150863583256867829)
XLA Ops:
  0.7 1.5 %copy-done = bf16[896,2,512]{2,1,0:T(2,128)(2,1)S(1)} copy-done((bf16[896,2,512]{2,1,0:T(2,128)(2,1)S(1)}, bf16[896,2,512]{2,1,0:T(2,128)(2,1)}, u32[]{:S(2)}) %copy-start) | copy-done | bytes 1835032
  2.2 1.0 %copy-done.1 = bf16[256,896]{1,0:T(8,128)(2,1)S(1)} copy-done((bf16[256,896]{1,0:T(8,128)(2,1)S(1)}, bf16[256,896]{1,0:T(8,128)(2,1)}, u32[]{:S(2)}) %copy-start.1) | copy-done | bytes 458776
  3.2 0.9 %copy-done.5 = bf16[512,96]{0,1:T(8,128)(2,1)S(1)} copy-done((bf16[512,96]{0,1:T(8,128)(2,1)S(1)}, bf16[512,96]{0,1:T(8,128)(2,1)}, u32[]{:S(2)}) %copy-start.5) | copy-done | bytes 98328
  4.1 0.7 %copy-done.8 = f32[4,512]{1,0:T(4,128)S(1)} copy-done((f32[4,512]{1,0:T(4,128)S(1)}, f32[4,512]{1,0:T(4,128)}, u32[]{:S(2)}) %copy-start.8) | copy-done | bytes 8216
  4.8 0.7 %copy-done.9 = s32[1,2]{1,0:T(1,128)S(1)} copy-done((s32[1,2]{1,0:T(1,128)S(1)}, s32[1,2]{1,0:T(1,128)}, u32[]{:S(2)}) %copy-start.9) | copy-done | bytes 32
  5.5 2.6 %mix.1 = (f32[96,256]{1,0:T(8,128)S(1)}, bf16[256,512]{1,0:T(8,128)(2,1)S(1)}, f32[8,512]{1,0:T(8,128)S(1)}) custom-call(s32[1,2]{1,0:T(1,128)S(1)} %copy-done.9, bf16[256,896]{1,0:T(8,128)(2,1)S(1)} %copy-done.1, bf16[896,2,512]{2,1,0:T(2,128)(2,1)S(1)} %copy-done, f32[4,512]{1,0:T(4,128)S(1)} %copy-done.8, bf16[96,512]{1,0:T(8,128)(2,1)S(1)} %bitcast.19), custom_call_target="tpu_custom_call" | custom-call | tf_op jit(solution)/shard_map/mix/pallas_call | solution.py:448
  8.0 0.0 copy-start.6
  8.1 0.0 copy-start.10
  8.1 0.0 copy-start.11
  8.1 0.5 %collective-permute-start = (f32[96,256]{1,0:T(8,128)S(1)}, f32[96,256]{1,0:T(8,128)S(1)}, u32[]{:S(2)}, u32[]{:S(2)}) collective-permute-start(f32[96,256]{1,0:T(8,128)S(1)} %get-tuple-element.22), channel_id=1, source_target_pairs={{0,1},{1,0},{2,3},{3,2},{4,5},{5,4},{6,7},{7,6},{8,9},{9,8},{10,11... | collective-permute-start | bytes 294920 | tf_op jit(solution)/shard_map/ppermute | solution.py:468
  8.6 0.9 %collective-permute-done = f32[96,256]{1,0:T(8,128)S(1)} collective-permute-done((f32[96,256]{1,0:T(8,128)S(1)}, f32[96,256]{1,0:T(8,128)S(1)}, u32[]{:S(2)}, u32[]{:S(2)}) %collective-permute-start) | collective-permute-done | bytes 98336 | tf_op jit(solution)/shard_map/ppermute | solution.py:468
  9.6 2.9 %collective-permute-start.1 = (f32[96,256]{1,0:T(8,128)S(1)}, f32[96,256]{1,0:T(8,128)S(1)}, u32[]{:S(2)}, u32[]{:S(2)}) collective-permute-start(f32[96,256]{1,0:T(8,128)S(1)} %add.6.own_ref), channel_id=1, source_target_pairs={{0,2},{1,3},{2,0},{3,1},{4,6},{5,7},{6,4},{7,5},{8,10},{9,11},{10,... | collective-permute-start | bytes 294920 | tf_op jit(solution)/shard_map/ppermute | solution.py:468
  12.5 3.2 %attend.1 = (f32[256,256]{1,0:T(8,128)S(1)}, f32[8,256]{1,0:T(8,128)S(1)}, bf16[256,512]{1,0:T(8,128)(2,1)S(1)}, bf16[128,128]{1,0:T(8,128)(2,1)S(1)}) custom-call(s32[1,2]{1,0:T(1,128)S(1)} %copy-done.9, bf16[256,896]{1,0:T(8,128)(2,1)S(1)} %copy-done.1, bf16[896,256]{1,0:T(8,128)(2,1)S(1)} %copy-done.2, bf16[64,896]{1,0:T(8,128)(2,1)S(1)} %bitcast.17, ...), custom_call_target="tpu_custom_call" | custom-call | flops 352321536 | bytes 4194304 | tf_op jit(solution)/shard_map/attend/pallas_call | solution.py:472
  15.7 5.3 %scan.1 = (f32[256,512]{1,0:T(8,128)S(1)}, f32[2,256]{1,0:T(2,128)S(1)}, bf16[256,128]{1,0:T(8,128)(2,1)S(1)}) custom-call(s32[1,2]{1,0:T(1,128)S(1)} %copy-done.9, f32[96,256]{1,0:T(8,128)S(1)} %add.6.own_ref, f32[96,256]{1,0:T(8,128)S(1)} %collective-permute-done.1.other_ref, bf16[256,512]{1,0:T(8,128)(2,1)S(1)} %get-tuple-element.23.mixed_ref, ...), custom_call_target="tpu_custom_call" | custom-call | tf_op jit(solution)/shard_map/scan/pallas_call | solution.py:512
  21.1 3.5 %collective-permute-start.4 = (bf16[1,256,128]{2,1,0:T(8,128)(2,1)S(1)}, bf16[1,256,128]{2,1,0:T(8,128)(2,1)S(1)}, u32[]{:S(2)}, u32[]{:S(2)}) collective-permute-start(bf16[1,256,128]{2,1,0:T(8,128)(2,1)S(1)} %bitcast.13), channel_id=1, source_target_pairs={{0,16},{4,20},{8,24},{12,28},{16,0},{20,4},{24,8},{28,12},{1,17},{... | collective-permute-start | bytes 196616 | tf_op jit(solution)/shard_map/ppermute | solution.py:468
  24.5 2.9 %collective-permute-done.4.refs_1_ = bf16[1,256,128]{2,1,0:T(8,128)(2,1)S(1)} collective-permute-done((bf16[1,256,128]{2,1,0:T(8,128)(2,1)S(1)}, bf16[1,256,128]{2,1,0:T(8,128)(2,1)S(1)}, u32[]{:S(2)}, u32[]{:S(2)}) %collective-permute-start.4) | collective-permute-done | bytes 65568 | tf_op jit(solution)/shard_map/ppermute | solution.py:468
  27.5 1.7 %collective-permute-start.5 = (bf16[2,256,128]{2,1,0:T(8,128)(2,1)S(1)}, bf16[2,256,128]{2,1,0:T(8,128)(2,1)S(1)}, u32[]{:S(2)}, u32[]{:S(2)}) collective-permute-start(bf16[2,256,128]{2,1,0:T(8,128)(2,1)S(1)} %pad_maximum_fusion.1), channel_id=1, source_target_pairs={{0,8},{4,12},{8,0},{12,4},{16,24},{20,28},{24,16},{28,20},{1,9},{5... | collective-permute-start | bytes 393224 | tf_op jit(solution)/shard_map/ppermute | solution.py:468
  29.2 3.3 %collective-permute-done.5.refs_2_ = bf16[2,256,128]{2,1,0:T(8,128)(2,1)S(1)} collective-permute-done((bf16[2,256,128]{2,1,0:T(8,128)(2,1)S(1)}, bf16[2,256,128]{2,1,0:T(8,128)(2,1)S(1)}, u32[]{:S(2)}, u32[]{:S(2)}) %collective-permute-start.5) | collective-permute-done | bytes 131104 | tf_op jit(solution)/shard_map/ppermute | solution.py:468
  32.6 1.7 %collective-permute-start.6 = (bf16[4,256,128]{2,1,0:T(8,128)(2,1)S(1)}, bf16[4,256,128]{2,1,0:T(8,128)(2,1)S(1)}, u32[]{:S(2)}, u32[]{:S(2)}) collective-permute-start(bf16[4,256,128]{2,1,0:T(8,128)(2,1)S(1)} %pad_maximum_fusion), channel_id=1, source_target_pairs={{0,4},{4,0},{8,12},{12,8},{16,20},{20,16},{24,28},{28,24},{1,5},{5... | collective-permute-start | bytes 786440 | tf_op jit(solution)/shard_map/ppermute | solution.py:468
  34.2 1.2 %collective-permute-done.2 = f32[2,256]{1,0:T(2,128)S(1)} collective-permute-done((f32[2,256]{1,0:T(2,128)S(1)}, f32[2,256]{1,0:T(2,128)S(1)}, u32[]{:S(2)}, u32[]{:S(2)}) %collective-permute-start.2) | collective-permute-done | bytes 2080 | tf_op jit(solution)/shard_map/ppermute | solution.py:468
  35.4 1.4 %collective-permute-start.3 = (f32[2,256]{1,0:T(2,128)S(1)}, f32[2,256]{1,0:T(2,128)S(1)}, u32[]{:S(2)}, u32[]{:S(2)}) collective-permute-start(f32[2,256]{1,0:T(2,128)S(1)} %add.7.own_ref), channel_id=1, source_target_pairs={{0,2},{1,3},{2,0},{3,1},{4,6},{5,7},{6,4},{7,5},{8,10},{9,11},{10,... | collective-permute-start | bytes 6152 | tf_op jit(solution)/shard_map/ppermute | solution.py:468
  36.7 2.2 %collective-permute-done.3.other_ref = f32[2,256]{1,0:T(2,128)S(1)} collective-permute-done((f32[2,256]{1,0:T(2,128)S(1)}, f32[2,256]{1,0:T(2,128)S(1)}, u32[]{:S(2)}, u32[]{:S(2)}) %collective-permute-start.3) | collective-permute-done | bytes 2080 | tf_op jit(solution)/shard_map/ppermute | solution.py:468
  39.0 0.0 collective-permute-done.6.refs_3_
  39.0 4.7 %finish.1 = (bf16[256,256]{1,0:T(8,128)(2,1)}, bf16[256,512]{1,0:T(8,128)(2,1)}, bf16[56,2,32,64]{3,2,1,0:T(8,128)(2,1)}, bf16[56,16,512]{2,1,0:T(8,128)(2,1)}, bf16[3,56,512]{2,1,0:T(8,128)(2,1)}) custom-call(s32[1]{0:T(128)} %bitcast.me_ref, f32[256,256]{1,0:T(8,128)S(1)} %get-tuple-element.21.attended_ref, f32[256,512]{1,0:T(8,128)S(1)} %get-tuple-element.27.gated_ref, ...), custom_call_target="tpu_custom_call" | custom-call | tf_op jit(solution)/shard_map/finish/pallas_call | solution.py:561
  (32 shorter events, 0.1 us)
Async XLA Ops:
  0.6 11.8 %copy-start.16 = (s32[56]{0:T(128)S(1)}, s32[56]{0:T(128)}, u32[]{:S(2)}) copy-start(s32[56]{0:T(128)} %param.33) | copy-start | bytes 676
  0.6 11.8 %copy-start.15 = (s32[56]{0:T(128)S(1)}, s32[56]{0:T(128)}, u32[]{:S(2)}) copy-start(s32[56]{0:T(128)} %param.32) | copy-start | bytes 676
  0.7 11.8 %copy-start.14 = (s32[56]{0:T(128)S(1)}, s32[56]{0:T(128)}, u32[]{:S(2)}) copy-start(s32[56]{0:T(128)} %param.31) | copy-start | bytes 676
  0.7 1.5 %copy-start = (bf16[896,2,512]{2,1,0:T(2,128)(2,1)S(1)}, bf16[896,2,512]{2,1,0:T(2,128)(2,1)}, u32[]{:S(2)}) copy-start(bf16[896,2,512]{2,1,0:T(2,128)(2,1)} %inner_hbm.3) | copy-start | bytes 5505028
  2.2 1.0 %copy-start.1 = (bf16[256,896]{1,0:T(8,128)(2,1)S(1)}, bf16[256,896]{1,0:T(8,128)(2,1)}, u32[]{:S(2)}) copy-start(bf16[256,896]{1,0:T(8,128)(2,1)} %tokens_ref.1) | copy-start | bytes 1376260
  3.2 0.9 %copy-start.5 = (bf16[512,96]{0,1:T(8,128)(2,1)S(1)}, bf16[512,96]{0,1:T(8,128)(2,1)}, u32[]{:S(2)}) copy-start(bf16[512,96]{0,1:T(8,128)(2,1)} %param.25) | copy-start | bytes 294916
  4.1 0.7 %copy-start.8 = (f32[4,512]{1,0:T(4,128)S(1)}, f32[4,512]{1,0:T(4,128)}, u32[]{:S(2)}) copy-start(f32[4,512]{1,0:T(4,128)} %conv_ref.1) | copy-start | bytes 24580
  4.8 0.7 %copy-start.9 = (s32[1,2]{1,0:T(1,128)S(1)}, s32[1,2]{1,0:T(1,128)}, u32[]{:S(2)}) copy-start(s32[1,2]{1,0:T(1,128)} %len_ref.5) | copy-start | bytes 28
  5.4 7.0 %copy-start.2 = (bf16[896,256]{1,0:T(8,128)(2,1)S(1)}, bf16[896,256]{1,0:T(8,128)(2,1)}, u32[]{:S(2)}) copy-start(bf16[896,256]{1,0:T(8,128)(2,1)} %query_ref.1) | copy-start | bytes 1376260
  5.5 7.0 %copy-start.3 = (bf16[896,64]{0,1:T(8,128)(2,1)S(1)}, bf16[896,64]{0,1:T(8,128)(2,1)}, u32[]{:S(2)}) copy-start(bf16[896,64]{0,1:T(8,128)(2,1)} %param.20) | copy-start | bytes 344068
  5.5 7.0 %copy-start.4 = (bf16[896,64]{0,1:T(8,128)(2,1)S(1)}, bf16[896,64]{0,1:T(8,128)(2,1)}, u32[]{:S(2)}) copy-start(bf16[896,64]{0,1:T(8,128)(2,1)} %param.21) | copy-start | bytes 344068
  8.0 7.7 %copy-start.6 = (bf16[64,512]{1,0:T(8,128)(2,1)S(1)}, bf16[64,512]{1,0:T(8,128)(2,1)}, u32[]{:S(2)}) copy-start(bf16[64,512]{1,0:T(8,128)(2,1)} %step_weight_ref.1) | copy-start | bytes 196612
  8.1 7.7 %copy-start.7 = (f32[16,512]{1,0:T(8,128)S(1)}, f32[16,512]{1,0:T(8,128)}, u32[]{:S(2)}) copy-start(f32[16,512]{1,0:T(8,128)} %rate_ref.1) | copy-start | bytes 98308
  8.1 7.7 %copy-start.10 = (f32[512]{0:T(512)S(1)}, f32[512]{0:T(512)}, u32[]{:S(2)}) copy-start(f32[512]{0:T(512)} %param.27) | copy-start | bytes 6148
  8.1 7.7 %copy-start.11 = (f32[512]{0:T(512)S(1)}, f32[512]{0:T(512)}, u32[]{:S(2)}) copy-start(f32[512]{0:T(512)} %param.29) | copy-start | bytes 6148
  8.1 1.5 %collective-permute-start = (f32[96,256]{1,0:T(8,128)S(1)}, f32[96,256]{1,0:T(8,128)S(1)}, u32[]{:S(2)}, u32[]{:S(2)}) collective-permute-start(f32[96,256]{1,0:T(8,128)S(1)} %get-tuple-element.22), channel_id=1, source_target_pairs={{0,1},{1,0},{2,3},{3,2},{4,5},{5,4},{6,7},{7,6},{8,9},{9,8},{10,11... | collective-permute-start | bytes 294920 | tf_op jit(solution)/shard_map/ppermute | solution.py:468
  9.6 6.1 %collective-permute-start.1 = (f32[96,256]{1,0:T(8,128)S(1)}, f32[96,256]{1,0:T(8,128)S(1)}, u32[]{:S(2)}, u32[]{:S(2)}) collective-permute-start(f32[96,256]{1,0:T(8,128)S(1)} %add.6.own_ref), channel_id=1, source_target_pairs={{0,2},{1,3},{2,0},{3,1},{4,6},{5,7},{6,4},{7,5},{8,10},{9,11},{10,... | collective-permute-start | bytes 294920 | tf_op jit(solution)/shard_map/ppermute | solution.py:468
  12.5 26.5 %copy-start.12 = (f32[512]{0:T(512)S(1)}, f32[512]{0:T(512)}, u32[]{:S(2)}) copy-start(f32[512]{0:T(512)} %param.30) | copy-start | bytes 6148
  12.5 26.5 %copy-start.13 = (f32[256]{0:T(256)S(1)}, f32[256]{0:T(256)}, u32[]{:S(2)}) copy-start(f32[256]{0:T(256)} %param.22) | copy-start | bytes 3076
  21.1 6.4 %collective-permute-start.4 = (bf16[1,256,128]{2,1,0:T(8,128)(2,1)S(1)}, bf16[1,256,128]{2,1,0:T(8,128)(2,1)S(1)}, u32[]{:S(2)}, u32[]{:S(2)}) collective-permute-start(bf16[1,256,128]{2,1,0:T(8,128)(2,1)S(1)} %bitcast.13), channel_id=1, source_target_pairs={{0,16},{4,20},{8,24},{12,28},{16,0},{20,4},{24,8},{28,12},{1,17},{... | collective-permute-start | bytes 196616 | tf_op jit(solution)/shard_map/ppermute | solution.py:468
  27.5 5.0 %collective-permute-start.5 = (bf16[2,256,128]{2,1,0:T(8,128)(2,1)S(1)}, bf16[2,256,128]{2,1,0:T(8,128)(2,1)S(1)}, u32[]{:S(2)}, u32[]{:S(2)}) collective-permute-start(bf16[2,256,128]{2,1,0:T(8,128)(2,1)S(1)} %pad_maximum_fusion.1), channel_id=1, source_target_pairs={{0,8},{4,12},{8,0},{12,4},{16,24},{20,28},{24,16},{28,20},{1,9},{5... | collective-permute-start | bytes 393224 | tf_op jit(solution)/shard_map/ppermute | solution.py:468
  32.6 6.4 %collective-permute-start.6 = (bf16[4,256,128]{2,1,0:T(8,128)(2,1)S(1)}, bf16[4,256,128]{2,1,0:T(8,128)(2,1)S(1)}, u32[]{:S(2)}, u32[]{:S(2)}) collective-permute-start(bf16[4,256,128]{2,1,0:T(8,128)(2,1)S(1)} %pad_maximum_fusion), channel_id=1, source_target_pairs={{0,4},{4,0},{8,12},{12,8},{16,20},{20,16},{24,28},{28,24},{1,5},{5... | collective-permute-start | bytes 786440 | tf_op jit(solution)/shard_map/ppermute | solution.py:468
  34.2 1.2 %collective-permute-start.2 = (f32[2,256]{1,0:T(2,128)S(1)}, f32[2,256]{1,0:T(2,128)S(1)}, u32[]{:S(2)}, u32[]{:S(2)}) collective-permute-start(f32[2,256]{1,0:T(2,128)S(1)} %get-tuple-element.28), channel_id=1, source_target_pairs={{0,1},{1,0},{2,3},{3,2},{4,5},{5,4},{6,7},{7,6},{8,9},{9,8},{10,11... | collective-permute-start | bytes 6152 | tf_op jit(solution)/shard_map/ppermute | solution.py:468
  35.4 3.6 %collective-permute-start.3 = (f32[2,256]{1,0:T(2,128)S(1)}, f32[2,256]{1,0:T(2,128)S(1)}, u32[]{:S(2)}, u32[]{:S(2)}) collective-permute-start(f32[2,256]{1,0:T(2,128)S(1)} %add.7.own_ref), channel_id=1, source_target_pairs={{0,2},{1,3},{2,0},{3,1},{4,6},{5,7},{6,4},{7,5},{8,10},{9,11},{10,... | collective-permute-start | bytes 6152 | tf_op jit(solution)/shard_map/ppermute | solution.py:468

commit v2 on v1

--- a/solution.py
+++ b/solution.py
@@ -82,26 +82,35 @@
 
 def mix_kernel(
     prompts,
-    len_ref,
+    len_hbm,
     tokens_hbm,
     inner_hbm,
-    conv_ref,
-    scan_ref,
+    conv_hbm,
+    scan_hbm,
     partial_ref,
     mixed_ref,
     tail_ref,
+    len_ref,
     tokens_ref,
     inner_ref,
+    conv_ref,
+    scan_ref,
     raw_ref,
     sems,
 ):
     tokens_copy = pltpu.make_async_copy(tokens_hbm, tokens_ref, sems.at[0])
     inner_copy = pltpu.make_async_copy(inner_hbm, inner_ref, sems.at[1])
+    small_copies = [
+        pltpu.make_async_copy(len_hbm, len_ref, sems.at[2]),
+        pltpu.make_async_copy(conv_hbm, conv_ref, sems.at[3]),
+        pltpu.make_async_copy(scan_hbm, scan_ref, sems.at[4]),
+    ]
     tokens_copy.start()
     inner_copy.start()
+    for copy in small_copies:
+        copy.start()
     rows, width = tokens_ref.shape
     channels = inner_ref.shape[2]
-    starts, ends = bounds(len_ref, prompts)
     tokens_copy.wait()
     spread = interleave(tokens_ref[...], 0)
     inner_copy.wait()
@@ -109,6 +118,9 @@
     raw = jnp.dot(spread, weight, preferred_element_type=F32).astype(BF16).astype(F32)
     raw_ref[pl.ds(0, 8), :] = jnp.zeros((8, channels), F32)
     raw_ref[pl.ds(8, rows), :] = raw
+    for copy in small_copies:
+        copy.wait()
+    starts, ends = bounds(len_ref, prompts)
     position = lax.broadcasted_iota(jnp.int32, (rows, 1), 0)
     offset = position - first_row_of(position, starts, prompts)
     total = raw * conv_ref[CONV - 1 : CONV, :]
@@ -180,18 +192,29 @@
     packed_ref[: prompts * WINDOW, :] = jnp.dot(pick, both, preferred_element_type=F32).astype(
         BF16
     )
-    request_ref[...] = jnp.zeros(request_ref.shape, F32)
     requests = owner_ref.shape[1]
-    request_ref[0:1, 0:requests] = owner_ref[...].astype(F32)
-    request_ref[1:2, 0:requests] = slot_ref[...].astype(F32)
-    request_ref[2:3, 0:requests] = prompt_ref[...].astype(F32)
+    request_ref[...] = jnp.full(request_ref.shape, -1, jnp.int32)
+    request_ref[0:1, 0:requests] = owner_ref[...]
+    request_ref[1:2, 0:requests] = slot_ref[...]
+    request_ref[2:3, 0:requests] = prompt_ref[...]
+    owners = packed_ref.shape[0] - prompts * WINDOW - 8 * (channels // LANES)
+    owner = lax.broadcasted_iota(jnp.int32, (owners, LANES), 0) == request_ref[0:1, :]
+    slot = lax.broadcasted_iota(jnp.int32, (LANES, LANES), 0) == request_ref[1:2, :]
+    number = request_ref[2:3, :] + 1
+    filled = dot_nt(
+        jnp.where(owner, 1.0, 0.0).astype(BF16),
+        jnp.where(slot, number, 0).astype(F32).astype(BF16),
+    )
     base = prompts * WINDOW
-    for tile in range(channels // LANES):
-        tail = tail_ref[:, tile * LANES : (tile + 1) * LANES]
-        extra = request_ref[...] if tile == 0 else jnp.zeros((8, LANES), F32)
-        packed_ref[base + 16 * tile : base + 16 * (tile + 1), :] = jnp.concatenate(
-            [tail, extra], axis=0
+    for tile in range(0, channels // LANES, 2):
+        packed_ref[base + 8 * tile : base + 8 * (tile + 2), :] = jnp.concatenate(
+            [
+                tail_ref[:, tile * LANES : (tile + 1) * LANES],
+                tail_ref[:, (tile + 1) * LANES : (tile + 2) * LANES],
+            ],
+            axis=0,
         ).astype(BF16)
+    packed_ref[base + 8 * (channels // LANES) :, :] = filled.astype(BF16)
     inner_copy.wait()
     spread = interleave(tokens, 1)
     gate_ref[...] = jnp.dot(
@@ -301,77 +324,23 @@
     sums_ref[1:2, :] = dot_nt(ones, (gated * gated).astype(BF16))[0:1, :]
 
 
-def finish_kernel(
-    prompts,
-    pieces,
-    order,
-    me_ref,
+def join_kernel(held_ref, new_ref, own_ref, other_ref, joined_ref, sums_ref):
+    count = held_ref.shape[0]
+    joined_ref[:count] = held_ref[...]
+    joined_ref[count:] = new_ref[...]
+    sums_ref[...] = own_ref[...] + other_ref[...]
+
+
+def norm_kernel(
     attended_ref,
     gated_ref,
-    own_ref,
-    other_ref,
+    sums_ref,
     attention_gain_ref,
     mamba_gain_ref,
-    *refs,
+    attention_ref,
+    mamba_ref,
 ):
-    piece_refs = refs[:pieces]
-    (
-        attention_ref,
-        mamba_ref,
-        keyval_ref,
-        state_ref,
-        conv_ref,
-        window_ref,
-        tail_ref,
-        pick_vmem,
-        pick_smem,
-        sem,
-    ) = refs[pieces:]
-    me = me_ref[0]
-    slots = keyval_ref.shape[0]
-    channels = state_ref.shape[2]
-    tiles = channels // LANES
-    state_rows = prompts * tiles * STATE
-    early = state_rows + prompts * WINDOW
-    where = []
-    for piece in range(pieces):
-        for block in range(piece_refs[piece].shape[0]):
-            where.append((piece, block))
-    sources = len(where)
-
-    key_rows, value_rows = [], []
-    for index, (piece, block) in enumerate(where):
-        request = piece_refs[piece][block, early : early + 16, :].astype(F32)
-        mine = request[8:9, :] == me.astype(F32)
-        key_rows.append(jnp.where(mine, request[9:10, :], -1.0))
-        value_rows.append(request[10:11, :] + float(index * prompts))
-    keys = jnp.concatenate(key_rows, axis=0).T
-    values = jnp.concatenate(value_rows, axis=0).T
-    lane = lax.broadcasted_iota(jnp.int32, (LANES, LANES), 1).astype(F32)
-    total = jnp.zeros((LANES, LANES), F32)
-    requests = LANES
-    lane_ok = lax.broadcasted_iota(jnp.int32, (LANES, LANES), 0) < slots
-    for index in range(sources):
-        hit = (keys[:, index : index + 1] == lane) & lane_ok
-        total = total + jnp.where(hit, values[:, index : index + 1], 0.0)
-    pick = jnp.sum(total, axis=0, keepdims=True).astype(jnp.int32)
-    pick_vmem[...] = pick
-    pick_copy = pltpu.make_async_copy(pick_vmem, pick_smem, sem)
-    pick_copy.start()
-
-    for index, (piece, block) in enumerate(where):
-        rows = piece_refs[piece]
-        for p in range(prompts):
-            at = state_rows + p * WINDOW
-            pair = rows[block, at : at + WINDOW, :]
-            window_ref[index * prompts + p, 0] = pair[:, :HEAD_DIM]
-            window_ref[index * prompts + p, 1] = pair[:, HEAD_DIM:]
-        for tile in range(tiles):
-            tail_ref[index * 16 : (index + 1) * 16, tile * LANES : (tile + 1) * LANES] = rows[
-                block, early + 16 * tile : early + 16 * (tile + 1), :
-            ]
-
-    sums = (own_ref[...] + other_ref[...])
+    sums = sums_ref[...]
     sums = jnp.concatenate([sums, jnp.zeros((6, sums.shape[1]), F32)], axis=0).T
     attention_scale = lax.rsqrt(sums[:, 0:1] / (HEADS * HEAD_DIM) + EPSILON)
     attention_ref[...] = (attended_ref[...] * attention_scale * attention_gain_ref[...]).astype(
@@ -380,38 +349,140 @@
     mamba_scale = lax.rsqrt(sums[:, 1:2] / INNER + EPSILON)
     mamba_ref[...] = (gated_ref[...] * mamba_scale * mamba_gain_ref[...]).astype(BF16)
 
-    row = lax.broadcasted_iota(jnp.int32, (sources * 16, LANES), 0)
+
+def one_hot(hit):
+    return jnp.where(hit, 1.0, 0.0).astype(BF16)
+
+
+def deliver_kernel(
+    prompts,
+    me_ref,
+    held_ref,
+    new_ref,
+    keyval_hbm,
+    state_hbm,
+    conv_hbm,
+    keyval_ref,
+    state_ref,
+    conv_ref,
+    sems,
+):
+    me = me_ref[0]
+    slots, _, channels = state_ref.shape
+    tiles = channels // LANES
+    half = held_ref.shape[0]
+    sources = 2 * half
+    window_at = prompts * tiles * STATE
+    tail_at = window_at + prompts * WINDOW
+    table_at = tail_at + 8 * tiles
+    owners = held_ref.shape[1] - table_at
+
+    def rows_of(source, at, size):
+        ref, index = (held_ref, source) if source < half else (new_ref, source - half)
+        return ref[index, at : at + size, :]
+
+    owner = lax.broadcasted_iota(jnp.int32, (owners, LANES), 0)
+    pick = jnp.zeros((1, LANES), F32)
+    for source in range(sources):
+        filled = rows_of(source, table_at, owners).astype(F32)
+        filled = jnp.sum(jnp.where(owner == me, filled, 0.0), axis=0, keepdims=True)
+        pick = pick + jnp.where(filled > 0.5, filled + float(source * prompts - 1), 0.0)
+    pick = pick.astype(jnp.int32)
+
+    chunk = min(sources, 8)
+    picked_rows = slots * STATE
+    row = lax.broadcasted_iota(jnp.int32, (picked_rows, LANES), 0)
+    lane = lax.broadcasted_iota(jnp.int32, (picked_rows, LANES), 1)
+    spread = one_hot(row // STATE == lane)
+    span = chunk * prompts * STATE
+    row = lax.broadcasted_iota(jnp.int32, (picked_rows, span), 0)
+    lane = lax.broadcasted_iota(jnp.int32, (picked_rows, span), 1)
+    same = row % STATE == lane % STATE
+    states, windows, tails = None, None, None
+    wide = -(-slots // 16) * 16
+    row = lax.broadcasted_iota(jnp.int32, (wide, LANES), 0)
+    lane = lax.broadcasted_iota(jnp.int32, (wide, LANES), 1)
+    unit = one_hot(row == lane)
     depth = CONV - 1
-    first = (pick // prompts) * 16 + (pick % prompts) * depth
-    for tap in range(depth):
-        hot = jnp.where(row == first + tap, 1.0, 0.0).T.astype(BF16)
-        conv_ref[tap] = jnp.dot(hot[:slots, :], tail_ref[...], preferred_element_type=F32).astype(
-            BF16
+    for first in range(0, sources, chunk):
+        wanted = lax.broadcasted_iota(jnp.int32, (span, LANES), 0) // STATE + first * prompts
+        take = dot_nt(spread, one_hot(wanted == pick))
+        take = jnp.where(same, take, 0.0).astype(BF16)
+        table = []
+        for source in range(first, first + chunk):
+            for p in range(prompts):
+                at = p * tiles * STATE
+                table.append(
+                    jnp.concatenate(
+                        [
+                            rows_of(source, at + tile * STATE, STATE)
+                            for tile in range(tiles)
+                        ],
+                        axis=1,
+                    )
+                )
+        part = jnp.dot(take, jnp.concatenate(table, axis=0), preferred_element_type=F32)
+        states = part if states is None else states + part
+        table = []
+        for source in range(first, first + chunk):
+            for p in range(prompts):
+                at = window_at + p * WINDOW
+                table.append(
+                    jnp.concatenate(
+                        [
+                            rows_of(source, at, WINDOW // 2),
+                            rows_of(source, at + WINDOW // 2, WINDOW // 2),
+                        ],
+                        axis=1,
+                    )
+                )
+        part = jnp.dot(take, jnp.concatenate(table, axis=0), preferred_element_type=F32)
+        windows = part if windows is None else windows + part
+        table = []
+        for source in range(first, first + chunk):
+            table.append(
+                jnp.concatenate(
+                    [rows_of(source, tail_at + 8 * tile, 16) for tile in range(0, tiles, 2)],
+                    axis=1,
+                )
+            )
+        span_rows = chunk * 16
+        row = lax.broadcasted_iota(jnp.int32, (span_rows, LANES), 0)
+        local = pick - first * prompts
+        base = (local // prompts) * 16 + (local % prompts) * depth
+        hits = [one_hot(row == base + 8 * odd + tap) for odd in (0, 1) for tap in range(depth)]
+        hits = dot_nt(unit, jnp.concatenate(hits, axis=0)).astype(BF16)
+        hits = jnp.concatenate(
+            [hits[:, i * span_rows : (i + 1) * span_rows] for i in range(2 * depth)], axis=0
         )
-
-    pick_copy.wait()
-
-    def deliver(slot, _):
-        wanted = pick_smem[0, slot]
-        keyval_ref[slot] = window_ref[wanted]
-        index = wanted // prompts
-        p = wanted - index * prompts
-        at = 0
-        for piece in range(pieces):
-            count = piece_refs[piece].shape[0]
-
-            @pl.when((index >= at) & (index < at + count))
-            def _(piece=piece, at=at):
-                for tile in range(tiles):
-                    start = pl.multiple_of((p * tiles + tile) * STATE, STATE)
-                    state_ref[slot, :, tile * LANES : (tile + 1) * LANES] = piece_refs[piece][
-                        index - at, pl.ds(start, STATE), :
-                    ]
-
-            at += count
-        return 0
-
-    lax.fori_loop(0, slots, deliver, 0)
+        part = jnp.dot(hits, jnp.concatenate(table, axis=0), preferred_element_type=F32)
+        tails = part if tails is None else tails + part
+
+    state_ref[...] = states.astype(BF16).reshape(slots, STATE, channels)
+    state_copy = pltpu.make_async_copy(state_ref, state_hbm, sems.at[0])
+    state_copy.start()
+    windows = windows.astype(BF16).reshape(slots, WINDOW // 2, 2 * LANES)
+    for upper in range(2):
+        for kind in range(2):
+            at = upper * LANES + kind * HEAD_DIM
+            keyval_ref[:, kind, upper * WINDOW // 2 : (upper + 1) * WINDOW // 2, :] = windows[
+                :, :, at : at + HEAD_DIM
+            ]
+    keyval_copy = pltpu.make_async_copy(keyval_ref, keyval_hbm, sems.at[1])
+    keyval_copy.start()
+    for odd in range(2):
+        for tap in range(depth):
+            at = (odd * depth + tap) * wide
+            for pair in range(tiles // 2):
+                tile = 2 * pair + odd
+                conv_ref[tap, :, tile * LANES : (tile + 1) * LANES] = tails[
+                    at : at + slots, pair * LANES : (pair + 1) * LANES
+                ].astype(BF16)
+    conv_copy = pltpu.make_async_copy(conv_ref, conv_hbm, sems.at[2])
+    conv_copy.start()
+    state_copy.wait()
+    keyval_copy.wait()
+    conv_copy.wait()
 
 
 def on_device(
@@ -452,15 +523,18 @@
             shape((rows, channels), BF16),
             shape((8, channels)),
         ),
-        in_specs=[SMEM, ANY, ANY, VMEM, VMEM],
+        in_specs=[ANY] * 5,
         out_specs=(VMEM, VMEM, VMEM),
         scratch_shapes=[
+            pltpu.SMEM((1, prompts), jnp.int32),
             pltpu.VMEM((rows, width), BF16),
             pltpu.VMEM((width, 2, channels), BF16),
+            pltpu.VMEM(conv_weight.shape, F32),
+            pltpu.VMEM(scan_weight.shape[::-1], BF16),
             pltpu.VMEM((rows + 8, channels), F32),
-            pltpu.SemaphoreType.DMA((2,)),
+            pltpu.SemaphoreType.DMA((5,)),
         ],
-        compiler_params=params(32),
+        compiler_params=params(56),
         name="mix",
     )(prompt_lengths, tokens, inner_weight, conv_weight, scan_weight.T)
 
@@ -468,7 +542,8 @@
         return lax.ppermute(x, axis, [(i, i ^ bit) for i in range(size)])
 
     near = swap(partial, "tp", tp_size, 1)
-    early_rows = prompts * WINDOW + 16 * tiles
+    owners = -(-pr_size // 16) * 16
+    early_rows = prompts * WINDOW + 8 * tiles + owners
     attended, square, gate, early = pl.pallas_call(
         functools.partial(attend_kernel, prompts),
         out_shape=(
@@ -481,7 +556,7 @@
         out_specs=(VMEM, VMEM, VMEM, VMEM),
         scratch_shapes=[
             pltpu.VMEM((width, 2, channels), BF16),
-            pltpu.VMEM((8, LANES), F32),
+            pltpu.VMEM((8, LANES), jnp.int32),
             pltpu.SemaphoreType.DMA,
         ],
         compiler_params=params(32),
@@ -544,50 +619,54 @@
     )
 
     me = lax.axis_index("pr").astype(jnp.int32)
-    pieces = [payload[None]]
-    order = []
-    bit = pr_size // 2
-    while bit:
-        held = pieces[0] if len(pieces) == 1 else jnp.concatenate(pieces, axis=0)
-        pieces.append(swap(held, "pr", pr_size, bit))
-        order.append(bit)
-        bit //= 2
-    bit = 1
-    while bit < tp_size // 2:
-        sums = sums + swap(sums, "tp", tp_size, bit)
-        bit *= 2
-    sums_far = swap(sums, "tp", tp_size, bit)
-
-    attention_out, mamba_out, keyval, state, conv = pl.pallas_call(
-        functools.partial(finish_kernel, prompts, len(pieces), tuple(order)),
+    held = payload[None]
+    pr_bits = [1 << i for i in reversed(range((pr_size - 1).bit_length()))]
+    tp_bits = [1 << i for i in range((tp_size - 1).bit_length())]
+    for index in range(max(len(pr_bits) - 1, len(tp_bits))):
+        new = swap(held, "pr", pr_size, pr_bits[index]) if index < len(pr_bits) - 1 else None
+        other = swap(sums, "tp", tp_size, tp_bits[index]) if index < len(tp_bits) else None
+        if new is None:
+            sums = sums + other
+        elif other is None:
+            held = jnp.concatenate([held, new], axis=0)
+        else:
+            held, sums = pl.pallas_call(
+                join_kernel,
+                out_shape=(
+                    shape((2 * held.shape[0],) + held.shape[1:], BF16),
+                    shape(sums.shape),
+                ),
+                in_specs=[VMEM] * 4,
+                out_specs=(VMEM, VMEM),
+                name="join",
+            )(held, new, sums, other)
+    new = swap(held, "pr", pr_size, pr_bits[-1])
+    attention_out, mamba_out = pl.pallas_call(
+        norm_kernel,
+        out_shape=(shape((rows, features), BF16), shape((rows, channels), BF16)),
+        in_specs=[VMEM] * 5,
+        out_specs=(VMEM, VMEM),
+        cost_estimate=pl.CostEstimate(flops=1 << 24, bytes_accessed=2 << 20, transcendentals=0),
+        name="norm",
+    )(attended, gated, sums, attention_gain[None], mamba_gain[None])
+    keyval, state, conv = pl.pallas_call(
+        functools.partial(deliver_kernel, prompts),
         out_shape=(
-            shape((rows, features), BF16),
-            shape((rows, channels), BF16),
             shape((slots, 2, WINDOW, HEAD_DIM), BF16),
             shape((slots, STATE, channels), BF16),
             shape((CONV - 1, slots, channels), BF16),
         ),
-        in_specs=[SMEM] + [VMEM] * (6 + len(pieces)),
-        out_specs=(VMEM,) * 5,
+        in_specs=[SMEM, VMEM, VMEM],
+        out_specs=(ANY, ANY, ANY),
         scratch_shapes=[
-            pltpu.VMEM((pr_size * prompts, 2, WINDOW, HEAD_DIM), BF16),
-            pltpu.VMEM((pr_size * 16, channels), BF16),
-            pltpu.VMEM((1, LANES), jnp.int32),
-            pltpu.SMEM((1, LANES), jnp.int32),
-            pltpu.SemaphoreType.DMA,
+            pltpu.VMEM((slots, 2, WINDOW, HEAD_DIM), BF16),
+            pltpu.VMEM((slots, STATE, channels), BF16),
+            pltpu.VMEM((CONV - 1, slots, channels), BF16),
+            pltpu.SemaphoreType.DMA((3,)),
         ],
         compiler_params=params(32),
-        name="finish",
-    )(
-        me[None],
-        attended,
-        gated,
-        sums,
-        sums_far,
-        attention_gain[None],
-        mamba_gain[None],
-        *pieces,
-    )
+        name="deliver",
+    )(me[None], held, new)
     return (attention_out, mamba_out, keyval, state, conv.transpose(1, 0, 2))
 
 

time: 44.3 us -> 48.5 us (1.095); the launches traced: 43.7 us -> 48.5 us
  Pallas kernels: 15.7 us -> 20.7 us
  starting transfers between devices: 11.6 us -> 7.51 us
  waiting for transfers between devices: 10.6 us -> 12.8 us
  local copies, waits for them, and re-layouts: 4.83 us -> 5.73 us
  other arithmetic: 0.06 us -> 0.91 us
    ppermute x7, starting transfers between devices: 11.6 us -> 7.51 us  [swap(): return lax.ppermute(x, axis, [(i, i ^ bit) for i in range(size)])]
    pallas_call x1 -> x4, Pallas kernels: 4.67 us -> 7.44 us  [the longest x2 3.19 us: on_device(): pl.pallas_call(join_kernel, out_shape=(shape((2 * held.shape[0],) + held....]
    ppermute x7, waiting for transfers between devices: 10.6 us -> 12.8 us  [swap(): return lax.ppermute(x, axis, [(i, i ^ bit) for i in range(size)])]
    pallas_call x1, Pallas kernels: 2.58 us -> 3.75 us  [on_device(): pl.pallas_call(functools.partial(mix_kernel, prompts), out_shape=(shape((...]
    pallas_call x1, Pallas kernels: 5.32 us -> 6.32 us  [on_device(): pl.pallas_call(functools.partial(scan_kernel, prompts), out_shape=(shape(...]
    add x1, other arithmetic: 0.01 us -> 0.91 us  [on_device(): pair = partial + near]
    unnamed x34 -> x48, local copies, waits for them, and re-layouts: 4.83 us -> 5.73 us
  transfers between devices with their start and end apart: 7 -> 7, of which waited for: 5 -> 6; matrix products, arithmetic and copies ran while one was open for 0% -> 0% of each run, Pallas kernels for 7% -> 11%
where the time goes in v2:
time: 48.5 us
  Pallas kernels  20.7 us (43%)
  waiting for transfers between devices  12.8 us (26%)
  starting transfers between devices  7.51 us (15%)
  local copies, waits for them, and re-layouts  5.73 us (12%)
  other arithmetic  0.91 us (2%)
  between operations  0.87 us (2%)
    ppermute x7, waiting for transfers between devices, swap(): return lax.ppermute(x, axis, [(i, i ^ bit) for i in range(size)])  12.8 us
    ppermute x7, starting transfers between devices, swap(): return lax.ppermute(x, axis, [(i, i ^ bit) for i in range(size)])  7.51 us
    pallas_call x1, Pallas kernels, on_device(): pl.pallas_call(functools.partial(scan_kernel, prompts), out_shape=(shape(...  6.32 us
    unnamed x48, local copies, waits for them, and re-layouts  5.73 us
    pallas_call x1, Pallas kernels, on_device(): pl.pallas_call(functools.partial(mix_kernel, prompts), out_shape=(shape((...  3.75 us
    pallas_call x2, Pallas kernels, on_device(): pl.pallas_call(join_kernel, out_shape=(shape((2 * held.shape[0],) + held....  3.19 us
    pallas_call x1, Pallas kernels, on_device(): pl.pallas_call(functools.partial(attend_kernel, prompts), out_shape=(shap...  3.16 us
    pallas_call x1, Pallas kernels, on_device(): pl.pallas_call(norm_kernel, out_shape=(shape((rows, features), BF16), sha...  2.16 us
  transfers between devices with their start and end apart: 7, of which 6 were waited for; matrix products, arithmetic and copies ran while one was open for 0% of the time, Pallas kernels for 11%

profile of v2, /device:TPU:0, one launch (start us, length us, event | category | flops | bytes accessed | tf_op | source)
XLA Modules:
  0.0 48.5 jit_solution(3524179827661797147)
XLA Ops:
  0.7 3.7 %mix.1 = (f32[96,256]{1,0:T(8,128)}, bf16[256,512]{1,0:T(8,128)(2,1)}, f32[8,512]{1,0:T(8,128)}) custom-call(s32[1,2]{1,0:T(1,128)} %len_ref.3, bf16[256,896]{1,0:T(8,128)(2,1)} %tokens_ref.1, bf16[896,2,512]{2,1,0:T(2,128)(2,1)} %inner_hbm.3, f32[4,512]{1,0:T(4,128)} %conv_hbm.1, bf16[96,512]{1,0:T(8,128)(2,1)} %bitcast.22), custom_call_target="tpu_custom_call" | custom-call | tf_op jit(solution)/shard_map/mix/pallas_call | solution.py:519
  5.0 1.2 %collective-permute-done = f32[96,256]{1,0:T(8,128)S(1)} collective-permute-done((f32[96,256]{1,0:T(8,128)}, f32[96,256]{1,0:T(8,128)S(1)}, u32[]{:S(2)}, u32[]{:S(2)}) %collective-permute-start) | collective-permute-done | bytes 98336 | tf_op jit(solution)/shard_map/ppermute | solution.py:542
  6.2 0.9 %add.3.own_ref = f32[96,256]{1,0:T(8,128)S(1)} add(f32[96,256]{1,0:T(8,128)} %get-tuple-element.26, f32[96,256]{1,0:T(8,128)S(1)} %collective-permute-done) | non-fusion elementwise | flops 24576 | bytes 294912 | tf_op jit(solution)/shard_map/add | solution.py:579
  7.1 2.9 %collective-permute-start.1 = (f32[96,256]{1,0:T(8,128)S(1)}, f32[96,256]{1,0:T(8,128)S(1)}, u32[]{:S(2)}, u32[]{:S(2)}) collective-permute-start(f32[96,256]{1,0:T(8,128)S(1)} %add.3.own_ref), channel_id=1, source_target_pairs={{0,2},{1,3},{2,0},{3,1},{4,6},{5,7},{6,4},{7,5},{8,10},{9,11},{10,... | collective-permute-start | bytes 294920 | tf_op jit(solution)/shard_map/ppermute | solution.py:542
  10.1 1.0 %copy-done.3 = bf16[896,256]{1,0:T(8,128)(2,1)S(1)} copy-done((bf16[896,256]{1,0:T(8,128)(2,1)S(1)}, bf16[896,256]{1,0:T(8,128)(2,1)}, u32[]{:S(2)}) %copy-start.3) | copy-done | bytes 458776
  11.1 0.9 %copy-done.8 = bf16[896,64]{0,1:T(8,128)(2,1)S(1)} copy-done((bf16[896,64]{0,1:T(8,128)(2,1)S(1)}, bf16[896,64]{0,1:T(8,128)(2,1)}, u32[]{:S(2)}) %copy-start.8) | copy-done | bytes 114712
  12.0 0.7 %copy-done.12 = f32[8,512]{1,0:T(8,128)S(1)} copy-done((f32[8,512]{1,0:T(8,128)S(1)}, f32[8,512]{1,0:T(8,128)}, u32[]{:S(2)}) %copy-start.12) | copy-done | bytes 16408
  12.7 3.2 %attend.1 = (f32[256,256]{1,0:T(8,128)S(1)}, f32[8,256]{1,0:T(8,128)S(1)}, bf16[256,512]{1,0:T(8,128)(2,1)S(1)}, bf16[112,128]{1,0:T(8,128)(2,1)S(1)}) custom-call(s32[1,2]{1,0:T(1,128)S(1)} %copy-done.13, bf16[256,896]{1,0:T(8,128)(2,1)S(1)} %copy-done.1, bf16[896,256]{1,0:T(8,128)(2,1)S(1)} %copy-done.3, bf16[64,896]{1,0:T(8,128)(2,1)S(1)} %bitcast.13, ...), custom_call_target="tpu_custom_call" | custom-call | flops 352321536 | bytes 4194304 | tf_op jit(solution)/shard_map/attend/pallas_call | solution.py:547
  15.9 6.3 %scan.1 = (f32[256,512]{1,0:T(8,128)S(1)}, f32[2,256]{1,0:T(2,128)S(1)}, bf16[240,128]{1,0:T(8,128)(2,1)S(1)}) custom-call(s32[1,2]{1,0:T(1,128)S(1)} %copy-done.13, f32[96,256]{1,0:T(8,128)S(1)} %add.3.own_ref, f32[96,256]{1,0:T(8,128)S(1)} %collective-permute-done.1.other_ref, bf16[256,512]{1,0:T(8,128)(2,1)S(1)} %copy-done.4, ...), custom_call_target="tpu_custom_call" | custom-call | tf_op jit(solution)/shard_map/scan/pallas_call | solution.py:587
  22.3 0.8 %copy-done.2 = f32[256,512]{1,0:T(8,128)} copy-done((f32[256,512]{1,0:T(8,128)}, f32[256,512]{1,0:T(8,128)S(1)}, u32[]{:S(2)}) %copy-start.2) | copy-done | bytes 524312
  23.1 2.5 %collective-permute-start.2 = (bf16[1,240,128]{2,1,0:T(8,128)(2,1)S(1)}, bf16[1,240,128]{2,1,0:T(8,128)(2,1)S(1)}, u32[]{:S(2)}, u32[]{:S(2)}) collective-permute-start(bf16[1,240,128]{2,1,0:T(8,128)(2,1)S(1)} %bitcast.15), channel_id=1, source_target_pairs={{0,16},{4,20},{8,24},{12,28},{16,0},{20,4},{24,8},{28,12},{1,17},{... | collective-permute-start | bytes 184328 | tf_op jit(solution)/shard_map/ppermute | solution.py:542
  25.6 1.2 %collective-permute-done.3.other_ref = f32[2,256]{1,0:T(2,128)S(1)} collective-permute-done((f32[2,256]{1,0:T(2,128)S(1)}, f32[2,256]{1,0:T(2,128)S(1)}, u32[]{:S(2)}, u32[]{:S(2)}) %collective-permute-start.3) | collective-permute-done | bytes 2080 | tf_op jit(solution)/shard_map/ppermute | solution.py:542
  26.7 2.7 %collective-permute-done.2.new_ref = bf16[1,240,128]{2,1,0:T(8,128)(2,1)S(1)} collective-permute-done((bf16[1,240,128]{2,1,0:T(8,128)(2,1)S(1)}, bf16[1,240,128]{2,1,0:T(8,128)(2,1)S(1)}, u32[]{:S(2)}, u32[]{:S(2)}) %collective-permute-start.2) | collective-permute-done | bytes 61472 | tf_op jit(solution)/shard_map/ppermute | solution.py:542
  29.5 0.6 %copy-done.21 = bf16[1,240,128]{2,1,0:T(8,128)(2,1)} copy-done((bf16[1,240,128]{2,1,0:T(8,128)(2,1)}, bf16[1,240,128]{2,1,0:T(8,128)(2,1)S(1)}, u32[]{:S(2)}) %copy-start.21) | copy-done | bytes 61464
  30.1 1.5 %join.2 = (bf16[2,240,128]{2,1,0:T(8,128)(2,1)}, f32[2,256]{1,0:T(2,128)}) custom-call(bf16[1,240,128]{2,1,0:T(8,128)(2,1)} %bitcast.16, bf16[1,240,128]{2,1,0:T(8,128)(2,1)} %copy-done.21, f32[2,256]{1,0:T(2,128)} %copy-done.16, f32[2,256]{1,0:T(2,128)} %copy-done.22), custom_call_target="tpu_custom_call" | custom-call | tf_op jit(solution)/shard_map/join/pallas_call | solution.py:633
  32.3 3.3 %collective-permute-done.5.other_ref = f32[2,256]{1,0:T(2,128)S(1)} collective-permute-done((f32[2,256]{1,0:T(2,128)}, f32[2,256]{1,0:T(2,128)S(1)}, u32[]{:S(2)}, u32[]{:S(2)}) %collective-permute-start.5) | collective-permute-done | bytes 2080 | tf_op jit(solution)/shard_map/ppermute | solution.py:542
  35.6 1.1 %collective-permute-done.4.new_ref = bf16[2,240,128]{2,1,0:T(8,128)(2,1)S(1)} collective-permute-done((bf16[2,240,128]{2,1,0:T(8,128)(2,1)}, bf16[2,240,128]{2,1,0:T(8,128)(2,1)S(1)}, u32[]{:S(2)}, u32[]{:S(2)}) %collective-permute-start.4) | collective-permute-done | bytes 122912 | tf_op jit(solution)/shard_map/ppermute | solution.py:542
  36.7 0.6 %copy-done.20 = bf16[2,240,128]{2,1,0:T(8,128)(2,1)} copy-done((bf16[2,240,128]{2,1,0:T(8,128)(2,1)}, bf16[2,240,128]{2,1,0:T(8,128)(2,1)S(1)}, u32[]{:S(2)}) %copy-start.20) | copy-done | bytes 122904
  37.4 1.7 %join.3 = (bf16[4,240,128]{2,1,0:T(8,128)(2,1)}, f32[2,256]{1,0:T(2,128)}) custom-call(bf16[2,240,128]{2,1,0:T(8,128)(2,1)} %get-tuple-element.34.held_ref, bf16[2,240,128]{2,1,0:T(8,128)(2,1)} %copy-done.20, f32[2,256]{1,0:T(2,128)} %get-tuple-element.35.own_ref, f32[2,256]{1,0:T(2,128)} %copy-done.23), custom_call_target="tpu_custom_call" | custom-call | tf_op jit(solution)/shard_map/join/pallas_call | solution.py:633
  39.0 0.9 %collective-permute-start.6 = (bf16[4,240,128]{2,1,0:T(8,128)(2,1)}, bf16[4,240,128]{2,1,0:T(8,128)(2,1)S(1)}, u32[]{:S(2)}, u32[]{:S(2)}) collective-permute-start(bf16[4,240,128]{2,1,0:T(8,128)(2,1)} %get-tuple-element.39.held_ref), channel_id=1, source_target_pairs={{0,4},{4,0},{8,12},{12,8},{16,20},{20,16},{24,28},{28,24},{1,5},{5... | collective-permute-start | bytes 737288 | tf_op jit(solution)/shard_map/ppermute | solution.py:542
  39.9 2.2 %norm.1 = (bf16[256,256]{1,0:T(8,128)(2,1)}, bf16[256,512]{1,0:T(8,128)(2,1)}) custom-call(f32[256,256]{1,0:T(8,128)} %copy-done.5, f32[256,512]{1,0:T(8,128)} %copy-done.2, f32[2,256]{1,0:T(2,128)} %get-tuple-element.36.sums_ref, f32[1,256]{1,0:T(1,128)} %bitcast.24, f32[1,512]{1,0:T(1,128)} %bitcast.23), custom_call_target="tpu_custom_call" | custom-call | flops 16777216 | bytes 2097152 | tf_op jit(solution)/shard_map/norm/pallas_call | solution.py:644
  42.0 3.4 %collective-permute-done.6.new_ref = bf16[4,240,128]{2,1,0:T(8,128)(2,1)S(1)} collective-permute-done((bf16[4,240,128]{2,1,0:T(8,128)(2,1)}, bf16[4,240,128]{2,1,0:T(8,128)(2,1)S(1)}, u32[]{:S(2)}, u32[]{:S(2)}) %collective-permute-start.6) | collective-permute-done | bytes 245792 | tf_op jit(solution)/shard_map/ppermute | solution.py:542
  45.4 0.9 %copy-done.6 = bf16[4,240,128]{2,1,0:T(8,128)(2,1)S(1)} copy-done((bf16[4,240,128]{2,1,0:T(8,128)(2,1)S(1)}, bf16[4,240,128]{2,1,0:T(8,128)(2,1)}, u32[]{:S(2)}) %copy-start.6) | copy-done | bytes 245784
  46.4 2.1 %deliver.1 = (bf16[56,2,32,64]{3,2,1,0:T(8,128)(2,1)}, bf16[56,16,512]{2,1,0:T(8,128)(2,1)}, bf16[3,56,512]{2,1,0:T(8,128)(2,1)}) custom-call(s32[1]{0:T(128)} %bitcast.11.me_ref, bf16[4,240,128]{2,1,0:T(8,128)(2,1)S(1)} %copy-done.6, bf16[4,240,128]{2,1,0:T(8,128)(2,1)S(1)} %collective-permute-done.6.new_ref), custom_call_target="tpu_custom_call" | custom-call | tf_op jit(solution)/shard_map/deliver/pallas_call | solution.py:652
  (46 shorter events, 1.4 us)
Async XLA Ops:
  0.6 9.4 %copy-start.13 = (s32[1,2]{1,0:T(1,128)S(1)}, s32[1,2]{1,0:T(1,128)}, u32[]{:S(2)}) copy-start(s32[1,2]{1,0:T(1,128)} %len_ref.3) | copy-start | bytes 28
  0.6 9.4 %copy-start = (bf16[896,2,512]{2,1,0:T(2,128)(2,1)S(1)}, bf16[896,2,512]{2,1,0:T(2,128)(2,1)}, u32[]{:S(2)}) copy-start(bf16[896,2,512]{2,1,0:T(2,128)(2,1)} %inner_hbm.3) | copy-start | bytes 5505028
  0.7 9.4 %copy-start.1 = (bf16[256,896]{1,0:T(8,128)(2,1)S(1)}, bf16[256,896]{1,0:T(8,128)(2,1)}, u32[]{:S(2)}) copy-start(bf16[256,896]{1,0:T(8,128)(2,1)} %tokens_ref.1) | copy-start | bytes 1376260
  0.7 9.3 %copy-start.19 = (s32[56]{0:T(128)S(1)}, s32[56]{0:T(128)}, u32[]{:S(2)}) copy-start(s32[56]{0:T(128)} %param.33) | copy-start | bytes 676
  0.7 9.3 %copy-start.18 = (s32[56]{0:T(128)S(1)}, s32[56]{0:T(128)}, u32[]{:S(2)}) copy-start(s32[56]{0:T(128)} %param.32) | copy-start | bytes 676
  0.7 9.3 %copy-start.17 = (s32[56]{0:T(128)S(1)}, s32[56]{0:T(128)}, u32[]{:S(2)}) copy-start(s32[56]{0:T(128)} %param.31) | copy-start | bytes 676
  0.7 9.3 %copy-start.7 = (bf16[896,64]{0,1:T(8,128)(2,1)S(1)}, bf16[896,64]{0,1:T(8,128)(2,1)}, u32[]{:S(2)}) copy-start(bf16[896,64]{0,1:T(8,128)(2,1)} %param.20) | copy-start | bytes 344068
  4.5 11.4 %copy-start.4 = (bf16[256,512]{1,0:T(8,128)(2,1)S(1)}, bf16[256,512]{1,0:T(8,128)(2,1)}, u32[]{:S(2)}) copy-start(bf16[256,512]{1,0:T(8,128)(2,1)} %get-tuple-element.27.mixed_ref) | copy-start | bytes 786436
  4.5 11.4 %copy-start.11 = (f32[16,512]{1,0:T(8,128)S(1)}, f32[16,512]{1,0:T(8,128)}, u32[]{:S(2)}) copy-start(f32[16,512]{1,0:T(8,128)} %rate_ref.1) | copy-start | bytes 98308
  4.5 11.4 %copy-start.14 = (f32[512]{0:T(512)S(1)}, f32[512]{0:T(512)}, u32[]{:S(2)}) copy-start(f32[512]{0:T(512)} %param.27) | copy-start | bytes 6148
  4.5 11.4 %copy-start.15 = (f32[512]{0:T(512)S(1)}, f32[512]{0:T(512)}, u32[]{:S(2)}) copy-start(f32[512]{0:T(512)} %param.29) | copy-start | bytes 6148
  4.5 1.7 %collective-permute-start = (f32[96,256]{1,0:T(8,128)}, f32[96,256]{1,0:T(8,128)S(1)}, u32[]{:S(2)}, u32[]{:S(2)}) collective-permute-start(f32[96,256]{1,0:T(8,128)} %get-tuple-element.26), channel_id=1, source_target_pairs={{0,1},{1,0},{2,3},{3,2},{4,5},{5,4},{6,7},{7,6},{8,9},{9,8},{10,11... | collective-permute-start | bytes 294920 | tf_op jit(solution)/shard_map/ppermute | solution.py:542
  7.1 8.8 %collective-permute-start.1 = (f32[96,256]{1,0:T(8,128)S(1)}, f32[96,256]{1,0:T(8,128)S(1)}, u32[]{:S(2)}, u32[]{:S(2)}) collective-permute-start(f32[96,256]{1,0:T(8,128)S(1)} %add.3.own_ref), channel_id=1, source_target_pairs={{0,2},{1,3},{2,0},{3,1},{4,6},{5,7},{6,4},{7,5},{8,10},{9,11},{10,... | collective-permute-start | bytes 294920 | tf_op jit(solution)/shard_map/ppermute | solution.py:542
  12.7 3.2 %copy-start.9 = (bf16[64,512]{1,0:T(8,128)(2,1)S(1)}, bf16[64,512]{1,0:T(8,128)(2,1)}, u32[]{:S(2)}) copy-start(bf16[64,512]{1,0:T(8,128)(2,1)} %step_weight_ref.1) | copy-start | bytes 196612
  15.9 6.4 %copy-start.5 = (f32[256,256]{1,0:T(8,128)}, f32[256,256]{1,0:T(8,128)S(1)}, u32[]{:S(2)}) copy-start(f32[256,256]{1,0:T(8,128)S(1)} %get-tuple-element.25.attended_ref) | copy-start | bytes 786436
  23.1 6.4 %copy-start.10 = (bf16[240,128]{1,0:T(8,128)(2,1)}, bf16[240,128]{1,0:T(8,128)(2,1)S(1)}, u32[]{:S(2)}) copy-start(bf16[240,128]{1,0:T(8,128)(2,1)S(1)} %get-tuple-element.32) | copy-start | bytes 184324
  23.1 6.4 %copy-start.16 = (f32[2,256]{1,0:T(2,128)}, f32[2,256]{1,0:T(2,128)S(1)}, u32[]{:S(2)}) copy-start(f32[2,256]{1,0:T(2,128)S(1)} %get-tuple-element.33.own_ref) | copy-start | bytes 6148
  23.1 6.4 %collective-permute-start.2 = (bf16[1,240,128]{2,1,0:T(8,128)(2,1)S(1)}, bf16[1,240,128]{2,1,0:T(8,128)(2,1)S(1)}, u32[]{:S(2)}, u32[]{:S(2)}) collective-permute-start(bf16[1,240,128]{2,1,0:T(8,128)(2,1)S(1)} %bitcast.15), channel_id=1, source_target_pairs={{0,16},{4,20},{8,24},{12,28},{16,0},{20,4},{24,8},{28,12},{1,17},{... | collective-permute-start | bytes 184328 | tf_op jit(solution)/shard_map/ppermute | solution.py:542
  25.6 1.2 %collective-permute-start.3 = (f32[2,256]{1,0:T(2,128)S(1)}, f32[2,256]{1,0:T(2,128)S(1)}, u32[]{:S(2)}, u32[]{:S(2)}) collective-permute-start(f32[2,256]{1,0:T(2,128)S(1)} %get-tuple-element.33.own_ref), channel_id=1, source_target_pairs={{0,1},{1,0},{2,3},{3,2},{4,5},{5,4},{6,7},{7,6},{8,9},{9,8},{10,11... | collective-permute-start | bytes 6152 | tf_op jit(solution)/shard_map/ppermute | solution.py:542
  26.7 2.7 %copy-start.22 = (f32[2,256]{1,0:T(2,128)}, f32[2,256]{1,0:T(2,128)S(1)}, u32[]{:S(2)}) copy-start(f32[2,256]{1,0:T(2,128)S(1)} %collective-permute-done.3.other_ref) | copy-start | bytes 6148
  31.6 5.1 %collective-permute-start.4 = (bf16[2,240,128]{2,1,0:T(8,128)(2,1)}, bf16[2,240,128]{2,1,0:T(8,128)(2,1)S(1)}, u32[]{:S(2)}, u32[]{:S(2)}) collective-permute-start(bf16[2,240,128]{2,1,0:T(8,128)(2,1)} %get-tuple-element.34.held_ref), channel_id=1, source_target_pairs={{0,8},{4,12},{8,0},{12,4},{16,24},{20,28},{24,16},{28,20},{1,9},{5... | collective-permute-start | bytes 368648 | tf_op jit(solution)/shard_map/ppermute | solution.py:542
  31.8 3.8 %collective-permute-start.5 = (f32[2,256]{1,0:T(2,128)}, f32[2,256]{1,0:T(2,128)S(1)}, u32[]{:S(2)}, u32[]{:S(2)}) collective-permute-start(f32[2,256]{1,0:T(2,128)} %get-tuple-element.35.own_ref), channel_id=1, source_target_pairs={{0,2},{1,3},{2,0},{3,1},{4,6},{5,7},{6,4},{7,5},{8,10},{9,11},{10,... | collective-permute-start | bytes 6152 | tf_op jit(solution)/shard_map/ppermute | solution.py:542
  35.6 1.1 %copy-start.23 = (f32[2,256]{1,0:T(2,128)}, f32[2,256]{1,0:T(2,128)S(1)}, u32[]{:S(2)}) copy-start(f32[2,256]{1,0:T(2,128)S(1)} %collective-permute-done.5.other_ref) | copy-start | bytes 6148
  39.0 6.4 %collective-permute-start.6 = (bf16[4,240,128]{2,1,0:T(8,128)(2,1)}, bf16[4,240,128]{2,1,0:T(8,128)(2,1)S(1)}, u32[]{:S(2)}, u32[]{:S(2)}) collective-permute-start(bf16[4,240,128]{2,1,0:T(8,128)(2,1)} %get-tuple-element.39.held_ref), channel_id=1, source_target_pairs={{0,4},{4,0},{8,12},{12,8},{16,20},{20,16},{24,28},{28,24},{1,5},{5... | collective-permute-start | bytes 737288 | tf_op jit(solution)/shard_map/ppermute | solution.py:542
  (7 other events, 5.7 us)

commit v3 on v2

--- a/solution.py
+++ b/solution.py
@@ -26,6 +26,7 @@
 VMEM = pl.BlockSpec(memory_space=pltpu.VMEM)
 SMEM = pl.BlockSpec(memory_space=pltpu.SMEM)
 ANY = pl.BlockSpec(memory_space=pl.ANY)
+HBM = pl.BlockSpec(memory_space=pltpu.HBM)
 
 
 def params(mib):
@@ -523,7 +524,7 @@
             shape((rows, channels), BF16),
             shape((8, channels)),
         ),
-        in_specs=[ANY] * 5,
+        in_specs=[HBM] * 5,
         out_specs=(VMEM, VMEM, VMEM),
         scratch_shapes=[
             pltpu.SMEM((1, prompts), jnp.int32),
@@ -534,7 +535,7 @@
             pltpu.VMEM((rows + 8, channels), F32),
             pltpu.SemaphoreType.DMA((5,)),
         ],
-        compiler_params=params(56),
+        compiler_params=params(24),
         name="mix",
     )(prompt_lengths, tokens, inner_weight, conv_weight, scan_weight.T)
 
@@ -638,6 +639,7 @@
                 ),
                 in_specs=[VMEM] * 4,
                 out_specs=(VMEM, VMEM),
+                compiler_params=params(16),
                 name="join",
             )(held, new, sums, other)
     new = swap(held, "pr", pr_size, pr_bits[-1])
@@ -646,6 +648,7 @@
         out_shape=(shape((rows, features), BF16), shape((rows, channels), BF16)),
         in_specs=[VMEM] * 5,
         out_specs=(VMEM, VMEM),
+        compiler_params=params(16),
         cost_estimate=pl.CostEstimate(flops=1 << 24, bytes_accessed=2 << 20, transcendentals=0),
         name="norm",
     )(attended, gated, sums, attention_gain[None], mamba_gain[None])
@@ -657,7 +660,7 @@
             shape((CONV - 1, slots, channels), BF16),
         ),
         in_specs=[SMEM, VMEM, VMEM],
-        out_specs=(ANY, ANY, ANY),
+        out_specs=(HBM, HBM, HBM),
         scratch_shapes=[
             pltpu.VMEM((slots, 2, WINDOW, HEAD_DIM), BF16),
             pltpu.VMEM((slots, STATE, channels), BF16),

time: 48.5 us -> 42.2 us (0.87)
  Pallas kernels: 20.7 us -> 14.4 us
  starting transfers between devices: 7.51 us -> 8.91 us
  waiting for transfers between devices: 12.8 us -> 11.9 us
  other arithmetic: 0.91 us -> 0.01 us
    pallas_call x2, Pallas kernels: 3.19 us -> 0.03 us  [on_device(): pl.pallas_call(join_kernel, out_shape=(shape((2 * held.shape[0],) + held....]
    pallas_call x1, Pallas kernels: 3.75 us -> 2.27 us  [on_device(): pl.pallas_call(functools.partial(mix_kernel, prompts), out_shape=(shape((...]
    ppermute x7, starting transfers between devices: 7.51 us -> 8.91 us  [swap(): return lax.ppermute(x, axis, [(i, i ^ bit) for i in range(size)])]
    pallas_call x1, Pallas kernels: 2.16 us -> 1.03 us  [on_device(): pl.pallas_call(norm_kernel, out_shape=(shape((rows, features), BF16), sha...]
    add x1, other arithmetic: 0.91 us -> 0.01 us  [on_device(): pair = partial + near]
    ppermute x7, waiting for transfers between devices: 12.8 us -> 11.9 us  [swap(): return lax.ppermute(x, axis, [(i, i ^ bit) for i in range(size)])]
    pallas_call x1, Pallas kernels: 6.32 us -> 5.81 us  [on_device(): pl.pallas_call(functools.partial(scan_kernel, prompts), out_shape=(shape(...]
    unnamed x48 -> x40, local copies, waits for them, and re-layouts: 5.73 us -> 5.85 us
  transfers between devices with their start and end apart: 7 -> 7, of which waited for: 6 -> 6; matrix products, arithmetic and copies ran while one was open for 0% -> 0% of each run, Pallas kernels for 11% -> 10%
where the time goes in v3:
time: 42.2 us; the launch traced here: 41.9 us
  Pallas kernels  14.4 us (34%)
  waiting for transfers between devices  11.9 us (28%)
  starting transfers between devices  8.91 us (21%)
  local copies, waits for them, and re-layouts  5.85 us (14%)
  between operations  0.83 us (2%)
    ppermute x7, waiting for transfers between devices, swap(): return lax.ppermute(x, axis, [(i, i ^ bit) for i in range(size)])  11.9 us
    ppermute x7, starting transfers between devices, swap(): return lax.ppermute(x, axis, [(i, i ^ bit) for i in range(size)])  8.91 us
    unnamed x40, local copies, waits for them, and re-layouts  5.85 us
    pallas_call x1, Pallas kernels, on_device(): pl.pallas_call(functools.partial(scan_kernel, prompts), out_shape=(shape(...  5.81 us
    pallas_call x1, Pallas kernels, on_device(): pl.pallas_call(functools.partial(attend_kernel, prompts), out_shape=(shap...  3.16 us
    pallas_call x1, Pallas kernels, on_device(): pl.pallas_call(functools.partial(mix_kernel, prompts), out_shape=(shape((...  2.27 us
    pallas_call x1, Pallas kernels, on_device(): pl.pallas_call(functools.partial(deliver_kernel, prompts), out_shape=(sha...  2.08 us
    pallas_call x1, Pallas kernels, on_device(): pl.pallas_call(norm_kernel, out_shape=(shape((rows, features), BF16), sha...  1.03 us
  transfers between devices with their start and end apart: 7, of which 6 were waited for; matrix products, arithmetic and copies ran while one was open for 0% of the time, Pallas kernels for 10%

profile of v3, /device:TPU:0, one launch (start us, length us, event | category | flops | bytes accessed | tf_op | source)
XLA Modules:
  0.0 41.9 jit_solution(14837515780735318026)
XLA Ops:
  0.7 1.5 %copy-done = bf16[896,2,512]{2,1,0:T(2,128)(2,1)S(1)} copy-done((bf16[896,2,512]{2,1,0:T(2,128)(2,1)S(1)}, bf16[896,2,512]{2,1,0:T(2,128)(2,1)}, u32[]{:S(2)}) %copy-start) | copy-done | bytes 1835032
  2.2 1.0 %copy-done.2 = bf16[256,896]{1,0:T(8,128)(2,1)S(1)} copy-done((bf16[256,896]{1,0:T(8,128)(2,1)S(1)}, bf16[256,896]{1,0:T(8,128)(2,1)}, u32[]{:S(2)}) %copy-start.2) | copy-done | bytes 458776
  3.2 0.9 %copy-done.7 = bf16[512,96]{0,1:T(8,128)(2,1)S(1)} copy-done((bf16[512,96]{0,1:T(8,128)(2,1)S(1)}, bf16[512,96]{0,1:T(8,128)(2,1)}, u32[]{:S(2)}) %copy-start.7) | copy-done | bytes 98328
  4.1 0.7 %copy-done.10 = f32[4,512]{1,0:T(4,128)S(1)} copy-done((f32[4,512]{1,0:T(4,128)S(1)}, f32[4,512]{1,0:T(4,128)}, u32[]{:S(2)}) %copy-start.10) | copy-done | bytes 8216
  4.8 0.7 %copy-done.11 = s32[1,2]{1,0:T(1,128)S(1)} copy-done((s32[1,2]{1,0:T(1,128)S(1)}, s32[1,2]{1,0:T(1,128)}, u32[]{:S(2)}) %copy-start.11) | copy-done | bytes 32
  5.5 2.3 %mix.1 = (f32[96,256]{1,0:T(8,128)S(1)}, bf16[256,512]{1,0:T(8,128)(2,1)S(1)}, f32[8,512]{1,0:T(8,128)S(1)}) custom-call(s32[1,2]{1,0:T(1,128)S(1)} %copy-done.11, bf16[256,896]{1,0:T(8,128)(2,1)S(1)} %copy-done.2, bf16[896,2,512]{2,1,0:T(2,128)(2,1)S(1)} %copy-done, f32[4,512]{1,0:T(4,128)S(1)} %copy-done.10, bf16[96,512]{1,0:T(8,128)(2,1)S(1)} %bitcast.15), custom_call_target="tpu_custom_call" | custom-call | tf_op jit(solution)/shard_map/mix/pallas_call | solution.py:520
  7.7 0.0 copy-start.8
  7.8 0.5 %collective-permute-start = (f32[96,256]{1,0:T(8,128)S(1)}, f32[96,256]{1,0:T(8,128)S(1)}, u32[]{:S(2)}, u32[]{:S(2)}) collective-permute-start(f32[96,256]{1,0:T(8,128)S(1)} %get-tuple-element.26), channel_id=1, source_target_pairs={{0,1},{1,0},{2,3},{3,2},{4,5},{5,4},{6,7},{7,6},{8,9},{9,8},{10,11... | collective-permute-start | bytes 294920 | tf_op jit(solution)/shard_map/ppermute | solution.py:543
  8.3 0.9 %collective-permute-done = f32[96,256]{1,0:T(8,128)S(1)} collective-permute-done((f32[96,256]{1,0:T(8,128)S(1)}, f32[96,256]{1,0:T(8,128)S(1)}, u32[]{:S(2)}, u32[]{:S(2)}) %collective-permute-start) | collective-permute-done | bytes 98336 | tf_op jit(solution)/shard_map/ppermute | solution.py:543
  9.3 2.9 %collective-permute-start.1 = (f32[96,256]{1,0:T(8,128)S(1)}, f32[96,256]{1,0:T(8,128)S(1)}, u32[]{:S(2)}, u32[]{:S(2)}) collective-permute-start(f32[96,256]{1,0:T(8,128)S(1)} %add.3.own_ref), channel_id=1, source_target_pairs={{0,2},{1,3},{2,0},{3,1},{4,6},{5,7},{6,4},{7,5},{8,10},{9,11},{10,... | collective-permute-start | bytes 294920 | tf_op jit(solution)/shard_map/ppermute | solution.py:543
  12.3 1.0 %copy-done.4 = bf16[896,256]{1,0:T(8,128)(2,1)S(1)} copy-done((bf16[896,256]{1,0:T(8,128)(2,1)S(1)}, bf16[896,256]{1,0:T(8,128)(2,1)}, u32[]{:S(2)}) %copy-start.4) | copy-done | bytes 458776
  13.3 3.2 %attend.1 = (f32[256,256]{1,0:T(8,128)S(1)}, f32[8,256]{1,0:T(8,128)S(1)}, bf16[256,512]{1,0:T(8,128)(2,1)S(1)}, bf16[112,128]{1,0:T(8,128)(2,1)S(1)}) custom-call(s32[1,2]{1,0:T(1,128)S(1)} %copy-done.12, bf16[256,896]{1,0:T(8,128)(2,1)S(1)} %copy-done.3, bf16[896,256]{1,0:T(8,128)(2,1)S(1)} %copy-done.4, bf16[64,896]{1,0:T(8,128)(2,1)S(1)} %bitcast.13, ...), custom_call_target="tpu_custom_call" | custom-call | flops 352321536 | bytes 4194304 | tf_op jit(solution)/shard_map/attend/pallas_call | solution.py:548
  16.5 5.8 %scan.1 = (f32[256,512]{1,0:T(8,128)S(1)}, f32[2,256]{1,0:T(2,128)S(1)}, bf16[240,128]{1,0:T(8,128)(2,1)S(1)}) custom-call(s32[1,2]{1,0:T(1,128)S(1)} %copy-done.12, f32[96,256]{1,0:T(8,128)S(1)} %add.3.own_ref, f32[96,256]{1,0:T(8,128)S(1)} %collective-permute-done.1.other_ref, bf16[256,512]{1,0:T(8,128)(2,1)S(1)} %get-tuple-element.27.mixed_ref, ...), custom_call_target="tpu_custom_call" | custom-call | tf_op jit(solution)/shard_map/scan/pallas_call | solution.py:588
  22.3 2.1 %collective-permute-start.2 = (bf16[1,240,128]{2,1,0:T(8,128)(2,1)S(1)}, bf16[1,240,128]{2,1,0:T(8,128)(2,1)S(1)}, u32[]{:S(2)}, u32[]{:S(2)}) collective-permute-start(bf16[1,240,128]{2,1,0:T(8,128)(2,1)S(1)} %bitcast.16), channel_id=1, source_target_pairs={{0,16},{4,20},{8,24},{12,28},{16,0},{20,4},{24,8},{28,12},{1,17},{... | collective-permute-start | bytes 184328 | tf_op jit(solution)/shard_map/ppermute | solution.py:543
  24.4 1.2 %collective-permute-done.3.other_ref = f32[2,256]{1,0:T(2,128)S(1)} collective-permute-done((f32[2,256]{1,0:T(2,128)S(1)}, f32[2,256]{1,0:T(2,128)S(1)}, u32[]{:S(2)}, u32[]{:S(2)}) %collective-permute-start.3) | collective-permute-done | bytes 2080 | tf_op jit(solution)/shard_map/ppermute | solution.py:543
  25.6 2.8 %collective-permute-done.2.new_ref = bf16[1,240,128]{2,1,0:T(8,128)(2,1)S(1)} collective-permute-done((bf16[1,240,128]{2,1,0:T(8,128)(2,1)S(1)}, bf16[1,240,128]{2,1,0:T(8,128)(2,1)S(1)}, u32[]{:S(2)}, u32[]{:S(2)}) %collective-permute-start.2) | collective-permute-done | bytes 61472 | tf_op jit(solution)/shard_map/ppermute | solution.py:543
  28.3 0.3 collective-permute-start.4
  28.7 0.7 %collective-permute-start.5 = (f32[2,256]{1,0:T(2,128)S(1)}, f32[2,256]{1,0:T(2,128)S(1)}, u32[]{:S(2)}, u32[]{:S(2)}) collective-permute-start(f32[2,256]{1,0:T(2,128)S(1)} %get-tuple-element.35.own_ref), channel_id=1, source_target_pairs={{0,2},{1,3},{2,0},{3,1},{4,6},{5,7},{6,4},{7,5},{8,10},{9,11},{10,... | collective-permute-start | bytes 6152 | tf_op jit(solution)/shard_map/ppermute | solution.py:543
  29.4 2.9 %collective-permute-done.5.other_ref = f32[2,256]{1,0:T(2,128)S(1)} collective-permute-done((f32[2,256]{1,0:T(2,128)S(1)}, f32[2,256]{1,0:T(2,128)S(1)}, u32[]{:S(2)}, u32[]{:S(2)}) %collective-permute-start.5) | collective-permute-done | bytes 2080 | tf_op jit(solution)/shard_map/ppermute | solution.py:543
  32.3 1.0 %collective-permute-done.4.new_ref = bf16[2,240,128]{2,1,0:T(8,128)(2,1)S(1)} collective-permute-done((bf16[2,240,128]{2,1,0:T(8,128)(2,1)S(1)}, bf16[2,240,128]{2,1,0:T(8,128)(2,1)S(1)}, u32[]{:S(2)}, u32[]{:S(2)}) %collective-permute-start.4) | collective-permute-done | bytes 122912 | tf_op jit(solution)/shard_map/ppermute | solution.py:543
  33.3 2.4 %collective-permute-start.6 = (bf16[4,240,128]{2,1,0:T(8,128)(2,1)S(1)}, bf16[4,240,128]{2,1,0:T(8,128)(2,1)S(1)}, u32[]{:S(2)}, u32[]{:S(2)}) collective-permute-start(bf16[4,240,128]{2,1,0:T(8,128)(2,1)S(1)} %get-tuple-element.39.held_ref), channel_id=1, source_target_pairs={{0,4},{4,0},{8,12},{12,8},{16,20},{20,16},{24,28},{28,24},{1,5},{5... | collective-permute-start | bytes 737288 | tf_op jit(solution)/shard_map/ppermute | solution.py:543
  35.7 1.0 %norm.1 = (bf16[256,256]{1,0:T(8,128)(2,1)}, bf16[256,512]{1,0:T(8,128)(2,1)}) custom-call(f32[256,256]{1,0:T(8,128)S(1)} %get-tuple-element.25.attended_ref, f32[256,512]{1,0:T(8,128)S(1)} %get-tuple-element.31.gated_ref, f32[2,256]{1,0:T(2,128)S(1)} %get-tuple-element.36.sums_ref, f32[1,256]{1,0:T(1,128)S(1)} %bitcast.21, f32[1,512]{1,0:T(1,128)S(1)} %bitcast.20), custom_call_target="tpu_custom_call" | custom-call | flops 16777216 | bytes 2097152 | tf_op jit(solution)/shard_map/norm/pallas_call | solution.py:646
  36.7 3.1 %collective-permute-done.6.new_ref = bf16[4,240,128]{2,1,0:T(8,128)(2,1)S(1)} collective-permute-done((bf16[4,240,128]{2,1,0:T(8,128)(2,1)S(1)}, bf16[4,240,128]{2,1,0:T(8,128)(2,1)S(1)}, u32[]{:S(2)}, u32[]{:S(2)}) %collective-permute-start.6) | collective-permute-done | bytes 245792 | tf_op jit(solution)/shard_map/ppermute | solution.py:543
  39.8 2.1 %deliver.1 = (bf16[56,2,32,64]{3,2,1,0:T(8,128)(2,1)}, bf16[56,16,512]{2,1,0:T(8,128)(2,1)}, bf16[3,56,512]{2,1,0:T(8,128)(2,1)}) custom-call(s32[1]{0:T(128)} %bitcast.11.me_ref, bf16[4,240,128]{2,1,0:T(8,128)(2,1)S(1)} %get-tuple-element.39.held_ref, bf16[4,240,128]{2,1,0:T(8,128)(2,1)S(1)} %collective-permute-done.6.new_ref), custom_call_target="tpu_custom_call" | custom-call | tf_op jit(solution)/shard_map/deliver/pallas_call | solution.py:655
  (38 shorter events, 0.1 us)
Async XLA Ops:
  0.6 11.6 %copy-start.12 = (s32[1,2]{1,0:T(1,128)S(1)}, s32[1,2]{1,0:T(1,128)}, u32[]{:S(2)}) copy-start(s32[1,2]{1,0:T(1,128)} %len_ref.3) | copy-start | bytes 28
  0.6 11.5 %copy-start.18 = (s32[56]{0:T(128)S(1)}, s32[56]{0:T(128)}, u32[]{:S(2)}) copy-start(s32[56]{0:T(128)} %param.32) | copy-start | bytes 676
  0.7 11.5 %copy-start.17 = (s32[56]{0:T(128)S(1)}, s32[56]{0:T(128)}, u32[]{:S(2)}) copy-start(s32[56]{0:T(128)} %param.31) | copy-start | bytes 676
  0.7 1.5 %copy-start = (bf16[896,2,512]{2,1,0:T(2,128)(2,1)S(1)}, bf16[896,2,512]{2,1,0:T(2,128)(2,1)}, u32[]{:S(2)}) copy-start(bf16[896,2,512]{2,1,0:T(2,128)(2,1)} %inner_hbm.3) | copy-start | bytes 5505028
  2.2 1.0 %copy-start.2 = (bf16[256,896]{1,0:T(8,128)(2,1)S(1)}, bf16[256,896]{1,0:T(8,128)(2,1)}, u32[]{:S(2)}) copy-start(bf16[256,896]{1,0:T(8,128)(2,1)} %tokens_ref.1) | copy-start | bytes 1376260
  5.4 6.8 %copy-start.1 = (bf16[896,2,512]{2,1,0:T(2,128)(2,1)S(1)}, bf16[896,2,512]{2,1,0:T(2,128)(2,1)}, u32[]{:S(2)}) copy-start(bf16[896,2,512]{2,1,0:T(2,128)(2,1)} %inner_hbm.3) | copy-start | bytes 5505028
  5.5 6.8 %copy-start.3 = (bf16[256,896]{1,0:T(8,128)(2,1)S(1)}, bf16[256,896]{1,0:T(8,128)(2,1)}, u32[]{:S(2)}) copy-start(bf16[256,896]{1,0:T(8,128)(2,1)} %tokens_ref.1) | copy-start | bytes 1376260
  5.5 6.8 %copy-start.5 = (bf16[896,64]{0,1:T(8,128)(2,1)S(1)}, bf16[896,64]{0,1:T(8,128)(2,1)}, u32[]{:S(2)}) copy-start(bf16[896,64]{0,1:T(8,128)(2,1)} %param.20) | copy-start | bytes 344068
  5.5 6.8 %copy-start.6 = (bf16[896,64]{0,1:T(8,128)(2,1)S(1)}, bf16[896,64]{0,1:T(8,128)(2,1)}, u32[]{:S(2)}) copy-start(bf16[896,64]{0,1:T(8,128)(2,1)} %param.21) | copy-start | bytes 344068
  5.5 6.8 %copy-start.19 = (s32[56]{0:T(128)S(1)}, s32[56]{0:T(128)}, u32[]{:S(2)}) copy-start(s32[56]{0:T(128)} %param.33) | copy-start | bytes 676
  7.7 8.7 %copy-start.8 = (bf16[64,512]{1,0:T(8,128)(2,1)S(1)}, bf16[64,512]{1,0:T(8,128)(2,1)}, u32[]{:S(2)}) copy-start(bf16[64,512]{1,0:T(8,128)(2,1)} %step_weight_ref.1) | copy-start | bytes 196612
  7.8 8.7 %copy-start.9 = (f32[16,512]{1,0:T(8,128)S(1)}, f32[16,512]{1,0:T(8,128)}, u32[]{:S(2)}) copy-start(f32[16,512]{1,0:T(8,128)} %rate_ref.1) | copy-start | bytes 98308
  7.8 8.7 %copy-start.13 = (f32[512]{0:T(512)S(1)}, f32[512]{0:T(512)}, u32[]{:S(2)}) copy-start(f32[512]{0:T(512)} %param.27) | copy-start | bytes 6148
  7.8 8.7 %copy-start.14 = (f32[512]{0:T(512)S(1)}, f32[512]{0:T(512)}, u32[]{:S(2)}) copy-start(f32[512]{0:T(512)} %param.29) | copy-start | bytes 6148
  7.8 1.5 %collective-permute-start = (f32[96,256]{1,0:T(8,128)S(1)}, f32[96,256]{1,0:T(8,128)S(1)}, u32[]{:S(2)}, u32[]{:S(2)}) collective-permute-start(f32[96,256]{1,0:T(8,128)S(1)} %get-tuple-element.26), channel_id=1, source_target_pairs={{0,1},{1,0},{2,3},{3,2},{4,5},{5,4},{6,7},{7,6},{8,9},{9,8},{10,11... | collective-permute-start | bytes 294920 | tf_op jit(solution)/shard_map/ppermute | solution.py:543
  9.3 7.2 %collective-permute-start.1 = (f32[96,256]{1,0:T(8,128)S(1)}, f32[96,256]{1,0:T(8,128)S(1)}, u32[]{:S(2)}, u32[]{:S(2)}) collective-permute-start(f32[96,256]{1,0:T(8,128)S(1)} %add.3.own_ref), channel_id=1, source_target_pairs={{0,2},{1,3},{2,0},{3,1},{4,6},{5,7},{6,4},{7,5},{8,10},{9,11},{10,... | collective-permute-start | bytes 294920 | tf_op jit(solution)/shard_map/ppermute | solution.py:543
  12.2 1.0 %copy-start.4 = (bf16[896,256]{1,0:T(8,128)(2,1)S(1)}, bf16[896,256]{1,0:T(8,128)(2,1)}, u32[]{:S(2)}) copy-start(bf16[896,256]{1,0:T(8,128)(2,1)} %query_ref.1) | copy-start | bytes 1376260
  13.3 22.4 %copy-start.15 = (f32[512]{0:T(512)S(1)}, f32[512]{0:T(512)}, u32[]{:S(2)}) copy-start(f32[512]{0:T(512)} %param.30) | copy-start | bytes 6148
  13.3 22.4 %copy-start.16 = (f32[256]{0:T(256)S(1)}, f32[256]{0:T(256)}, u32[]{:S(2)}) copy-start(f32[256]{0:T(256)} %param.22) | copy-start | bytes 3076
  22.3 6.0 %collective-permute-start.2 = (bf16[1,240,128]{2,1,0:T(8,128)(2,1)S(1)}, bf16[1,240,128]{2,1,0:T(8,128)(2,1)S(1)}, u32[]{:S(2)}, u32[]{:S(2)}) collective-permute-start(bf16[1,240,128]{2,1,0:T(8,128)(2,1)S(1)} %bitcast.16), channel_id=1, source_target_pairs={{0,16},{4,20},{8,24},{12,28},{16,0},{20,4},{24,8},{28,12},{1,17},{... | collective-permute-start | bytes 184328 | tf_op jit(solution)/shard_map/ppermute | solution.py:543
  24.4 1.2 %collective-permute-start.3 = (f32[2,256]{1,0:T(2,128)S(1)}, f32[2,256]{1,0:T(2,128)S(1)}, u32[]{:S(2)}, u32[]{:S(2)}) collective-permute-start(f32[2,256]{1,0:T(2,128)S(1)} %get-tuple-element.33.own_ref), channel_id=1, source_target_pairs={{0,1},{1,0},{2,3},{3,2},{4,5},{5,4},{6,7},{7,6},{8,9},{9,8},{10,11... | collective-permute-start | bytes 6152 | tf_op jit(solution)/shard_map/ppermute | solution.py:543
  28.3 4.9 %collective-permute-start.4 = (bf16[2,240,128]{2,1,0:T(8,128)(2,1)S(1)}, bf16[2,240,128]{2,1,0:T(8,128)(2,1)S(1)}, u32[]{:S(2)}, u32[]{:S(2)}) collective-permute-start(bf16[2,240,128]{2,1,0:T(8,128)(2,1)S(1)} %get-tuple-element.34.held_ref), channel_id=1, source_target_pairs={{0,8},{4,12},{8,0},{12,4},{16,24},{20,28},{24,16},{28,20},{1,9},{5... | collective-permute-start | bytes 368648 | tf_op jit(solution)/shard_map/ppermute | solution.py:543
  28.7 3.6 %collective-permute-start.5 = (f32[2,256]{1,0:T(2,128)S(1)}, f32[2,256]{1,0:T(2,128)S(1)}, u32[]{:S(2)}, u32[]{:S(2)}) collective-permute-start(f32[2,256]{1,0:T(2,128)S(1)} %get-tuple-element.35.own_ref), channel_id=1, source_target_pairs={{0,2},{1,3},{2,0},{3,1},{4,6},{5,7},{6,4},{7,5},{8,10},{9,11},{10,... | collective-permute-start | bytes 6152 | tf_op jit(solution)/shard_map/ppermute | solution.py:543
  33.3 6.5 %collective-permute-start.6 = (bf16[4,240,128]{2,1,0:T(8,128)(2,1)S(1)}, bf16[4,240,128]{2,1,0:T(8,128)(2,1)S(1)}, u32[]{:S(2)}, u32[]{:S(2)}) collective-permute-start(bf16[4,240,128]{2,1,0:T(8,128)(2,1)S(1)} %get-tuple-element.39.held_ref), channel_id=1, source_target_pairs={{0,4},{4,0},{8,12},{12,8},{16,20},{20,16},{24,28},{28,24},{1,5},{5... | collective-permute-start | bytes 737288 | tf_op jit(solution)/shard_map/ppermute | solution.py:543
  (3 other events, 2.2 us)

commit v4 on v3

--- a/solution.py
+++ b/solution.py
@@ -25,7 +25,6 @@
 BF16 = jnp.bfloat16
 VMEM = pl.BlockSpec(memory_space=pltpu.VMEM)
 SMEM = pl.BlockSpec(memory_space=pltpu.SMEM)
-ANY = pl.BlockSpec(memory_space=pl.ANY)
 HBM = pl.BlockSpec(memory_space=pltpu.HBM)
 
 
@@ -54,19 +53,6 @@
     return first
 
 
-def interleave(tokens, which):
-    out = []
-    for at in range(0, tokens.shape[1], LANES):
-        wide = min(LANES, tokens.shape[1] - at)
-        row = lax.broadcasted_iota(jnp.int32, (wide, 2 * wide), 0)
-        column = lax.broadcasted_iota(jnp.int32, (wide, 2 * wide), 1)
-        pick = jnp.where(column == 2 * row + which, 1.0, 0.0).astype(BF16)
-        out.append(
-            jnp.dot(tokens[:, at : at + wide], pick, preferred_element_type=F32).astype(BF16)
-        )
-    return jnp.concatenate(out, axis=1)
-
-
 def last_rows(shape, depth, starts, ends):
     row = lax.broadcasted_iota(jnp.int32, shape, 0)
     position = lax.broadcasted_iota(jnp.int32, shape, 1)
@@ -83,45 +69,20 @@
 
 def mix_kernel(
     prompts,
-    len_hbm,
-    tokens_hbm,
-    inner_hbm,
-    conv_hbm,
-    scan_hbm,
+    len_ref,
+    inner_ref,
+    conv_ref,
+    scan_ref,
     partial_ref,
     mixed_ref,
     tail_ref,
-    len_ref,
-    tokens_ref,
-    inner_ref,
-    conv_ref,
-    scan_ref,
     raw_ref,
-    sems,
 ):
-    tokens_copy = pltpu.make_async_copy(tokens_hbm, tokens_ref, sems.at[0])
-    inner_copy = pltpu.make_async_copy(inner_hbm, inner_ref, sems.at[1])
-    small_copies = [
-        pltpu.make_async_copy(len_hbm, len_ref, sems.at[2]),
-        pltpu.make_async_copy(conv_hbm, conv_ref, sems.at[3]),
-        pltpu.make_async_copy(scan_hbm, scan_ref, sems.at[4]),
-    ]
-    tokens_copy.start()
-    inner_copy.start()
-    for copy in small_copies:
-        copy.start()
-    rows, width = tokens_ref.shape
-    channels = inner_ref.shape[2]
-    tokens_copy.wait()
-    spread = interleave(tokens_ref[...], 0)
-    inner_copy.wait()
-    weight = inner_ref[...].reshape(2 * width, channels)
-    raw = jnp.dot(spread, weight, preferred_element_type=F32).astype(BF16).astype(F32)
+    _, rows, channels = inner_ref.shape
+    starts, ends = bounds(len_ref, prompts)
+    raw = inner_ref[0].astype(F32)
     raw_ref[pl.ds(0, 8), :] = jnp.zeros((8, channels), F32)
     raw_ref[pl.ds(8, rows), :] = raw
-    for copy in small_copies:
-        copy.wait()
-    starts, ends = bounds(len_ref, prompts)
     position = lax.broadcasted_iota(jnp.int32, (rows, 1), 0)
     offset = position - first_row_of(position, starts, prompts)
     total = raw * conv_ref[CONV - 1 : CONV, :]
@@ -133,7 +94,7 @@
     mixed_ref[...] = mixed
     partial_ref[...] = dot_nt(scan_ref[...], mixed)
     pick = last_rows((8, rows), CONV - 1, starts, ends)
-    tail_ref[...] = jnp.dot(pick, raw.astype(BF16), preferred_element_type=F32)
+    tail_ref[...] = jnp.dot(pick, inner_ref[0], preferred_element_type=F32)
 
 
 def attend_kernel(
@@ -143,23 +104,17 @@
     query_ref,
     key_ref,
     value_ref,
-    inner_hbm,
     tail_ref,
     prompt_ref,
     owner_ref,
     slot_ref,
     attended_ref,
     square_ref,
-    gate_ref,
     packed_ref,
-    inner_ref,
     request_ref,
-    sem,
 ):
-    inner_copy = pltpu.make_async_copy(inner_hbm, inner_ref, sem)
-    inner_copy.start()
     rows, width = tokens_ref.shape
-    channels = inner_ref.shape[2]
+    channels = tail_ref.shape[1]
     features = query_ref.shape[1]
     group = features // HEAD_DIM
     starts, ends = bounds(len_ref, prompts)
@@ -216,11 +171,6 @@
             axis=0,
         ).astype(BF16)
     packed_ref[base + 8 * (channels // LANES) :, :] = filled.astype(BF16)
-    inner_copy.wait()
-    spread = interleave(tokens, 1)
-    gate_ref[...] = jnp.dot(
-        spread, inner_ref[...].reshape(2 * width, channels), preferred_element_type=F32
-    ).astype(BF16)
 
 
 def scan_kernel(
@@ -317,7 +267,7 @@
             total = total + partial_ref[tile, pl.ds(index, rows, stride=8), :]
         scanned.append(total)
     scanned = jnp.concatenate(scanned, axis=1)
-    gate = gate_ref[...].astype(F32)
+    gate = gate_ref[1].astype(F32)
     gated = (scanned + skip_ref[...] * mixed_ref[...].astype(F32)) * (gate * sigmoid(gate))
     gated_ref[...] = gated
     ones = jnp.ones((8, channels), BF16)
@@ -325,11 +275,17 @@
     sums_ref[1:2, :] = dot_nt(ones, (gated * gated).astype(BF16))[0:1, :]
 
 
-def join_kernel(held_ref, new_ref, own_ref, other_ref, joined_ref, sums_ref):
+def join_kernel(held_ref, new_ref, own_ref, other_ref, *refs):
+    across_refs, (joined_ref, fresh_ref, sums_ref, crossed_ref) = refs[:-4], refs[-4:]
     count = held_ref.shape[0]
     joined_ref[:count] = held_ref[...]
     joined_ref[count:] = new_ref[...]
+    fresh_ref[...] = new_ref[...]
     sums_ref[...] = own_ref[...] + other_ref[...]
+    at = 0
+    for across_ref in across_refs:
+        crossed_ref[at : at + across_ref.shape[0]] = across_ref[...]
+        at += across_ref.shape[0]
 
 
 def norm_kernel(
@@ -357,29 +313,23 @@
 
 def deliver_kernel(
     prompts,
+    pieces,
     me_ref,
-    held_ref,
-    new_ref,
-    keyval_hbm,
-    state_hbm,
-    conv_hbm,
-    keyval_ref,
-    state_ref,
-    conv_ref,
-    sems,
+    *refs,
 ):
+    keyval_hbm, state_hbm, conv_hbm, keyval_ref, state_ref, conv_ref, sems = refs[pieces:]
     me = me_ref[0]
     slots, _, channels = state_ref.shape
     tiles = channels // LANES
-    half = held_ref.shape[0]
-    sources = 2 * half
+    blocks = [(ref, index) for ref in refs[:pieces] for index in range(ref.shape[0])]
+    sources = len(blocks)
     window_at = prompts * tiles * STATE
     tail_at = window_at + prompts * WINDOW
     table_at = tail_at + 8 * tiles
-    owners = held_ref.shape[1] - table_at
+    owners = refs[0].shape[1] - table_at
 
     def rows_of(source, at, size):
-        ref, index = (held_ref, source) if source < half else (new_ref, source - half)
+        ref, index = blocks[source]
         return ref[index, at : at + size, :]
 
     owner = lax.broadcasted_iota(jnp.int32, (owners, LANES), 0)
@@ -517,6 +467,8 @@
     def shape(dims, dtype=F32):
         return jax.ShapeDtypeStruct(dims, dtype)
 
+    inner = jnp.einsum("td,dgc->gtc", tokens, inner_weight, preferred_element_type=F32)
+    inner = inner.astype(BF16)
     partial, mixed, tail = pl.pallas_call(
         functools.partial(mix_kernel, prompts),
         out_shape=(
@@ -524,20 +476,12 @@
             shape((rows, channels), BF16),
             shape((8, channels)),
         ),
-        in_specs=[HBM] * 5,
+        in_specs=[SMEM] + [VMEM] * 3,
         out_specs=(VMEM, VMEM, VMEM),
-        scratch_shapes=[
-            pltpu.SMEM((1, prompts), jnp.int32),
-            pltpu.VMEM((rows, width), BF16),
-            pltpu.VMEM((width, 2, channels), BF16),
-            pltpu.VMEM(conv_weight.shape, F32),
-            pltpu.VMEM(scan_weight.shape[::-1], BF16),
-            pltpu.VMEM((rows + 8, channels), F32),
-            pltpu.SemaphoreType.DMA((5,)),
-        ],
-        compiler_params=params(24),
+        scratch_shapes=[pltpu.VMEM((rows + 8, channels), F32)],
+        compiler_params=params(16),
         name="mix",
-    )(prompt_lengths, tokens, inner_weight, conv_weight, scan_weight.T)
+    )(prompt_lengths, inner, conv_weight, scan_weight.T)
 
     def swap(x, axis, size, bit):
         return lax.ppermute(x, axis, [(i, i ^ bit) for i in range(size)])
@@ -545,22 +489,19 @@
     near = swap(partial, "tp", tp_size, 1)
     owners = -(-pr_size // 16) * 16
     early_rows = prompts * WINDOW + 8 * tiles + owners
-    attended, square, gate, early = pl.pallas_call(
+    attended, square, early = pl.pallas_call(
         functools.partial(attend_kernel, prompts),
         out_shape=(
             shape((rows, features)),
             shape((8, rows)),
-            shape((rows, channels), BF16),
             shape((early_rows, LANES), BF16),
         ),
-        in_specs=[SMEM, VMEM, VMEM, VMEM, VMEM, ANY, VMEM, VMEM, VMEM, VMEM],
-        out_specs=(VMEM, VMEM, VMEM, VMEM),
+        in_specs=[SMEM] + [VMEM] * 8,
+        out_specs=(VMEM, VMEM, VMEM),
         scratch_shapes=[
-            pltpu.VMEM((width, 2, channels), BF16),
             pltpu.VMEM((8, LANES), jnp.int32),
-            pltpu.SemaphoreType.DMA,
         ],
-        compiler_params=params(32),
+        compiler_params=params(16),
         cost_estimate=pl.CostEstimate(
             flops=2 * rows * width * (features + channels), bytes_accessed=4 << 20, transcendentals=0
         ),
@@ -571,7 +512,6 @@
         query_weight,
         key_weight.T,
         value_weight.T,
-        inner_weight,
         tail,
         request_prompt[None],
         request_owner[None],
@@ -610,7 +550,7 @@
         pair,
         far,
         mixed,
-        gate,
+        inner,
         step_weight,
         step_bias[None],
         mamba_rate,
@@ -623,26 +563,31 @@
     held = payload[None]
     pr_bits = [1 << i for i in reversed(range((pr_size - 1).bit_length()))]
     tp_bits = [1 << i for i in range((tp_size - 1).bit_length())]
+    fresh, crossed = held, []
     for index in range(max(len(pr_bits) - 1, len(tp_bits))):
-        new = swap(held, "pr", pr_size, pr_bits[index]) if index < len(pr_bits) - 1 else None
         other = swap(sums, "tp", tp_size, tp_bits[index]) if index < len(tp_bits) else None
-        if new is None:
-            sums = sums + other
-        elif other is None:
-            held = jnp.concatenate([held, new], axis=0)
-        else:
-            held, sums = pl.pallas_call(
+        if index < len(pr_bits) - 1:
+            new = swap(held, "pr", pr_size, pr_bits[index])
+            crossed.append(swap(fresh, "pr", pr_size, pr_bits[-1]))
+            count = held.shape[0]
+            held, fresh, sums, across = pl.pallas_call(
                 join_kernel,
                 out_shape=(
-                    shape((2 * held.shape[0],) + held.shape[1:], BF16),
+                    shape((2 * count,) + held.shape[1:], BF16),
+                    shape((count,) + held.shape[1:], BF16),
                     shape(sums.shape),
+                    shape((count,) + held.shape[1:], BF16),
                 ),
-                in_specs=[VMEM] * 4,
-                out_specs=(VMEM, VMEM),
+                in_specs=[VMEM] * (4 + len(crossed)),
+                out_specs=(VMEM,) * 4,
                 compiler_params=params(16),
                 name="join",
-            )(held, new, sums, other)
-    new = swap(held, "pr", pr_size, pr_bits[-1])
+            )(held, new, sums, jnp.zeros_like(sums) if other is None else other, *crossed)
+            crossed = [across]
+        else:
+            sums = sums + other
+    crossed.append(swap(fresh, "pr", pr_size, pr_bits[-1]))
+    pieces = [held] + crossed
     attention_out, mamba_out = pl.pallas_call(
         norm_kernel,
         out_shape=(shape((rows, features), BF16), shape((rows, channels), BF16)),
@@ -653,13 +598,13 @@
         name="norm",
     )(attended, gated, sums, attention_gain[None], mamba_gain[None])
     keyval, state, conv = pl.pallas_call(
-        functools.partial(deliver_kernel, prompts),
+        functools.partial(deliver_kernel, prompts, len(pieces)),
         out_shape=(
             shape((slots, 2, WINDOW, HEAD_DIM), BF16),
             shape((slots, STATE, channels), BF16),
             shape((CONV - 1, slots, channels), BF16),
         ),
-        in_specs=[SMEM, VMEM, VMEM],
+        in_specs=[SMEM] + [VMEM] * len(pieces),
         out_specs=(HBM, HBM, HBM),
         scratch_shapes=[
             pltpu.VMEM((slots, 2, WINDOW, HEAD_DIM), BF16),
@@ -669,7 +614,7 @@
         ],
         compiler_params=params(32),
         name="deliver",
-    )(me[None], held, new)
+    )(me[None], *pieces)
     return (attention_out, mamba_out, keyval, state, conv.transpose(1, 0, 2))
 
 

time: 42.2 us -> 38.8 us (0.919)
  starting transfers between devices: 8.91 us -> 13.9 us
  local copies, waits for them, and re-layouts: 5.85 us -> 1.56 us
  waiting for transfers between devices: 11.9 us -> 8.73 us
  Pallas kernels: 14.4 us -> 11.8 us
  matrix products: 0 us -> 1.73 us
    ppermute x7 -> x9, starting transfers between devices: 8.91 us -> 13.9 us  [swap(): return lax.ppermute(x, axis, [(i, i ^ bit) for i in range(size)])]
    unnamed x40 -> x34, local copies, waits for them, and re-layouts: 5.85 us -> 1.56 us
    ppermute x7 -> x9, waiting for transfers between devices: 11.9 us -> 8.73 us  [swap(): return lax.ppermute(x, axis, [(i, i ^ bit) for i in range(size)])]
    dot_general x0 -> x1, matrix products: none -> 1.73 us  [on_device(): jnp.einsum('td,dgc->gtc', tokens, inner_weight, preferred_element_type=F32)]
    pallas_call x1, Pallas kernels: 2.27 us -> 1.14 us  [on_device(): pl.pallas_call(functools.partial(mix_kernel, prompts), out_shape=(shape((...]
    pallas_call x1, Pallas kernels: 3.16 us -> 2.08 us  [on_device(): pl.pallas_call(functools.partial(attend_kernel, prompts), out_shape=(shap...]
  transfers between devices with their start and end apart: 7 -> 9, of which waited for: 6 -> 6; matrix products, arithmetic and copies ran while one was open for 0% -> 0% of each run, Pallas kernels for 10% -> 8%
where the time goes in v4:
time: 38.8 us; the launch traced here: 38.6 us
  starting transfers between devices  13.9 us (36%)
  Pallas kernels  11.8 us (30%)
  waiting for transfers between devices  8.73 us (22%)
  matrix products  1.73 us (4%)
  local copies, waits for them, and re-layouts  1.56 us (4%)
  between operations  0.88 us (2%)
    ppermute x9, starting transfers between devices, swap(): return lax.ppermute(x, axis, [(i, i ^ bit) for i in range(size)])  13.9 us
    ppermute x9, waiting for transfers between devices, swap(): return lax.ppermute(x, axis, [(i, i ^ bit) for i in range(size)])  8.73 us
    pallas_call x1, Pallas kernels, on_device(): pl.pallas_call(functools.partial(scan_kernel, prompts), out_shape=(shape(...  5.4 us
    pallas_call x1, Pallas kernels, on_device(): pl.pallas_call(functools.partial(deliver_kernel, prompts, len(pieces)), o...  2.08 us
    pallas_call x1, Pallas kernels, on_device(): pl.pallas_call(functools.partial(attend_kernel, prompts), out_shape=(shap...  2.08 us
    dot_general x1, matrix products, on_device(): jnp.einsum('td,dgc->gtc', tokens, inner_weight, preferred_element_type=F32)  1.73 us
    unnamed x34, local copies, waits for them, and re-layouts  1.56 us
    pallas_call x1, Pallas kernels, on_device(): pl.pallas_call(functools.partial(mix_kernel, prompts), out_shape=(shape((...  1.14 us
  transfers between devices with their start and end apart: 9, of which 6 were waited for; matrix products, arithmetic and copies ran while one was open for 0% of the time, Pallas kernels for 8%

profile of v4, /device:TPU:0, one launch (start us, length us, event | category | flops | bytes accessed | tf_op | source)
XLA Modules:
  0.0 38.6 jit_solution(13048438121347161420)
XLA Ops:
  0.6 0.0 copy-start
  0.8 1.5 %copy-done = bf16[896,2,512]{2,1,0:T(2,128)(2,1)S(1)} copy-done((bf16[896,2,512]{2,1,0:T(2,128)(2,1)S(1)}, bf16[896,2,512]{2,1,0:T(2,128)(2,1)}, u32[]{:S(2)}) %copy-start) | copy-done | bytes 1835032
  2.2 1.7 %fusion.5.inner_ref.gate_ref = bf16[2,256,512]{2,1,0:T(8,128)(2,1)S(1)} fusion(bf16[896,2,512]{2,1,0:T(2,128)(2,1)S(1)} %copy-done, bf16[256,896]{1,0:T(8,128)(2,1)} %tokens_ref.1), kind=kOutput, calls=%fused_computation.3 | convolution fusion | flops 470024192 | bytes 2818048 | tf_op jit(solution)/shard_map/td,dgc->gtc/dot_general | solution.py:470
  4.0 0.0 copy-start.2
  4.0 0.0 copy-start.3
  4.1 1.1 %mix.1 = (f32[96,256]{1,0:T(8,128)S(1)}, bf16[256,512]{1,0:T(8,128)(2,1)S(1)}, f32[8,512]{1,0:T(8,128)S(1)}) custom-call(s32[1,2]{1,0:T(1,128)S(1)} %copy-done.8, bf16[2,256,512]{2,1,0:T(8,128)(2,1)S(1)} %fusion.5.inner_ref.gate_ref, f32[4,512]{1,0:T(4,128)S(1)} %copy-done.4, bf16[96,512]{1,0:T(8,128)(2,1)S(1)} %bitcast.18), custom_call_target="tpu_custom_call" | custom-call | tf_op jit(solution)/shard_map/mix/pallas_call | solution.py:472
  5.2 0.5 %collective-permute-start = (f32[96,256]{1,0:T(8,128)S(1)}, f32[96,256]{1,0:T(8,128)S(1)}, u32[]{:S(2)}, u32[]{:S(2)}) collective-permute-start(f32[96,256]{1,0:T(8,128)S(1)} %get-tuple-element.29), channel_id=1, source_target_pairs={{0,1},{1,0},{2,3},{3,2},{4,5},{5,4},{6,7},{7,6},{8,9},{9,8},{10,11... | collective-permute-start | bytes 294920 | tf_op jit(solution)/shard_map/ppermute | solution.py:487
  5.7 0.9 %collective-permute-done = f32[96,256]{1,0:T(8,128)S(1)} collective-permute-done((f32[96,256]{1,0:T(8,128)S(1)}, f32[96,256]{1,0:T(8,128)S(1)}, u32[]{:S(2)}, u32[]{:S(2)}) %collective-permute-start) | collective-permute-done | bytes 98336 | tf_op jit(solution)/shard_map/ppermute | solution.py:487
  6.7 2.9 %collective-permute-start.1 = (f32[96,256]{1,0:T(8,128)S(1)}, f32[96,256]{1,0:T(8,128)S(1)}, u32[]{:S(2)}, u32[]{:S(2)}) collective-permute-start(f32[96,256]{1,0:T(8,128)S(1)} %add.3.own_ref), channel_id=1, source_target_pairs={{0,2},{1,3},{2,0},{3,1},{4,6},{5,7},{6,4},{7,5},{8,10},{9,11},{10,... | collective-permute-start | bytes 294920 | tf_op jit(solution)/shard_map/ppermute | solution.py:487
  9.6 2.1 %attend.1 = (f32[256,256]{1,0:T(8,128)S(1)}, f32[8,256]{1,0:T(8,128)S(1)}, bf16[112,128]{1,0:T(8,128)(2,1)S(1)}) custom-call(s32[1,2]{1,0:T(1,128)S(1)} %copy-done.8, bf16[256,896]{1,0:T(8,128)(2,1)S(1)} %copy-done.10, bf16[896,256]{1,0:T(8,128)(2,1)S(1)} %copy-done.11, bf16[64,896]{1,0:T(8,128)(2,1)S(1)} %bitcast.26, bf16[64,896]{1,0:T(8,128)(2,1)S(1)} %bitcast.27, ...), custom_call_target="tpu_custom_call" | custom-call | flops 352321536 | bytes 4194304 | tf_op jit(solution)/shard_map/attend/pallas_call | solution.py:492
  11.7 1.0 %collective-permute-done.1.other_ref = f32[96,256]{1,0:T(8,128)S(1)} collective-permute-done((f32[96,256]{1,0:T(8,128)S(1)}, f32[96,256]{1,0:T(8,128)S(1)}, u32[]{:S(2)}, u32[]{:S(2)}) %collective-permute-start.1) | collective-permute-done | bytes 98336 | tf_op jit(solution)/shard_map/ppermute | solution.py:487
  12.7 5.4 %scan.1 = (f32[256,512]{1,0:T(8,128)S(1)}, f32[2,256]{1,0:T(2,128)S(1)}, bf16[240,128]{1,0:T(8,128)(2,1)S(1)}) custom-call(s32[1,2]{1,0:T(1,128)S(1)} %copy-done.8, f32[96,256]{1,0:T(8,128)S(1)} %add.3.own_ref, f32[96,256]{1,0:T(8,128)S(1)} %collective-permute-done.1.other_ref, bf16[256,512]{1,0:T(8,128)(2,1)S(1)} %get-tuple-element.30.mixed_ref, ...), custom_call_target="tpu_custom_call" | custom-call | tf_op jit(solution)/shard_map/scan/pallas_call | solution.py:528
  18.1 2.2 %collective-permute-start.4 = (bf16[1,240,128]{2,1,0:T(8,128)(2,1)S(1)}, bf16[1,240,128]{2,1,0:T(8,128)(2,1)S(1)}, u32[]{:S(2)}, u32[]{:S(2)}) collective-permute-start(bf16[1,240,128]{2,1,0:T(8,128)(2,1)S(1)} %bitcast.19), channel_id=1, source_target_pairs={{0,4},{4,0},{8,12},{12,8},{16,20},{20,16},{24,28},{28,24},{1,5},{5... | collective-permute-start | bytes 184328 | tf_op jit(solution)/shard_map/ppermute | solution.py:487
  20.3 3.2 %collective-permute-start.2 = (bf16[1,240,128]{2,1,0:T(8,128)(2,1)S(1)}, bf16[1,240,128]{2,1,0:T(8,128)(2,1)S(1)}, u32[]{:S(2)}, u32[]{:S(2)}) collective-permute-start(bf16[1,240,128]{2,1,0:T(8,128)(2,1)S(1)} %bitcast.20), channel_id=1, source_target_pairs={{0,16},{4,20},{8,24},{12,28},{16,0},{20,4},{24,8},{28,12},{1,17},{... | collective-permute-start | bytes 184328 | tf_op jit(solution)/shard_map/ppermute | solution.py:487
  23.5 1.2 %collective-permute-done.3.other_ref = f32[2,256]{1,0:T(2,128)S(1)} collective-permute-done((f32[2,256]{1,0:T(2,128)S(1)}, f32[2,256]{1,0:T(2,128)S(1)}, u32[]{:S(2)}, u32[]{:S(2)}) %collective-permute-start.3) | collective-permute-done | bytes 2080 | tf_op jit(solution)/shard_map/ppermute | solution.py:487
  24.7 1.0 %collective-permute-done.2.new_ref = bf16[1,240,128]{2,1,0:T(8,128)(2,1)S(1)} collective-permute-done((bf16[1,240,128]{2,1,0:T(8,128)(2,1)S(1)}, bf16[1,240,128]{2,1,0:T(8,128)(2,1)S(1)}, u32[]{:S(2)}, u32[]{:S(2)}) %collective-permute-start.2) | collective-permute-done | bytes 61472 | tf_op jit(solution)/shard_map/ppermute | solution.py:487
  25.7 1.5 %collective-permute-start.5 = (bf16[2,240,128]{2,1,0:T(8,128)(2,1)S(1)}, bf16[2,240,128]{2,1,0:T(8,128)(2,1)S(1)}, u32[]{:S(2)}, u32[]{:S(2)}) collective-permute-start(bf16[2,240,128]{2,1,0:T(8,128)(2,1)S(1)} %get-tuple-element.36.held_ref), channel_id=1, source_target_pairs={{0,8},{4,12},{8,0},{12,4},{16,24},{20,28},{24,16},{28,20},{1,9},{5... | collective-permute-start | bytes 368648 | tf_op jit(solution)/shard_map/ppermute | solution.py:487
  27.3 0.7 %collective-permute-start.7 = (bf16[1,240,128]{2,1,0:T(8,128)(2,1)S(1)}, bf16[1,240,128]{2,1,0:T(8,128)(2,1)S(1)}, u32[]{:S(2)}, u32[]{:S(2)}) collective-permute-start(bf16[1,240,128]{2,1,0:T(8,128)(2,1)S(1)} %get-tuple-element.39), channel_id=1, source_target_pairs={{0,4},{4,0},{8,12},{12,8},{16,20},{20,16},{24,28},{28,24},{1,5},{5... | collective-permute-start | bytes 184328 | tf_op jit(solution)/shard_map/ppermute | solution.py:487
  28.0 1.5 %collective-permute-start.6 = (f32[2,256]{1,0:T(2,128)S(1)}, f32[2,256]{1,0:T(2,128)S(1)}, u32[]{:S(2)}, u32[]{:S(2)}) collective-permute-start(f32[2,256]{1,0:T(2,128)S(1)} %get-tuple-element.37.own_ref), channel_id=1, source_target_pairs={{0,2},{1,3},{2,0},{3,1},{4,6},{5,7},{6,4},{7,5},{8,10},{9,11},{10,... | collective-permute-start | bytes 6152 | tf_op jit(solution)/shard_map/ppermute | solution.py:487
  29.5 2.1 %collective-permute-done.6.other_ref = f32[2,256]{1,0:T(2,128)S(1)} collective-permute-done((f32[2,256]{1,0:T(2,128)S(1)}, f32[2,256]{1,0:T(2,128)S(1)}, u32[]{:S(2)}, u32[]{:S(2)}) %collective-permute-start.6) | collective-permute-done | bytes 2080 | tf_op jit(solution)/shard_map/ppermute | solution.py:487
  31.6 1.4 %collective-permute-start.8 = (bf16[2,240,128]{2,1,0:T(8,128)(2,1)S(1)}, bf16[2,240,128]{2,1,0:T(8,128)(2,1)S(1)}, u32[]{:S(2)}, u32[]{:S(2)}) collective-permute-start(bf16[2,240,128]{2,1,0:T(8,128)(2,1)S(1)} %get-tuple-element.45), channel_id=1, source_target_pairs={{0,4},{4,0},{8,12},{12,8},{16,20},{20,16},{24,28},{28,24},{1,5},{5... | collective-permute-start | bytes 368648 | tf_op jit(solution)/shard_map/ppermute | solution.py:487
  33.0 1.0 %norm.1 = (bf16[256,256]{1,0:T(8,128)(2,1)}, bf16[256,512]{1,0:T(8,128)(2,1)}) custom-call(f32[256,256]{1,0:T(8,128)S(1)} %get-tuple-element.28.attended_ref, f32[256,512]{1,0:T(8,128)S(1)} %get-tuple-element.33.gated_ref, f32[2,256]{1,0:T(2,128)S(1)} %get-tuple-element.40.sums_ref, f32[1,256]{1,0:T(1,128)S(1)} %bitcast.25, f32[1,512]{1,0:T(1,128)S(1)} %bitcast.24), custom_call_target="tpu_custom_call" | custom-call | flops 16777216 | bytes 2097152 | tf_op jit(solution)/shard_map/norm/pallas_call | solution.py:591
  34.0 2.5 %collective-permute-done.8.refs_2_ = bf16[2,240,128]{2,1,0:T(8,128)(2,1)S(1)} collective-permute-done((bf16[2,240,128]{2,1,0:T(8,128)(2,1)S(1)}, bf16[2,240,128]{2,1,0:T(8,128)(2,1)S(1)}, u32[]{:S(2)}, u32[]{:S(2)}) %collective-permute-start.8) | collective-permute-done | bytes 122912 | tf_op jit(solution)/shard_map/ppermute | solution.py:487
  36.6 2.1 %deliver.1 = (bf16[56,2,32,64]{3,2,1,0:T(8,128)(2,1)}, bf16[56,16,512]{2,1,0:T(8,128)(2,1)}, bf16[3,56,512]{2,1,0:T(8,128)(2,1)}) custom-call(s32[1]{0:T(128)} %bitcast.13.me_ref, bf16[4,240,128]{2,1,0:T(8,128)(2,1)S(1)} %get-tuple-element.43.refs_0_, bf16[2,240,128]{2,1,0:T(8,128)(2,1)S(1)} %get-tuple-element.44.refs_1_, ...), custom_call_target="tpu_custom_call" | custom-call | tf_op jit(solution)/shard_map/deliver/pallas_call | solution.py:600
  (37 shorter events, 0.2 us)
Async XLA Ops:
  0.7 8.9 %copy-start.10 = (bf16[256,896]{1,0:T(8,128)(2,1)S(1)}, bf16[256,896]{1,0:T(8,128)(2,1)}, u32[]{:S(2)}) copy-start(bf16[256,896]{1,0:T(8,128)(2,1)} %tokens_ref.1) | copy-start | bytes 1376260
  0.7 3.3 %copy-start.8 = (s32[1,2]{1,0:T(1,128)S(1)}, s32[1,2]{1,0:T(1,128)}, u32[]{:S(2)}) copy-start(s32[1,2]{1,0:T(1,128)} %len_ref.5) | copy-start | bytes 28
  0.7 3.3 %copy-start.1 = (bf16[512,96]{0,1:T(8,128)(2,1)S(1)}, bf16[512,96]{0,1:T(8,128)(2,1)}, u32[]{:S(2)}) copy-start(bf16[512,96]{0,1:T(8,128)(2,1)} %param.25) | copy-start | bytes 294916
  0.7 8.9 %copy-start.16 = (s32[56]{0:T(128)S(1)}, s32[56]{0:T(128)}, u32[]{:S(2)}) copy-start(s32[56]{0:T(128)} %param.33) | copy-start | bytes 676
  0.7 8.9 %copy-start.15 = (s32[56]{0:T(128)S(1)}, s32[56]{0:T(128)}, u32[]{:S(2)}) copy-start(s32[56]{0:T(128)} %param.32) | copy-start | bytes 676
  0.7 8.9 %copy-start.14 = (s32[56]{0:T(128)S(1)}, s32[56]{0:T(128)}, u32[]{:S(2)}) copy-start(s32[56]{0:T(128)} %param.31) | copy-start | bytes 676
  0.7 8.9 %copy-start.13 = (bf16[896,64]{0,1:T(8,128)(2,1)S(1)}, bf16[896,64]{0,1:T(8,128)(2,1)}, u32[]{:S(2)}) copy-start(bf16[896,64]{0,1:T(8,128)(2,1)} %param.21) | copy-start | bytes 344068
  0.7 8.9 %copy-start.12 = (bf16[896,64]{0,1:T(8,128)(2,1)S(1)}, bf16[896,64]{0,1:T(8,128)(2,1)}, u32[]{:S(2)}) copy-start(bf16[896,64]{0,1:T(8,128)(2,1)} %param.20) | copy-start | bytes 344068
  0.7 8.9 %copy-start.11 = (bf16[896,256]{1,0:T(8,128)(2,1)S(1)}, bf16[896,256]{1,0:T(8,128)(2,1)}, u32[]{:S(2)}) copy-start(bf16[896,256]{1,0:T(8,128)(2,1)} %query_ref.1) | copy-start | bytes 1376260
  4.0 8.7 %copy-start.2 = (bf16[64,512]{1,0:T(8,128)(2,1)S(1)}, bf16[64,512]{1,0:T(8,128)(2,1)}, u32[]{:S(2)}) copy-start(bf16[64,512]{1,0:T(8,128)(2,1)} %step_weight_ref.1) | copy-start | bytes 196612
  4.0 8.7 %copy-start.3 = (f32[16,512]{1,0:T(8,128)S(1)}, f32[16,512]{1,0:T(8,128)}, u32[]{:S(2)}) copy-start(f32[16,512]{1,0:T(8,128)} %rate_ref.1) | copy-start | bytes 98308
  4.0 8.7 %copy-start.5 = (f32[512]{0:T(512)S(1)}, f32[512]{0:T(512)}, u32[]{:S(2)}) copy-start(f32[512]{0:T(512)} %param.27) | copy-start | bytes 6148
  4.0 8.7 %copy-start.6 = (f32[512]{0:T(512)S(1)}, f32[512]{0:T(512)}, u32[]{:S(2)}) copy-start(f32[512]{0:T(512)} %param.29) | copy-start | bytes 6148
  4.0 29.0 %copy-start.7 = (f32[512]{0:T(512)S(1)}, f32[512]{0:T(512)}, u32[]{:S(2)}) copy-start(f32[512]{0:T(512)} %param.30) | copy-start | bytes 6148
  4.0 29.0 %copy-start.9 = (f32[256]{0:T(256)S(1)}, f32[256]{0:T(256)}, u32[]{:S(2)}) copy-start(f32[256]{0:T(256)} %param.22) | copy-start | bytes 3076
  5.2 1.5 %collective-permute-start = (f32[96,256]{1,0:T(8,128)S(1)}, f32[96,256]{1,0:T(8,128)S(1)}, u32[]{:S(2)}, u32[]{:S(2)}) collective-permute-start(f32[96,256]{1,0:T(8,128)S(1)} %get-tuple-element.29), channel_id=1, source_target_pairs={{0,1},{1,0},{2,3},{3,2},{4,5},{5,4},{6,7},{7,6},{8,9},{9,8},{10,11... | collective-permute-start | bytes 294920 | tf_op jit(solution)/shard_map/ppermute | solution.py:487
  6.7 6.0 %collective-permute-start.1 = (f32[96,256]{1,0:T(8,128)S(1)}, f32[96,256]{1,0:T(8,128)S(1)}, u32[]{:S(2)}, u32[]{:S(2)}) collective-permute-start(f32[96,256]{1,0:T(8,128)S(1)} %add.3.own_ref), channel_id=1, source_target_pairs={{0,2},{1,3},{2,0},{3,1},{4,6},{5,7},{6,4},{7,5},{8,10},{9,11},{10,... | collective-permute-start | bytes 294920 | tf_op jit(solution)/shard_map/ppermute | solution.py:487
  18.1 6.5 %collective-permute-start.4 = (bf16[1,240,128]{2,1,0:T(8,128)(2,1)S(1)}, bf16[1,240,128]{2,1,0:T(8,128)(2,1)S(1)}, u32[]{:S(2)}, u32[]{:S(2)}) collective-permute-start(bf16[1,240,128]{2,1,0:T(8,128)(2,1)S(1)} %bitcast.19), channel_id=1, source_target_pairs={{0,4},{4,0},{8,12},{12,8},{16,20},{20,16},{24,28},{28,24},{1,5},{5... | collective-permute-start | bytes 184328 | tf_op jit(solution)/shard_map/ppermute | solution.py:487
  20.3 5.4 %collective-permute-start.2 = (bf16[1,240,128]{2,1,0:T(8,128)(2,1)S(1)}, bf16[1,240,128]{2,1,0:T(8,128)(2,1)S(1)}, u32[]{:S(2)}, u32[]{:S(2)}) collective-permute-start(bf16[1,240,128]{2,1,0:T(8,128)(2,1)S(1)} %bitcast.20), channel_id=1, source_target_pairs={{0,16},{4,20},{8,24},{12,28},{16,0},{20,4},{24,8},{28,12},{1,17},{... | collective-permute-start | bytes 184328 | tf_op jit(solution)/shard_map/ppermute | solution.py:487
  23.5 1.2 %collective-permute-start.3 = (f32[2,256]{1,0:T(2,128)S(1)}, f32[2,256]{1,0:T(2,128)S(1)}, u32[]{:S(2)}, u32[]{:S(2)}) collective-permute-start(f32[2,256]{1,0:T(2,128)S(1)} %get-tuple-element.35.own_ref), channel_id=1, source_target_pairs={{0,1},{1,0},{2,3},{3,2},{4,5},{5,4},{6,7},{7,6},{8,9},{9,8},{10,11... | collective-permute-start | bytes 6152 | tf_op jit(solution)/shard_map/ppermute | solution.py:487
  25.7 5.8 %collective-permute-start.5 = (bf16[2,240,128]{2,1,0:T(8,128)(2,1)S(1)}, bf16[2,240,128]{2,1,0:T(8,128)(2,1)S(1)}, u32[]{:S(2)}, u32[]{:S(2)}) collective-permute-start(bf16[2,240,128]{2,1,0:T(8,128)(2,1)S(1)} %get-tuple-element.36.held_ref), channel_id=1, source_target_pairs={{0,8},{4,12},{8,0},{12,4},{16,24},{20,28},{24,16},{28,20},{1,9},{5... | collective-permute-start | bytes 368648 | tf_op jit(solution)/shard_map/ppermute | solution.py:487
  27.3 4.3 %collective-permute-start.7 = (bf16[1,240,128]{2,1,0:T(8,128)(2,1)S(1)}, bf16[1,240,128]{2,1,0:T(8,128)(2,1)S(1)}, u32[]{:S(2)}, u32[]{:S(2)}) collective-permute-start(bf16[1,240,128]{2,1,0:T(8,128)(2,1)S(1)} %get-tuple-element.39), channel_id=1, source_target_pairs={{0,4},{4,0},{8,12},{12,8},{16,20},{20,16},{24,28},{28,24},{1,5},{5... | collective-permute-start | bytes 184328 | tf_op jit(solution)/shard_map/ppermute | solution.py:487
  28.0 3.6 %collective-permute-start.6 = (f32[2,256]{1,0:T(2,128)S(1)}, f32[2,256]{1,0:T(2,128)S(1)}, u32[]{:S(2)}, u32[]{:S(2)}) collective-permute-start(f32[2,256]{1,0:T(2,128)S(1)} %get-tuple-element.37.own_ref), channel_id=1, source_target_pairs={{0,2},{1,3},{2,0},{3,1},{4,6},{5,7},{6,4},{7,5},{8,10},{9,11},{10,... | collective-permute-start | bytes 6152 | tf_op jit(solution)/shard_map/ppermute | solution.py:487
  31.6 4.9 %collective-permute-start.8 = (bf16[2,240,128]{2,1,0:T(8,128)(2,1)S(1)}, bf16[2,240,128]{2,1,0:T(8,128)(2,1)S(1)}, u32[]{:S(2)}, u32[]{:S(2)}) collective-permute-start(bf16[2,240,128]{2,1,0:T(8,128)(2,1)S(1)} %get-tuple-element.45), channel_id=1, source_target_pairs={{0,4},{4,0},{8,12},{12,8},{16,20},{20,16},{24,28},{28,24},{1,5},{5... | collective-permute-start | bytes 368648 | tf_op jit(solution)/shard_map/ppermute | solution.py:487
  (2 other events, 4.9 us)

commit v5 on v4

--- a/solution.py
+++ b/solution.py
@@ -61,6 +61,13 @@
         here = (row >= p * depth) & (row < (p + 1) * depth) & (position >= starts[p])
         hit = jnp.where(here & (position - row == ends[p] - (p + 1) * depth), 1.0, hit)
     return hit.astype(BF16)
+
+
+def row_sums(squares):
+    total = squares[:, :LANES]
+    for at in range(LANES, squares.shape[1], LANES):
+        total = total + squares[:, at : at + LANES]
+    return jnp.sum(total.T, axis=0, keepdims=True)
 
 
 def sigmoid(x):
@@ -140,8 +147,7 @@
             weights.astype(BF16), jnp.where(mine, values, zero), preferred_element_type=F32
         )
     attended_ref[...] = attended
-    ones = jnp.ones((8, features), BF16)
-    square_ref[...] = dot_nt(ones, (attended * attended).astype(BF16))
+    square_ref[...] = jnp.broadcast_to(row_sums(attended * attended), square_ref.shape)
     lane = lax.broadcasted_iota(jnp.int32, (rows, LANES), 1)
     both = jnp.where(lane < HEAD_DIM, keys[:, :LANES], values[:, :LANES])
     pick = last_rows((prompts * WINDOW, rows), WINDOW, starts, ends)
@@ -153,7 +159,10 @@
     request_ref[0:1, 0:requests] = owner_ref[...]
     request_ref[1:2, 0:requests] = slot_ref[...]
     request_ref[2:3, 0:requests] = prompt_ref[...]
-    owners = packed_ref.shape[0] - prompts * WINDOW - 8 * (channels // LANES)
+    depth = prompts * (CONV - 1)
+    groups = channels // LANES // 2
+    spare = 16 - 2 * depth
+    owners = packed_ref.shape[0] - prompts * WINDOW - 16 * groups + spare * groups
     owner = lax.broadcasted_iota(jnp.int32, (owners, LANES), 0) == request_ref[0:1, :]
     slot = lax.broadcasted_iota(jnp.int32, (LANES, LANES), 0) == request_ref[1:2, :]
     number = request_ref[2:3, :] + 1
@@ -162,15 +171,18 @@
         jnp.where(slot, number, 0).astype(F32).astype(BF16),
     )
     base = prompts * WINDOW
-    for tile in range(0, channels // LANES, 2):
-        packed_ref[base + 8 * tile : base + 8 * (tile + 2), :] = jnp.concatenate(
+    for group in range(groups):
+        at = 2 * group * LANES
+        packed_ref[base + 16 * group : base + 16 * (group + 1), :] = jnp.concatenate(
             [
-                tail_ref[:, tile * LANES : (tile + 1) * LANES],
-                tail_ref[:, (tile + 1) * LANES : (tile + 2) * LANES],
+                tail_ref[:depth, at : at + LANES],
+                tail_ref[:depth, at + LANES : at + 2 * LANES],
+                filled[spare * group : spare * (group + 1), :],
             ],
             axis=0,
         ).astype(BF16)
-    packed_ref[base + 8 * (channels // LANES) :, :] = filled.astype(BF16)
+    if owners > spare * groups:
+        packed_ref[base + 16 * groups :, :] = filled[spare * groups :, :].astype(BF16)
 
 
 def scan_kernel(
@@ -191,16 +203,17 @@
     payload_ref,
     decay_ref,
     input_ref,
-    partial_ref,
     in_map_ref,
     out_map_ref,
-    begin_ref,
-    final_ref,
+    scanned_ref,
+    states_even_ref,
+    states_odd_ref,
 ):
     rows, channels = mixed_ref.shape
-    blocks = rows // BLOCK
+    span = BLOCK * STATE
+    pairs = rows // BLOCK // 2
     starts, ends = bounds(len_ref, prompts)
-    projected = own_ref[...] + other_ref[...]
+    projected = own_ref[...] + other_ref[...].astype(F32)
     low = projected[:DT_RANK, :].T.astype(BF16)
     pre = jnp.dot(low, step_weight_ref[...], preferred_element_type=F32) + step_bias_ref[...]
     step = jnp.maximum(pre, 0.0) + jnp.log1p(jnp.exp(-jnp.abs(pre)))
@@ -210,94 +223,119 @@
         is_first = is_first | (position == starts[p])
     decay_ref[...] = jnp.where(is_first, RESET, step)
     input_ref[...] = step * mixed_ref[...].astype(F32)
-    for block in range(blocks):
+    for block in range(rows // BLOCK):
         columns = slice(block * BLOCK, (block + 1) * BLOCK)
         in_map_ref[block, :, 0:BLOCK] = projected[DT_RANK : DT_RANK + STATE, columns]
-        out_map_ref[block, :, 0:BLOCK] = projected[DT_RANK + STATE :, columns]
+    row = lax.broadcasted_iota(jnp.int32, (STATE, span), 0)
+    column = lax.broadcasted_iota(jnp.int32, (STATE, span), 1)
+    tiled = jnp.dot(
+        projected[DT_RANK + STATE :, :].T.astype(BF16),
+        jnp.where(column % STATE == row, 1.0, 0.0).astype(BF16),
+        preferred_element_type=F32,
+    )
+    row = lax.broadcasted_iota(jnp.int32, (rows, span), 0)
+    column = lax.broadcasted_iota(jnp.int32, (rows, span), 1)
+    out_map_ref[...] = jnp.where(column // STATE == row % BLOCK, tiled, 0.0).astype(BF16)
     rate = rate_ref[...] * (-math.log2(math.e))
 
-    def advance(state, block, index):
-        at = pl.multiple_of(block * BLOCK, BLOCK) + index
-        decay = jnp.exp2(decay_ref[pl.ds(at, 1), :] * rate)
-        entering = in_map_ref[block, :, index : index + 1] * input_ref[pl.ds(at, 1), :]
-        return state * decay + entering
-
-    def step_block(block, state):
-        begin_ref[block] = state
-        for index in range(BLOCK):
-            state = advance(state, block, index)
-            leaving = out_map_ref[block, :, index : index + 1] * state
-            at = pl.multiple_of(block * BLOCK * 8, BLOCK * 8) + 8 * index
-            half = leaving[:8, :] + leaving[8:, :]
-            for tile in range(channels // LANES):
-                partial_ref[tile, pl.ds(at, 8), :] = half[:, tile * LANES : (tile + 1) * LANES]
+    def leave(block, states):
+        at = pl.multiple_of(block * BLOCK, BLOCK)
+        scanned_ref[pl.ds(at, BLOCK), :] = jnp.dot(
+            out_map_ref[pl.ds(at, BLOCK), :], states, preferred_element_type=F32
+        )
+
+    def advance(block, state, states_ref, index):
+        at = pl.multiple_of(block * BLOCK, BLOCK)
+        for token in range(BLOCK):
+            decay = jnp.exp2(decay_ref[pl.ds(at + token, 1), :] * rate)
+            entering = in_map_ref[block, :, token : token + 1] * input_ref[pl.ds(at + token, 1), :]
+            state = state * decay + entering
+            states_ref[index, token * STATE : (token + 1) * STATE, :] = state.astype(BF16)
         return state
 
-    state = lax.fori_loop(0, blocks, step_block, jnp.zeros((STATE, channels), F32))
+
+    def two_blocks(pair, state):
+        before = jnp.maximum(pair - 1, 0)
+        leave(2 * before + 1, states_odd_ref[before])
+        state = advance(2 * pair, state, states_even_ref, pair)
+        leave(2 * pair, states_even_ref[pair])
+        return advance(2 * pair + 1, state, states_odd_ref, pair)
+
+    lax.fori_loop(0, pairs, two_blocks, jnp.zeros((STATE, channels), F32))
+    leave(2 * pairs - 1, states_odd_ref[pairs - 1])
     for p in range(prompts):
-        if p < prompts - 1:
-            last = ends[p] - 1
-            block = last // BLOCK
-            final_ref[...] = begin_ref[block]
-
-            def again(index, _, block=block):
-                at = block * BLOCK + index
-                decay = jnp.exp2(decay_ref[pl.ds(at, 1), :] * rate)
-                lane = lax.broadcasted_iota(jnp.int32, (STATE, LANES), 1)
-                column = jnp.sum(
-                    jnp.where(lane == index, in_map_ref[block], 0.0), axis=1, keepdims=True
-                )
-                entering = column * input_ref[pl.ds(at, 1), :]
-                final_ref[...] = final_ref[...] * decay + entering
-                return 0
-
-            lax.fori_loop(0, last - block * BLOCK + 1, again, 0)
-            final = final_ref[...].astype(BF16)
-        else:
-            final = state.astype(BF16)
+        last = ends[p] - 1
+        block = last // BLOCK
+        at = pl.multiple_of((last - block * BLOCK) * STATE, STATE)
+        final = jnp.where(
+            block % 2 == 0,
+            states_even_ref[block // 2, pl.ds(at, STATE), :],
+            states_odd_ref[block // 2, pl.ds(at, STATE), :],
+        )
         for tile in range(channels // LANES):
             at = (p * (channels // LANES) + tile) * STATE
             payload_ref[at : at + STATE, :] = final[:, tile * LANES : (tile + 1) * LANES]
     base = prompts * channels // LANES * STATE
     payload_ref[base:, :] = early_ref[...]
-    scanned = []
-    for tile in range(channels // LANES):
-        total = partial_ref[tile, pl.ds(0, rows, stride=8), :]
-        for index in range(1, 8):
-            total = total + partial_ref[tile, pl.ds(index, rows, stride=8), :]
-        scanned.append(total)
-    scanned = jnp.concatenate(scanned, axis=1)
     gate = gate_ref[1].astype(F32)
-    gated = (scanned + skip_ref[...] * mixed_ref[...].astype(F32)) * (gate * sigmoid(gate))
+    gated = (scanned_ref[...] + skip_ref[...] * mixed_ref[...].astype(F32)) * (
+        gate * sigmoid(gate)
+    )
     gated_ref[...] = gated
-    ones = jnp.ones((8, channels), BF16)
     sums_ref[0:1, :] = square_ref[0:1, :]
-    sums_ref[1:2, :] = dot_nt(ones, (gated * gated).astype(BF16))[0:1, :]
-
-
-def join_kernel(held_ref, new_ref, own_ref, other_ref, *refs):
-    across_refs, (joined_ref, fresh_ref, sums_ref, crossed_ref) = refs[:-4], refs[-4:]
+    sums_ref[1:2, :] = row_sums(gated * gated)
+
+
+def scan_call(prompts, lengths, own, other, mixed, inner, *rest):
+    rows, channels = mixed.shape
+    tiles = channels // LANES
+    payload_rows = prompts * tiles * STATE + rest[-2].shape[0]
+    return pl.pallas_call(
+        functools.partial(scan_kernel, prompts),
+        out_shape=(
+            jax.ShapeDtypeStruct((rows, channels), F32),
+            jax.ShapeDtypeStruct((2, rows), F32),
+            jax.ShapeDtypeStruct((payload_rows, LANES), BF16),
+        ),
+        in_specs=[SMEM] + [VMEM] * 10,
+        out_specs=(VMEM, VMEM, VMEM),
+        scratch_shapes=[
+            pltpu.VMEM((rows, channels), F32),
+            pltpu.VMEM((rows, channels), F32),
+            pltpu.VMEM((rows // BLOCK, STATE, LANES), F32),
+            pltpu.VMEM((rows, BLOCK * STATE), BF16),
+            pltpu.VMEM((rows, channels), F32),
+            pltpu.VMEM((rows // BLOCK // 2, BLOCK * STATE, channels), BF16),
+            pltpu.VMEM((rows // BLOCK // 2, BLOCK * STATE, channels), BF16),
+        ],
+        compiler_params=params(32),
+        name="scan",
+    )(lengths, own, other, mixed, inner, *rest)
+
+
+def join_kernel(held_ref, new_ref, own_ref, other_ref, joined_ref, sums_ref):
     count = held_ref.shape[0]
     joined_ref[:count] = held_ref[...]
     joined_ref[count:] = new_ref[...]
+    sums_ref[...] = own_ref[...] + other_ref[...]
+
+
+def hold_kernel(new_ref, far_ref, crossed_hbm, fresh_ref, sums_ref):
     fresh_ref[...] = new_ref[...]
-    sums_ref[...] = own_ref[...] + other_ref[...]
-    at = 0
-    for across_ref in across_refs:
-        crossed_ref[at : at + across_ref.shape[0]] = across_ref[...]
-        at += across_ref.shape[0]
+    sums_ref[...] = far_ref[...]
 
 
 def norm_kernel(
     attended_ref,
     gated_ref,
-    sums_ref,
+    own_ref,
+    other_ref,
     attention_gain_ref,
     mamba_gain_ref,
     attention_ref,
     mamba_ref,
 ):
-    sums = sums_ref[...]
+    sums = own_ref[...] + other_ref[...]
     sums = jnp.concatenate([sums, jnp.zeros((6, sums.shape[1]), F32)], axis=0).T
     attention_scale = lax.rsqrt(sums[:, 0:1] / (HEADS * HEAD_DIM) + EPSILON)
     attention_ref[...] = (attended_ref[...] * attention_scale * attention_gain_ref[...]).astype(
@@ -325,17 +363,23 @@
     sources = len(blocks)
     window_at = prompts * tiles * STATE
     tail_at = window_at + prompts * WINDOW
-    table_at = tail_at + 8 * tiles
-    owners = refs[0].shape[1] - table_at
+    depth = CONV - 1
+    spare = 16 - 2 * prompts * depth
+    table_rows = refs[0].shape[1] - tail_at
 
     def rows_of(source, at, size):
         ref, index = blocks[source]
         return ref[index, at : at + size, :]
 
-    owner = lax.broadcasted_iota(jnp.int32, (owners, LANES), 0)
+    row = lax.broadcasted_iota(jnp.int32, (table_rows, LANES), 0)
+    grouped = row < 8 * tiles
+    owner = jnp.where(
+        grouped, row // 16 * spare + row % 16 - (16 - spare), row - 8 * tiles + spare * (tiles // 2)
+    )
+    owner = jnp.where(grouped & (row % 16 < 16 - spare), -1, owner)
     pick = jnp.zeros((1, LANES), F32)
     for source in range(sources):
-        filled = rows_of(source, table_at, owners).astype(F32)
+        filled = rows_of(source, tail_at, table_rows).astype(F32)
         filled = jnp.sum(jnp.where(owner == me, filled, 0.0), axis=0, keepdims=True)
         pick = pick + jnp.where(filled > 0.5, filled + float(source * prompts - 1), 0.0)
     pick = pick.astype(jnp.int32)
@@ -354,7 +398,6 @@
     row = lax.broadcasted_iota(jnp.int32, (wide, LANES), 0)
     lane = lax.broadcasted_iota(jnp.int32, (wide, LANES), 1)
     unit = one_hot(row == lane)
-    depth = CONV - 1
     for first in range(0, sources, chunk):
         wanted = lax.broadcasted_iota(jnp.int32, (span, LANES), 0) // STATE + first * prompts
         take = dot_nt(spread, one_hot(wanted == pick))
@@ -401,7 +444,7 @@
         row = lax.broadcasted_iota(jnp.int32, (span_rows, LANES), 0)
         local = pick - first * prompts
         base = (local // prompts) * 16 + (local % prompts) * depth
-        hits = [one_hot(row == base + 8 * odd + tap) for odd in (0, 1) for tap in range(depth)]
+        hits = [one_hot(row == base + prompts * depth * odd + tap) for odd in (0, 1) for tap in range(depth)]
         hits = dot_nt(unit, jnp.concatenate(hits, axis=0)).astype(BF16)
         hits = jnp.concatenate(
             [hits[:, i * span_rows : (i + 1) * span_rows] for i in range(2 * depth)], axis=0
@@ -487,8 +530,8 @@
         return lax.ppermute(x, axis, [(i, i ^ bit) for i in range(size)])
 
     near = swap(partial, "tp", tp_size, 1)
-    owners = -(-pr_size // 16) * 16
-    early_rows = prompts * WINDOW + 8 * tiles + owners
+    spare = (16 - 2 * prompts * (CONV - 1)) * (tiles // 2)
+    early_rows = prompts * WINDOW + 8 * tiles + -(-max(pr_size - spare, 0) // 16) * 16
     attended, square, early = pl.pallas_call(
         functools.partial(attend_kernel, prompts),
         out_shape=(
@@ -522,30 +565,10 @@
     while bit < tp_size // 2:
         pair = pair + swap(pair, "tp", tp_size, bit)
         bit *= 2
-    far = swap(pair, "tp", tp_size, bit)
-
-    payload_rows = prompts * tiles * STATE + early_rows
-    gated, sums, payload = pl.pallas_call(
-        functools.partial(scan_kernel, prompts),
-        out_shape=(
-            shape((rows, channels)),
-            shape((2, rows)),
-            shape((payload_rows, LANES), BF16),
-        ),
-        in_specs=[SMEM] + [VMEM] * 10,
-        out_specs=(VMEM, VMEM, VMEM),
-        scratch_shapes=[
-            pltpu.VMEM((rows, channels), F32),
-            pltpu.VMEM((rows, channels), F32),
-            pltpu.VMEM((tiles, rows * 8, LANES), F32),
-            pltpu.VMEM((rows // BLOCK, STATE, LANES), F32),
-            pltpu.VMEM((rows // BLOCK, STATE, LANES), F32),
-            pltpu.VMEM((rows // BLOCK, STATE, channels), F32),
-            pltpu.VMEM((STATE, channels), F32),
-        ],
-        compiler_params=params(32),
-        name="scan",
-    )(
+    far = swap(pair.astype(BF16), "tp", tp_size, bit)
+
+    gated, sums, payload = scan_call(
+        prompts,
         prompt_lengths,
         pair,
         far,
@@ -563,40 +586,46 @@
     held = payload[None]
     pr_bits = [1 << i for i in reversed(range((pr_size - 1).bit_length()))]
     tp_bits = [1 << i for i in range((tp_size - 1).bit_length())]
-    fresh, crossed = held, []
-    for index in range(max(len(pr_bits) - 1, len(tp_bits))):
-        other = swap(sums, "tp", tp_size, tp_bits[index]) if index < len(tp_bits) else None
-        if index < len(pr_bits) - 1:
-            new = swap(held, "pr", pr_size, pr_bits[index])
-            crossed.append(swap(fresh, "pr", pr_size, pr_bits[-1]))
-            count = held.shape[0]
-            held, fresh, sums, across = pl.pallas_call(
-                join_kernel,
-                out_shape=(
-                    shape((2 * count,) + held.shape[1:], BF16),
-                    shape((count,) + held.shape[1:], BF16),
-                    shape(sums.shape),
-                    shape((count,) + held.shape[1:], BF16),
-                ),
-                in_specs=[VMEM] * (4 + len(crossed)),
-                out_specs=(VMEM,) * 4,
-                compiler_params=params(16),
-                name="join",
-            )(held, new, sums, jnp.zeros_like(sums) if other is None else other, *crossed)
-            crossed = [across]
-        else:
+    main, last = pr_bits[:-1], pr_bits[-1]
+    near, far = tp_bits[:-1], tp_bits[-1]
+    for index in range(max(len(main) - 1, len(near))):
+        other = swap(sums, "tp", tp_size, near[index]) if index < len(near) else None
+        if index >= len(main) - 1:
             sums = sums + other
-    crossed.append(swap(fresh, "pr", pr_size, pr_bits[-1]))
-    pieces = [held] + crossed
+            continue
+        new = swap(held, "pr", pr_size, main[index])
+        held, sums = pl.pallas_call(
+            join_kernel,
+            out_shape=(
+                shape((2 * held.shape[0],) + held.shape[1:], BF16),
+                shape(sums.shape),
+            ),
+            in_specs=[VMEM] * 4,
+            out_specs=(VMEM, VMEM),
+            compiler_params=params(16),
+            name="join",
+        )(held, new, sums, jnp.zeros_like(sums) if other is None else other)
+    fresh = swap(held, "pr", pr_size, main[-1])
+    crossed = swap(held, "pr", pr_size, last)
+    sums_far = swap(sums, "tp", tp_size, far)
+    fresh, sums_far = pl.pallas_call(
+        hold_kernel,
+        out_shape=(shape(fresh.shape, BF16), shape(sums.shape)),
+        in_specs=[VMEM, VMEM, HBM],
+        out_specs=(VMEM, VMEM),
+        compiler_params=params(16),
+        name="hold",
+    )(fresh, sums_far, crossed)
+    pieces = [held, fresh, crossed, swap(fresh, "pr", pr_size, last)]
     attention_out, mamba_out = pl.pallas_call(
         norm_kernel,
         out_shape=(shape((rows, features), BF16), shape((rows, channels), BF16)),
-        in_specs=[VMEM] * 5,
+        in_specs=[VMEM] * 6,
         out_specs=(VMEM, VMEM),
         compiler_params=params(16),
         cost_estimate=pl.CostEstimate(flops=1 << 24, bytes_accessed=2 << 20, transcendentals=0),
         name="norm",
-    )(attended, gated, sums, attention_gain[None], mamba_gain[None])
+    )(attended, gated, sums, sums_far, attention_gain[None], mamba_gain[None])
     keyval, state, conv = pl.pallas_call(
         functools.partial(deliver_kernel, prompts, len(pieces)),
         out_shape=(

time: 38.8 us -> 35 us (0.902)
  starting transfers between devices: 13.9 us -> 11.8 us
  Pallas kernels: 11.8 us -> 10 us
    ppermute x9 -> x8, starting transfers between devices: 13.9 us -> 11.8 us  [swap(): return lax.ppermute(x, axis, [(i, i ^ bit) for i in range(size)])]
    pallas_call x3, Pallas kernels: 5.47 us -> 3.72 us  [the longest x1 3.7 us: scan_call(): pl.pallas_call(functools.partial(scan_kernel, prompts), out_shape=(jax.Sh...]
    ppermute x9 -> x8, waiting for transfers between devices: 8.73 us -> 8.79 us  [swap(): return lax.ppermute(x, axis, [(i, i ^ bit) for i in range(size)])]
  transfers between devices with their start and end apart: 9 -> 8, of which waited for: 6 -> 5; matrix products, arithmetic and copies ran while one was open for 0% -> 0% of each run, Pallas kernels for 8% -> 9%
where the time goes in v5:
time: 35 us; the launch traced here: 34.8 us
  starting transfers between devices  11.8 us (34%)
  Pallas kernels  10 us (29%)
  waiting for transfers between devices  8.79 us (25%)
  matrix products  1.73 us (5%)
  local copies, waits for them, and re-layouts  1.56 us (4%)
  between operations  0.89 us (3%)
    ppermute x8, starting transfers between devices, swap(): return lax.ppermute(x, axis, [(i, i ^ bit) for i in range(size)])  11.8 us
    ppermute x8, waiting for transfers between devices, swap(): return lax.ppermute(x, axis, [(i, i ^ bit) for i in range(size)])  8.79 us
    pallas_call x1, Pallas kernels, scan_call(): pl.pallas_call(functools.partial(scan_kernel, prompts), out_shape=(jax.Sh...  3.7 us
    pallas_call x1, Pallas kernels, on_device(): pl.pallas_call(functools.partial(deliver_kernel, prompts, len(pieces)), o...  2.09 us
    pallas_call x1, Pallas kernels, on_device(): pl.pallas_call(functools.partial(attend_kernel, prompts), out_shape=(shap...  2.01 us
    dot_general x1, matrix products, on_device(): jnp.einsum('td,dgc->gtc', tokens, inner_weight, preferred_element_type=F32)  1.73 us
    unnamed x34, local copies, waits for them, and re-layouts  1.56 us
    pallas_call x1, Pallas kernels, on_device(): pl.pallas_call(functools.partial(mix_kernel, prompts), out_shape=(shape((...  1.14 us
  transfers between devices with their start and end apart: 8, of which 5 were waited for; matrix products, arithmetic and copies ran while one was open for 0% of the time, Pallas kernels for 9%

profile of v5, /device:TPU:0, one launch (start us, length us, event | category | flops | bytes accessed | tf_op | source)
XLA Modules:
  0.0 34.8 jit_solution(1767619133210628287)
XLA Ops:
  0.6 0.0 copy-start
  0.8 1.5 %copy-done = bf16[896,2,512]{2,1,0:T(2,128)(2,1)S(1)} copy-done((bf16[896,2,512]{2,1,0:T(2,128)(2,1)S(1)}, bf16[896,2,512]{2,1,0:T(2,128)(2,1)}, u32[]{:S(2)}) %copy-start) | copy-done | bytes 1835032
  2.2 1.7 %fusion.5.inner_ref.gate_ref = bf16[2,256,512]{2,1,0:T(8,128)(2,1)S(1)} fusion(bf16[896,2,512]{2,1,0:T(2,128)(2,1)S(1)} %copy-done, bf16[256,896]{1,0:T(8,128)(2,1)} %tokens_ref.1), kind=kOutput, calls=%fused_computation.3 | convolution fusion | flops 470024192 | bytes 2818048 | tf_op jit(solution)/shard_map/td,dgc->gtc/dot_general | solution.py:513
  4.0 0.0 copy-start.2
  4.0 0.0 copy-start.6
  4.0 0.0 copy-start.7
  4.1 1.1 %mix.1 = (f32[96,256]{1,0:T(8,128)S(1)}, bf16[256,512]{1,0:T(8,128)(2,1)S(1)}, f32[8,512]{1,0:T(8,128)S(1)}) custom-call(s32[1,2]{1,0:T(1,128)S(1)} %copy-done.8, bf16[2,256,512]{2,1,0:T(8,128)(2,1)S(1)} %fusion.5.inner_ref.gate_ref, f32[4,512]{1,0:T(4,128)S(1)} %copy-done.4, bf16[96,512]{1,0:T(8,128)(2,1)S(1)} %bitcast.18), custom_call_target="tpu_custom_call" | custom-call | tf_op jit(solution)/shard_map/mix/pallas_call | solution.py:515
  5.2 0.5 %collective-permute-start = (f32[96,256]{1,0:T(8,128)S(1)}, f32[96,256]{1,0:T(8,128)S(1)}, u32[]{:S(2)}, u32[]{:S(2)}) collective-permute-start(f32[96,256]{1,0:T(8,128)S(1)} %get-tuple-element.25), channel_id=1, source_target_pairs={{0,1},{1,0},{2,3},{3,2},{4,5},{5,4},{6,7},{7,6},{8,9},{9,8},{10,11... | collective-permute-start | bytes 294920 | tf_op jit(solution)/shard_map/ppermute | solution.py:530
  5.7 0.9 %collective-permute-done = f32[96,256]{1,0:T(8,128)S(1)} collective-permute-done((f32[96,256]{1,0:T(8,128)S(1)}, f32[96,256]{1,0:T(8,128)S(1)}, u32[]{:S(2)}, u32[]{:S(2)}) %collective-permute-start) | collective-permute-done | bytes 98336 | tf_op jit(solution)/shard_map/ppermute | solution.py:530
  6.7 2.9 %collective-permute-start.1 = (bf16[96,256]{1,0:T(8,128)(2,1)S(1)}, bf16[96,256]{1,0:T(8,128)(2,1)S(1)}, u32[]{:S(2)}, u32[]{:S(2)}) collective-permute-start(bf16[96,256]{1,0:T(8,128)(2,1)S(1)} %get-tuple-element.41), channel_id=1, source_target_pairs={{0,2},{1,3},{2,0},{3,1},{4,6},{5,7},{6,4},{7,5},{8,10},{9,11},{10,... | collective-permute-start | bytes 147464 | tf_op jit(solution)/shard_map/ppermute | solution.py:530
  9.6 2.0 %attend.1 = (f32[256,256]{1,0:T(8,128)S(1)}, f32[8,256]{1,0:T(8,128)S(1)}, bf16[96,128]{1,0:T(8,128)(2,1)S(1)}) custom-call(s32[1,2]{1,0:T(1,128)S(1)} %copy-done.8, bf16[256,896]{1,0:T(8,128)(2,1)S(1)} %copy-done.10, bf16[896,256]{1,0:T(8,128)(2,1)S(1)} %copy-done.11, bf16[64,896]{1,0:T(8,128)(2,1)S(1)} %bitcast.25, bf16[64,896]{1,0:T(8,128)(2,1)S(1)} %bitcast.26, ...), custom_call_target="tpu_custom_call" | custom-call | flops 352321536 | bytes 4194304 | tf_op jit(solution)/shard_map/attend/pallas_call | solution.py:535
  11.6 0.0 collective-permute-done.1.other_ref
  11.7 3.7 %scan.1 = (f32[256,512]{1,0:T(8,128)S(1)}, f32[2,256]{1,0:T(2,128)S(1)}, bf16[224,128]{1,0:T(8,128)(2,1)S(1)}) custom-call(s32[1,2]{1,0:T(1,128)S(1)} %copy-done.8, f32[96,256]{1,0:T(8,128)S(1)} %get-tuple-element.42.own_ref, bf16[96,256]{1,0:T(8,128)(2,1)S(1)} %collective-permute-done.1.other_ref, bf16[256,512]{1,0:T(8,128)(2,1)S(1)} %get-tuple-element.26.mixed_ref, ...), custom_call_target="tpu_custom_call" | custom-call | tf_op jit(solution)/shard_map/scan/pallas_call | solution.py:293
  15.4 3.2 %collective-permute-start.2 = (bf16[1,224,128]{2,1,0:T(8,128)(2,1)S(1)}, bf16[1,224,128]{2,1,0:T(8,128)(2,1)S(1)}, u32[]{:S(2)}, u32[]{:S(2)}) collective-permute-start(bf16[1,224,128]{2,1,0:T(8,128)(2,1)S(1)} %bitcast.19), channel_id=1, source_target_pairs={{0,16},{4,20},{8,24},{12,28},{16,0},{20,4},{24,8},{28,12},{1,17},{... | collective-permute-start | bytes 172040 | tf_op jit(solution)/shard_map/ppermute | solution.py:530
  18.6 1.2 %collective-permute-done.3.other_ref = f32[2,256]{1,0:T(2,128)S(1)} collective-permute-done((f32[2,256]{1,0:T(2,128)S(1)}, f32[2,256]{1,0:T(2,128)S(1)}, u32[]{:S(2)}, u32[]{:S(2)}) %collective-permute-start.3) | collective-permute-done | bytes 2080 | tf_op jit(solution)/shard_map/ppermute | solution.py:530
  19.7 1.3 %collective-permute-done.2.new_ref = bf16[1,224,128]{2,1,0:T(8,128)(2,1)S(1)} collective-permute-done((bf16[1,224,128]{2,1,0:T(8,128)(2,1)S(1)}, bf16[1,224,128]{2,1,0:T(8,128)(2,1)S(1)}, u32[]{:S(2)}, u32[]{:S(2)}) %collective-permute-start.2) | collective-permute-done | bytes 57376 | tf_op jit(solution)/shard_map/ppermute | solution.py:530
  21.1 1.6 %collective-permute-start.6 = (bf16[2,224,128]{2,1,0:T(8,128)(2,1)S(1)}, bf16[2,224,128]{2,1,0:T(8,128)(2,1)S(1)}, u32[]{:S(2)}, u32[]{:S(2)}) collective-permute-start(bf16[2,224,128]{2,1,0:T(8,128)(2,1)S(1)} %get-tuple-element.33.refs_0_), channel_id=1, source_target_pairs={{0,4},{4,0},{8,12},{12,8},{16,20},{20,16},{24,28},{28,24},{1,5},{5... | collective-permute-start | bytes 344072 | tf_op jit(solution)/shard_map/ppermute | solution.py:530
  22.7 1.5 %collective-permute-start.4 = (bf16[2,224,128]{2,1,0:T(8,128)(2,1)S(1)}, bf16[2,224,128]{2,1,0:T(8,128)(2,1)S(1)}, u32[]{:S(2)}, u32[]{:S(2)}) collective-permute-start(bf16[2,224,128]{2,1,0:T(8,128)(2,1)S(1)} %get-tuple-element.33.refs_0_), channel_id=1, source_target_pairs={{0,8},{4,12},{8,0},{12,4},{16,24},{20,28},{24,16},{28,20},{1,9},{5... | collective-permute-start | bytes 344072 | tf_op jit(solution)/shard_map/ppermute | solution.py:530
  24.2 1.5 %collective-permute-start.5 = (f32[2,256]{1,0:T(2,128)S(1)}, f32[2,256]{1,0:T(2,128)S(1)}, u32[]{:S(2)}, u32[]{:S(2)}) collective-permute-start(f32[2,256]{1,0:T(2,128)S(1)} %get-tuple-element.32.own_ref), channel_id=1, source_target_pairs={{0,2},{1,3},{2,0},{3,1},{4,6},{5,7},{6,4},{7,5},{8,10},{9,11},{10,... | collective-permute-start | bytes 6152 | tf_op jit(solution)/shard_map/ppermute | solution.py:530
  25.7 2.1 %collective-permute-done.5.far_ref = f32[2,256]{1,0:T(2,128)S(1)} collective-permute-done((f32[2,256]{1,0:T(2,128)S(1)}, f32[2,256]{1,0:T(2,128)S(1)}, u32[]{:S(2)}, u32[]{:S(2)}) %collective-permute-start.5) | collective-permute-done | bytes 2080 | tf_op jit(solution)/shard_map/ppermute | solution.py:530
  27.8 0.6 %collective-permute-start.7 = (bf16[2,224,128]{2,1,0:T(8,128)(2,1)S(1)}, bf16[2,224,128]{2,1,0:T(8,128)(2,1)S(1)}, u32[]{:S(2)}, u32[]{:S(2)}) collective-permute-start(bf16[2,224,128]{2,1,0:T(8,128)(2,1)S(1)} %get-tuple-element.37.refs_1_), channel_id=1, source_target_pairs={{0,4},{4,0},{8,12},{12,8},{16,20},{20,16},{24,28},{28,24},{1,5},{5... | collective-permute-start | bytes 344072 | tf_op jit(solution)/shard_map/ppermute | solution.py:530
  28.4 1.0 %norm.1 = (bf16[256,256]{1,0:T(8,128)(2,1)}, bf16[256,512]{1,0:T(8,128)(2,1)}) custom-call(f32[256,256]{1,0:T(8,128)S(1)} %get-tuple-element.24.attended_ref, f32[256,512]{1,0:T(8,128)S(1)} %get-tuple-element.29.gated_ref, f32[2,256]{1,0:T(2,128)S(1)} %get-tuple-element.32.own_ref, f32[2,256]{1,0:T(2,128)S(1)} %get-tuple-element.34.other_ref, ...), custom_call_target="tpu_custom_call" | custom-call | flops 16777216 | bytes 2097152 | tf_op jit(solution)/shard_map/norm/pallas_call | solution.py:620
  29.5 3.2 %collective-permute-done.7.refs_3_ = bf16[2,224,128]{2,1,0:T(8,128)(2,1)S(1)} collective-permute-done((bf16[2,224,128]{2,1,0:T(8,128)(2,1)S(1)}, bf16[2,224,128]{2,1,0:T(8,128)(2,1)S(1)}, u32[]{:S(2)}, u32[]{:S(2)}) %collective-permute-start.7) | collective-permute-done | bytes 114720 | tf_op jit(solution)/shard_map/ppermute | solution.py:530
  32.7 2.1 %deliver.1 = (bf16[56,2,32,64]{3,2,1,0:T(8,128)(2,1)}, bf16[56,16,512]{2,1,0:T(8,128)(2,1)}, bf16[3,56,512]{2,1,0:T(8,128)(2,1)}) custom-call(s32[1]{0:T(128)} %bitcast.13.me_ref, bf16[2,224,128]{2,1,0:T(8,128)(2,1)S(1)} %get-tuple-element.33.refs_0_, bf16[2,224,128]{2,1,0:T(8,128)(2,1)S(1)} %get-tuple-element.37.refs_1_, ...), custom_call_target="tpu_custom_call" | custom-call | tf_op jit(solution)/shard_map/deliver/pallas_call | solution.py:629
  (35 shorter events, 0.1 us)
Async XLA Ops:
  0.7 8.9 %copy-start.10 = (bf16[256,896]{1,0:T(8,128)(2,1)S(1)}, bf16[256,896]{1,0:T(8,128)(2,1)}, u32[]{:S(2)}) copy-start(bf16[256,896]{1,0:T(8,128)(2,1)} %tokens_ref.1) | copy-start | bytes 1376260
  0.7 3.3 %copy-start.8 = (s32[1,2]{1,0:T(1,128)S(1)}, s32[1,2]{1,0:T(1,128)}, u32[]{:S(2)}) copy-start(s32[1,2]{1,0:T(1,128)} %len_ref.5) | copy-start | bytes 28
  0.7 3.3 %copy-start.1 = (bf16[512,96]{0,1:T(8,128)(2,1)S(1)}, bf16[512,96]{0,1:T(8,128)(2,1)}, u32[]{:S(2)}) copy-start(bf16[512,96]{0,1:T(8,128)(2,1)} %param.25) | copy-start | bytes 294916
  0.7 3.3 %copy-start.4 = (f32[4,512]{1,0:T(4,128)S(1)}, f32[4,512]{1,0:T(4,128)}, u32[]{:S(2)}) copy-start(f32[4,512]{1,0:T(4,128)} %conv_ref.1) | copy-start | bytes 24580
  0.7 8.9 %copy-start.16 = (s32[56]{0:T(128)S(1)}, s32[56]{0:T(128)}, u32[]{:S(2)}) copy-start(s32[56]{0:T(128)} %param.33) | copy-start | bytes 676
  0.7 8.9 %copy-start.15 = (s32[56]{0:T(128)S(1)}, s32[56]{0:T(128)}, u32[]{:S(2)}) copy-start(s32[56]{0:T(128)} %param.32) | copy-start | bytes 676
  0.7 8.9 %copy-start.14 = (s32[56]{0:T(128)S(1)}, s32[56]{0:T(128)}, u32[]{:S(2)}) copy-start(s32[56]{0:T(128)} %param.31) | copy-start | bytes 676
  0.7 8.9 %copy-start.13 = (bf16[896,64]{0,1:T(8,128)(2,1)S(1)}, bf16[896,64]{0,1:T(8,128)(2,1)}, u32[]{:S(2)}) copy-start(bf16[896,64]{0,1:T(8,128)(2,1)} %param.21) | copy-start | bytes 344068
  0.7 8.9 %copy-start.12 = (bf16[896,64]{0,1:T(8,128)(2,1)S(1)}, bf16[896,64]{0,1:T(8,128)(2,1)}, u32[]{:S(2)}) copy-start(bf16[896,64]{0,1:T(8,128)(2,1)} %param.20) | copy-start | bytes 344068
  0.7 8.9 %copy-start.11 = (bf16[896,256]{1,0:T(8,128)(2,1)S(1)}, bf16[896,256]{1,0:T(8,128)(2,1)}, u32[]{:S(2)}) copy-start(bf16[896,256]{1,0:T(8,128)(2,1)} %query_ref.1) | copy-start | bytes 1376260
  4.0 7.7 %copy-start.2 = (bf16[64,512]{1,0:T(8,128)(2,1)S(1)}, bf16[64,512]{1,0:T(8,128)(2,1)}, u32[]{:S(2)}) copy-start(bf16[64,512]{1,0:T(8,128)(2,1)} %step_weight_ref.1) | copy-start | bytes 196612
  4.0 7.7 %copy-start.3 = (f32[16,512]{1,0:T(8,128)S(1)}, f32[16,512]{1,0:T(8,128)}, u32[]{:S(2)}) copy-start(f32[16,512]{1,0:T(8,128)} %rate_ref.1) | copy-start | bytes 98308
  4.0 7.7 %copy-start.5 = (f32[512]{0:T(512)S(1)}, f32[512]{0:T(512)}, u32[]{:S(2)}) copy-start(f32[512]{0:T(512)} %param.27) | copy-start | bytes 6148
  4.0 7.7 %copy-start.6 = (f32[512]{0:T(512)S(1)}, f32[512]{0:T(512)}, u32[]{:S(2)}) copy-start(f32[512]{0:T(512)} %param.29) | copy-start | bytes 6148
  4.0 24.4 %copy-start.7 = (f32[512]{0:T(512)S(1)}, f32[512]{0:T(512)}, u32[]{:S(2)}) copy-start(f32[512]{0:T(512)} %param.30) | copy-start | bytes 6148
  4.0 24.4 %copy-start.9 = (f32[256]{0:T(256)S(1)}, f32[256]{0:T(256)}, u32[]{:S(2)}) copy-start(f32[256]{0:T(256)} %param.22) | copy-start | bytes 3076
  5.2 1.5 %collective-permute-start = (f32[96,256]{1,0:T(8,128)S(1)}, f32[96,256]{1,0:T(8,128)S(1)}, u32[]{:S(2)}, u32[]{:S(2)}) collective-permute-start(f32[96,256]{1,0:T(8,128)S(1)} %get-tuple-element.25), channel_id=1, source_target_pairs={{0,1},{1,0},{2,3},{3,2},{4,5},{5,4},{6,7},{7,6},{8,9},{9,8},{10,11... | collective-permute-start | bytes 294920 | tf_op jit(solution)/shard_map/ppermute | solution.py:530
  6.7 5.0 %collective-permute-start.1 = (bf16[96,256]{1,0:T(8,128)(2,1)S(1)}, bf16[96,256]{1,0:T(8,128)(2,1)S(1)}, u32[]{:S(2)}, u32[]{:S(2)}) collective-permute-start(bf16[96,256]{1,0:T(8,128)(2,1)S(1)} %get-tuple-element.41), channel_id=1, source_target_pairs={{0,2},{1,3},{2,0},{3,1},{4,6},{5,7},{6,4},{7,5},{8,10},{9,11},{10,... | collective-permute-start | bytes 147464 | tf_op jit(solution)/shard_map/ppermute | solution.py:530
  15.4 5.7 %collective-permute-start.2 = (bf16[1,224,128]{2,1,0:T(8,128)(2,1)S(1)}, bf16[1,224,128]{2,1,0:T(8,128)(2,1)S(1)}, u32[]{:S(2)}, u32[]{:S(2)}) collective-permute-start(bf16[1,224,128]{2,1,0:T(8,128)(2,1)S(1)} %bitcast.19), channel_id=1, source_target_pairs={{0,16},{4,20},{8,24},{12,28},{16,0},{20,4},{24,8},{28,12},{1,17},{... | collective-permute-start | bytes 172040 | tf_op jit(solution)/shard_map/ppermute | solution.py:530
  18.6 1.2 %collective-permute-start.3 = (f32[2,256]{1,0:T(2,128)S(1)}, f32[2,256]{1,0:T(2,128)S(1)}, u32[]{:S(2)}, u32[]{:S(2)}) collective-permute-start(f32[2,256]{1,0:T(2,128)S(1)} %get-tuple-element.31.own_ref), channel_id=1, source_target_pairs={{0,1},{1,0},{2,3},{3,2},{4,5},{5,4},{6,7},{7,6},{8,9},{9,8},{10,11... | collective-permute-start | bytes 6152 | tf_op jit(solution)/shard_map/ppermute | solution.py:530
  21.1 6.7 %collective-permute-start.6 = (bf16[2,224,128]{2,1,0:T(8,128)(2,1)S(1)}, bf16[2,224,128]{2,1,0:T(8,128)(2,1)S(1)}, u32[]{:S(2)}, u32[]{:S(2)}) collective-permute-start(bf16[2,224,128]{2,1,0:T(8,128)(2,1)S(1)} %get-tuple-element.33.refs_0_), channel_id=1, source_target_pairs={{0,4},{4,0},{8,12},{12,8},{16,20},{20,16},{24,28},{28,24},{1,5},{5... | collective-permute-start | bytes 344072 | tf_op jit(solution)/shard_map/ppermute | solution.py:530
  22.7 5.1 %collective-permute-start.4 = (bf16[2,224,128]{2,1,0:T(8,128)(2,1)S(1)}, bf16[2,224,128]{2,1,0:T(8,128)(2,1)S(1)}, u32[]{:S(2)}, u32[]{:S(2)}) collective-permute-start(bf16[2,224,128]{2,1,0:T(8,128)(2,1)S(1)} %get-tuple-element.33.refs_0_), channel_id=1, source_target_pairs={{0,8},{4,12},{8,0},{12,4},{16,24},{20,28},{24,16},{28,20},{1,9},{5... | collective-permute-start | bytes 344072 | tf_op jit(solution)/shard_map/ppermute | solution.py:530
  24.2 3.6 %collective-permute-start.5 = (f32[2,256]{1,0:T(2,128)S(1)}, f32[2,256]{1,0:T(2,128)S(1)}, u32[]{:S(2)}, u32[]{:S(2)}) collective-permute-start(f32[2,256]{1,0:T(2,128)S(1)} %get-tuple-element.32.own_ref), channel_id=1, source_target_pairs={{0,2},{1,3},{2,0},{3,1},{4,6},{5,7},{6,4},{7,5},{8,10},{9,11},{10,... | collective-permute-start | bytes 6152 | tf_op jit(solution)/shard_map/ppermute | solution.py:530
  27.8 4.9 %collective-permute-start.7 = (bf16[2,224,128]{2,1,0:T(8,128)(2,1)S(1)}, bf16[2,224,128]{2,1,0:T(8,128)(2,1)S(1)}, u32[]{:S(2)}, u32[]{:S(2)}) collective-permute-start(bf16[2,224,128]{2,1,0:T(8,128)(2,1)S(1)} %get-tuple-element.37.refs_1_), channel_id=1, source_target_pairs={{0,4},{4,0},{8,12},{12,8},{16,20},{20,16},{24,28},{28,24},{1,5},{5... | collective-permute-start | bytes 344072 | tf_op jit(solution)/shard_map/ppermute | solution.py:530
  (1 other events, 1.6 us)

commit v6 on v5

--- a/solution.py
+++ b/solution.py
@@ -82,11 +82,10 @@
     scan_ref,
     partial_ref,
     mixed_ref,
-    tail_ref,
     raw_ref,
 ):
     _, rows, channels = inner_ref.shape
-    starts, ends = bounds(len_ref, prompts)
+    starts, _ = bounds(len_ref, prompts)
     raw = inner_ref[0].astype(F32)
     raw_ref[pl.ds(0, 8), :] = jnp.zeros((8, channels), F32)
     raw_ref[pl.ds(8, rows), :] = raw
@@ -100,8 +99,6 @@
     mixed = (total * sigmoid(total)).astype(BF16)
     mixed_ref[...] = mixed
     partial_ref[...] = dot_nt(scan_ref[...], mixed)
-    pick = last_rows((8, rows), CONV - 1, starts, ends)
-    tail_ref[...] = jnp.dot(pick, inner_ref[0], preferred_element_type=F32)
 
 
 def attend_kernel(
@@ -111,7 +108,7 @@
     query_ref,
     key_ref,
     value_ref,
-    tail_ref,
+    inner_ref,
     prompt_ref,
     owner_ref,
     slot_ref,
@@ -121,7 +118,7 @@
     request_ref,
 ):
     rows, width = tokens_ref.shape
-    channels = tail_ref.shape[1]
+    channels = inner_ref.shape[2]
     features = query_ref.shape[1]
     group = features // HEAD_DIM
     starts, ends = bounds(len_ref, prompts)
@@ -170,13 +167,15 @@
         jnp.where(owner, 1.0, 0.0).astype(BF16),
         jnp.where(slot, number, 0).astype(F32).astype(BF16),
     )
+    pick = last_rows((8, rows), CONV - 1, starts, ends)
+    tail = jnp.dot(pick, inner_ref[0], preferred_element_type=F32)
     base = prompts * WINDOW
     for group in range(groups):
         at = 2 * group * LANES
         packed_ref[base + 16 * group : base + 16 * (group + 1), :] = jnp.concatenate(
             [
-                tail_ref[:depth, at : at + LANES],
-                tail_ref[:depth, at + LANES : at + 2 * LANES],
+                tail[:depth, at : at + LANES],
+                tail[:depth, at + LANES : at + 2 * LANES],
                 filled[spare * group : spare * (group + 1), :],
             ],
             axis=0,
@@ -191,26 +190,18 @@
     own_ref,
     other_ref,
     mixed_ref,
-    gate_ref,
     step_weight_ref,
     step_bias_ref,
     rate_ref,
-    skip_ref,
     early_ref,
-    square_ref,
-    gated_ref,
-    sums_ref,
     payload_ref,
+    states_even_ref,
+    states_odd_ref,
     decay_ref,
     input_ref,
     in_map_ref,
-    out_map_ref,
-    scanned_ref,
-    states_even_ref,
-    states_odd_ref,
 ):
     rows, channels = mixed_ref.shape
-    span = BLOCK * STATE
     pairs = rows // BLOCK // 2
     starts, ends = bounds(len_ref, prompts)
     projected = own_ref[...] + other_ref[...].astype(F32)
@@ -226,23 +217,7 @@
     for block in range(rows // BLOCK):
         columns = slice(block * BLOCK, (block + 1) * BLOCK)
         in_map_ref[block, :, 0:BLOCK] = projected[DT_RANK : DT_RANK + STATE, columns]
-    row = lax.broadcasted_iota(jnp.int32, (STATE, span), 0)
-    column = lax.broadcasted_iota(jnp.int32, (STATE, span), 1)
-    tiled = jnp.dot(
-        projected[DT_RANK + STATE :, :].T.astype(BF16),
-        jnp.where(column % STATE == row, 1.0, 0.0).astype(BF16),
-        preferred_element_type=F32,
-    )
-    row = lax.broadcasted_iota(jnp.int32, (rows, span), 0)
-    column = lax.broadcasted_iota(jnp.int32, (rows, span), 1)
-    out_map_ref[...] = jnp.where(column // STATE == row % BLOCK, tiled, 0.0).astype(BF16)
     rate = rate_ref[...] * (-math.log2(math.e))
-
-    def leave(block, states):
-        at = pl.multiple_of(block * BLOCK, BLOCK)
-        scanned_ref[pl.ds(at, BLOCK), :] = jnp.dot(
-            out_map_ref[pl.ds(at, BLOCK), :], states, preferred_element_type=F32
-        )
 
     def advance(block, state, states_ref, index):
         at = pl.multiple_of(block * BLOCK, BLOCK)
@@ -253,16 +228,11 @@
             states_ref[index, token * STATE : (token + 1) * STATE, :] = state.astype(BF16)
         return state
 
-
     def two_blocks(pair, state):
-        before = jnp.maximum(pair - 1, 0)
-        leave(2 * before + 1, states_odd_ref[before])
         state = advance(2 * pair, state, states_even_ref, pair)
-        leave(2 * pair, states_even_ref[pair])
         return advance(2 * pair + 1, state, states_odd_ref, pair)
 
     lax.fori_loop(0, pairs, two_blocks, jnp.zeros((STATE, channels), F32))
-    leave(2 * pairs - 1, states_odd_ref[pairs - 1])
     for p in range(prompts):
         last = ends[p] - 1
         block = last // BLOCK
@@ -277,52 +247,81 @@
             payload_ref[at : at + STATE, :] = final[:, tile * LANES : (tile + 1) * LANES]
     base = prompts * channels // LANES * STATE
     payload_ref[base:, :] = early_ref[...]
-    gate = gate_ref[1].astype(F32)
-    gated = (scanned_ref[...] + skip_ref[...] * mixed_ref[...].astype(F32)) * (
-        gate * sigmoid(gate)
-    )
-    gated_ref[...] = gated
-    sums_ref[0:1, :] = square_ref[0:1, :]
-    sums_ref[1:2, :] = row_sums(gated * gated)
-
-
-def scan_call(prompts, lengths, own, other, mixed, inner, *rest):
+
+
+def scan_call(prompts, lengths, own, other, mixed, *rest):
     rows, channels = mixed.shape
     tiles = channels // LANES
-    payload_rows = prompts * tiles * STATE + rest[-2].shape[0]
+    payload_rows = prompts * tiles * STATE + rest[-1].shape[0]
+    states = jax.ShapeDtypeStruct((rows // BLOCK // 2, BLOCK * STATE, channels), BF16)
     return pl.pallas_call(
         functools.partial(scan_kernel, prompts),
-        out_shape=(
-            jax.ShapeDtypeStruct((rows, channels), F32),
-            jax.ShapeDtypeStruct((2, rows), F32),
-            jax.ShapeDtypeStruct((payload_rows, LANES), BF16),
-        ),
-        in_specs=[SMEM] + [VMEM] * 10,
-        out_specs=(VMEM, VMEM, VMEM),
+        out_shape=(jax.ShapeDtypeStruct((payload_rows, LANES), BF16), states, states),
+        in_specs=[SMEM] + [VMEM] * 7,
+        out_specs=(VMEM,) * 3,
         scratch_shapes=[
             pltpu.VMEM((rows, channels), F32),
             pltpu.VMEM((rows, channels), F32),
             pltpu.VMEM((rows // BLOCK, STATE, LANES), F32),
-            pltpu.VMEM((rows, BLOCK * STATE), BF16),
-            pltpu.VMEM((rows, channels), F32),
-            pltpu.VMEM((rows // BLOCK // 2, BLOCK * STATE, channels), BF16),
-            pltpu.VMEM((rows // BLOCK // 2, BLOCK * STATE, channels), BF16),
         ],
-        compiler_params=params(32),
+        compiler_params=params(16),
         name="scan",
-    )(lengths, own, other, mixed, inner, *rest)
-
-
-def join_kernel(held_ref, new_ref, own_ref, other_ref, joined_ref, sums_ref):
+    )(lengths, own, other, mixed, *rest)
+
+
+def gate_kernel(
+    own_ref,
+    other_ref,
+    states_even_ref,
+    states_odd_ref,
+    mixed_ref,
+    inner_ref,
+    skip_ref,
+    square_ref,
+    gated_ref,
+    sums_ref,
+    out_map_ref,
+    scanned_ref,
+):
+    rows, channels = mixed_ref.shape
+    span = BLOCK * STATE
+    maps = slice(DT_RANK + STATE, DT_RANK + 2 * STATE)
+    out_map = own_ref[maps, :] + other_ref[maps, :].astype(F32)
+    row = lax.broadcasted_iota(jnp.int32, (STATE, span), 0)
+    column = lax.broadcasted_iota(jnp.int32, (STATE, span), 1)
+    tiled = jnp.dot(
+        out_map.T.astype(BF16),
+        jnp.where(column % STATE == row, 1.0, 0.0).astype(BF16),
+        preferred_element_type=F32,
+    )
+    row = lax.broadcasted_iota(jnp.int32, (rows, span), 0)
+    column = lax.broadcasted_iota(jnp.int32, (rows, span), 1)
+    out_map_ref[...] = jnp.where(column // STATE == row % BLOCK, tiled, 0.0).astype(BF16)
+    for block in range(rows // BLOCK):
+        states_ref = states_odd_ref if block % 2 else states_even_ref
+        at = slice(block * BLOCK, (block + 1) * BLOCK)
+        scanned_ref[at, :] = jnp.dot(
+            out_map_ref[at, :], states_ref[block // 2], preferred_element_type=F32
+        )
+    gate = inner_ref[1].astype(F32)
+    gated = (scanned_ref[...] + skip_ref[...] * mixed_ref[...].astype(F32)) * (
+        gate * sigmoid(gate)
+    )
+    gated_ref[...] = gated
+    sums_ref[0:1, :] = square_ref[0:1, :]
+    sums_ref[1:2, :] = row_sums(gated * gated)
+
+
+def join_kernel(held_ref, new_ref, sums_ref, joined_ref, same_ref):
     count = held_ref.shape[0]
     joined_ref[:count] = held_ref[...]
     joined_ref[count:] = new_ref[...]
+    same_ref[...] = sums_ref[...]
+
+
+def hold_kernel(new_ref, own_ref, other_ref, crossed_hbm, fresh_ref, sums_ref):
+    fresh_ref[...] = new_ref[...]
     sums_ref[...] = own_ref[...] + other_ref[...]
-
-
-def hold_kernel(new_ref, far_ref, crossed_hbm, fresh_ref, sums_ref):
-    fresh_ref[...] = new_ref[...]
-    sums_ref[...] = far_ref[...]
 
 
 def norm_kernel(
@@ -512,15 +511,14 @@
 
     inner = jnp.einsum("td,dgc->gtc", tokens, inner_weight, preferred_element_type=F32)
     inner = inner.astype(BF16)
-    partial, mixed, tail = pl.pallas_call(
+    partial, mixed = pl.pallas_call(
         functools.partial(mix_kernel, prompts),
         out_shape=(
             shape((DT_RANK + 2 * STATE, rows)),
             shape((rows, channels), BF16),
-            shape((8, channels)),
         ),
         in_specs=[SMEM] + [VMEM] * 3,
-        out_specs=(VMEM, VMEM, VMEM),
+        out_specs=(VMEM, VMEM),
         scratch_shapes=[pltpu.VMEM((rows + 8, channels), F32)],
         compiler_params=params(16),
         name="mix",
@@ -555,7 +553,7 @@
         query_weight,
         key_weight.T,
         value_weight.T,
-        tail,
+        inner,
         request_prompt[None],
         request_owner[None],
         request_slot[None],
@@ -567,56 +565,64 @@
         bit *= 2
     far = swap(pair.astype(BF16), "tp", tp_size, bit)
 
-    gated, sums, payload = scan_call(
+    payload, states_even, states_odd = scan_call(
         prompts,
         prompt_lengths,
         pair,
         far,
         mixed,
-        inner,
         step_weight,
         step_bias[None],
         mamba_rate,
-        mamba_skip[None],
         early,
-        square,
-    )
+    )
+    gated, sums = pl.pallas_call(
+        gate_kernel,
+        out_shape=(shape((rows, channels)), shape((2, rows))),
+        in_specs=[VMEM] * 8,
+        out_specs=(VMEM, VMEM),
+        scratch_shapes=[
+            pltpu.VMEM((rows, BLOCK * STATE), BF16),
+            pltpu.VMEM((rows, channels), F32),
+        ],
+        compiler_params=params(16),
+        cost_estimate=pl.CostEstimate(flops=1 << 24, bytes_accessed=4 << 20, transcendentals=0),
+        name="gate",
+    )(pair, far, states_even, states_odd, mixed, inner, mamba_skip[None], square)
 
     me = lax.axis_index("pr").astype(jnp.int32)
     held = payload[None]
     pr_bits = [1 << i for i in reversed(range((pr_size - 1).bit_length()))]
     tp_bits = [1 << i for i in range((tp_size - 1).bit_length())]
     main, last = pr_bits[:-1], pr_bits[-1]
-    near, far = tp_bits[:-1], tp_bits[-1]
-    for index in range(max(len(main) - 1, len(near))):
-        other = swap(sums, "tp", tp_size, near[index]) if index < len(near) else None
-        if index >= len(main) - 1:
-            sums = sums + other
-            continue
-        new = swap(held, "pr", pr_size, main[index])
+    for bit in main[:-1]:
+        new = swap(held, "pr", pr_size, bit)
         held, sums = pl.pallas_call(
             join_kernel,
             out_shape=(
                 shape((2 * held.shape[0],) + held.shape[1:], BF16),
                 shape(sums.shape),
             ),
-            in_specs=[VMEM] * 4,
+            in_specs=[VMEM] * 3,
             out_specs=(VMEM, VMEM),
             compiler_params=params(16),
             name="join",
-        )(held, new, sums, jnp.zeros_like(sums) if other is None else other)
+        )(held, new, sums)
+    for bit in tp_bits[:-2]:
+        sums = sums + swap(sums, "tp", tp_size, bit)
+    crossed = swap(held, "pr", pr_size, last)
     fresh = swap(held, "pr", pr_size, main[-1])
-    crossed = swap(held, "pr", pr_size, last)
-    sums_far = swap(sums, "tp", tp_size, far)
-    fresh, sums_far = pl.pallas_call(
+    other = swap(sums, "tp", tp_size, tp_bits[-2])
+    fresh, sums = pl.pallas_call(
         hold_kernel,
         out_shape=(shape(fresh.shape, BF16), shape(sums.shape)),
-        in_specs=[VMEM, VMEM, HBM],
+        in_specs=[VMEM, VMEM, VMEM, HBM],
         out_specs=(VMEM, VMEM),
         compiler_params=params(16),
         name="hold",
-    )(fresh, sums_far, crossed)
+    )(fresh, sums, other, crossed)
     pieces = [held, fresh, crossed, swap(fresh, "pr", pr_size, last)]
+    sums_far = swap(sums, "tp", tp_size, tp_bits[-1])
     attention_out, mamba_out = pl.pallas_call(
         norm_kernel,
         out_shape=(shape((rows, features), BF16), shape((rows, channels), BF16)),

time: 35 us -> 35.6 us (1.017)
  starting transfers between devices: 11.8 us -> 13.2 us
  waiting for transfers between devices: 8.79 us -> 7.89 us
    ppermute x8, starting transfers between devices: 11.8 us -> 13.2 us  [swap(): return lax.ppermute(x, axis, [(i, i ^ bit) for i in range(size)])]
    pallas_call x0 -> x1, Pallas kernels: none -> 0.93 us  [on_device(): pl.pallas_call(gate_kernel, out_shape=(shape((rows, channels)), shape((2,...]
    ppermute x8, waiting for transfers between devices: 8.79 us -> 7.89 us  [swap(): return lax.ppermute(x, axis, [(i, i ^ bit) for i in range(size)])]
    pallas_call x1, Pallas kernels: 3.7 us -> 3.08 us  [scan_call(): pl.pallas_call(functools.partial(scan_kernel, prompts), out_shape=(jax.Sh...]
  transfers between devices with their start and end apart: 8 -> 8, of which waited for: 5 -> 7; matrix products, arithmetic and copies ran while one was open for 0% -> 0% of each run, Pallas kernels for 9% -> 11%
where the time goes in v6:
time: 35.6 us; the launch traced here: 35.5 us
  starting transfers between devices  13.2 us (37%)
  Pallas kernels  10.2 us (29%)
  waiting for transfers between devices  7.89 us (22%)
  matrix products  1.73 us (5%)
  local copies, waits for them, and re-layouts  1.55 us (4%)
  between operations  0.86 us (2%)
    ppermute x8, starting transfers between devices, swap(): return lax.ppermute(x, axis, [(i, i ^ bit) for i in range(size)])  13.2 us
    ppermute x8, waiting for transfers between devices, swap(): return lax.ppermute(x, axis, [(i, i ^ bit) for i in range(size)])  7.89 us
    pallas_call x1, Pallas kernels, scan_call(): pl.pallas_call(functools.partial(scan_kernel, prompts), out_shape=(jax.Sh...  3.08 us
    pallas_call x1, Pallas kernels, on_device(): pl.pallas_call(functools.partial(deliver_kernel, prompts, len(pieces)), o...  2.1 us
    pallas_call x1, Pallas kernels, on_device(): pl.pallas_call(functools.partial(attend_kernel, prompts), out_shape=(shap...  1.95 us
    dot_general x1, matrix products, on_device(): jnp.einsum('td,dgc->gtc', tokens, inner_weight, preferred_element_type=F32)  1.73 us
    unnamed x34, local copies, waits for them, and re-layouts  1.55 us
    pallas_call x1, Pallas kernels, on_device(): pl.pallas_call(functools.partial(mix_kernel, prompts), out_shape=(shape((...  1.13 us
  transfers between devices with their start and end apart: 8, of which 7 were waited for; matrix products, arithmetic and copies ran while one was open for 0% of the time, Pallas kernels for 11%

profile of v6, /device:TPU:0, one launch (start us, length us, event | category | flops | bytes accessed | tf_op | source)
XLA Modules:
  0.0 35.5 jit_solution(10114779218040255563)
XLA Ops:
  0.6 0.0 copy-start
  0.8 1.5 %copy-done = bf16[896,2,512]{2,1,0:T(2,128)(2,1)S(1)} copy-done((bf16[896,2,512]{2,1,0:T(2,128)(2,1)S(1)}, bf16[896,2,512]{2,1,0:T(2,128)(2,1)}, u32[]{:S(2)}) %copy-start) | copy-done | bytes 1835032
  2.2 1.7 %fusion.5.inner_ref = bf16[2,256,512]{2,1,0:T(8,128)(2,1)S(1)} fusion(bf16[896,2,512]{2,1,0:T(2,128)(2,1)S(1)} %copy-done, bf16[256,896]{1,0:T(8,128)(2,1)} %tokens_ref.1), kind=kOutput, calls=%fused_computation.3 | convolution fusion | flops 470024192 | bytes 2818048 | tf_op jit(solution)/shard_map/td,dgc->gtc/dot_general | solution.py:512
  4.0 0.0 copy-start.6
  4.0 1.1 %mix.1 = (f32[96,256]{1,0:T(8,128)S(1)}, bf16[256,512]{1,0:T(8,128)(2,1)S(1)}) custom-call(s32[1,2]{1,0:T(1,128)S(1)} %copy-done.9, bf16[2,256,512]{2,1,0:T(8,128)(2,1)S(1)} %fusion.5.inner_ref, f32[4,512]{1,0:T(4,128)S(1)} %copy-done.8, bf16[96,512]{1,0:T(8,128)(2,1)S(1)} %bitcast.20), custom_call_target="tpu_custom_call" | custom-call | tf_op jit(solution)/shard_map/mix/pallas_call | solution.py:514
  5.2 0.5 %collective-permute-start = (f32[96,256]{1,0:T(8,128)S(1)}, f32[96,256]{1,0:T(8,128)S(1)}, u32[]{:S(2)}, u32[]{:S(2)}) collective-permute-start(f32[96,256]{1,0:T(8,128)S(1)} %get-tuple-element.25), channel_id=1, source_target_pairs={{0,1},{1,0},{2,3},{3,2},{4,5},{5,4},{6,7},{7,6},{8,9},{9,8},{10,11... | collective-permute-start | bytes 294920 | tf_op jit(solution)/shard_map/ppermute | solution.py:528
  5.7 0.9 %collective-permute-done = f32[96,256]{1,0:T(8,128)S(1)} collective-permute-done((f32[96,256]{1,0:T(8,128)S(1)}, f32[96,256]{1,0:T(8,128)S(1)}, u32[]{:S(2)}, u32[]{:S(2)}) %collective-permute-start) | collective-permute-done | bytes 98336 | tf_op jit(solution)/shard_map/ppermute | solution.py:528
  6.7 2.9 %collective-permute-start.1 = (bf16[96,256]{1,0:T(8,128)(2,1)S(1)}, bf16[96,256]{1,0:T(8,128)(2,1)S(1)}, u32[]{:S(2)}, u32[]{:S(2)}) collective-permute-start(bf16[96,256]{1,0:T(8,128)(2,1)S(1)} %get-tuple-element.43), channel_id=1, source_target_pairs={{0,2},{1,3},{2,0},{3,1},{4,6},{5,7},{6,4},{7,5},{8,10},{9,11},{10,... | collective-permute-start | bytes 147464 | tf_op jit(solution)/shard_map/ppermute | solution.py:528
  9.6 1.9 %attend.1 = (f32[256,256]{1,0:T(8,128)S(1)}, f32[8,256]{1,0:T(8,128)S(1)}, bf16[96,128]{1,0:T(8,128)(2,1)S(1)}) custom-call(s32[1,2]{1,0:T(1,128)S(1)} %copy-done.9, bf16[256,896]{1,0:T(8,128)(2,1)S(1)} %copy-done.1, bf16[896,256]{1,0:T(8,128)(2,1)S(1)} %copy-done.2, bf16[64,896]{1,0:T(8,128)(2,1)S(1)} %bitcast.18, bf16[64,896]{1,0:T(8,128)(2,1)S(1)} %bitcast.19, ...), custom_call_target="tpu_custom_call" | custom-call | flops 352321536 | bytes 4194304 | tf_op jit(solution)/shard_map/attend/pallas_call | solution.py:533
  11.6 0.1 collective-permute-done.1.other_ref
  11.6 3.1 %scan.1 = (bf16[224,128]{1,0:T(8,128)(2,1)S(1)}, bf16[8,256,512]{2,1,0:T(8,128)(2,1)S(1)}, bf16[8,256,512]{2,1,0:T(8,128)(2,1)S(1)}) custom-call(s32[1,2]{1,0:T(1,128)S(1)} %copy-done.9, f32[96,256]{1,0:T(8,128)S(1)} %get-tuple-element.44.own_ref, bf16[96,256]{1,0:T(8,128)(2,1)S(1)} %collective-permute-done.1.other_ref, ...), custom_call_target="tpu_custom_call" | custom-call | tf_op jit(solution)/shard_map/scan/pallas_call | solution.py:257
  14.7 3.2 %collective-permute-start.2 = (bf16[1,224,128]{2,1,0:T(8,128)(2,1)S(1)}, bf16[1,224,128]{2,1,0:T(8,128)(2,1)S(1)}, u32[]{:S(2)}, u32[]{:S(2)}) collective-permute-start(bf16[1,224,128]{2,1,0:T(8,128)(2,1)S(1)} %bitcast.21), channel_id=1, source_target_pairs={{0,16},{4,20},{8,24},{12,28},{16,0},{20,4},{24,8},{28,12},{1,17},{... | collective-permute-start | bytes 172040 | tf_op jit(solution)/shard_map/ppermute | solution.py:528
  17.9 0.9 %gate.1 = (f32[256,512]{1,0:T(8,128)S(1)}, f32[2,256]{1,0:T(2,128)S(1)}) custom-call(f32[96,256]{1,0:T(8,128)S(1)} %get-tuple-element.44.own_ref, bf16[96,256]{1,0:T(8,128)(2,1)S(1)} %collective-permute-done.1.other_ref, bf16[8,256,512]{2,1,0:T(8,128)(2,1)S(1)} %get-tuple-element.28.states_even_ref, ...), custom_call_target="tpu_custom_call" | custom-call | flops 16777216 | bytes 4194304 | tf_op jit(solution)/shard_map/gate/pallas_call | solution.py:579
  18.8 1.5 %collective-permute-done.2.new_ref = bf16[1,224,128]{2,1,0:T(8,128)(2,1)S(1)} collective-permute-done((bf16[1,224,128]{2,1,0:T(8,128)(2,1)S(1)}, bf16[1,224,128]{2,1,0:T(8,128)(2,1)S(1)}, u32[]{:S(2)}, u32[]{:S(2)}) %collective-permute-start.2) | collective-permute-done | bytes 57376 | tf_op jit(solution)/shard_map/ppermute | solution.py:528
  20.4 1.7 %collective-permute-start.3 = (bf16[2,224,128]{2,1,0:T(8,128)(2,1)S(1)}, bf16[2,224,128]{2,1,0:T(8,128)(2,1)S(1)}, u32[]{:S(2)}, u32[]{:S(2)}) collective-permute-start(bf16[2,224,128]{2,1,0:T(8,128)(2,1)S(1)} %get-tuple-element.34.refs_0_), channel_id=1, source_target_pairs={{0,8},{4,12},{8,0},{12,4},{16,24},{20,28},{24,16},{28,20},{1,9},{5... | collective-permute-start | bytes 344072 | tf_op jit(solution)/shard_map/ppermute | solution.py:528
  22.0 1.5 %collective-permute-start.5 = (bf16[2,224,128]{2,1,0:T(8,128)(2,1)S(1)}, bf16[2,224,128]{2,1,0:T(8,128)(2,1)S(1)}, u32[]{:S(2)}, u32[]{:S(2)}) collective-permute-start(bf16[2,224,128]{2,1,0:T(8,128)(2,1)S(1)} %get-tuple-element.34.refs_0_), channel_id=1, source_target_pairs={{0,4},{4,0},{8,12},{12,8},{16,20},{20,16},{24,28},{28,24},{1,5},{5... | collective-permute-start | bytes 344072 | tf_op jit(solution)/shard_map/ppermute | solution.py:528
  23.6 1.2 %collective-permute-done.4.other_ref = f32[2,256]{1,0:T(2,128)S(1)} collective-permute-done((f32[2,256]{1,0:T(2,128)S(1)}, f32[2,256]{1,0:T(2,128)S(1)}, u32[]{:S(2)}, u32[]{:S(2)}) %collective-permute-start.4) | collective-permute-done | bytes 2080 | tf_op jit(solution)/shard_map/ppermute | solution.py:528
  24.7 0.5 %collective-permute-done.3.new_ref = bf16[2,224,128]{2,1,0:T(8,128)(2,1)S(1)} collective-permute-done((bf16[2,224,128]{2,1,0:T(8,128)(2,1)S(1)}, bf16[2,224,128]{2,1,0:T(8,128)(2,1)S(1)}, u32[]{:S(2)}, u32[]{:S(2)}) %collective-permute-start.3) | collective-permute-done | bytes 114720 | tf_op jit(solution)/shard_map/ppermute | solution.py:528
  25.2 1.6 %collective-permute-done.5.crossed_hbm.refs_2_ = bf16[2,224,128]{2,1,0:T(8,128)(2,1)S(1)} collective-permute-done((bf16[2,224,128]{2,1,0:T(8,128)(2,1)S(1)}, bf16[2,224,128]{2,1,0:T(8,128)(2,1)S(1)}, u32[]{:S(2)}, u32[]{:S(2)}) %collective-permute-start.5) | collective-permute-done | bytes 114720 | tf_op jit(solution)/shard_map/ppermute | solution.py:528
  26.9 1.9 %collective-permute-start.7 = (bf16[2,224,128]{2,1,0:T(8,128)(2,1)S(1)}, bf16[2,224,128]{2,1,0:T(8,128)(2,1)S(1)}, u32[]{:S(2)}, u32[]{:S(2)}) collective-permute-start(bf16[2,224,128]{2,1,0:T(8,128)(2,1)S(1)} %get-tuple-element.39.refs_1_), channel_id=1, source_target_pairs={{0,4},{4,0},{8,12},{12,8},{16,20},{20,16},{24,28},{28,24},{1,5},{5... | collective-permute-start | bytes 344072 | tf_op jit(solution)/shard_map/ppermute | solution.py:528
  28.7 1.5 %collective-permute-start.6 = (f32[2,256]{1,0:T(2,128)S(1)}, f32[2,256]{1,0:T(2,128)S(1)}, u32[]{:S(2)}, u32[]{:S(2)}) collective-permute-start(f32[2,256]{1,0:T(2,128)S(1)} %get-tuple-element.36.own_ref), channel_id=1, source_target_pairs={{0,2},{1,3},{2,0},{3,1},{4,6},{5,7},{6,4},{7,5},{8,10},{9,11},{10,... | collective-permute-start | bytes 6152 | tf_op jit(solution)/shard_map/ppermute | solution.py:528
  30.2 2.1 %collective-permute-done.6.other_ref = f32[2,256]{1,0:T(2,128)S(1)} collective-permute-done((f32[2,256]{1,0:T(2,128)S(1)}, f32[2,256]{1,0:T(2,128)S(1)}, u32[]{:S(2)}, u32[]{:S(2)}) %collective-permute-start.6) | collective-permute-done | bytes 2080 | tf_op jit(solution)/shard_map/ppermute | solution.py:528
  32.3 1.0 %norm.1 = (bf16[256,256]{1,0:T(8,128)(2,1)}, bf16[256,512]{1,0:T(8,128)(2,1)}) custom-call(f32[256,256]{1,0:T(8,128)S(1)} %get-tuple-element.24.attended_ref, f32[256,512]{1,0:T(8,128)S(1)} %get-tuple-element.31.gated_ref, f32[2,256]{1,0:T(2,128)S(1)} %get-tuple-element.36.own_ref, f32[2,256]{1,0:T(2,128)S(1)} %collective-permute-done.6.other_ref, ...), custom_call_target="tpu_custom_call" | custom-call | flops 16777216 | bytes 2097152 | tf_op jit(solution)/shard_map/norm/pallas_call | solution.py:626
  33.4 2.1 %deliver.1 = (bf16[56,2,32,64]{3,2,1,0:T(8,128)(2,1)}, bf16[56,16,512]{2,1,0:T(8,128)(2,1)}, bf16[3,56,512]{2,1,0:T(8,128)(2,1)}) custom-call(s32[1]{0:T(128)} %bitcast.13.me_ref, bf16[2,224,128]{2,1,0:T(8,128)(2,1)S(1)} %get-tuple-element.34.refs_0_, bf16[2,224,128]{2,1,0:T(8,128)(2,1)S(1)} %get-tuple-element.39.refs_1_, ...), custom_call_target="tpu_custom_call" | custom-call | tf_op jit(solution)/shard_map/deliver/pallas_call | solution.py:635
  (36 shorter events, 0.1 us)
Async XLA Ops:
  0.7 8.9 %copy-start.1 = (bf16[256,896]{1,0:T(8,128)(2,1)S(1)}, bf16[256,896]{1,0:T(8,128)(2,1)}, u32[]{:S(2)}) copy-start(bf16[256,896]{1,0:T(8,128)(2,1)} %tokens_ref.1) | copy-start | bytes 1376260
  0.7 3.3 %copy-start.9 = (s32[1,2]{1,0:T(1,128)S(1)}, s32[1,2]{1,0:T(1,128)}, u32[]{:S(2)}) copy-start(s32[1,2]{1,0:T(1,128)} %len_ref.5) | copy-start | bytes 28
  0.7 3.3 %copy-start.8 = (f32[4,512]{1,0:T(4,128)S(1)}, f32[4,512]{1,0:T(4,128)}, u32[]{:S(2)}) copy-start(f32[4,512]{1,0:T(4,128)} %conv_ref.1) | copy-start | bytes 24580
  0.7 3.3 %copy-start.5 = (bf16[512,96]{0,1:T(8,128)(2,1)S(1)}, bf16[512,96]{0,1:T(8,128)(2,1)}, u32[]{:S(2)}) copy-start(bf16[512,96]{0,1:T(8,128)(2,1)} %param.25) | copy-start | bytes 294916
  0.7 8.9 %copy-start.2 = (bf16[896,256]{1,0:T(8,128)(2,1)S(1)}, bf16[896,256]{1,0:T(8,128)(2,1)}, u32[]{:S(2)}) copy-start(bf16[896,256]{1,0:T(8,128)(2,1)} %query_ref.1) | copy-start | bytes 1376260
  0.7 8.9 %copy-start.3 = (bf16[896,64]{0,1:T(8,128)(2,1)S(1)}, bf16[896,64]{0,1:T(8,128)(2,1)}, u32[]{:S(2)}) copy-start(bf16[896,64]{0,1:T(8,128)(2,1)} %param.20) | copy-start | bytes 344068
  0.7 8.9 %copy-start.4 = (bf16[896,64]{0,1:T(8,128)(2,1)S(1)}, bf16[896,64]{0,1:T(8,128)(2,1)}, u32[]{:S(2)}) copy-start(bf16[896,64]{0,1:T(8,128)(2,1)} %param.21) | copy-start | bytes 344068
  0.7 8.9 %copy-start.14 = (s32[56]{0:T(128)S(1)}, s32[56]{0:T(128)}, u32[]{:S(2)}) copy-start(s32[56]{0:T(128)} %param.31) | copy-start | bytes 676
  0.7 8.9 %copy-start.15 = (s32[56]{0:T(128)S(1)}, s32[56]{0:T(128)}, u32[]{:S(2)}) copy-start(s32[56]{0:T(128)} %param.32) | copy-start | bytes 676
  0.7 8.9 %copy-start.16 = (s32[56]{0:T(128)S(1)}, s32[56]{0:T(128)}, u32[]{:S(2)}) copy-start(s32[56]{0:T(128)} %param.33) | copy-start | bytes 676
  4.0 7.7 %copy-start.6 = (bf16[64,512]{1,0:T(8,128)(2,1)S(1)}, bf16[64,512]{1,0:T(8,128)(2,1)}, u32[]{:S(2)}) copy-start(bf16[64,512]{1,0:T(8,128)(2,1)} %step_weight_ref.1) | copy-start | bytes 196612
  4.0 7.7 %copy-start.7 = (f32[16,512]{1,0:T(8,128)S(1)}, f32[16,512]{1,0:T(8,128)}, u32[]{:S(2)}) copy-start(f32[16,512]{1,0:T(8,128)} %rate_ref.1) | copy-start | bytes 98308
  4.0 7.7 %copy-start.10 = (f32[512]{0:T(512)S(1)}, f32[512]{0:T(512)}, u32[]{:S(2)}) copy-start(f32[512]{0:T(512)} %param.27) | copy-start | bytes 6148
  4.0 13.9 %copy-start.11 = (f32[512]{0:T(512)S(1)}, f32[512]{0:T(512)}, u32[]{:S(2)}) copy-start(f32[512]{0:T(512)} %param.29) | copy-start | bytes 6148
  5.2 1.5 %collective-permute-start = (f32[96,256]{1,0:T(8,128)S(1)}, f32[96,256]{1,0:T(8,128)S(1)}, u32[]{:S(2)}, u32[]{:S(2)}) collective-permute-start(f32[96,256]{1,0:T(8,128)S(1)} %get-tuple-element.25), channel_id=1, source_target_pairs={{0,1},{1,0},{2,3},{3,2},{4,5},{5,4},{6,7},{7,6},{8,9},{9,8},{10,11... | collective-permute-start | bytes 294920 | tf_op jit(solution)/shard_map/ppermute | solution.py:528
  6.7 5.0 %collective-permute-start.1 = (bf16[96,256]{1,0:T(8,128)(2,1)S(1)}, bf16[96,256]{1,0:T(8,128)(2,1)S(1)}, u32[]{:S(2)}, u32[]{:S(2)}) collective-permute-start(bf16[96,256]{1,0:T(8,128)(2,1)S(1)} %get-tuple-element.43), channel_id=1, source_target_pairs={{0,2},{1,3},{2,0},{3,1},{4,6},{5,7},{6,4},{7,5},{8,10},{9,11},{10,... | collective-permute-start | bytes 147464 | tf_op jit(solution)/shard_map/ppermute | solution.py:528
  14.7 5.6 %collective-permute-start.2 = (bf16[1,224,128]{2,1,0:T(8,128)(2,1)S(1)}, bf16[1,224,128]{2,1,0:T(8,128)(2,1)S(1)}, u32[]{:S(2)}, u32[]{:S(2)}) collective-permute-start(bf16[1,224,128]{2,1,0:T(8,128)(2,1)S(1)} %bitcast.21), channel_id=1, source_target_pairs={{0,16},{4,20},{8,24},{12,28},{16,0},{20,4},{24,8},{28,12},{1,17},{... | collective-permute-start | bytes 172040 | tf_op jit(solution)/shard_map/ppermute | solution.py:528
  17.9 14.4 %copy-start.12 = (f32[512]{0:T(512)S(1)}, f32[512]{0:T(512)}, u32[]{:S(2)}) copy-start(f32[512]{0:T(512)} %param.30) | copy-start | bytes 6148
  17.9 14.4 %copy-start.13 = (f32[256]{0:T(256)S(1)}, f32[256]{0:T(256)}, u32[]{:S(2)}) copy-start(f32[256]{0:T(256)} %param.22) | copy-start | bytes 3076
  20.4 4.9 %collective-permute-start.3 = (bf16[2,224,128]{2,1,0:T(8,128)(2,1)S(1)}, bf16[2,224,128]{2,1,0:T(8,128)(2,1)S(1)}, u32[]{:S(2)}, u32[]{:S(2)}) collective-permute-start(bf16[2,224,128]{2,1,0:T(8,128)(2,1)S(1)} %get-tuple-element.34.refs_0_), channel_id=1, source_target_pairs={{0,8},{4,12},{8,0},{12,4},{16,24},{20,28},{24,16},{28,20},{1,9},{5... | collective-permute-start | bytes 344072 | tf_op jit(solution)/shard_map/ppermute | solution.py:528
  22.0 4.8 %collective-permute-start.5 = (bf16[2,224,128]{2,1,0:T(8,128)(2,1)S(1)}, bf16[2,224,128]{2,1,0:T(8,128)(2,1)S(1)}, u32[]{:S(2)}, u32[]{:S(2)}) collective-permute-start(bf16[2,224,128]{2,1,0:T(8,128)(2,1)S(1)} %get-tuple-element.34.refs_0_), channel_id=1, source_target_pairs={{0,4},{4,0},{8,12},{12,8},{16,20},{20,16},{24,28},{28,24},{1,5},{5... | collective-permute-start | bytes 344072 | tf_op jit(solution)/shard_map/ppermute | solution.py:528
  23.6 1.2 %collective-permute-start.4 = (f32[2,256]{1,0:T(2,128)S(1)}, f32[2,256]{1,0:T(2,128)S(1)}, u32[]{:S(2)}, u32[]{:S(2)}) collective-permute-start(f32[2,256]{1,0:T(2,128)S(1)} %get-tuple-element.35.own_ref), channel_id=1, source_target_pairs={{0,1},{1,0},{2,3},{3,2},{4,5},{5,4},{6,7},{7,6},{8,9},{9,8},{10,11... | collective-permute-start | bytes 6152 | tf_op jit(solution)/shard_map/ppermute | solution.py:528
  26.9 6.5 %collective-permute-start.7 = (bf16[2,224,128]{2,1,0:T(8,128)(2,1)S(1)}, bf16[2,224,128]{2,1,0:T(8,128)(2,1)S(1)}, u32[]{:S(2)}, u32[]{:S(2)}) collective-permute-start(bf16[2,224,128]{2,1,0:T(8,128)(2,1)S(1)} %get-tuple-element.39.refs_1_), channel_id=1, source_target_pairs={{0,4},{4,0},{8,12},{12,8},{16,20},{20,16},{24,28},{28,24},{1,5},{5... | collective-permute-start | bytes 344072 | tf_op jit(solution)/shard_map/ppermute | solution.py:528
  28.7 3.6 %collective-permute-start.6 = (f32[2,256]{1,0:T(2,128)S(1)}, f32[2,256]{1,0:T(2,128)S(1)}, u32[]{:S(2)}, u32[]{:S(2)}) collective-permute-start(f32[2,256]{1,0:T(2,128)S(1)} %get-tuple-element.36.own_ref), channel_id=1, source_target_pairs={{0,2},{1,3},{2,0},{3,1},{4,6},{5,7},{6,4},{7,5},{8,10},{9,11},{10,... | collective-permute-start | bytes 6152 | tf_op jit(solution)/shard_map/ppermute | solution.py:528
  (1 other events, 1.6 us)

commit v7 on v6

--- a/solution.py
+++ b/solution.py
@@ -312,14 +312,14 @@
     sums_ref[1:2, :] = row_sums(gated * gated)
 
 
-def join_kernel(held_ref, new_ref, sums_ref, joined_ref, same_ref):
+def join_kernel(held_ref, new_ref, own_ref, other_ref, joined_ref, sums_ref):
     count = held_ref.shape[0]
     joined_ref[:count] = held_ref[...]
     joined_ref[count:] = new_ref[...]
-    same_ref[...] = sums_ref[...]
-
-
-def hold_kernel(new_ref, own_ref, other_ref, crossed_hbm, fresh_ref, sums_ref):
+    sums_ref[...] = own_ref[...] + other_ref[...]
+
+
+def hold_kernel(new_ref, own_ref, other_ref, fresh_ref, sums_ref):
     fresh_ref[...] = new_ref[...]
     sums_ref[...] = own_ref[...] + other_ref[...]
 
@@ -327,14 +327,14 @@
 def norm_kernel(
     attended_ref,
     gated_ref,
-    own_ref,
-    other_ref,
+    sums_ref,
     attention_gain_ref,
     mamba_gain_ref,
+    crossed_hbm,
     attention_ref,
     mamba_ref,
 ):
-    sums = own_ref[...] + other_ref[...]
+    sums = sums_ref[...]
     sums = jnp.concatenate([sums, jnp.zeros((6, sums.shape[1]), F32)], axis=0).T
     attention_scale = lax.rsqrt(sums[:, 0:1] / (HEADS * HEAD_DIM) + EPSILON)
     attention_ref[...] = (attended_ref[...] * attention_scale * attention_gain_ref[...]).astype(
@@ -595,43 +595,44 @@
     pr_bits = [1 << i for i in reversed(range((pr_size - 1).bit_length()))]
     tp_bits = [1 << i for i in range((tp_size - 1).bit_length())]
     main, last = pr_bits[:-1], pr_bits[-1]
+    near, far = list(tp_bits[:-1]), tp_bits[-1]
     for bit in main[:-1]:
         new = swap(held, "pr", pr_size, bit)
+        other = swap(sums, "tp", tp_size, near.pop(0)) if near else jnp.zeros_like(sums)
         held, sums = pl.pallas_call(
             join_kernel,
             out_shape=(
                 shape((2 * held.shape[0],) + held.shape[1:], BF16),
                 shape(sums.shape),
             ),
-            in_specs=[VMEM] * 3,
+            in_specs=[VMEM] * 4,
             out_specs=(VMEM, VMEM),
             compiler_params=params(16),
             name="join",
-        )(held, new, sums)
-    for bit in tp_bits[:-2]:
+        )(held, new, sums, other)
+    for bit in near:
         sums = sums + swap(sums, "tp", tp_size, bit)
     crossed = swap(held, "pr", pr_size, last)
     fresh = swap(held, "pr", pr_size, main[-1])
-    other = swap(sums, "tp", tp_size, tp_bits[-2])
+    other = swap(sums, "tp", tp_size, far)
     fresh, sums = pl.pallas_call(
         hold_kernel,
         out_shape=(shape(fresh.shape, BF16), shape(sums.shape)),
-        in_specs=[VMEM, VMEM, VMEM, HBM],
+        in_specs=[VMEM] * 3,
         out_specs=(VMEM, VMEM),
         compiler_params=params(16),
         name="hold",
-    )(fresh, sums, other, crossed)
+    )(fresh, sums, other)
     pieces = [held, fresh, crossed, swap(fresh, "pr", pr_size, last)]
-    sums_far = swap(sums, "tp", tp_size, tp_bits[-1])
     attention_out, mamba_out = pl.pallas_call(
         norm_kernel,
         out_shape=(shape((rows, features), BF16), shape((rows, channels), BF16)),
-        in_specs=[VMEM] * 6,
+        in_specs=[VMEM] * 5 + [HBM],
         out_specs=(VMEM, VMEM),
         compiler_params=params(16),
         cost_estimate=pl.CostEstimate(flops=1 << 24, bytes_accessed=2 << 20, transcendentals=0),
         name="norm",
-    )(attended, gated, sums, sums_far, attention_gain[None], mamba_gain[None])
+    )(attended, gated, sums, attention_gain[None], mamba_gain[None], crossed)
     keyval, state, conv = pl.pallas_call(
         functools.partial(deliver_kernel, prompts, len(pieces)),
         out_shape=(

time: 35.6 us -> 33 us (0.927)
  waiting for transfers between devices: 7.89 us -> 5.5 us
    ppermute x8, waiting for transfers between devices: 7.89 us -> 5.5 us  [swap(): return lax.ppermute(x, axis, [(i, i ^ bit) for i in range(size)])]
  transfers between devices with their start and end apart: 8 -> 8, of which waited for: 7 -> 7; matrix products, arithmetic and copies ran while one was open for 0% -> 0% of each run, Pallas kernels for 11% -> 12%
where the time goes in v7:
time: 33 us; the launch traced here: 32.9 us
  starting transfers between devices  13 us (39%)
  Pallas kernels  10.2 us (31%)
  waiting for transfers between devices  5.5 us (17%)
  matrix products  1.73 us (5%)
  local copies, waits for them, and re-layouts  1.55 us (5%)
  between operations  0.87 us (3%)
    ppermute x8, starting transfers between devices, swap(): return lax.ppermute(x, axis, [(i, i ^ bit) for i in range(size)])  13 us
    ppermute x8, waiting for transfers between devices, swap(): return lax.ppermute(x, axis, [(i, i ^ bit) for i in range(size)])  5.5 us
    pallas_call x1, Pallas kernels, scan_call(): pl.pallas_call(functools.partial(scan_kernel, prompts), out_shape=(jax.Sh...  3.08 us
    pallas_call x1, Pallas kernels, on_device(): pl.pallas_call(functools.partial(deliver_kernel, prompts, len(pieces)), o...  2.1 us
    pallas_call x1, Pallas kernels, on_device(): pl.pallas_call(functools.partial(attend_kernel, prompts), out_shape=(shap...  1.95 us
    dot_general x1, matrix products, on_device(): jnp.einsum('td,dgc->gtc', tokens, inner_weight, preferred_element_type=F32)  1.73 us
    unnamed x34, local copies, waits for them, and re-layouts  1.55 us
    pallas_call x1, Pallas kernels, on_device(): pl.pallas_call(functools.partial(mix_kernel, prompts), out_shape=(shape((...  1.13 us
  transfers between devices with their start and end apart: 8, of which 7 were waited for; matrix products, arithmetic and copies ran while one was open for 0% of the time, Pallas kernels for 12%

profile of v7, /device:TPU:0, one launch (start us, length us, event | category | flops | bytes accessed | tf_op | source)
XLA Modules:
  0.0 32.9 jit_solution(10067704606401102233)
XLA Ops:
  0.6 0.0 copy-start
  0.8 1.5 %copy-done = bf16[896,2,512]{2,1,0:T(2,128)(2,1)S(1)} copy-done((bf16[896,2,512]{2,1,0:T(2,128)(2,1)S(1)}, bf16[896,2,512]{2,1,0:T(2,128)(2,1)}, u32[]{:S(2)}) %copy-start) | copy-done | bytes 1835032
  2.2 1.7 %fusion.5.inner_ref = bf16[2,256,512]{2,1,0:T(8,128)(2,1)S(1)} fusion(bf16[896,2,512]{2,1,0:T(2,128)(2,1)S(1)} %copy-done, bf16[256,896]{1,0:T(8,128)(2,1)} %tokens_ref.1), kind=kOutput, calls=%fused_computation.3 | convolution fusion | flops 470024192 | bytes 2818048 | tf_op jit(solution)/shard_map/td,dgc->gtc/dot_general | solution.py:512
  4.0 1.1 %mix.1 = (f32[96,256]{1,0:T(8,128)S(1)}, bf16[256,512]{1,0:T(8,128)(2,1)S(1)}) custom-call(s32[1,2]{1,0:T(1,128)S(1)} %copy-done.9, bf16[2,256,512]{2,1,0:T(8,128)(2,1)S(1)} %fusion.5.inner_ref, f32[4,512]{1,0:T(4,128)S(1)} %copy-done.8, bf16[96,512]{1,0:T(8,128)(2,1)S(1)} %bitcast.20), custom_call_target="tpu_custom_call" | custom-call | tf_op jit(solution)/shard_map/mix/pallas_call | solution.py:514
  5.2 0.5 %collective-permute-start = (f32[96,256]{1,0:T(8,128)S(1)}, f32[96,256]{1,0:T(8,128)S(1)}, u32[]{:S(2)}, u32[]{:S(2)}) collective-permute-start(f32[96,256]{1,0:T(8,128)S(1)} %get-tuple-element.25), channel_id=1, source_target_pairs={{0,1},{1,0},{2,3},{3,2},{4,5},{5,4},{6,7},{7,6},{8,9},{9,8},{10,11... | collective-permute-start | bytes 294920 | tf_op jit(solution)/shard_map/ppermute | solution.py:528
  5.7 0.9 %collective-permute-done = f32[96,256]{1,0:T(8,128)S(1)} collective-permute-done((f32[96,256]{1,0:T(8,128)S(1)}, f32[96,256]{1,0:T(8,128)S(1)}, u32[]{:S(2)}, u32[]{:S(2)}) %collective-permute-start) | collective-permute-done | bytes 98336 | tf_op jit(solution)/shard_map/ppermute | solution.py:528
  6.7 2.9 %collective-permute-start.1 = (bf16[96,256]{1,0:T(8,128)(2,1)S(1)}, bf16[96,256]{1,0:T(8,128)(2,1)S(1)}, u32[]{:S(2)}, u32[]{:S(2)}) collective-permute-start(bf16[96,256]{1,0:T(8,128)(2,1)S(1)} %get-tuple-element.43), channel_id=1, source_target_pairs={{0,2},{1,3},{2,0},{3,1},{4,6},{5,7},{6,4},{7,5},{8,10},{9,11},{10,... | collective-permute-start | bytes 147464 | tf_op jit(solution)/shard_map/ppermute | solution.py:528
  9.6 1.9 %attend.1 = (f32[256,256]{1,0:T(8,128)S(1)}, f32[8,256]{1,0:T(8,128)S(1)}, bf16[96,128]{1,0:T(8,128)(2,1)S(1)}) custom-call(s32[1,2]{1,0:T(1,128)S(1)} %copy-done.9, bf16[256,896]{1,0:T(8,128)(2,1)S(1)} %copy-done.1, bf16[896,256]{1,0:T(8,128)(2,1)S(1)} %copy-done.2, bf16[64,896]{1,0:T(8,128)(2,1)S(1)} %bitcast.18, bf16[64,896]{1,0:T(8,128)(2,1)S(1)} %bitcast.19, ...), custom_call_target="tpu_custom_call" | custom-call | flops 352321536 | bytes 4194304 | tf_op jit(solution)/shard_map/attend/pallas_call | solution.py:533
  11.6 0.1 collective-permute-done.1.other_ref
  11.6 3.1 %scan.1 = (bf16[224,128]{1,0:T(8,128)(2,1)S(1)}, bf16[8,256,512]{2,1,0:T(8,128)(2,1)S(1)}, bf16[8,256,512]{2,1,0:T(8,128)(2,1)S(1)}) custom-call(s32[1,2]{1,0:T(1,128)S(1)} %copy-done.9, f32[96,256]{1,0:T(8,128)S(1)} %get-tuple-element.44.own_ref, bf16[96,256]{1,0:T(8,128)(2,1)S(1)} %collective-permute-done.1.other_ref, ...), custom_call_target="tpu_custom_call" | custom-call | tf_op jit(solution)/shard_map/scan/pallas_call | solution.py:257
  14.7 3.2 %collective-permute-start.2 = (bf16[1,224,128]{2,1,0:T(8,128)(2,1)S(1)}, bf16[1,224,128]{2,1,0:T(8,128)(2,1)S(1)}, u32[]{:S(2)}, u32[]{:S(2)}) collective-permute-start(bf16[1,224,128]{2,1,0:T(8,128)(2,1)S(1)} %bitcast.21), channel_id=1, source_target_pairs={{0,16},{4,20},{8,24},{12,28},{16,0},{20,4},{24,8},{28,12},{1,17},{... | collective-permute-start | bytes 172040 | tf_op jit(solution)/shard_map/ppermute | solution.py:528
  17.9 0.9 %gate.1 = (f32[256,512]{1,0:T(8,128)S(1)}, f32[2,256]{1,0:T(2,128)S(1)}) custom-call(f32[96,256]{1,0:T(8,128)S(1)} %get-tuple-element.44.own_ref, bf16[96,256]{1,0:T(8,128)(2,1)S(1)} %collective-permute-done.1.other_ref, bf16[8,256,512]{2,1,0:T(8,128)(2,1)S(1)} %get-tuple-element.28.states_even_ref, ...), custom_call_target="tpu_custom_call" | custom-call | flops 16777216 | bytes 4194304 | tf_op jit(solution)/shard_map/gate/pallas_call | solution.py:579
  18.8 0.1 collective-permute-start.3
  18.9 1.1 %collective-permute-done.3.other_ref = f32[2,256]{1,0:T(2,128)S(1)} collective-permute-done((f32[2,256]{1,0:T(2,128)S(1)}, f32[2,256]{1,0:T(2,128)S(1)}, u32[]{:S(2)}, u32[]{:S(2)}) %collective-permute-start.3) | collective-permute-done | bytes 2080 | tf_op jit(solution)/shard_map/ppermute | solution.py:528
  20.1 0.3 collective-permute-done.2.new_ref
  20.4 1.7 %collective-permute-start.4 = (bf16[2,224,128]{2,1,0:T(8,128)(2,1)S(1)}, bf16[2,224,128]{2,1,0:T(8,128)(2,1)S(1)}, u32[]{:S(2)}, u32[]{:S(2)}) collective-permute-start(bf16[2,224,128]{2,1,0:T(8,128)(2,1)S(1)} %get-tuple-element.34.refs_0_), channel_id=1, source_target_pairs={{0,8},{4,12},{8,0},{12,4},{16,24},{20,28},{24,16},{28,20},{1,9},{5... | collective-permute-start | bytes 344072 | tf_op jit(solution)/shard_map/ppermute | solution.py:528
  22.0 1.5 %collective-permute-start.5 = (f32[2,256]{1,0:T(2,128)S(1)}, f32[2,256]{1,0:T(2,128)S(1)}, u32[]{:S(2)}, u32[]{:S(2)}) collective-permute-start(f32[2,256]{1,0:T(2,128)S(1)} %get-tuple-element.35.own_ref), channel_id=1, source_target_pairs={{0,2},{1,3},{2,0},{3,1},{4,6},{5,7},{6,4},{7,5},{8,10},{9,11},{10,... | collective-permute-start | bytes 6152 | tf_op jit(solution)/shard_map/ppermute | solution.py:528
  23.5 1.5 %collective-permute-start.6 = (bf16[2,224,128]{2,1,0:T(8,128)(2,1)S(1)}, bf16[2,224,128]{2,1,0:T(8,128)(2,1)S(1)}, u32[]{:S(2)}, u32[]{:S(2)}) collective-permute-start(bf16[2,224,128]{2,1,0:T(8,128)(2,1)S(1)} %get-tuple-element.34.refs_0_), channel_id=1, source_target_pairs={{0,4},{4,0},{8,12},{12,8},{16,20},{20,16},{24,28},{28,24},{1,5},{5... | collective-permute-start | bytes 344072 | tf_op jit(solution)/shard_map/ppermute | solution.py:528
  25.1 0.6 %collective-permute-done.5.other_ref = f32[2,256]{1,0:T(2,128)S(1)} collective-permute-done((f32[2,256]{1,0:T(2,128)S(1)}, f32[2,256]{1,0:T(2,128)S(1)}, u32[]{:S(2)}, u32[]{:S(2)}) %collective-permute-start.5) | collective-permute-done | bytes 2080 | tf_op jit(solution)/shard_map/ppermute | solution.py:528
  25.7 1.6 %collective-permute-start.7 = (bf16[2,224,128]{2,1,0:T(8,128)(2,1)S(1)}, bf16[2,224,128]{2,1,0:T(8,128)(2,1)S(1)}, u32[]{:S(2)}, u32[]{:S(2)}) collective-permute-start(bf16[2,224,128]{2,1,0:T(8,128)(2,1)S(1)} %get-tuple-element.39.refs_1_), channel_id=1, source_target_pairs={{0,4},{4,0},{8,12},{12,8},{16,20},{20,16},{24,28},{28,24},{1,5},{5... | collective-permute-start | bytes 344072 | tf_op jit(solution)/shard_map/ppermute | solution.py:528
  27.2 2.3 %collective-permute-done.6.crossed_hbm.refs_2_ = bf16[2,224,128]{2,1,0:T(8,128)(2,1)S(1)} collective-permute-done((bf16[2,224,128]{2,1,0:T(8,128)(2,1)S(1)}, bf16[2,224,128]{2,1,0:T(8,128)(2,1)S(1)}, u32[]{:S(2)}, u32[]{:S(2)}) %collective-permute-start.6) | collective-permute-done | bytes 114720 | tf_op jit(solution)/shard_map/ppermute | solution.py:528
  29.5 1.0 %norm.1 = (bf16[256,256]{1,0:T(8,128)(2,1)}, bf16[256,512]{1,0:T(8,128)(2,1)}) custom-call(f32[256,256]{1,0:T(8,128)S(1)} %get-tuple-element.24.attended_ref, f32[256,512]{1,0:T(8,128)S(1)} %get-tuple-element.31.gated_ref, f32[2,256]{1,0:T(2,128)S(1)} %get-tuple-element.36.sums_ref, f32[1,256]{1,0:T(1,128)S(1)} %bitcast.26, f32[1,512]{1,0:T(1,128)S(1)} %bitcast.25, ...), custom_call_target="tpu_custom_call" | custom-call | flops 16777216 | bytes 2097152 | tf_op jit(solution)/shard_map/norm/pallas_call | solution.py:627
  30.6 0.2 collective-permute-done.7.refs_3_
  30.8 2.1 %deliver.1 = (bf16[56,2,32,64]{3,2,1,0:T(8,128)(2,1)}, bf16[56,16,512]{2,1,0:T(8,128)(2,1)}, bf16[3,56,512]{2,1,0:T(8,128)(2,1)}) custom-call(s32[1]{0:T(128)} %bitcast.13.me_ref, bf16[2,224,128]{2,1,0:T(8,128)(2,1)S(1)} %get-tuple-element.34.refs_0_, bf16[2,224,128]{2,1,0:T(8,128)(2,1)S(1)} %get-tuple-element.39.refs_1_, ...), custom_call_target="tpu_custom_call" | custom-call | tf_op jit(solution)/shard_map/deliver/pallas_call | solution.py:636
  (36 shorter events, 0.1 us)
Async XLA Ops:
  0.7 8.9 %copy-start.1 = (bf16[256,896]{1,0:T(8,128)(2,1)S(1)}, bf16[256,896]{1,0:T(8,128)(2,1)}, u32[]{:S(2)}) copy-start(bf16[256,896]{1,0:T(8,128)(2,1)} %tokens_ref.1) | copy-start | bytes 1376260
  0.7 3.3 %copy-start.9 = (s32[1,2]{1,0:T(1,128)S(1)}, s32[1,2]{1,0:T(1,128)}, u32[]{:S(2)}) copy-start(s32[1,2]{1,0:T(1,128)} %len_ref.5) | copy-start | bytes 28
  0.7 3.3 %copy-start.8 = (f32[4,512]{1,0:T(4,128)S(1)}, f32[4,512]{1,0:T(4,128)}, u32[]{:S(2)}) copy-start(f32[4,512]{1,0:T(4,128)} %conv_ref.1) | copy-start | bytes 24580
  0.7 3.3 %copy-start.5 = (bf16[512,96]{0,1:T(8,128)(2,1)S(1)}, bf16[512,96]{0,1:T(8,128)(2,1)}, u32[]{:S(2)}) copy-start(bf16[512,96]{0,1:T(8,128)(2,1)} %param.25) | copy-start | bytes 294916
  0.7 8.9 %copy-start.2 = (bf16[896,256]{1,0:T(8,128)(2,1)S(1)}, bf16[896,256]{1,0:T(8,128)(2,1)}, u32[]{:S(2)}) copy-start(bf16[896,256]{1,0:T(8,128)(2,1)} %query_ref.1) | copy-start | bytes 1376260
  0.7 8.9 %copy-start.3 = (bf16[896,64]{0,1:T(8,128)(2,1)S(1)}, bf16[896,64]{0,1:T(8,128)(2,1)}, u32[]{:S(2)}) copy-start(bf16[896,64]{0,1:T(8,128)(2,1)} %param.20) | copy-start | bytes 344068
  0.7 8.9 %copy-start.4 = (bf16[896,64]{0,1:T(8,128)(2,1)S(1)}, bf16[896,64]{0,1:T(8,128)(2,1)}, u32[]{:S(2)}) copy-start(bf16[896,64]{0,1:T(8,128)(2,1)} %param.21) | copy-start | bytes 344068
  0.7 8.9 %copy-start.14 = (s32[56]{0:T(128)S(1)}, s32[56]{0:T(128)}, u32[]{:S(2)}) copy-start(s32[56]{0:T(128)} %param.31) | copy-start | bytes 676
  0.7 8.9 %copy-start.15 = (s32[56]{0:T(128)S(1)}, s32[56]{0:T(128)}, u32[]{:S(2)}) copy-start(s32[56]{0:T(128)} %param.32) | copy-start | bytes 676
  0.7 8.9 %copy-start.16 = (s32[56]{0:T(128)S(1)}, s32[56]{0:T(128)}, u32[]{:S(2)}) copy-start(s32[56]{0:T(128)} %param.33) | copy-start | bytes 676
  4.0 7.7 %copy-start.6 = (bf16[64,512]{1,0:T(8,128)(2,1)S(1)}, bf16[64,512]{1,0:T(8,128)(2,1)}, u32[]{:S(2)}) copy-start(bf16[64,512]{1,0:T(8,128)(2,1)} %step_weight_ref.1) | copy-start | bytes 196612
  4.0 7.7 %copy-start.7 = (f32[16,512]{1,0:T(8,128)S(1)}, f32[16,512]{1,0:T(8,128)}, u32[]{:S(2)}) copy-start(f32[16,512]{1,0:T(8,128)} %rate_ref.1) | copy-start | bytes 98308
  4.0 7.7 %copy-start.10 = (f32[512]{0:T(512)S(1)}, f32[512]{0:T(512)}, u32[]{:S(2)}) copy-start(f32[512]{0:T(512)} %param.27) | copy-start | bytes 6148
  4.0 13.9 %copy-start.11 = (f32[512]{0:T(512)S(1)}, f32[512]{0:T(512)}, u32[]{:S(2)}) copy-start(f32[512]{0:T(512)} %param.29) | copy-start | bytes 6148
  5.2 1.5 %collective-permute-start = (f32[96,256]{1,0:T(8,128)S(1)}, f32[96,256]{1,0:T(8,128)S(1)}, u32[]{:S(2)}, u32[]{:S(2)}) collective-permute-start(f32[96,256]{1,0:T(8,128)S(1)} %get-tuple-element.25), channel_id=1, source_target_pairs={{0,1},{1,0},{2,3},{3,2},{4,5},{5,4},{6,7},{7,6},{8,9},{9,8},{10,11... | collective-permute-start | bytes 294920 | tf_op jit(solution)/shard_map/ppermute | solution.py:528
  6.7 5.0 %collective-permute-start.1 = (bf16[96,256]{1,0:T(8,128)(2,1)S(1)}, bf16[96,256]{1,0:T(8,128)(2,1)S(1)}, u32[]{:S(2)}, u32[]{:S(2)}) collective-permute-start(bf16[96,256]{1,0:T(8,128)(2,1)S(1)} %get-tuple-element.43), channel_id=1, source_target_pairs={{0,2},{1,3},{2,0},{3,1},{4,6},{5,7},{6,4},{7,5},{8,10},{9,11},{10,... | collective-permute-start | bytes 147464 | tf_op jit(solution)/shard_map/ppermute | solution.py:528
  14.7 5.6 %collective-permute-start.2 = (bf16[1,224,128]{2,1,0:T(8,128)(2,1)S(1)}, bf16[1,224,128]{2,1,0:T(8,128)(2,1)S(1)}, u32[]{:S(2)}, u32[]{:S(2)}) collective-permute-start(bf16[1,224,128]{2,1,0:T(8,128)(2,1)S(1)} %bitcast.21), channel_id=1, source_target_pairs={{0,16},{4,20},{8,24},{12,28},{16,0},{20,4},{24,8},{28,12},{1,17},{... | collective-permute-start | bytes 172040 | tf_op jit(solution)/shard_map/ppermute | solution.py:528
  17.9 11.6 %copy-start.12 = (f32[512]{0:T(512)S(1)}, f32[512]{0:T(512)}, u32[]{:S(2)}) copy-start(f32[512]{0:T(512)} %param.30) | copy-start | bytes 6148
  17.9 11.6 %copy-start.13 = (f32[256]{0:T(256)S(1)}, f32[256]{0:T(256)}, u32[]{:S(2)}) copy-start(f32[256]{0:T(256)} %param.22) | copy-start | bytes 3076
  18.8 1.2 %collective-permute-start.3 = (f32[2,256]{1,0:T(2,128)S(1)}, f32[2,256]{1,0:T(2,128)S(1)}, u32[]{:S(2)}, u32[]{:S(2)}) collective-permute-start(f32[2,256]{1,0:T(2,128)S(1)} %get-tuple-element.33.own_ref), channel_id=1, source_target_pairs={{0,1},{1,0},{2,3},{3,2},{4,5},{5,4},{6,7},{7,6},{8,9},{9,8},{10,11... | collective-permute-start | bytes 6152 | tf_op jit(solution)/shard_map/ppermute | solution.py:528
  20.4 5.3 %collective-permute-start.4 = (bf16[2,224,128]{2,1,0:T(8,128)(2,1)S(1)}, bf16[2,224,128]{2,1,0:T(8,128)(2,1)S(1)}, u32[]{:S(2)}, u32[]{:S(2)}) collective-permute-start(bf16[2,224,128]{2,1,0:T(8,128)(2,1)S(1)} %get-tuple-element.34.refs_0_), channel_id=1, source_target_pairs={{0,8},{4,12},{8,0},{12,4},{16,24},{20,28},{24,16},{28,20},{1,9},{5... | collective-permute-start | bytes 344072 | tf_op jit(solution)/shard_map/ppermute | solution.py:528
  22.0 3.6 %collective-permute-start.5 = (f32[2,256]{1,0:T(2,128)S(1)}, f32[2,256]{1,0:T(2,128)S(1)}, u32[]{:S(2)}, u32[]{:S(2)}) collective-permute-start(f32[2,256]{1,0:T(2,128)S(1)} %get-tuple-element.35.own_ref), channel_id=1, source_target_pairs={{0,2},{1,3},{2,0},{3,1},{4,6},{5,7},{6,4},{7,5},{8,10},{9,11},{10,... | collective-permute-start | bytes 6152 | tf_op jit(solution)/shard_map/ppermute | solution.py:528
  23.5 6.0 %collective-permute-start.6 = (bf16[2,224,128]{2,1,0:T(8,128)(2,1)S(1)}, bf16[2,224,128]{2,1,0:T(8,128)(2,1)S(1)}, u32[]{:S(2)}, u32[]{:S(2)}) collective-permute-start(bf16[2,224,128]{2,1,0:T(8,128)(2,1)S(1)} %get-tuple-element.34.refs_0_), channel_id=1, source_target_pairs={{0,4},{4,0},{8,12},{12,8},{16,20},{20,16},{24,28},{28,24},{1,5},{5... | collective-permute-start | bytes 344072 | tf_op jit(solution)/shard_map/ppermute | solution.py:528
  25.7 5.1 %collective-permute-start.7 = (bf16[2,224,128]{2,1,0:T(8,128)(2,1)S(1)}, bf16[2,224,128]{2,1,0:T(8,128)(2,1)S(1)}, u32[]{:S(2)}, u32[]{:S(2)}) collective-permute-start(bf16[2,224,128]{2,1,0:T(8,128)(2,1)S(1)} %get-tuple-element.39.refs_1_), channel_id=1, source_target_pairs={{0,4},{4,0},{8,12},{12,8},{16,20},{20,16},{24,28},{28,24},{1,5},{5... | collective-permute-start | bytes 344072 | tf_op jit(solution)/shard_map/ppermute | solution.py:528
  (1 other events, 1.6 us)

commit v8 on v7

--- a/solution.py
+++ b/solution.py
@@ -19,6 +19,7 @@
 EPSILON = 1e-06
 LANES = 128
 BLOCK = 16
+PARTS = 2
 RESET = 1e30
 
 F32 = jnp.float32
@@ -331,6 +332,7 @@
     attention_gain_ref,
     mamba_gain_ref,
     crossed_hbm,
+    inner_hbm,
     attention_ref,
     mamba_ref,
 ):
@@ -383,99 +385,89 @@
         pick = pick + jnp.where(filled > 0.5, filled + float(source * prompts - 1), 0.0)
     pick = pick.astype(jnp.int32)
 
-    chunk = min(sources, 8)
-    picked_rows = slots * STATE
-    row = lax.broadcasted_iota(jnp.int32, (picked_rows, LANES), 0)
-    lane = lax.broadcasted_iota(jnp.int32, (picked_rows, LANES), 1)
-    spread = one_hot(row // STATE == lane)
-    span = chunk * prompts * STATE
-    row = lax.broadcasted_iota(jnp.int32, (picked_rows, span), 0)
-    lane = lax.broadcasted_iota(jnp.int32, (picked_rows, span), 1)
+    span = sources * prompts * STATE
+    wanted = one_hot(lax.broadcasted_iota(jnp.int32, (span, LANES), 0) // STATE == pick)
+    states, windows, tails = [], [], []
+    for source in range(sources):
+        for p in range(prompts):
+            at = p * tiles * STATE
+            states.append(
+                jnp.concatenate(
+                    [rows_of(source, at + tile * STATE, STATE) for tile in range(tiles)], axis=1
+                )
+            )
+            at = window_at + p * WINDOW
+            windows.append(
+                jnp.concatenate(
+                    [
+                        rows_of(source, at, WINDOW // 2),
+                        rows_of(source, at + WINDOW // 2, WINDOW // 2),
+                    ],
+                    axis=1,
+                )
+            )
+        tails.append(
+            jnp.concatenate(
+                [rows_of(source, tail_at + 8 * tile, 16) for tile in range(0, tiles, 2)], axis=1
+            )
+        )
+    states = jnp.concatenate(states, axis=0)
+    windows = jnp.concatenate(windows, axis=0)
+    part = slots // PARTS
+    picked = part * STATE
+    row = lax.broadcasted_iota(jnp.int32, (picked, LANES), 0)
+    lane = lax.broadcasted_iota(jnp.int32, (picked, LANES), 1)
+    slot_of = row // STATE - lane
+    row = lax.broadcasted_iota(jnp.int32, (picked, span), 0)
+    lane = lax.broadcasted_iota(jnp.int32, (picked, span), 1)
     same = row % STATE == lane % STATE
-    states, windows, tails = None, None, None
+    copies = []
+
+    def send(source_ref, target_ref):
+        copies.append(pltpu.make_async_copy(source_ref, target_ref, sems.at[len(copies)]))
+        copies[-1].start()
+
+    for first in range(0, slots, part):
+        here = slice(first, first + part)
+        take = dot_nt(one_hot(slot_of == -first), wanted)
+        take = jnp.where(same, take, 0.0).astype(BF16)
+        moved = jnp.dot(take, states, preferred_element_type=F32)
+        state_ref[here] = moved.astype(BF16).reshape(part, STATE, channels)
+        send(state_ref.at[here], state_hbm.at[here])
+        moved = jnp.dot(take, windows, preferred_element_type=F32)
+        moved = moved.astype(BF16).reshape(part, WINDOW // 2, 2 * LANES)
+        for upper in range(2):
+            for kind in range(2):
+                at = upper * LANES + kind * HEAD_DIM
+                keyval_ref[here, kind, upper * WINDOW // 2 : (upper + 1) * WINDOW // 2, :] = moved[
+                    :, :, at : at + HEAD_DIM
+                ]
+        send(keyval_ref.at[here], keyval_hbm.at[here])
+
     wide = -(-slots // 16) * 16
     row = lax.broadcasted_iota(jnp.int32, (wide, LANES), 0)
     lane = lax.broadcasted_iota(jnp.int32, (wide, LANES), 1)
     unit = one_hot(row == lane)
-    for first in range(0, sources, chunk):
-        wanted = lax.broadcasted_iota(jnp.int32, (span, LANES), 0) // STATE + first * prompts
-        take = dot_nt(spread, one_hot(wanted == pick))
-        take = jnp.where(same, take, 0.0).astype(BF16)
-        table = []
-        for source in range(first, first + chunk):
-            for p in range(prompts):
-                at = p * tiles * STATE
-                table.append(
-                    jnp.concatenate(
-                        [
-                            rows_of(source, at + tile * STATE, STATE)
-                            for tile in range(tiles)
-                        ],
-                        axis=1,
-                    )
-                )
-        part = jnp.dot(take, jnp.concatenate(table, axis=0), preferred_element_type=F32)
-        states = part if states is None else states + part
-        table = []
-        for source in range(first, first + chunk):
-            for p in range(prompts):
-                at = window_at + p * WINDOW
-                table.append(
-                    jnp.concatenate(
-                        [
-                            rows_of(source, at, WINDOW // 2),
-                            rows_of(source, at + WINDOW // 2, WINDOW // 2),
-                        ],
-                        axis=1,
-                    )
-                )
-        part = jnp.dot(take, jnp.concatenate(table, axis=0), preferred_element_type=F32)
-        windows = part if windows is None else windows + part
-        table = []
-        for source in range(first, first + chunk):
-            table.append(
-                jnp.concatenate(
-                    [rows_of(source, tail_at + 8 * tile, 16) for tile in range(0, tiles, 2)],
-                    axis=1,
-                )
-            )
-        span_rows = chunk * 16
-        row = lax.broadcasted_iota(jnp.int32, (span_rows, LANES), 0)
-        local = pick - first * prompts
-        base = (local // prompts) * 16 + (local % prompts) * depth
-        hits = [one_hot(row == base + prompts * depth * odd + tap) for odd in (0, 1) for tap in range(depth)]
-        hits = dot_nt(unit, jnp.concatenate(hits, axis=0)).astype(BF16)
-        hits = jnp.concatenate(
-            [hits[:, i * span_rows : (i + 1) * span_rows] for i in range(2 * depth)], axis=0
-        )
-        part = jnp.dot(hits, jnp.concatenate(table, axis=0), preferred_element_type=F32)
-        tails = part if tails is None else tails + part
-
-    state_ref[...] = states.astype(BF16).reshape(slots, STATE, channels)
-    state_copy = pltpu.make_async_copy(state_ref, state_hbm, sems.at[0])
-    state_copy.start()
-    windows = windows.astype(BF16).reshape(slots, WINDOW // 2, 2 * LANES)
-    for upper in range(2):
-        for kind in range(2):
-            at = upper * LANES + kind * HEAD_DIM
-            keyval_ref[:, kind, upper * WINDOW // 2 : (upper + 1) * WINDOW // 2, :] = windows[
-                :, :, at : at + HEAD_DIM
-            ]
-    keyval_copy = pltpu.make_async_copy(keyval_ref, keyval_hbm, sems.at[1])
-    keyval_copy.start()
+    span = sources * 16
+    row = lax.broadcasted_iota(jnp.int32, (span, LANES), 0)
+    base = (pick // prompts) * 16 + (pick % prompts) * depth
+    hits = [
+        one_hot(row == base + prompts * depth * odd + tap) for odd in (0, 1) for tap in range(depth)
+    ]
+    hits = dot_nt(unit, jnp.concatenate(hits, axis=0)).astype(BF16)
+    hits = jnp.concatenate([hits[:, i * span : (i + 1) * span] for i in range(2 * depth)], axis=0)
+    moved = jnp.dot(hits, jnp.concatenate(tails, axis=0), preferred_element_type=F32)
     for odd in range(2):
         for tap in range(depth):
             at = (odd * depth + tap) * wide
             for pair in range(tiles // 2):
                 tile = 2 * pair + odd
-                conv_ref[tap, :, tile * LANES : (tile + 1) * LANES] = tails[
+                conv_ref[tap, :, tile * LANES : (tile + 1) * LANES] = moved[
                     at : at + slots, pair * LANES : (pair + 1) * LANES
                 ].astype(BF16)
-    conv_copy = pltpu.make_async_copy(conv_ref, conv_hbm, sems.at[2])
-    conv_copy.start()
-    state_copy.wait()
-    keyval_copy.wait()
-    conv_copy.wait()
+    send(conv_ref, conv_hbm)
+    for copy in copies:
+        copy.wait()
 
 
 def on_device(
@@ -627,12 +619,12 @@
     attention_out, mamba_out = pl.pallas_call(
         norm_kernel,
         out_shape=(shape((rows, features), BF16), shape((rows, channels), BF16)),
-        in_specs=[VMEM] * 5 + [HBM],
+        in_specs=[VMEM] * 5 + [HBM] * 2,
         out_specs=(VMEM, VMEM),
         compiler_params=params(16),
         cost_estimate=pl.CostEstimate(flops=1 << 24, bytes_accessed=2 << 20, transcendentals=0),
         name="norm",
-    )(attended, gated, sums, attention_gain[None], mamba_gain[None], crossed)
+    )(attended, gated, sums, attention_gain[None], mamba_gain[None], crossed, inner_weight)
     keyval, state, conv = pl.pallas_call(
         functools.partial(deliver_kernel, prompts, len(pieces)),
         out_shape=(
@@ -646,7 +638,7 @@
             pltpu.VMEM((slots, 2, WINDOW, HEAD_DIM), BF16),
             pltpu.VMEM((slots, STATE, channels), BF16),
             pltpu.VMEM((CONV - 1, slots, channels), BF16),
-            pltpu.SemaphoreType.DMA((3,)),
+            pltpu.SemaphoreType.DMA((2 * PARTS + 1,)),
         ],
         compiler_params=params(32),
         name="deliver",

time: 33 us -> 31.9 us (0.967)
  local copies, waits for them, and re-layouts: 1.55 us -> 0.08 us
  matrix products: 1.73 us -> 2.44 us
    unnamed x34, local copies, waits for them, and re-layouts: 1.55 us -> 0.08 us
    dot_general x1, matrix products: 1.73 us -> 2.44 us  [on_device(): jnp.einsum('td,dgc->gtc', tokens, inner_weight, preferred_element_type=F32)]
where the time goes in v8:
time: 31.9 us; the launch traced here: 31.8 us
  starting transfers between devices  13 us (41%)
  Pallas kernels  9.93 us (31%)
  waiting for transfers between devices  5.51 us (17%)
  matrix products  2.44 us (8%)
  between operations  0.87 us (3%)
    ppermute x8, starting transfers between devices, swap(): return lax.ppermute(x, axis, [(i, i ^ bit) for i in range(size)])  13 us
    ppermute x8, waiting for transfers between devices, swap(): return lax.ppermute(x, axis, [(i, i ^ bit) for i in range(size)])  5.51 us
    pallas_call x1, Pallas kernels, scan_call(): pl.pallas_call(functools.partial(scan_kernel, prompts), out_shape=(jax.Sh...  3.08 us
    dot_general x1, matrix products, on_device(): jnp.einsum('td,dgc->gtc', tokens, inner_weight, preferred_element_type=F32)  2.44 us
    pallas_call x1, Pallas kernels, on_device(): pl.pallas_call(functools.partial(attend_kernel, prompts), out_shape=(shap...  1.95 us
    pallas_call x1, Pallas kernels, on_device(): pl.pallas_call(functools.partial(deliver_kernel, prompts, len(pieces)), o...  1.79 us
    pallas_call x1, Pallas kernels, on_device(): pl.pallas_call(functools.partial(mix_kernel, prompts), out_shape=(shape((...  1.13 us
    pallas_call x1, Pallas kernels, on_device(): pl.pallas_call(norm_kernel, out_shape=(shape((rows, features), BF16), sha...  1.03 us
  transfers between devices with their start and end apart: 8, of which 7 were waited for; matrix products, arithmetic and copies ran while one was open for 0% of the time, Pallas kernels for 12%

profile of v8, /device:TPU:0, one launch (start us, length us, event | category | flops | bytes accessed | tf_op | source)
XLA Modules:
  0.0 31.8 jit_solution(3260256113150888998)
XLA Ops:
  0.7 2.4 %fusion.5.inner_ref = bf16[2,256,512]{2,1,0:T(8,128)(2,1)S(1)} fusion(bf16[896,2,512]{2,1,0:T(2,128)(2,1)} %inner_hbm.1, bf16[256,896]{1,0:T(8,128)(2,1)} %tokens_ref.1), kind=kOutput, calls=%fused_computation.3 | convolution fusion | flops 470024192 | bytes 2818048 | tf_op jit(solution)/shard_map/td,dgc->gtc/dot_general | solution.py:504
  3.2 0.0 copy-start.10
  3.2 0.0 copy-start.11
  3.3 1.1 %mix.1 = (f32[96,256]{1,0:T(8,128)S(1)}, bf16[256,512]{1,0:T(8,128)(2,1)S(1)}) custom-call(s32[1,2]{1,0:T(1,128)S(1)} %copy-done.9, bf16[2,256,512]{2,1,0:T(8,128)(2,1)S(1)} %fusion.5.inner_ref, f32[4,512]{1,0:T(4,128)S(1)} %copy-done.8, bf16[96,512]{1,0:T(8,128)(2,1)S(1)} %bitcast.20), custom_call_target="tpu_custom_call" | custom-call | tf_op jit(solution)/shard_map/mix/pallas_call | solution.py:506
  4.4 0.5 %collective-permute-start = (f32[96,256]{1,0:T(8,128)S(1)}, f32[96,256]{1,0:T(8,128)S(1)}, u32[]{:S(2)}, u32[]{:S(2)}) collective-permute-start(f32[96,256]{1,0:T(8,128)S(1)} %get-tuple-element.25), channel_id=1, source_target_pairs={{0,1},{1,0},{2,3},{3,2},{4,5},{5,4},{6,7},{7,6},{8,9},{9,8},{10,11... | collective-permute-start | bytes 294920 | tf_op jit(solution)/shard_map/ppermute | solution.py:520
  4.9 0.9 %collective-permute-done = f32[96,256]{1,0:T(8,128)S(1)} collective-permute-done((f32[96,256]{1,0:T(8,128)S(1)}, f32[96,256]{1,0:T(8,128)S(1)}, u32[]{:S(2)}, u32[]{:S(2)}) %collective-permute-start) | collective-permute-done | bytes 98336 | tf_op jit(solution)/shard_map/ppermute | solution.py:520
  5.9 2.9 %collective-permute-start.1 = (bf16[96,256]{1,0:T(8,128)(2,1)S(1)}, bf16[96,256]{1,0:T(8,128)(2,1)S(1)}, u32[]{:S(2)}, u32[]{:S(2)}) collective-permute-start(bf16[96,256]{1,0:T(8,128)(2,1)S(1)} %get-tuple-element.43), channel_id=1, source_target_pairs={{0,2},{1,3},{2,0},{3,1},{4,6},{5,7},{6,4},{7,5},{8,10},{9,11},{10,... | collective-permute-start | bytes 147464 | tf_op jit(solution)/shard_map/ppermute | solution.py:520
  8.8 1.9 %attend.1 = (f32[256,256]{1,0:T(8,128)S(1)}, f32[8,256]{1,0:T(8,128)S(1)}, bf16[96,128]{1,0:T(8,128)(2,1)S(1)}) custom-call(s32[1,2]{1,0:T(1,128)S(1)} %copy-done.9, bf16[256,896]{1,0:T(8,128)(2,1)S(1)} %copy-done.1, bf16[896,256]{1,0:T(8,128)(2,1)S(1)} %copy-done.2, bf16[64,896]{1,0:T(8,128)(2,1)S(1)} %bitcast.18, bf16[64,896]{1,0:T(8,128)(2,1)S(1)} %bitcast.19, ...), custom_call_target="tpu_custom_call" | custom-call | flops 352321536 | bytes 4194304 | tf_op jit(solution)/shard_map/attend/pallas_call | solution.py:525
  10.8 0.1 collective-permute-done.1.other_ref
  10.9 3.1 %scan.1 = (bf16[224,128]{1,0:T(8,128)(2,1)S(1)}, bf16[8,256,512]{2,1,0:T(8,128)(2,1)S(1)}, bf16[8,256,512]{2,1,0:T(8,128)(2,1)S(1)}) custom-call(s32[1,2]{1,0:T(1,128)S(1)} %copy-done.9, f32[96,256]{1,0:T(8,128)S(1)} %get-tuple-element.44.own_ref, bf16[96,256]{1,0:T(8,128)(2,1)S(1)} %collective-permute-done.1.other_ref, ...), custom_call_target="tpu_custom_call" | custom-call | tf_op jit(solution)/shard_map/scan/pallas_call | solution.py:258
  13.9 3.2 %collective-permute-start.2 = (bf16[1,224,128]{2,1,0:T(8,128)(2,1)S(1)}, bf16[1,224,128]{2,1,0:T(8,128)(2,1)S(1)}, u32[]{:S(2)}, u32[]{:S(2)}) collective-permute-start(bf16[1,224,128]{2,1,0:T(8,128)(2,1)S(1)} %bitcast.21), channel_id=1, source_target_pairs={{0,16},{4,20},{8,24},{12,28},{16,0},{20,4},{24,8},{28,12},{1,17},{... | collective-permute-start | bytes 172040 | tf_op jit(solution)/shard_map/ppermute | solution.py:520
  17.1 0.9 %gate.1 = (f32[256,512]{1,0:T(8,128)S(1)}, f32[2,256]{1,0:T(2,128)S(1)}) custom-call(f32[96,256]{1,0:T(8,128)S(1)} %get-tuple-element.44.own_ref, bf16[96,256]{1,0:T(8,128)(2,1)S(1)} %collective-permute-done.1.other_ref, bf16[8,256,512]{2,1,0:T(8,128)(2,1)S(1)} %get-tuple-element.28.states_even_ref, ...), custom_call_target="tpu_custom_call" | custom-call | flops 16777216 | bytes 4194304 | tf_op jit(solution)/shard_map/gate/pallas_call | solution.py:571
  18.1 0.1 collective-permute-start.3
  18.2 1.1 %collective-permute-done.3.other_ref = f32[2,256]{1,0:T(2,128)S(1)} collective-permute-done((f32[2,256]{1,0:T(2,128)S(1)}, f32[2,256]{1,0:T(2,128)S(1)}, u32[]{:S(2)}, u32[]{:S(2)}) %collective-permute-start.3) | collective-permute-done | bytes 2080 | tf_op jit(solution)/shard_map/ppermute | solution.py:520
  19.3 0.3 collective-permute-done.2.new_ref
  19.6 1.7 %collective-permute-start.4 = (bf16[2,224,128]{2,1,0:T(8,128)(2,1)S(1)}, bf16[2,224,128]{2,1,0:T(8,128)(2,1)S(1)}, u32[]{:S(2)}, u32[]{:S(2)}) collective-permute-start(bf16[2,224,128]{2,1,0:T(8,128)(2,1)S(1)} %get-tuple-element.34.refs_0_), channel_id=1, source_target_pairs={{0,8},{4,12},{8,0},{12,4},{16,24},{20,28},{24,16},{28,20},{1,9},{5... | collective-permute-start | bytes 344072 | tf_op jit(solution)/shard_map/ppermute | solution.py:520
  21.3 1.5 %collective-permute-start.5 = (f32[2,256]{1,0:T(2,128)S(1)}, f32[2,256]{1,0:T(2,128)S(1)}, u32[]{:S(2)}, u32[]{:S(2)}) collective-permute-start(f32[2,256]{1,0:T(2,128)S(1)} %get-tuple-element.35.own_ref), channel_id=1, source_target_pairs={{0,2},{1,3},{2,0},{3,1},{4,6},{5,7},{6,4},{7,5},{8,10},{9,11},{10,... | collective-permute-start | bytes 6152 | tf_op jit(solution)/shard_map/ppermute | solution.py:520
  22.8 1.5 %collective-permute-start.6 = (bf16[2,224,128]{2,1,0:T(8,128)(2,1)S(1)}, bf16[2,224,128]{2,1,0:T(8,128)(2,1)S(1)}, u32[]{:S(2)}, u32[]{:S(2)}) collective-permute-start(bf16[2,224,128]{2,1,0:T(8,128)(2,1)S(1)} %get-tuple-element.34.refs_0_), channel_id=1, source_target_pairs={{0,4},{4,0},{8,12},{12,8},{16,20},{20,16},{24,28},{28,24},{1,5},{5... | collective-permute-start | bytes 344072 | tf_op jit(solution)/shard_map/ppermute | solution.py:520
  24.3 0.6 %collective-permute-done.5.other_ref = f32[2,256]{1,0:T(2,128)S(1)} collective-permute-done((f32[2,256]{1,0:T(2,128)S(1)}, f32[2,256]{1,0:T(2,128)S(1)}, u32[]{:S(2)}, u32[]{:S(2)}) %collective-permute-start.5) | collective-permute-done | bytes 2080 | tf_op jit(solution)/shard_map/ppermute | solution.py:520
  24.9 1.6 %collective-permute-start.7 = (bf16[2,224,128]{2,1,0:T(8,128)(2,1)S(1)}, bf16[2,224,128]{2,1,0:T(8,128)(2,1)S(1)}, u32[]{:S(2)}, u32[]{:S(2)}) collective-permute-start(bf16[2,224,128]{2,1,0:T(8,128)(2,1)S(1)} %get-tuple-element.39.refs_1_), channel_id=1, source_target_pairs={{0,4},{4,0},{8,12},{12,8},{16,20},{20,16},{24,28},{28,24},{1,5},{5... | collective-permute-start | bytes 344072 | tf_op jit(solution)/shard_map/ppermute | solution.py:520
  26.5 2.3 %collective-permute-done.6.crossed_hbm.refs_2_ = bf16[2,224,128]{2,1,0:T(8,128)(2,1)S(1)} collective-permute-done((bf16[2,224,128]{2,1,0:T(8,128)(2,1)S(1)}, bf16[2,224,128]{2,1,0:T(8,128)(2,1)S(1)}, u32[]{:S(2)}, u32[]{:S(2)}) %collective-permute-start.6) | collective-permute-done | bytes 114720 | tf_op jit(solution)/shard_map/ppermute | solution.py:520
  28.8 1.0 %norm.1 = (bf16[256,256]{1,0:T(8,128)(2,1)}, bf16[256,512]{1,0:T(8,128)(2,1)}) custom-call(f32[256,256]{1,0:T(8,128)S(1)} %get-tuple-element.24.attended_ref, f32[256,512]{1,0:T(8,128)S(1)} %get-tuple-element.31.gated_ref, f32[2,256]{1,0:T(2,128)S(1)} %get-tuple-element.36.sums_ref, f32[1,256]{1,0:T(1,128)S(1)} %bitcast.26, f32[1,512]{1,0:T(1,128)S(1)} %bitcast.25, ...), custom_call_target="tpu_custom_call" | custom-call | flops 16777216 | bytes 2097152 | tf_op jit(solution)/shard_map/norm/pallas_call | solution.py:619
  29.8 0.2 collective-permute-done.7.refs_3_
  30.0 1.8 %deliver.1 = (bf16[56,2,32,64]{3,2,1,0:T(8,128)(2,1)}, bf16[56,16,512]{2,1,0:T(8,128)(2,1)}, bf16[3,56,512]{2,1,0:T(8,128)(2,1)}) custom-call(s32[1]{0:T(128)} %bitcast.13.me_ref, bf16[2,224,128]{2,1,0:T(8,128)(2,1)S(1)} %get-tuple-element.34.refs_0_, bf16[2,224,128]{2,1,0:T(8,128)(2,1)S(1)} %get-tuple-element.39.refs_1_, ...), custom_call_target="tpu_custom_call" | custom-call | tf_op jit(solution)/shard_map/deliver/pallas_call | solution.py:628
  (36 shorter events, 0.1 us)
Async XLA Ops:
  0.6 8.2 %copy-start.1 = (bf16[256,896]{1,0:T(8,128)(2,1)S(1)}, bf16[256,896]{1,0:T(8,128)(2,1)}, u32[]{:S(2)}) copy-start(bf16[256,896]{1,0:T(8,128)(2,1)} %tokens_ref.1) | copy-start | bytes 1376260
  0.6 2.6 %copy-start.9 = (s32[1,2]{1,0:T(1,128)S(1)}, s32[1,2]{1,0:T(1,128)}, u32[]{:S(2)}) copy-start(s32[1,2]{1,0:T(1,128)} %len_ref.5) | copy-start | bytes 28
  0.7 2.6 %copy-start.8 = (f32[4,512]{1,0:T(4,128)S(1)}, f32[4,512]{1,0:T(4,128)}, u32[]{:S(2)}) copy-start(f32[4,512]{1,0:T(4,128)} %conv_ref.1) | copy-start | bytes 24580
  0.7 8.1 %copy-start.2 = (bf16[896,256]{1,0:T(8,128)(2,1)S(1)}, bf16[896,256]{1,0:T(8,128)(2,1)}, u32[]{:S(2)}) copy-start(bf16[896,256]{1,0:T(8,128)(2,1)} %query_ref.1) | copy-start | bytes 1376260
  0.7 8.1 %copy-start.3 = (bf16[896,64]{0,1:T(8,128)(2,1)S(1)}, bf16[896,64]{0,1:T(8,128)(2,1)}, u32[]{:S(2)}) copy-start(bf16[896,64]{0,1:T(8,128)(2,1)} %param.20) | copy-start | bytes 344068
  0.7 8.1 %copy-start.4 = (bf16[896,64]{0,1:T(8,128)(2,1)S(1)}, bf16[896,64]{0,1:T(8,128)(2,1)}, u32[]{:S(2)}) copy-start(bf16[896,64]{0,1:T(8,128)(2,1)} %param.21) | copy-start | bytes 344068
  0.7 8.1 %copy-start.14 = (s32[56]{0:T(128)S(1)}, s32[56]{0:T(128)}, u32[]{:S(2)}) copy-start(s32[56]{0:T(128)} %param.31) | copy-start | bytes 676
  0.7 8.1 %copy-start.15 = (s32[56]{0:T(128)S(1)}, s32[56]{0:T(128)}, u32[]{:S(2)}) copy-start(s32[56]{0:T(128)} %param.32) | copy-start | bytes 676
  0.7 8.1 %copy-start.16 = (s32[56]{0:T(128)S(1)}, s32[56]{0:T(128)}, u32[]{:S(2)}) copy-start(s32[56]{0:T(128)} %param.33) | copy-start | bytes 676
  3.2 7.7 %copy-start.6 = (bf16[64,512]{1,0:T(8,128)(2,1)S(1)}, bf16[64,512]{1,0:T(8,128)(2,1)}, u32[]{:S(2)}) copy-start(bf16[64,512]{1,0:T(8,128)(2,1)} %step_weight_ref.1) | copy-start | bytes 196612
  3.2 7.7 %copy-start.7 = (f32[16,512]{1,0:T(8,128)S(1)}, f32[16,512]{1,0:T(8,128)}, u32[]{:S(2)}) copy-start(f32[16,512]{1,0:T(8,128)} %rate_ref.1) | copy-start | bytes 98308
  3.2 7.7 %copy-start.10 = (f32[512]{0:T(512)S(1)}, f32[512]{0:T(512)}, u32[]{:S(2)}) copy-start(f32[512]{0:T(512)} %param.27) | copy-start | bytes 6148
  3.2 13.9 %copy-start.11 = (f32[512]{0:T(512)S(1)}, f32[512]{0:T(512)}, u32[]{:S(2)}) copy-start(f32[512]{0:T(512)} %param.29) | copy-start | bytes 6148
  4.4 1.5 %collective-permute-start = (f32[96,256]{1,0:T(8,128)S(1)}, f32[96,256]{1,0:T(8,128)S(1)}, u32[]{:S(2)}, u32[]{:S(2)}) collective-permute-start(f32[96,256]{1,0:T(8,128)S(1)} %get-tuple-element.25), channel_id=1, source_target_pairs={{0,1},{1,0},{2,3},{3,2},{4,5},{5,4},{6,7},{7,6},{8,9},{9,8},{10,11... | collective-permute-start | bytes 294920 | tf_op jit(solution)/shard_map/ppermute | solution.py:520
  5.9 5.0 %collective-permute-start.1 = (bf16[96,256]{1,0:T(8,128)(2,1)S(1)}, bf16[96,256]{1,0:T(8,128)(2,1)S(1)}, u32[]{:S(2)}, u32[]{:S(2)}) collective-permute-start(bf16[96,256]{1,0:T(8,128)(2,1)S(1)} %get-tuple-element.43), channel_id=1, source_target_pairs={{0,2},{1,3},{2,0},{3,1},{4,6},{5,7},{6,4},{7,5},{8,10},{9,11},{10,... | collective-permute-start | bytes 147464 | tf_op jit(solution)/shard_map/ppermute | solution.py:520
  13.9 5.6 %collective-permute-start.2 = (bf16[1,224,128]{2,1,0:T(8,128)(2,1)S(1)}, bf16[1,224,128]{2,1,0:T(8,128)(2,1)S(1)}, u32[]{:S(2)}, u32[]{:S(2)}) collective-permute-start(bf16[1,224,128]{2,1,0:T(8,128)(2,1)S(1)} %bitcast.21), channel_id=1, source_target_pairs={{0,16},{4,20},{8,24},{12,28},{16,0},{20,4},{24,8},{28,12},{1,17},{... | collective-permute-start | bytes 172040 | tf_op jit(solution)/shard_map/ppermute | solution.py:520
  17.1 11.6 %copy-start = (bf16[896,2,512]{2,1,0:T(2,128)(2,1)S(1)}, bf16[896,2,512]{2,1,0:T(2,128)(2,1)}, u32[]{:S(2)}) copy-start(bf16[896,2,512]{2,1,0:T(2,128)(2,1)} %inner_hbm.1) | copy-start | bytes 5505028
  17.1 11.6 %copy-start.12 = (f32[512]{0:T(512)S(1)}, f32[512]{0:T(512)}, u32[]{:S(2)}) copy-start(f32[512]{0:T(512)} %param.30) | copy-start | bytes 6148
  17.1 11.6 %copy-start.13 = (f32[256]{0:T(256)S(1)}, f32[256]{0:T(256)}, u32[]{:S(2)}) copy-start(f32[256]{0:T(256)} %param.22) | copy-start | bytes 3076
  18.1 1.2 %collective-permute-start.3 = (f32[2,256]{1,0:T(2,128)S(1)}, f32[2,256]{1,0:T(2,128)S(1)}, u32[]{:S(2)}, u32[]{:S(2)}) collective-permute-start(f32[2,256]{1,0:T(2,128)S(1)} %get-tuple-element.33.own_ref), channel_id=1, source_target_pairs={{0,1},{1,0},{2,3},{3,2},{4,5},{5,4},{6,7},{7,6},{8,9},{9,8},{10,11... | collective-permute-start | bytes 6152 | tf_op jit(solution)/shard_map/ppermute | solution.py:520
  19.6 5.3 %collective-permute-start.4 = (bf16[2,224,128]{2,1,0:T(8,128)(2,1)S(1)}, bf16[2,224,128]{2,1,0:T(8,128)(2,1)S(1)}, u32[]{:S(2)}, u32[]{:S(2)}) collective-permute-start(bf16[2,224,128]{2,1,0:T(8,128)(2,1)S(1)} %get-tuple-element.34.refs_0_), channel_id=1, source_target_pairs={{0,8},{4,12},{8,0},{12,4},{16,24},{20,28},{24,16},{28,20},{1,9},{5... | collective-permute-start | bytes 344072 | tf_op jit(solution)/shard_map/ppermute | solution.py:520
  21.3 3.6 %collective-permute-start.5 = (f32[2,256]{1,0:T(2,128)S(1)}, f32[2,256]{1,0:T(2,128)S(1)}, u32[]{:S(2)}, u32[]{:S(2)}) collective-permute-start(f32[2,256]{1,0:T(2,128)S(1)} %get-tuple-element.35.own_ref), channel_id=1, source_target_pairs={{0,2},{1,3},{2,0},{3,1},{4,6},{5,7},{6,4},{7,5},{8,10},{9,11},{10,... | collective-permute-start | bytes 6152 | tf_op jit(solution)/shard_map/ppermute | solution.py:520
  22.8 6.0 %collective-permute-start.6 = (bf16[2,224,128]{2,1,0:T(8,128)(2,1)S(1)}, bf16[2,224,128]{2,1,0:T(8,128)(2,1)S(1)}, u32[]{:S(2)}, u32[]{:S(2)}) collective-permute-start(bf16[2,224,128]{2,1,0:T(8,128)(2,1)S(1)} %get-tuple-element.34.refs_0_), channel_id=1, source_target_pairs={{0,4},{4,0},{8,12},{12,8},{16,20},{20,16},{24,28},{28,24},{1,5},{5... | collective-permute-start | bytes 344072 | tf_op jit(solution)/shard_map/ppermute | solution.py:520
  24.9 5.1 %collective-permute-start.7 = (bf16[2,224,128]{2,1,0:T(8,128)(2,1)S(1)}, bf16[2,224,128]{2,1,0:T(8,128)(2,1)S(1)}, u32[]{:S(2)}, u32[]{:S(2)}) collective-permute-start(bf16[2,224,128]{2,1,0:T(8,128)(2,1)S(1)} %get-tuple-element.39.refs_1_), channel_id=1, source_target_pairs={{0,4},{4,0},{8,12},{12,8},{16,20},{20,16},{24,28},{28,24},{1,5},{5... | collective-permute-start | bytes 344072 | tf_op jit(solution)/shard_map/ppermute | solution.py:520
  (1 other events, 2.6 us)

commit v9 on v8

--- a/solution.py
+++ b/solution.py
@@ -331,8 +331,9 @@
     sums_ref,
     attention_gain_ref,
     mamba_gain_ref,
+    inner_hbm,
     crossed_hbm,
-    inner_hbm,
+    collected_hbm,
     attention_ref,
     mamba_ref,
 ):
@@ -350,122 +351,142 @@
     return jnp.where(hit, 1.0, 0.0).astype(BF16)
 
 
-def deliver_kernel(
-    prompts,
-    pieces,
-    me_ref,
-    *refs,
-):
-    keyval_hbm, state_hbm, conv_hbm, keyval_ref, state_ref, conv_ref, sems = refs[pieces:]
-    me = me_ref[0]
+class Gathered:
+    def __init__(self, prompts, tiles, refs, me):
+        self.blocks = [(ref, index) for ref in refs for index in range(ref.shape[0])]
+        self.prompts, self.tiles = prompts, tiles
+        self.window_at = prompts * tiles * STATE
+        self.tail_at = self.window_at + prompts * WINDOW
+        self.depth = CONV - 1
+        spare = 16 - 2 * prompts * self.depth
+        rows = refs[0].shape[1] - self.tail_at
+        row = lax.broadcasted_iota(jnp.int32, (rows, LANES), 0)
+        grouped = row < 8 * tiles
+        owner = jnp.where(
+            grouped, row // 16 * spare + row % 16 - (16 - spare), row - 8 * tiles + spare * (tiles // 2)
+        )
+        owner = jnp.where(grouped & (row % 16 < 16 - spare), -1, owner)
+        pick = jnp.full((1, LANES), -1.0, F32)
+        for source in range(len(self.blocks)):
+            filled = self.rows_of(source, self.tail_at, rows).astype(F32)
+            filled = jnp.sum(jnp.where(owner == me, filled, 0.0), axis=0, keepdims=True)
+            pick = jnp.where(filled > 0.5, filled + float(source * prompts - 1), pick)
+        self.pick = pick.astype(jnp.int32)
+        span = len(self.blocks) * prompts * STATE
+        row = lax.broadcasted_iota(jnp.int32, (span, LANES), 0)
+        self.wanted = one_hot(row // STATE == self.pick)
+
+    def rows_of(self, source, at, size):
+        ref, index = self.blocks[source]
+        return ref[index, at : at + size, :]
+
+    def take(self, first, count):
+        row = lax.broadcasted_iota(jnp.int32, (count * STATE, LANES), 0)
+        lane = lax.broadcasted_iota(jnp.int32, (count * STATE, LANES), 1)
+        take = dot_nt(one_hot(row // STATE + first == lane), self.wanted)
+        row = lax.broadcasted_iota(jnp.int32, take.shape, 0)
+        lane = lax.broadcasted_iota(jnp.int32, take.shape, 1)
+        return jnp.where(row % STATE == lane % STATE, take, 0.0).astype(BF16)
+
+    def table(self, rows_list):
+        rows = []
+        for source in range(len(self.blocks)):
+            for p in range(self.prompts):
+                parts = [self.rows_of(source, at, 16) for at in rows_list(p)]
+                rows.append(jnp.concatenate(parts, axis=1))
+        return jnp.concatenate(rows, axis=0)
+
+    def states(self):
+        return self.table(lambda p: [(p * self.tiles + i) * STATE for i in range(self.tiles)])
+
+    def windows(self):
+        return self.table(
+            lambda p: [self.window_at + p * WINDOW + i for i in range(0, WINDOW, 16)]
+        )
+
+    def tails(self, slots):
+        table = [
+            jnp.concatenate(
+                [self.rows_of(source, self.tail_at + 8 * i, 16) for i in range(0, self.tiles, 2)],
+                axis=1,
+            )
+            for source in range(len(self.blocks))
+        ]
+        row = lax.broadcasted_iota(jnp.int32, (slots, LANES), 0)
+        lane = lax.broadcasted_iota(jnp.int32, (slots, LANES), 1)
+        unit = one_hot(row == lane)
+        span = max(len(self.blocks) * 16, LANES)
+        if span > len(self.blocks) * 16:
+            table.append(jnp.zeros((span - len(self.blocks) * 16, table[0].shape[1]), BF16))
+        row = lax.broadcasted_iota(jnp.int32, (span, LANES), 0)
+        step = self.prompts * self.depth
+        base = (self.pick // self.prompts) * 16 + (self.pick % self.prompts) * self.depth
+        base = jnp.where(self.pick < 0, -span, base)
+        hits = [one_hot(row == base + step * odd + tap) for odd in (0, 1) for tap in range(self.depth)]
+        hits = dot_nt(unit, jnp.concatenate(hits, axis=0)).astype(BF16)
+        hits = [hits[:, i * span : (i + 1) * span] for i in range(2 * self.depth)]
+        return jnp.dot(
+            jnp.concatenate(hits, axis=0),
+            jnp.concatenate(table, axis=0),
+            preferred_element_type=F32,
+        )
+
+
+def collect_kernel(prompts, slots, me_ref, *refs):
+    states_ref, windows_ref, tails_ref = refs[-3:]
+    channels = states_ref.shape[1]
+    gathered = Gathered(prompts, channels // LANES, refs[:-3], me_ref[0])
+    take = gathered.take(0, slots)
+    states_ref[...] = jnp.dot(
+        take, gathered.states(), preferred_element_type=F32
+    ).astype(BF16)
+    windows_ref[...] = jnp.dot(
+        take, gathered.windows(), preferred_element_type=F32
+    ).astype(BF16)
+    wide = tails_ref.shape[0] // (2 * (CONV - 1))
+    tails_ref[...] = gathered.tails(wide).astype(BF16)
+
+
+def deliver_kernel(prompts, pieces, me_ref, states_ref, windows_ref, tails_ref, *refs):
+    keyval_hbm, state_hbm, conv_ref, keyval_ref, state_ref, sems = refs[pieces:]
     slots, _, channels = state_ref.shape
     tiles = channels // LANES
-    blocks = [(ref, index) for ref in refs[:pieces] for index in range(ref.shape[0])]
-    sources = len(blocks)
-    window_at = prompts * tiles * STATE
-    tail_at = window_at + prompts * WINDOW
-    depth = CONV - 1
-    spare = 16 - 2 * prompts * depth
-    table_rows = refs[0].shape[1] - tail_at
-
-    def rows_of(source, at, size):
-        ref, index = blocks[source]
-        return ref[index, at : at + size, :]
-
-    row = lax.broadcasted_iota(jnp.int32, (table_rows, LANES), 0)
-    grouped = row < 8 * tiles
-    owner = jnp.where(
-        grouped, row // 16 * spare + row % 16 - (16 - spare), row - 8 * tiles + spare * (tiles // 2)
-    )
-    owner = jnp.where(grouped & (row % 16 < 16 - spare), -1, owner)
-    pick = jnp.zeros((1, LANES), F32)
-    for source in range(sources):
-        filled = rows_of(source, tail_at, table_rows).astype(F32)
-        filled = jnp.sum(jnp.where(owner == me, filled, 0.0), axis=0, keepdims=True)
-        pick = pick + jnp.where(filled > 0.5, filled + float(source * prompts - 1), 0.0)
-    pick = pick.astype(jnp.int32)
-
-    span = sources * prompts * STATE
-    wanted = one_hot(lax.broadcasted_iota(jnp.int32, (span, LANES), 0) // STATE == pick)
-    states, windows, tails = [], [], []
-    for source in range(sources):
-        for p in range(prompts):
-            at = p * tiles * STATE
-            states.append(
-                jnp.concatenate(
-                    [rows_of(source, at + tile * STATE, STATE) for tile in range(tiles)], axis=1
-                )
-            )
-            at = window_at + p * WINDOW
-            windows.append(
-                jnp.concatenate(
-                    [
-                        rows_of(source, at, WINDOW // 2),
-                        rows_of(source, at + WINDOW // 2, WINDOW // 2),
-                    ],
-                    axis=1,
-                )
-            )
-        tails.append(
-            jnp.concatenate(
-                [rows_of(source, tail_at + 8 * tile, 16) for tile in range(0, tiles, 2)], axis=1
-            )
-        )
-    states = jnp.concatenate(states, axis=0)
-    windows = jnp.concatenate(windows, axis=0)
-    part = slots // PARTS
-    picked = part * STATE
-    row = lax.broadcasted_iota(jnp.int32, (picked, LANES), 0)
-    lane = lax.broadcasted_iota(jnp.int32, (picked, LANES), 1)
-    slot_of = row // STATE - lane
-    row = lax.broadcasted_iota(jnp.int32, (picked, span), 0)
-    lane = lax.broadcasted_iota(jnp.int32, (picked, span), 1)
-    same = row % STATE == lane % STATE
+    gathered = Gathered(prompts, tiles, refs[:pieces], me_ref[0])
+    states, windows = gathered.states(), gathered.windows()
     copies = []
 
     def send(source_ref, target_ref):
         copies.append(pltpu.make_async_copy(source_ref, target_ref, sems.at[len(copies)]))
         copies[-1].start()
 
+    part = slots // PARTS
     for first in range(0, slots, part):
         here = slice(first, first + part)
-        take = dot_nt(one_hot(slot_of == -first), wanted)
-        take = jnp.where(same, take, 0.0).astype(BF16)
-        moved = jnp.dot(take, states, preferred_element_type=F32)
+        rows = slice(first * STATE, (first + part) * STATE)
+        take = gathered.take(first, part)
+        moved = jnp.dot(take, states, preferred_element_type=F32) + states_ref[rows, :].astype(F32)
         state_ref[here] = moved.astype(BF16).reshape(part, STATE, channels)
         send(state_ref.at[here], state_hbm.at[here])
         moved = jnp.dot(take, windows, preferred_element_type=F32)
-        moved = moved.astype(BF16).reshape(part, WINDOW // 2, 2 * LANES)
+        moved = moved + windows_ref[rows, :].astype(F32)
+        moved = moved.astype(BF16).reshape(part, 16, 2 * LANES)
         for upper in range(2):
             for kind in range(2):
                 at = upper * LANES + kind * HEAD_DIM
-                keyval_ref[here, kind, upper * WINDOW // 2 : (upper + 1) * WINDOW // 2, :] = moved[
+                keyval_ref[here, kind, upper * 16 : (upper + 1) * 16, :] = moved[
                     :, :, at : at + HEAD_DIM
                 ]
         send(keyval_ref.at[here], keyval_hbm.at[here])
-
-    wide = -(-slots // 16) * 16
-    row = lax.broadcasted_iota(jnp.int32, (wide, LANES), 0)
-    lane = lax.broadcasted_iota(jnp.int32, (wide, LANES), 1)
-    unit = one_hot(row == lane)
-    span = sources * 16
-    row = lax.broadcasted_iota(jnp.int32, (span, LANES), 0)
-    base = (pick // prompts) * 16 + (pick % prompts) * depth
-    hits = [
-        one_hot(row == base + prompts * depth * odd + tap) for odd in (0, 1) for tap in range(depth)
-    ]
-    hits = dot_nt(unit, jnp.concatenate(hits, axis=0)).astype(BF16)
-    hits = jnp.concatenate([hits[:, i * span : (i + 1) * span] for i in range(2 * depth)], axis=0)
-    moved = jnp.dot(hits, jnp.concatenate(tails, axis=0), preferred_element_type=F32)
+    wide = tails_ref.shape[0] // (2 * (CONV - 1))
+    moved = gathered.tails(wide) + tails_ref[...].astype(F32)
     for odd in range(2):
-        for tap in range(depth):
-            at = (odd * depth + tap) * wide
+        for tap in range(CONV - 1):
+            at = (odd * (CONV - 1) + tap) * wide
             for pair in range(tiles // 2):
                 tile = 2 * pair + odd
                 conv_ref[tap, :, tile * LANES : (tile + 1) * LANES] = moved[
                     at : at + slots, pair * LANES : (pair + 1) * LANES
                 ].astype(BF16)
-    send(conv_ref, conv_hbm)
     for copy in copies:
         copy.wait()
 
@@ -615,34 +636,56 @@
         compiler_params=params(16),
         name="hold",
     )(fresh, sums, other)
-    pieces = [held, fresh, crossed, swap(fresh, "pr", pr_size, last)]
+    crossed_last = swap(fresh, "pr", pr_size, last)
+    wide = -(-slots // 16) * 16
+    collected = pl.pallas_call(
+        functools.partial(collect_kernel, prompts, slots),
+        out_shape=(
+            shape((slots * STATE, channels), BF16),
+            shape((slots * STATE, 2 * LANES), BF16),
+            shape((2 * (CONV - 1) * wide, tiles // 2 * LANES), BF16),
+        ),
+        in_specs=[SMEM, VMEM, VMEM],
+        out_specs=(VMEM, VMEM, VMEM),
+        compiler_params=params(32),
+        cost_estimate=pl.CostEstimate(flops=1 << 28, bytes_accessed=2 << 20, transcendentals=0),
+        name="collect",
+    )(me[None], held, fresh)
     attention_out, mamba_out = pl.pallas_call(
         norm_kernel,
         out_shape=(shape((rows, features), BF16), shape((rows, channels), BF16)),
-        in_specs=[VMEM] * 5 + [HBM] * 2,
+        in_specs=[VMEM] * 5 + [HBM] * 3,
         out_specs=(VMEM, VMEM),
         compiler_params=params(16),
         cost_estimate=pl.CostEstimate(flops=1 << 24, bytes_accessed=2 << 20, transcendentals=0),
         name="norm",
-    )(attended, gated, sums, attention_gain[None], mamba_gain[None], crossed, inner_weight)
+    )(
+        attended,
+        gated,
+        sums,
+        attention_gain[None],
+        mamba_gain[None],
+        inner_weight,
+        crossed,
+        collected[2],
+    )
     keyval, state, conv = pl.pallas_call(
-        functools.partial(deliver_kernel, prompts, len(pieces)),
+        functools.partial(deliver_kernel, prompts, 2),
         out_shape=(
             shape((slots, 2, WINDOW, HEAD_DIM), BF16),
             shape((slots, STATE, channels), BF16),
             shape((CONV - 1, slots, channels), BF16),
         ),
-        in_specs=[SMEM] + [VMEM] * len(pieces),
-        out_specs=(HBM, HBM, HBM),
+        in_specs=[SMEM] + [VMEM] * 5,
+        out_specs=(HBM, HBM, VMEM),
         scratch_shapes=[
             pltpu.VMEM((slots, 2, WINDOW, HEAD_DIM), BF16),
             pltpu.VMEM((slots, STATE, channels), BF16),
-            pltpu.VMEM((CONV - 1, slots, channels), BF16),
-            pltpu.SemaphoreType.DMA((2 * PARTS + 1,)),
+            pltpu.SemaphoreType.DMA((2 * PARTS,)),
         ],
         compiler_params=params(32),
         name="deliver",
-    )(me[None], *pieces)
+    )(me[None], *collected, crossed, crossed_last)
     return (attention_out, mamba_out, keyval, state, conv.transpose(1, 0, 2))
 
 

time: 31.9 us -> 32.6 us (1.022)
  Pallas kernels: 9.93 us -> 11.4 us
  waiting for transfers between devices: 5.51 us -> 4.68 us
    pallas_call x1 -> x2, Pallas kernels: 1.79 us -> 3.3 us  [the longest x1 2.48 us: on_device(): pl.pallas_call(functools.partial(deliver_kernel, prompts, 2), out_shape=(...]
    ppermute x8, waiting for transfers between devices: 5.51 us -> 4.68 us  [swap(): return lax.ppermute(x, axis, [(i, i ^ bit) for i in range(size)])]
  transfers between devices with their start and end apart: 8 -> 8, of which waited for: 7 -> 7; matrix products, arithmetic and copies ran while one was open for 0% -> 0% of each run, Pallas kernels for 12% -> 15%
where the time goes in v9:
time: 32.6 us; the launch traced here: 32.5 us
  starting transfers between devices  13 us (40%)
  Pallas kernels  11.4 us (35%)
  waiting for transfers between devices  4.68 us (14%)
  matrix products  2.44 us (7%)
  between operations  0.87 us (3%)
    ppermute x8, starting transfers between devices, swap(): return lax.ppermute(x, axis, [(i, i ^ bit) for i in range(size)])  13 us
    ppermute x8, waiting for transfers between devices, swap(): return lax.ppermute(x, axis, [(i, i ^ bit) for i in range(size)])  4.68 us
    pallas_call x1, Pallas kernels, scan_call(): pl.pallas_call(functools.partial(scan_kernel, prompts), out_shape=(jax.Sh...  3.08 us
    pallas_call x1, Pallas kernels, on_device(): pl.pallas_call(functools.partial(deliver_kernel, prompts, 2), out_shape=(...  2.48 us
    dot_general x1, matrix products, on_device(): jnp.einsum('td,dgc->gtc', tokens, inner_weight, preferred_element_type=F32)  2.44 us
    pallas_call x1, Pallas kernels, on_device(): pl.pallas_call(functools.partial(attend_kernel, prompts), out_shape=(shap...  1.95 us
    pallas_call x1, Pallas kernels, on_device(): pl.pallas_call(functools.partial(mix_kernel, prompts), out_shape=(shape((...  1.13 us
    pallas_call x1, Pallas kernels, on_device(): pl.pallas_call(norm_kernel, out_shape=(shape((rows, features), BF16), sha...  1.03 us
  transfers between devices with their start and end apart: 8, of which 7 were waited for; matrix products, arithmetic and copies ran while one was open for 0% of the time, Pallas kernels for 15%

profile of v9, /device:TPU:0, one launch (start us, length us, event | category | flops | bytes accessed | tf_op | source)
XLA Modules:
  0.0 32.5 jit_solution(924513951686628903)
XLA Ops:
  0.7 2.4 %fusion.5.inner_ref = bf16[2,256,512]{2,1,0:T(8,128)(2,1)S(1)} fusion(bf16[896,2,512]{2,1,0:T(2,128)(2,1)} %inner_hbm.1, bf16[256,896]{1,0:T(8,128)(2,1)} %tokens_ref.1), kind=kOutput, calls=%fused_computation.3 | convolution fusion | flops 470024192 | bytes 2818048 | tf_op jit(solution)/shard_map/td,dgc->gtc/dot_general | solution.py:525
  3.2 0.0 copy-start.7
  3.3 1.1 %mix.1 = (f32[96,256]{1,0:T(8,128)S(1)}, bf16[256,512]{1,0:T(8,128)(2,1)S(1)}) custom-call(s32[1,2]{1,0:T(1,128)S(1)} %copy-done.9, bf16[2,256,512]{2,1,0:T(8,128)(2,1)S(1)} %fusion.5.inner_ref, f32[4,512]{1,0:T(4,128)S(1)} %copy-done.8, bf16[96,512]{1,0:T(8,128)(2,1)S(1)} %bitcast.20), custom_call_target="tpu_custom_call" | custom-call | tf_op jit(solution)/shard_map/mix/pallas_call | solution.py:527
  4.4 0.5 %collective-permute-start = (f32[96,256]{1,0:T(8,128)S(1)}, f32[96,256]{1,0:T(8,128)S(1)}, u32[]{:S(2)}, u32[]{:S(2)}) collective-permute-start(f32[96,256]{1,0:T(8,128)S(1)} %get-tuple-element.28), channel_id=1, source_target_pairs={{0,1},{1,0},{2,3},{3,2},{4,5},{5,4},{6,7},{7,6},{8,9},{9,8},{10,11... | collective-permute-start | bytes 294920 | tf_op jit(solution)/shard_map/ppermute | solution.py:541
  4.9 0.9 %collective-permute-done = f32[96,256]{1,0:T(8,128)S(1)} collective-permute-done((f32[96,256]{1,0:T(8,128)S(1)}, f32[96,256]{1,0:T(8,128)S(1)}, u32[]{:S(2)}, u32[]{:S(2)}) %collective-permute-start) | collective-permute-done | bytes 98336 | tf_op jit(solution)/shard_map/ppermute | solution.py:541
  5.9 2.9 %collective-permute-start.1 = (bf16[96,256]{1,0:T(8,128)(2,1)S(1)}, bf16[96,256]{1,0:T(8,128)(2,1)S(1)}, u32[]{:S(2)}, u32[]{:S(2)}) collective-permute-start(bf16[96,256]{1,0:T(8,128)(2,1)S(1)} %get-tuple-element.49), channel_id=1, source_target_pairs={{0,2},{1,3},{2,0},{3,1},{4,6},{5,7},{6,4},{7,5},{8,10},{9,11},{10,... | collective-permute-start | bytes 147464 | tf_op jit(solution)/shard_map/ppermute | solution.py:541
  8.8 1.9 %attend.1 = (f32[256,256]{1,0:T(8,128)S(1)}, f32[8,256]{1,0:T(8,128)S(1)}, bf16[96,128]{1,0:T(8,128)(2,1)S(1)}) custom-call(s32[1,2]{1,0:T(1,128)S(1)} %copy-done.9, bf16[256,896]{1,0:T(8,128)(2,1)S(1)} %copy-done.1, bf16[896,256]{1,0:T(8,128)(2,1)S(1)} %copy-done.2, bf16[64,896]{1,0:T(8,128)(2,1)S(1)} %bitcast.18, bf16[64,896]{1,0:T(8,128)(2,1)S(1)} %bitcast.19, ...), custom_call_target="tpu_custom_call" | custom-call | flops 352321536 | bytes 4194304 | tf_op jit(solution)/shard_map/attend/pallas_call | solution.py:546
  10.8 0.1 collective-permute-done.1.other_ref
  10.9 3.1 %scan.1 = (bf16[224,128]{1,0:T(8,128)(2,1)S(1)}, bf16[8,256,512]{2,1,0:T(8,128)(2,1)S(1)}, bf16[8,256,512]{2,1,0:T(8,128)(2,1)S(1)}) custom-call(s32[1,2]{1,0:T(1,128)S(1)} %copy-done.9, f32[96,256]{1,0:T(8,128)S(1)} %get-tuple-element.50.own_ref, bf16[96,256]{1,0:T(8,128)(2,1)S(1)} %collective-permute-done.1.other_ref, ...), custom_call_target="tpu_custom_call" | custom-call | tf_op jit(solution)/shard_map/scan/pallas_call | solution.py:258
  13.9 3.2 %collective-permute-start.2 = (bf16[1,224,128]{2,1,0:T(8,128)(2,1)S(1)}, bf16[1,224,128]{2,1,0:T(8,128)(2,1)S(1)}, u32[]{:S(2)}, u32[]{:S(2)}) collective-permute-start(bf16[1,224,128]{2,1,0:T(8,128)(2,1)S(1)} %bitcast.21), channel_id=1, source_target_pairs={{0,16},{4,20},{8,24},{12,28},{16,0},{20,4},{24,8},{28,12},{1,17},{... | collective-permute-start | bytes 172040 | tf_op jit(solution)/shard_map/ppermute | solution.py:541
  17.1 0.9 %gate.1 = (f32[256,512]{1,0:T(8,128)S(1)}, f32[2,256]{1,0:T(2,128)S(1)}) custom-call(f32[96,256]{1,0:T(8,128)S(1)} %get-tuple-element.50.own_ref, bf16[96,256]{1,0:T(8,128)(2,1)S(1)} %collective-permute-done.1.other_ref, bf16[8,256,512]{2,1,0:T(8,128)(2,1)S(1)} %get-tuple-element.31.states_even_ref, ...), custom_call_target="tpu_custom_call" | custom-call | flops 16777216 | bytes 4194304 | tf_op jit(solution)/shard_map/gate/pallas_call | solution.py:592
  18.1 0.1 collective-permute-start.3
  18.2 1.1 %collective-permute-done.3.other_ref = f32[2,256]{1,0:T(2,128)S(1)} collective-permute-done((f32[2,256]{1,0:T(2,128)S(1)}, f32[2,256]{1,0:T(2,128)S(1)}, u32[]{:S(2)}, u32[]{:S(2)}) %collective-permute-start.3) | collective-permute-done | bytes 2080 | tf_op jit(solution)/shard_map/ppermute | solution.py:541
  19.3 0.3 collective-permute-done.2.new_ref
  19.6 1.7 %collective-permute-start.4 = (bf16[2,224,128]{2,1,0:T(8,128)(2,1)S(1)}, bf16[2,224,128]{2,1,0:T(8,128)(2,1)S(1)}, u32[]{:S(2)}, u32[]{:S(2)}) collective-permute-start(bf16[2,224,128]{2,1,0:T(8,128)(2,1)S(1)} %get-tuple-element.37.refs_0_), channel_id=1, source_target_pairs={{0,8},{4,12},{8,0},{12,4},{16,24},{20,28},{24,16},{28,20},{1,9},{5... | collective-permute-start | bytes 344072 | tf_op jit(solution)/shard_map/ppermute | solution.py:541
  21.3 1.5 %collective-permute-start.5 = (f32[2,256]{1,0:T(2,128)S(1)}, f32[2,256]{1,0:T(2,128)S(1)}, u32[]{:S(2)}, u32[]{:S(2)}) collective-permute-start(f32[2,256]{1,0:T(2,128)S(1)} %get-tuple-element.38.own_ref), channel_id=1, source_target_pairs={{0,2},{1,3},{2,0},{3,1},{4,6},{5,7},{6,4},{7,5},{8,10},{9,11},{10,... | collective-permute-start | bytes 6152 | tf_op jit(solution)/shard_map/ppermute | solution.py:541
  22.8 1.5 %collective-permute-start.6 = (bf16[2,224,128]{2,1,0:T(8,128)(2,1)S(1)}, bf16[2,224,128]{2,1,0:T(8,128)(2,1)S(1)}, u32[]{:S(2)}, u32[]{:S(2)}) collective-permute-start(bf16[2,224,128]{2,1,0:T(8,128)(2,1)S(1)} %get-tuple-element.37.refs_0_), channel_id=1, source_target_pairs={{0,4},{4,0},{8,12},{12,8},{16,20},{20,16},{24,28},{28,24},{1,5},{5... | collective-permute-start | bytes 344072 | tf_op jit(solution)/shard_map/ppermute | solution.py:541
  24.3 0.6 %collective-permute-done.5.other_ref = f32[2,256]{1,0:T(2,128)S(1)} collective-permute-done((f32[2,256]{1,0:T(2,128)S(1)}, f32[2,256]{1,0:T(2,128)S(1)}, u32[]{:S(2)}, u32[]{:S(2)}) %collective-permute-start.5) | collective-permute-done | bytes 2080 | tf_op jit(solution)/shard_map/ppermute | solution.py:541
  24.9 1.6 %collective-permute-start.7 = (bf16[2,224,128]{2,1,0:T(8,128)(2,1)S(1)}, bf16[2,224,128]{2,1,0:T(8,128)(2,1)S(1)}, u32[]{:S(2)}, u32[]{:S(2)}) collective-permute-start(bf16[2,224,128]{2,1,0:T(8,128)(2,1)S(1)} %get-tuple-element.40.refs_1_), channel_id=1, source_target_pairs={{0,4},{4,0},{8,12},{12,8},{16,20},{20,16},{24,28},{28,24},{1,5},{5... | collective-permute-start | bytes 344072 | tf_op jit(solution)/shard_map/ppermute | solution.py:541
  26.5 0.8 %collect.1 = (bf16[896,512]{1,0:T(8,128)(2,1)S(1)}, bf16[896,256]{1,0:T(8,128)(2,1)S(1)}, bf16[384,256]{1,0:T(8,128)(2,1)S(1)}) custom-call(s32[1]{0:T(128)} %bitcast.13.me_ref, bf16[2,224,128]{2,1,0:T(8,128)(2,1)S(1)} %get-tuple-element.37.refs_0_, bf16[2,224,128]{2,1,0:T(8,128)(2,1)S(1)} %get-tuple-element.40.refs_1_), custom_call_target="tpu_custom_call" | custom-call | flops 268435456 | bytes 2097152 | tf_op jit(solution)/shard_map/collect/pallas_call | solution.py:641
  27.3 1.5 %collective-permute-done.6.crossed_hbm.refs_0_ = bf16[2,224,128]{2,1,0:T(8,128)(2,1)S(1)} collective-permute-done((bf16[2,224,128]{2,1,0:T(8,128)(2,1)S(1)}, bf16[2,224,128]{2,1,0:T(8,128)(2,1)S(1)}, u32[]{:S(2)}, u32[]{:S(2)}) %collective-permute-start.6) | collective-permute-done | bytes 114720 | tf_op jit(solution)/shard_map/ppermute | solution.py:541
  28.8 1.0 %norm.1 = (bf16[256,256]{1,0:T(8,128)(2,1)}, bf16[256,512]{1,0:T(8,128)(2,1)}) custom-call(f32[256,256]{1,0:T(8,128)S(1)} %get-tuple-element.27.attended_ref, f32[256,512]{1,0:T(8,128)S(1)} %get-tuple-element.34.gated_ref, f32[2,256]{1,0:T(2,128)S(1)} %get-tuple-element.39.sums_ref, f32[1,256]{1,0:T(1,128)S(1)} %bitcast.26, f32[1,512]{1,0:T(1,128)S(1)} %bitcast.25, ...), custom_call_target="tpu_custom_call" | custom-call | flops 16777216 | bytes 2097152 | tf_op jit(solution)/shard_map/norm/pallas_call | solution.py:654
  29.8 0.2 collective-permute-done.7.refs_1_
  30.0 2.5 %deliver.1 = (bf16[56,2,32,64]{3,2,1,0:T(8,128)(2,1)}, bf16[56,16,512]{2,1,0:T(8,128)(2,1)}, bf16[3,56,512]{2,1,0:T(8,128)(2,1)}) custom-call(s32[1]{0:T(128)} %bitcast.13.me_ref, bf16[896,512]{1,0:T(8,128)(2,1)S(1)} %get-tuple-element.44.states_ref, bf16[896,256]{1,0:T(8,128)(2,1)S(1)} %get-tuple-element.45.windows_ref, ...), custom_call_target="tpu_custom_call" | custom-call | tf_op jit(solution)/shard_map/deliver/pallas_call | solution.py:672
  (37 shorter events, 0.1 us)
Async XLA Ops:
  0.6 8.2 %copy-start.1 = (bf16[256,896]{1,0:T(8,128)(2,1)S(1)}, bf16[256,896]{1,0:T(8,128)(2,1)}, u32[]{:S(2)}) copy-start(bf16[256,896]{1,0:T(8,128)(2,1)} %tokens_ref.1) | copy-start | bytes 1376260
  0.6 2.6 %copy-start.9 = (s32[1,2]{1,0:T(1,128)S(1)}, s32[1,2]{1,0:T(1,128)}, u32[]{:S(2)}) copy-start(s32[1,2]{1,0:T(1,128)} %len_ref.5) | copy-start | bytes 28
  0.7 2.6 %copy-start.8 = (f32[4,512]{1,0:T(4,128)S(1)}, f32[4,512]{1,0:T(4,128)}, u32[]{:S(2)}) copy-start(f32[4,512]{1,0:T(4,128)} %conv_ref.1) | copy-start | bytes 24580
  0.7 8.1 %copy-start.2 = (bf16[896,256]{1,0:T(8,128)(2,1)S(1)}, bf16[896,256]{1,0:T(8,128)(2,1)}, u32[]{:S(2)}) copy-start(bf16[896,256]{1,0:T(8,128)(2,1)} %query_ref.1) | copy-start | bytes 1376260
  0.7 8.1 %copy-start.3 = (bf16[896,64]{0,1:T(8,128)(2,1)S(1)}, bf16[896,64]{0,1:T(8,128)(2,1)}, u32[]{:S(2)}) copy-start(bf16[896,64]{0,1:T(8,128)(2,1)} %param.20) | copy-start | bytes 344068
  0.7 8.1 %copy-start.4 = (bf16[896,64]{0,1:T(8,128)(2,1)S(1)}, bf16[896,64]{0,1:T(8,128)(2,1)}, u32[]{:S(2)}) copy-start(bf16[896,64]{0,1:T(8,128)(2,1)} %param.21) | copy-start | bytes 344068
  0.7 8.1 %copy-start.14 = (s32[56]{0:T(128)S(1)}, s32[56]{0:T(128)}, u32[]{:S(2)}) copy-start(s32[56]{0:T(128)} %param.31) | copy-start | bytes 676
  0.7 8.1 %copy-start.15 = (s32[56]{0:T(128)S(1)}, s32[56]{0:T(128)}, u32[]{:S(2)}) copy-start(s32[56]{0:T(128)} %param.32) | copy-start | bytes 676
  0.7 8.1 %copy-start.16 = (s32[56]{0:T(128)S(1)}, s32[56]{0:T(128)}, u32[]{:S(2)}) copy-start(s32[56]{0:T(128)} %param.33) | copy-start | bytes 676
  3.2 7.7 %copy-start.6 = (bf16[64,512]{1,0:T(8,128)(2,1)S(1)}, bf16[64,512]{1,0:T(8,128)(2,1)}, u32[]{:S(2)}) copy-start(bf16[64,512]{1,0:T(8,128)(2,1)} %step_weight_ref.1) | copy-start | bytes 196612
  3.2 7.7 %copy-start.7 = (f32[16,512]{1,0:T(8,128)S(1)}, f32[16,512]{1,0:T(8,128)}, u32[]{:S(2)}) copy-start(f32[16,512]{1,0:T(8,128)} %rate_ref.1) | copy-start | bytes 98308
  3.2 7.7 %copy-start.10 = (f32[512]{0:T(512)S(1)}, f32[512]{0:T(512)}, u32[]{:S(2)}) copy-start(f32[512]{0:T(512)} %param.27) | copy-start | bytes 6148
  3.2 13.9 %copy-start.11 = (f32[512]{0:T(512)S(1)}, f32[512]{0:T(512)}, u32[]{:S(2)}) copy-start(f32[512]{0:T(512)} %param.29) | copy-start | bytes 6148
  4.4 1.5 %collective-permute-start = (f32[96,256]{1,0:T(8,128)S(1)}, f32[96,256]{1,0:T(8,128)S(1)}, u32[]{:S(2)}, u32[]{:S(2)}) collective-permute-start(f32[96,256]{1,0:T(8,128)S(1)} %get-tuple-element.28), channel_id=1, source_target_pairs={{0,1},{1,0},{2,3},{3,2},{4,5},{5,4},{6,7},{7,6},{8,9},{9,8},{10,11... | collective-permute-start | bytes 294920 | tf_op jit(solution)/shard_map/ppermute | solution.py:541
  5.9 5.0 %collective-permute-start.1 = (bf16[96,256]{1,0:T(8,128)(2,1)S(1)}, bf16[96,256]{1,0:T(8,128)(2,1)S(1)}, u32[]{:S(2)}, u32[]{:S(2)}) collective-permute-start(bf16[96,256]{1,0:T(8,128)(2,1)S(1)} %get-tuple-element.49), channel_id=1, source_target_pairs={{0,2},{1,3},{2,0},{3,1},{4,6},{5,7},{6,4},{7,5},{8,10},{9,11},{10,... | collective-permute-start | bytes 147464 | tf_op jit(solution)/shard_map/ppermute | solution.py:541
  13.9 5.6 %collective-permute-start.2 = (bf16[1,224,128]{2,1,0:T(8,128)(2,1)S(1)}, bf16[1,224,128]{2,1,0:T(8,128)(2,1)S(1)}, u32[]{:S(2)}, u32[]{:S(2)}) collective-permute-start(bf16[1,224,128]{2,1,0:T(8,128)(2,1)S(1)} %bitcast.21), channel_id=1, source_target_pairs={{0,16},{4,20},{8,24},{12,28},{16,0},{20,4},{24,8},{28,12},{1,17},{... | collective-permute-start | bytes 172040 | tf_op jit(solution)/shard_map/ppermute | solution.py:541
  17.1 11.6 %copy-start = (bf16[896,2,512]{2,1,0:T(2,128)(2,1)S(1)}, bf16[896,2,512]{2,1,0:T(2,128)(2,1)}, u32[]{:S(2)}) copy-start(bf16[896,2,512]{2,1,0:T(2,128)(2,1)} %inner_hbm.1) | copy-start | bytes 5505028
  17.1 11.6 %copy-start.12 = (f32[512]{0:T(512)S(1)}, f32[512]{0:T(512)}, u32[]{:S(2)}) copy-start(f32[512]{0:T(512)} %param.30) | copy-start | bytes 6148
  17.1 11.6 %copy-start.13 = (f32[256]{0:T(256)S(1)}, f32[256]{0:T(256)}, u32[]{:S(2)}) copy-start(f32[256]{0:T(256)} %param.22) | copy-start | bytes 3076
  18.1 1.2 %collective-permute-start.3 = (f32[2,256]{1,0:T(2,128)S(1)}, f32[2,256]{1,0:T(2,128)S(1)}, u32[]{:S(2)}, u32[]{:S(2)}) collective-permute-start(f32[2,256]{1,0:T(2,128)S(1)} %get-tuple-element.36.own_ref), channel_id=1, source_target_pairs={{0,1},{1,0},{2,3},{3,2},{4,5},{5,4},{6,7},{7,6},{8,9},{9,8},{10,11... | collective-permute-start | bytes 6152 | tf_op jit(solution)/shard_map/ppermute | solution.py:541
  19.6 5.3 %collective-permute-start.4 = (bf16[2,224,128]{2,1,0:T(8,128)(2,1)S(1)}, bf16[2,224,128]{2,1,0:T(8,128)(2,1)S(1)}, u32[]{:S(2)}, u32[]{:S(2)}) collective-permute-start(bf16[2,224,128]{2,1,0:T(8,128)(2,1)S(1)} %get-tuple-element.37.refs_0_), channel_id=1, source_target_pairs={{0,8},{4,12},{8,0},{12,4},{16,24},{20,28},{24,16},{28,20},{1,9},{5... | collective-permute-start | bytes 344072 | tf_op jit(solution)/shard_map/ppermute | solution.py:541
  21.3 3.6 %collective-permute-start.5 = (f32[2,256]{1,0:T(2,128)S(1)}, f32[2,256]{1,0:T(2,128)S(1)}, u32[]{:S(2)}, u32[]{:S(2)}) collective-permute-start(f32[2,256]{1,0:T(2,128)S(1)} %get-tuple-element.38.own_ref), channel_id=1, source_target_pairs={{0,2},{1,3},{2,0},{3,1},{4,6},{5,7},{6,4},{7,5},{8,10},{9,11},{10,... | collective-permute-start | bytes 6152 | tf_op jit(solution)/shard_map/ppermute | solution.py:541
  22.8 6.0 %collective-permute-start.6 = (bf16[2,224,128]{2,1,0:T(8,128)(2,1)S(1)}, bf16[2,224,128]{2,1,0:T(8,128)(2,1)S(1)}, u32[]{:S(2)}, u32[]{:S(2)}) collective-permute-start(bf16[2,224,128]{2,1,0:T(8,128)(2,1)S(1)} %get-tuple-element.37.refs_0_), channel_id=1, source_target_pairs={{0,4},{4,0},{8,12},{12,8},{16,20},{20,16},{24,28},{28,24},{1,5},{5... | collective-permute-start | bytes 344072 | tf_op jit(solution)/shard_map/ppermute | solution.py:541
  24.9 5.1 %collective-permute-start.7 = (bf16[2,224,128]{2,1,0:T(8,128)(2,1)S(1)}, bf16[2,224,128]{2,1,0:T(8,128)(2,1)S(1)}, u32[]{:S(2)}, u32[]{:S(2)}) collective-permute-start(bf16[2,224,128]{2,1,0:T(8,128)(2,1)S(1)} %get-tuple-element.40.refs_1_), channel_id=1, source_target_pairs={{0,4},{4,0},{8,12},{12,8},{16,20},{20,16},{24,28},{28,24},{1,5},{5... | collective-permute-start | bytes 344072 | tf_op jit(solution)/shard_map/ppermute | solution.py:541
  (1 other events, 2.6 us)

commit v10 on v8

--- a/solution.py
+++ b/solution.py
@@ -19,13 +19,11 @@
 EPSILON = 1e-06
 LANES = 128
 BLOCK = 16
-PARTS = 2
 RESET = 1e30
 
 F32 = jnp.float32
 BF16 = jnp.bfloat16
 VMEM = pl.BlockSpec(memory_space=pltpu.VMEM)
-SMEM = pl.BlockSpec(memory_space=pltpu.SMEM)
 HBM = pl.BlockSpec(memory_space=pltpu.HBM)
 
 
@@ -42,7 +40,7 @@
     at = 0
     for p in range(prompts):
         starts.append(at)
-        at = at + len_ref[0, p]
+        at = at + len_ref[0:1, p : p + 1]
         ends.append(at)
     return starts, ends
 
@@ -201,10 +199,14 @@
     decay_ref,
     input_ref,
     in_map_ref,
+    scalars_ref,
+    sem,
 ):
+    scalars_copy = pltpu.make_async_copy(len_ref, scalars_ref, sem)
+    scalars_copy.start()
     rows, channels = mixed_ref.shape
     pairs = rows // BLOCK // 2
-    starts, ends = bounds(len_ref, prompts)
+    starts, _ = bounds(len_ref, prompts)
     projected = own_ref[...] + other_ref[...].astype(F32)
     low = projected[:DT_RANK, :].T.astype(BF16)
     pre = jnp.dot(low, step_weight_ref[...], preferred_element_type=F32) + step_bias_ref[...]
@@ -234,8 +236,10 @@
         return advance(2 * pair + 1, state, states_odd_ref, pair)
 
     lax.fori_loop(0, pairs, two_blocks, jnp.zeros((STATE, channels), F32))
+    scalars_copy.wait()
+    last = -1
     for p in range(prompts):
-        last = ends[p] - 1
+        last = last + scalars_ref[0, p]
         block = last // BLOCK
         at = pl.multiple_of((last - block * BLOCK) * STATE, STATE)
         final = jnp.where(
@@ -258,12 +262,14 @@
     return pl.pallas_call(
         functools.partial(scan_kernel, prompts),
         out_shape=(jax.ShapeDtypeStruct((payload_rows, LANES), BF16), states, states),
-        in_specs=[SMEM] + [VMEM] * 7,
+        in_specs=[VMEM] * 8,
         out_specs=(VMEM,) * 3,
         scratch_shapes=[
             pltpu.VMEM((rows, channels), F32),
             pltpu.VMEM((rows, channels), F32),
             pltpu.VMEM((rows // BLOCK, STATE, LANES), F32),
+            pltpu.SMEM((1, prompts), jnp.int32),
+            pltpu.SemaphoreType.DMA,
         ],
         compiler_params=params(16),
         name="scan",
@@ -353,11 +359,10 @@
 def deliver_kernel(
     prompts,
     pieces,
-    me_ref,
     *refs,
 ):
-    keyval_hbm, state_hbm, conv_hbm, keyval_ref, state_ref, conv_ref, sems = refs[pieces:]
-    me = me_ref[0]
+    keyval_ref, state_ref, conv_ref = refs[pieces:]
+    me = lax.axis_index("pr")
     slots, _, channels = state_ref.shape
     tiles = channels // LANES
     blocks = [(ref, index) for ref in refs[:pieces] for index in range(ref.shape[0])]
@@ -413,36 +418,22 @@
         )
     states = jnp.concatenate(states, axis=0)
     windows = jnp.concatenate(windows, axis=0)
-    part = slots // PARTS
-    picked = part * STATE
-    row = lax.broadcasted_iota(jnp.int32, (picked, LANES), 0)
-    lane = lax.broadcasted_iota(jnp.int32, (picked, LANES), 1)
-    slot_of = row // STATE - lane
-    row = lax.broadcasted_iota(jnp.int32, (picked, span), 0)
-    lane = lax.broadcasted_iota(jnp.int32, (picked, span), 1)
-    same = row % STATE == lane % STATE
-    copies = []
-
-    def send(source_ref, target_ref):
-        copies.append(pltpu.make_async_copy(source_ref, target_ref, sems.at[len(copies)]))
-        copies[-1].start()
-
-    for first in range(0, slots, part):
-        here = slice(first, first + part)
-        take = dot_nt(one_hot(slot_of == -first), wanted)
-        take = jnp.where(same, take, 0.0).astype(BF16)
-        moved = jnp.dot(take, states, preferred_element_type=F32)
-        state_ref[here] = moved.astype(BF16).reshape(part, STATE, channels)
-        send(state_ref.at[here], state_hbm.at[here])
-        moved = jnp.dot(take, windows, preferred_element_type=F32)
-        moved = moved.astype(BF16).reshape(part, WINDOW // 2, 2 * LANES)
-        for upper in range(2):
-            for kind in range(2):
-                at = upper * LANES + kind * HEAD_DIM
-                keyval_ref[here, kind, upper * WINDOW // 2 : (upper + 1) * WINDOW // 2, :] = moved[
-                    :, :, at : at + HEAD_DIM
-                ]
-        send(keyval_ref.at[here], keyval_hbm.at[here])
+    row = lax.broadcasted_iota(jnp.int32, (slots * STATE, LANES), 0)
+    lane = lax.broadcasted_iota(jnp.int32, (slots * STATE, LANES), 1)
+    take = dot_nt(one_hot(row // STATE == lane), wanted)
+    row = lax.broadcasted_iota(jnp.int32, (slots * STATE, span), 0)
+    lane = lax.broadcasted_iota(jnp.int32, (slots * STATE, span), 1)
+    take = jnp.where(row % STATE == lane % STATE, take, 0.0).astype(BF16)
+    moved = jnp.dot(take, states, preferred_element_type=F32)
+    state_ref[...] = moved.astype(BF16).reshape(slots, STATE, channels)
+    moved = jnp.dot(take, windows, preferred_element_type=F32)
+    moved = moved.astype(BF16).reshape(slots, WINDOW // 2, 2 * LANES)
+    for upper in range(2):
+        for kind in range(2):
+            at = upper * LANES + kind * HEAD_DIM
+            keyval_ref[:, kind, upper * WINDOW // 2 : (upper + 1) * WINDOW // 2, :] = moved[
+                :, :, at : at + HEAD_DIM
+            ]
 
     wide = -(-slots // 16) * 16
     row = lax.broadcasted_iota(jnp.int32, (wide, LANES), 0)
@@ -465,9 +456,6 @@
                 conv_ref[tap, :, tile * LANES : (tile + 1) * LANES] = moved[
                     at : at + slots, pair * LANES : (pair + 1) * LANES
                 ].astype(BF16)
-    send(conv_ref, conv_hbm)
-    for copy in copies:
-        copy.wait()
 
 
 def on_device(
@@ -509,7 +497,7 @@
             shape((DT_RANK + 2 * STATE, rows)),
             shape((rows, channels), BF16),
         ),
-        in_specs=[SMEM] + [VMEM] * 3,
+        in_specs=[VMEM] * 4,
         out_specs=(VMEM, VMEM),
         scratch_shapes=[pltpu.VMEM((rows + 8, channels), F32)],
         compiler_params=params(16),
@@ -529,7 +517,7 @@
             shape((8, rows)),
             shape((early_rows, LANES), BF16),
         ),
-        in_specs=[SMEM] + [VMEM] * 8,
+        in_specs=[VMEM] * 9,
         out_specs=(VMEM, VMEM, VMEM),
         scratch_shapes=[
             pltpu.VMEM((8, LANES), jnp.int32),
@@ -582,7 +570,6 @@
         name="gate",
     )(pair, far, states_even, states_odd, mixed, inner, mamba_skip[None], square)
 
-    me = lax.axis_index("pr").astype(jnp.int32)
     held = payload[None]
     pr_bits = [1 << i for i in reversed(range((pr_size - 1).bit_length()))]
     tp_bits = [1 << i for i in range((tp_size - 1).bit_length())]
@@ -632,17 +619,11 @@
             shape((slots, STATE, channels), BF16),
             shape((CONV - 1, slots, channels), BF16),
         ),
-        in_specs=[SMEM] + [VMEM] * len(pieces),
-        out_specs=(HBM, HBM, HBM),
-        scratch_shapes=[
-            pltpu.VMEM((slots, 2, WINDOW, HEAD_DIM), BF16),
-            pltpu.VMEM((slots, STATE, channels), BF16),
-            pltpu.VMEM((CONV - 1, slots, channels), BF16),
-            pltpu.SemaphoreType.DMA((2 * PARTS + 1,)),
-        ],
+        in_specs=[VMEM] * len(pieces),
+        out_specs=(VMEM,) * 3,
         compiler_params=params(32),
         name="deliver",
-    )(me[None], *pieces)
+    )(*pieces)
     return (attention_out, mamba_out, keyval, state, conv.transpose(1, 0, 2))
 
 

time: 31.9 us -> 31.1 us (0.975)
  Pallas kernels: 9.93 us -> 8.57 us
    pallas_call x1, Pallas kernels: 1.95 us -> 1.4 us  [on_device(): pl.pallas_call(functools.partial(attend_kernel, prompts), out_shape=(shap...]
    pallas_call x1, Pallas kernels: 3.08 us -> 2.57 us  [scan_call(): pl.pallas_call(functools.partial(scan_kernel, prompts), out_shape=(jax.Sh...]
    pallas_call x1, Pallas kernels: 1.13 us -> 0.63 us  [on_device(): pl.pallas_call(functools.partial(mix_kernel, prompts), out_shape=(shape((...]
  transfers between devices with their start and end apart: 8 -> 8, of which waited for: 7 -> 6; matrix products, arithmetic and copies ran while one was open for 0% -> 0% of each run, Pallas kernels for 12% -> 11%
where the time goes in v10:
time: 31.1 us; the launch traced here: 31 us
  starting transfers between devices  13.2 us (42%)
  Pallas kernels  8.57 us (28%)
  waiting for transfers between devices  5.8 us (19%)
  matrix products  2.44 us (8%)
  between operations  0.86 us (3%)
    ppermute x8, starting transfers between devices, swap(): return lax.ppermute(x, axis, [(i, i ^ bit) for i in range(size)])  13.2 us
    ppermute x8, waiting for transfers between devices, swap(): return lax.ppermute(x, axis, [(i, i ^ bit) for i in range(size)])  5.8 us
    pallas_call x1, Pallas kernels, scan_call(): pl.pallas_call(functools.partial(scan_kernel, prompts), out_shape=(jax.Sh...  2.57 us
    dot_general x1, matrix products, on_device(): jnp.einsum('td,dgc->gtc', tokens, inner_weight, preferred_element_type=F32)  2.44 us
    pallas_call x1, Pallas kernels, on_device(): pl.pallas_call(functools.partial(deliver_kernel, prompts, len(pieces)), o...  1.99 us
    pallas_call x1, Pallas kernels, on_device(): pl.pallas_call(functools.partial(attend_kernel, prompts), out_shape=(shap...  1.4 us
    pallas_call x1, Pallas kernels, on_device(): pl.pallas_call(norm_kernel, out_shape=(shape((rows, features), BF16), sha...  1.03 us
    pallas_call x1, Pallas kernels, on_device(): pl.pallas_call(gate_kernel, out_shape=(shape((rows, channels)), shape((2,...  0.93 us
  transfers between devices with their start and end apart: 8, of which 6 were waited for; matrix products, arithmetic and copies ran while one was open for 0% of the time, Pallas kernels for 11%

profile of v10, /device:TPU:0, one launch (start us, length us, event | category | flops | bytes accessed | tf_op | source)
XLA Modules:
  0.0 31.0 jit_solution(8809677163287689915)
XLA Ops:
  0.7 2.4 %fusion.5.inner_ref = bf16[2,256,512]{2,1,0:T(8,128)(2,1)S(1)} fusion(bf16[896,2,512]{2,1,0:T(2,128)(2,1)} %inner_hbm.1, bf16[256,896]{1,0:T(8,128)(2,1)} %tokens_ref.1), kind=kOutput, calls=%fused_computation.3 | convolution fusion | flops 470024192 | bytes 2818048 | tf_op jit(solution)/shard_map/td,dgc->gtc/dot_general | solution.py:492
  3.2 0.0 copy-start.6
  3.2 0.0 copy-start.7
  3.2 0.0 copy-start.10
  3.3 0.6 %mix.1 = (f32[96,256]{1,0:T(8,128)S(1)}, bf16[256,512]{1,0:T(8,128)(2,1)S(1)}) custom-call(s32[1,2]{1,0:T(1,128)S(1)} %copy-done.9, bf16[2,256,512]{2,1,0:T(8,128)(2,1)S(1)} %fusion.5.inner_ref, f32[4,512]{1,0:T(4,128)S(1)} %copy-done.8, bf16[96,512]{1,0:T(8,128)(2,1)S(1)} %bitcast.19), custom_call_target="tpu_custom_call" | custom-call | tf_op jit(solution)/shard_map/mix/pallas_call | solution.py:494
  3.9 0.5 %collective-permute-start = (f32[96,256]{1,0:T(8,128)S(1)}, f32[96,256]{1,0:T(8,128)S(1)}, u32[]{:S(2)}, u32[]{:S(2)}) collective-permute-start(f32[96,256]{1,0:T(8,128)S(1)} %get-tuple-element.25), channel_id=1, source_target_pairs={{0,1},{1,0},{2,3},{3,2},{4,5},{5,4},{6,7},{7,6},{8,9},{9,8},{10,11... | collective-permute-start | bytes 294920 | tf_op jit(solution)/shard_map/ppermute | solution.py:508
  4.4 0.9 %collective-permute-done = f32[96,256]{1,0:T(8,128)S(1)} collective-permute-done((f32[96,256]{1,0:T(8,128)S(1)}, f32[96,256]{1,0:T(8,128)S(1)}, u32[]{:S(2)}, u32[]{:S(2)}) %collective-permute-start) | collective-permute-done | bytes 98336 | tf_op jit(solution)/shard_map/ppermute | solution.py:508
  5.4 2.9 %collective-permute-start.1 = (bf16[96,256]{1,0:T(8,128)(2,1)S(1)}, bf16[96,256]{1,0:T(8,128)(2,1)S(1)}, u32[]{:S(2)}, u32[]{:S(2)}) collective-permute-start(bf16[96,256]{1,0:T(8,128)(2,1)S(1)} %get-tuple-element.43), channel_id=1, source_target_pairs={{0,2},{1,3},{2,0},{3,1},{4,6},{5,7},{6,4},{7,5},{8,10},{9,11},{10,... | collective-permute-start | bytes 147464 | tf_op jit(solution)/shard_map/ppermute | solution.py:508
  8.3 1.4 %attend.1 = (f32[256,256]{1,0:T(8,128)S(1)}, f32[8,256]{1,0:T(8,128)S(1)}, bf16[96,128]{1,0:T(8,128)(2,1)S(1)}) custom-call(s32[1,2]{1,0:T(1,128)S(1)} %copy-done.9, bf16[256,896]{1,0:T(8,128)(2,1)S(1)} %copy-done.1, bf16[896,256]{1,0:T(8,128)(2,1)S(1)} %copy-done.2, bf16[64,896]{1,0:T(8,128)(2,1)S(1)} %bitcast.17, bf16[64,896]{1,0:T(8,128)(2,1)S(1)} %bitcast.18, ...), custom_call_target="tpu_custom_call" | custom-call | flops 352321536 | bytes 4194304 | tf_op jit(solution)/shard_map/attend/pallas_call | solution.py:513
  9.7 0.6 %collective-permute-done.1.other_ref = bf16[96,256]{1,0:T(8,128)(2,1)S(1)} collective-permute-done((bf16[96,256]{1,0:T(8,128)(2,1)S(1)}, bf16[96,256]{1,0:T(8,128)(2,1)S(1)}, u32[]{:S(2)}, u32[]{:S(2)}) %collective-permute-start.1) | collective-permute-done | bytes 49184 | tf_op jit(solution)/shard_map/ppermute | solution.py:508
  10.4 2.6 %scan.1 = (bf16[224,128]{1,0:T(8,128)(2,1)S(1)}, bf16[8,256,512]{2,1,0:T(8,128)(2,1)S(1)}, bf16[8,256,512]{2,1,0:T(8,128)(2,1)S(1)}) custom-call(s32[1,2]{1,0:T(1,128)S(1)} %copy-done.9, f32[96,256]{1,0:T(8,128)S(1)} %get-tuple-element.44.own_ref, bf16[96,256]{1,0:T(8,128)(2,1)S(1)} %collective-permute-done.1.other_ref, ...), custom_call_target="tpu_custom_call" | custom-call | tf_op jit(solution)/shard_map/scan/pallas_call | solution.py:262
  12.9 3.2 %collective-permute-start.2 = (bf16[1,224,128]{2,1,0:T(8,128)(2,1)S(1)}, bf16[1,224,128]{2,1,0:T(8,128)(2,1)S(1)}, u32[]{:S(2)}, u32[]{:S(2)}) collective-permute-start(bf16[1,224,128]{2,1,0:T(8,128)(2,1)S(1)} %bitcast.20), channel_id=1, source_target_pairs={{0,16},{4,20},{8,24},{12,28},{16,0},{20,4},{24,8},{28,12},{1,17},{... | collective-permute-start | bytes 172040 | tf_op jit(solution)/shard_map/ppermute | solution.py:508
  16.1 0.9 %gate.1 = (f32[256,512]{1,0:T(8,128)S(1)}, f32[2,256]{1,0:T(2,128)S(1)}) custom-call(f32[96,256]{1,0:T(8,128)S(1)} %get-tuple-element.44.own_ref, bf16[96,256]{1,0:T(8,128)(2,1)S(1)} %collective-permute-done.1.other_ref, bf16[8,256,512]{2,1,0:T(8,128)(2,1)S(1)} %get-tuple-element.28.states_even_ref, ...), custom_call_target="tpu_custom_call" | custom-call | flops 16777216 | bytes 4194304 | tf_op jit(solution)/shard_map/gate/pallas_call | solution.py:559
  17.1 0.1 collective-permute-start.3
  17.1 1.1 %collective-permute-done.3.other_ref = f32[2,256]{1,0:T(2,128)S(1)} collective-permute-done((f32[2,256]{1,0:T(2,128)S(1)}, f32[2,256]{1,0:T(2,128)S(1)}, u32[]{:S(2)}, u32[]{:S(2)}) %collective-permute-start.3) | collective-permute-done | bytes 2080 | tf_op jit(solution)/shard_map/ppermute | solution.py:508
  18.3 2.0 %collective-permute-start.4 = (bf16[2,224,128]{2,1,0:T(8,128)(2,1)S(1)}, bf16[2,224,128]{2,1,0:T(8,128)(2,1)S(1)}, u32[]{:S(2)}, u32[]{:S(2)}) collective-permute-start(bf16[2,224,128]{2,1,0:T(8,128)(2,1)S(1)} %get-tuple-element.34.refs_0_), channel_id=1, source_target_pairs={{0,8},{4,12},{8,0},{12,4},{16,24},{20,28},{24,16},{28,20},{1,9},{5... | collective-permute-start | bytes 344072 | tf_op jit(solution)/shard_map/ppermute | solution.py:508
  20.3 1.5 %collective-permute-start.5 = (f32[2,256]{1,0:T(2,128)S(1)}, f32[2,256]{1,0:T(2,128)S(1)}, u32[]{:S(2)}, u32[]{:S(2)}) collective-permute-start(f32[2,256]{1,0:T(2,128)S(1)} %get-tuple-element.35.own_ref), channel_id=1, source_target_pairs={{0,2},{1,3},{2,0},{3,1},{4,6},{5,7},{6,4},{7,5},{8,10},{9,11},{10,... | collective-permute-start | bytes 6152 | tf_op jit(solution)/shard_map/ppermute | solution.py:508
  21.8 1.5 %collective-permute-start.6 = (bf16[2,224,128]{2,1,0:T(8,128)(2,1)S(1)}, bf16[2,224,128]{2,1,0:T(8,128)(2,1)S(1)}, u32[]{:S(2)}, u32[]{:S(2)}) collective-permute-start(bf16[2,224,128]{2,1,0:T(8,128)(2,1)S(1)} %get-tuple-element.34.refs_0_), channel_id=1, source_target_pairs={{0,4},{4,0},{8,12},{12,8},{16,20},{20,16},{24,28},{28,24},{1,5},{5... | collective-permute-start | bytes 344072 | tf_op jit(solution)/shard_map/ppermute | solution.py:508
  23.3 0.6 %collective-permute-done.5.other_ref = f32[2,256]{1,0:T(2,128)S(1)} collective-permute-done((f32[2,256]{1,0:T(2,128)S(1)}, f32[2,256]{1,0:T(2,128)S(1)}, u32[]{:S(2)}, u32[]{:S(2)}) %collective-permute-start.5) | collective-permute-done | bytes 2080 | tf_op jit(solution)/shard_map/ppermute | solution.py:508
  23.9 1.6 %collective-permute-start.7 = (bf16[2,224,128]{2,1,0:T(8,128)(2,1)S(1)}, bf16[2,224,128]{2,1,0:T(8,128)(2,1)S(1)}, u32[]{:S(2)}, u32[]{:S(2)}) collective-permute-start(bf16[2,224,128]{2,1,0:T(8,128)(2,1)S(1)} %get-tuple-element.39.refs_1_), channel_id=1, source_target_pairs={{0,4},{4,0},{8,12},{12,8},{16,20},{20,16},{24,28},{28,24},{1,5},{5... | collective-permute-start | bytes 344072 | tf_op jit(solution)/shard_map/ppermute | solution.py:508
  25.5 2.0 %collective-permute-done.6.crossed_hbm.refs_2_ = bf16[2,224,128]{2,1,0:T(8,128)(2,1)S(1)} collective-permute-done((bf16[2,224,128]{2,1,0:T(8,128)(2,1)S(1)}, bf16[2,224,128]{2,1,0:T(8,128)(2,1)S(1)}, u32[]{:S(2)}, u32[]{:S(2)}) %collective-permute-start.6) | collective-permute-done | bytes 114720 | tf_op jit(solution)/shard_map/ppermute | solution.py:508
  27.5 1.0 %norm.1 = (bf16[256,256]{1,0:T(8,128)(2,1)}, bf16[256,512]{1,0:T(8,128)(2,1)}) custom-call(f32[256,256]{1,0:T(8,128)S(1)} %get-tuple-element.24.attended_ref, f32[256,512]{1,0:T(8,128)S(1)} %get-tuple-element.31.gated_ref, f32[2,256]{1,0:T(2,128)S(1)} %get-tuple-element.36.sums_ref, f32[1,256]{1,0:T(1,128)S(1)} %bitcast.25, f32[1,512]{1,0:T(1,128)S(1)} %bitcast.24, ...), custom_call_target="tpu_custom_call" | custom-call | flops 16777216 | bytes 2097152 | tf_op jit(solution)/shard_map/norm/pallas_call | solution.py:606
  28.5 0.5 %collective-permute-done.7.refs_3_ = bf16[2,224,128]{2,1,0:T(8,128)(2,1)S(1)} collective-permute-done((bf16[2,224,128]{2,1,0:T(8,128)(2,1)S(1)}, bf16[2,224,128]{2,1,0:T(8,128)(2,1)S(1)}, u32[]{:S(2)}, u32[]{:S(2)}) %collective-permute-start.7) | collective-permute-done | bytes 114720 | tf_op jit(solution)/shard_map/ppermute | solution.py:508
  29.0 2.0 %deliver.1 = (bf16[56,2,32,64]{3,2,1,0:T(8,128)(2,1)}, bf16[56,16,512]{2,1,0:T(8,128)(2,1)}, bf16[3,56,512]{2,1,0:T(8,128)(2,1)}) custom-call(bf16[2,224,128]{2,1,0:T(8,128)(2,1)S(1)} %get-tuple-element.34.refs_0_, bf16[2,224,128]{2,1,0:T(8,128)(2,1)S(1)} %get-tuple-element.39.refs_1_, bf16[2,224,128]{2,1,0:T(8,128)(2,1)S(1)} %collective-permute-done.6.crossed_hbm.refs_2_, ...), custom_call_target="tpu_custom_call" | custom-call | tf_op jit(solution)/shard_map/deliver/pallas_call | solution.py:615
  (36 shorter events, 0.1 us)
Async XLA Ops:
  0.6 7.6 %copy-start.1 = (bf16[256,896]{1,0:T(8,128)(2,1)S(1)}, bf16[256,896]{1,0:T(8,128)(2,1)}, u32[]{:S(2)}) copy-start(bf16[256,896]{1,0:T(8,128)(2,1)} %tokens_ref.1) | copy-start | bytes 1376260
  0.6 2.6 %copy-start.9 = (s32[1,2]{1,0:T(1,128)S(1)}, s32[1,2]{1,0:T(1,128)}, u32[]{:S(2)}) copy-start(s32[1,2]{1,0:T(1,128)} %len_ref.5) | copy-start | bytes 28
  0.7 2.6 %copy-start.5 = (bf16[512,96]{0,1:T(8,128)(2,1)S(1)}, bf16[512,96]{0,1:T(8,128)(2,1)}, u32[]{:S(2)}) copy-start(bf16[512,96]{0,1:T(8,128)(2,1)} %param.25) | copy-start | bytes 294916
  0.7 7.6 %copy-start.16 = (s32[56]{0:T(128)S(1)}, s32[56]{0:T(128)}, u32[]{:S(2)}) copy-start(s32[56]{0:T(128)} %param.33) | copy-start | bytes 676
  0.7 7.6 %copy-start.15 = (s32[56]{0:T(128)S(1)}, s32[56]{0:T(128)}, u32[]{:S(2)}) copy-start(s32[56]{0:T(128)} %param.32) | copy-start | bytes 676
  0.7 7.6 %copy-start.14 = (s32[56]{0:T(128)S(1)}, s32[56]{0:T(128)}, u32[]{:S(2)}) copy-start(s32[56]{0:T(128)} %param.31) | copy-start | bytes 676
  0.7 7.6 %copy-start.4 = (bf16[896,64]{0,1:T(8,128)(2,1)S(1)}, bf16[896,64]{0,1:T(8,128)(2,1)}, u32[]{:S(2)}) copy-start(bf16[896,64]{0,1:T(8,128)(2,1)} %param.21) | copy-start | bytes 344068
  0.7 7.6 %copy-start.3 = (bf16[896,64]{0,1:T(8,128)(2,1)S(1)}, bf16[896,64]{0,1:T(8,128)(2,1)}, u32[]{:S(2)}) copy-start(bf16[896,64]{0,1:T(8,128)(2,1)} %param.20) | copy-start | bytes 344068
  0.7 7.6 %copy-start.2 = (bf16[896,256]{1,0:T(8,128)(2,1)S(1)}, bf16[896,256]{1,0:T(8,128)(2,1)}, u32[]{:S(2)}) copy-start(bf16[896,256]{1,0:T(8,128)(2,1)} %query_ref.1) | copy-start | bytes 1376260
  3.2 7.2 %copy-start.6 = (bf16[64,512]{1,0:T(8,128)(2,1)S(1)}, bf16[64,512]{1,0:T(8,128)(2,1)}, u32[]{:S(2)}) copy-start(bf16[64,512]{1,0:T(8,128)(2,1)} %step_weight_ref.1) | copy-start | bytes 196612
  3.2 7.2 %copy-start.7 = (f32[16,512]{1,0:T(8,128)S(1)}, f32[16,512]{1,0:T(8,128)}, u32[]{:S(2)}) copy-start(f32[16,512]{1,0:T(8,128)} %rate_ref.1) | copy-start | bytes 98308
  3.2 7.1 %copy-start.10 = (f32[512]{0:T(512)S(1)}, f32[512]{0:T(512)}, u32[]{:S(2)}) copy-start(f32[512]{0:T(512)} %param.27) | copy-start | bytes 6148
  3.2 12.9 %copy-start.11 = (f32[512]{0:T(512)S(1)}, f32[512]{0:T(512)}, u32[]{:S(2)}) copy-start(f32[512]{0:T(512)} %param.29) | copy-start | bytes 6148
  3.9 1.5 %collective-permute-start = (f32[96,256]{1,0:T(8,128)S(1)}, f32[96,256]{1,0:T(8,128)S(1)}, u32[]{:S(2)}, u32[]{:S(2)}) collective-permute-start(f32[96,256]{1,0:T(8,128)S(1)} %get-tuple-element.25), channel_id=1, source_target_pairs={{0,1},{1,0},{2,3},{3,2},{4,5},{5,4},{6,7},{7,6},{8,9},{9,8},{10,11... | collective-permute-start | bytes 294920 | tf_op jit(solution)/shard_map/ppermute | solution.py:508
  5.4 5.0 %collective-permute-start.1 = (bf16[96,256]{1,0:T(8,128)(2,1)S(1)}, bf16[96,256]{1,0:T(8,128)(2,1)S(1)}, u32[]{:S(2)}, u32[]{:S(2)}) collective-permute-start(bf16[96,256]{1,0:T(8,128)(2,1)S(1)} %get-tuple-element.43), channel_id=1, source_target_pairs={{0,2},{1,3},{2,0},{3,1},{4,6},{5,7},{6,4},{7,5},{8,10},{9,11},{10,... | collective-permute-start | bytes 147464 | tf_op jit(solution)/shard_map/ppermute | solution.py:508
  12.9 5.4 %collective-permute-start.2 = (bf16[1,224,128]{2,1,0:T(8,128)(2,1)S(1)}, bf16[1,224,128]{2,1,0:T(8,128)(2,1)S(1)}, u32[]{:S(2)}, u32[]{:S(2)}) collective-permute-start(bf16[1,224,128]{2,1,0:T(8,128)(2,1)S(1)} %bitcast.20), channel_id=1, source_target_pairs={{0,16},{4,20},{8,24},{12,28},{16,0},{20,4},{24,8},{28,12},{1,17},{... | collective-permute-start | bytes 172040 | tf_op jit(solution)/shard_map/ppermute | solution.py:508
  16.1 11.4 %copy-start = (bf16[896,2,512]{2,1,0:T(2,128)(2,1)S(1)}, bf16[896,2,512]{2,1,0:T(2,128)(2,1)}, u32[]{:S(2)}) copy-start(bf16[896,2,512]{2,1,0:T(2,128)(2,1)} %inner_hbm.1) | copy-start | bytes 5505028
  16.1 11.4 %copy-start.12 = (f32[512]{0:T(512)S(1)}, f32[512]{0:T(512)}, u32[]{:S(2)}) copy-start(f32[512]{0:T(512)} %param.30) | copy-start | bytes 6148
  16.1 11.4 %copy-start.13 = (f32[256]{0:T(256)S(1)}, f32[256]{0:T(256)}, u32[]{:S(2)}) copy-start(f32[256]{0:T(256)} %param.22) | copy-start | bytes 3076
  17.1 1.2 %collective-permute-start.3 = (f32[2,256]{1,0:T(2,128)S(1)}, f32[2,256]{1,0:T(2,128)S(1)}, u32[]{:S(2)}, u32[]{:S(2)}) collective-permute-start(f32[2,256]{1,0:T(2,128)S(1)} %get-tuple-element.33.own_ref), channel_id=1, source_target_pairs={{0,1},{1,0},{2,3},{3,2},{4,5},{5,4},{6,7},{7,6},{8,9},{9,8},{10,11... | collective-permute-start | bytes 6152 | tf_op jit(solution)/shard_map/ppermute | solution.py:508
  18.3 5.5 %collective-permute-start.4 = (bf16[2,224,128]{2,1,0:T(8,128)(2,1)S(1)}, bf16[2,224,128]{2,1,0:T(8,128)(2,1)S(1)}, u32[]{:S(2)}, u32[]{:S(2)}) collective-permute-start(bf16[2,224,128]{2,1,0:T(8,128)(2,1)S(1)} %get-tuple-element.34.refs_0_), channel_id=1, source_target_pairs={{0,8},{4,12},{8,0},{12,4},{16,24},{20,28},{24,16},{28,20},{1,9},{5... | collective-permute-start | bytes 344072 | tf_op jit(solution)/shard_map/ppermute | solution.py:508
  20.3 3.6 %collective-permute-start.5 = (f32[2,256]{1,0:T(2,128)S(1)}, f32[2,256]{1,0:T(2,128)S(1)}, u32[]{:S(2)}, u32[]{:S(2)}) collective-permute-start(f32[2,256]{1,0:T(2,128)S(1)} %get-tuple-element.35.own_ref), channel_id=1, source_target_pairs={{0,2},{1,3},{2,0},{3,1},{4,6},{5,7},{6,4},{7,5},{8,10},{9,11},{10,... | collective-permute-start | bytes 6152 | tf_op jit(solution)/shard_map/ppermute | solution.py:508
  21.8 5.7 %collective-permute-start.6 = (bf16[2,224,128]{2,1,0:T(8,128)(2,1)S(1)}, bf16[2,224,128]{2,1,0:T(8,128)(2,1)S(1)}, u32[]{:S(2)}, u32[]{:S(2)}) collective-permute-start(bf16[2,224,128]{2,1,0:T(8,128)(2,1)S(1)} %get-tuple-element.34.refs_0_), channel_id=1, source_target_pairs={{0,4},{4,0},{8,12},{12,8},{16,20},{20,16},{24,28},{28,24},{1,5},{5... | collective-permute-start | bytes 344072 | tf_op jit(solution)/shard_map/ppermute | solution.py:508
  23.9 5.1 %collective-permute-start.7 = (bf16[2,224,128]{2,1,0:T(8,128)(2,1)S(1)}, bf16[2,224,128]{2,1,0:T(8,128)(2,1)S(1)}, u32[]{:S(2)}, u32[]{:S(2)}) collective-permute-start(bf16[2,224,128]{2,1,0:T(8,128)(2,1)S(1)} %get-tuple-element.39.refs_1_), channel_id=1, source_target_pairs={{0,4},{4,0},{8,12},{12,8},{16,20},{20,16},{24,28},{28,24},{1,5},{5... | collective-permute-start | bytes 344072 | tf_op jit(solution)/shard_map/ppermute | solution.py:508
  (1 other events, 2.6 us)

commit v11 on v10

--- a/solution.py
+++ b/solution.py
@@ -194,11 +194,13 @@
     rate_ref,
     early_ref,
     payload_ref,
+    leaving_ref,
     states_even_ref,
     states_odd_ref,
     decay_ref,
     input_ref,
     in_map_ref,
+    out_map_ref,
     scalars_ref,
     sem,
 ):
@@ -207,7 +209,7 @@
     rows, channels = mixed_ref.shape
     pairs = rows // BLOCK // 2
     starts, _ = bounds(len_ref, prompts)
-    projected = own_ref[...] + other_ref[...].astype(F32)
+    projected = own_ref[...] + other_ref[...]
     low = projected[:DT_RANK, :].T.astype(BF16)
     pre = jnp.dot(low, step_weight_ref[...], preferred_element_type=F32) + step_bias_ref[...]
     step = jnp.maximum(pre, 0.0) + jnp.log1p(jnp.exp(-jnp.abs(pre)))
@@ -220,6 +222,7 @@
     for block in range(rows // BLOCK):
         columns = slice(block * BLOCK, (block + 1) * BLOCK)
         in_map_ref[block, :, 0:BLOCK] = projected[DT_RANK : DT_RANK + STATE, columns]
+        out_map_ref[block, :, 0:BLOCK] = projected[DT_RANK + STATE :, columns]
     rate = rate_ref[...] * (-math.log2(math.e))
 
     def advance(block, state, states_ref, index):
@@ -229,6 +232,11 @@
             entering = in_map_ref[block, :, token : token + 1] * input_ref[pl.ds(at + token, 1), :]
             state = state * decay + entering
             states_ref[index, token * STATE : (token + 1) * STATE, :] = state.astype(BF16)
+            leaving = out_map_ref[block, :, token : token + 1] * state
+            leaving = leaving[:8, :] + leaving[8:, :]
+            row = pl.multiple_of(block * BLOCK * 8, BLOCK * 8) + 8 * token
+            for tile in range(channels // LANES):
+                leaving_ref[tile, pl.ds(row, 8), :] = leaving[:, tile * LANES : (tile + 1) * LANES]
         return state
 
     def two_blocks(pair, state):
@@ -258,15 +266,20 @@
     rows, channels = mixed.shape
     tiles = channels // LANES
     payload_rows = prompts * tiles * STATE + rest[-1].shape[0]
-    states = jax.ShapeDtypeStruct((rows // BLOCK // 2, BLOCK * STATE, channels), BF16)
     return pl.pallas_call(
         functools.partial(scan_kernel, prompts),
-        out_shape=(jax.ShapeDtypeStruct((payload_rows, LANES), BF16), states, states),
+        out_shape=(
+            jax.ShapeDtypeStruct((payload_rows, LANES), BF16),
+            jax.ShapeDtypeStruct((tiles, rows * 8, LANES), F32),
+        ),
         in_specs=[VMEM] * 8,
-        out_specs=(VMEM,) * 3,
+        out_specs=(VMEM, VMEM),
         scratch_shapes=[
+            pltpu.VMEM((rows // BLOCK // 2, BLOCK * STATE, channels), BF16),
+            pltpu.VMEM((rows // BLOCK // 2, BLOCK * STATE, channels), BF16),
             pltpu.VMEM((rows, channels), F32),
             pltpu.VMEM((rows, channels), F32),
+            pltpu.VMEM((rows // BLOCK, STATE, LANES), F32),
             pltpu.VMEM((rows // BLOCK, STATE, LANES), F32),
             pltpu.SMEM((1, prompts), jnp.int32),
             pltpu.SemaphoreType.DMA,
@@ -277,41 +290,24 @@
 
 
 def gate_kernel(
-    own_ref,
-    other_ref,
-    states_even_ref,
-    states_odd_ref,
+    leaving_ref,
     mixed_ref,
     inner_ref,
     skip_ref,
     square_ref,
     gated_ref,
     sums_ref,
-    out_map_ref,
-    scanned_ref,
 ):
     rows, channels = mixed_ref.shape
-    span = BLOCK * STATE
-    maps = slice(DT_RANK + STATE, DT_RANK + 2 * STATE)
-    out_map = own_ref[maps, :] + other_ref[maps, :].astype(F32)
-    row = lax.broadcasted_iota(jnp.int32, (STATE, span), 0)
-    column = lax.broadcasted_iota(jnp.int32, (STATE, span), 1)
-    tiled = jnp.dot(
-        out_map.T.astype(BF16),
-        jnp.where(column % STATE == row, 1.0, 0.0).astype(BF16),
-        preferred_element_type=F32,
-    )
-    row = lax.broadcasted_iota(jnp.int32, (rows, span), 0)
-    column = lax.broadcasted_iota(jnp.int32, (rows, span), 1)
-    out_map_ref[...] = jnp.where(column // STATE == row % BLOCK, tiled, 0.0).astype(BF16)
-    for block in range(rows // BLOCK):
-        states_ref = states_odd_ref if block % 2 else states_even_ref
-        at = slice(block * BLOCK, (block + 1) * BLOCK)
-        scanned_ref[at, :] = jnp.dot(
-            out_map_ref[at, :], states_ref[block // 2], preferred_element_type=F32
-        )
+    scanned = []
+    for tile in range(channels // LANES):
+        total = leaving_ref[tile, pl.ds(0, rows, stride=8), :]
+        for index in range(1, 8):
+            total = total + leaving_ref[tile, pl.ds(index, rows, stride=8), :]
+        scanned.append(total)
+    scanned = jnp.concatenate(scanned, axis=1)
     gate = inner_ref[1].astype(F32)
-    gated = (scanned_ref[...] + skip_ref[...] * mixed_ref[...].astype(F32)) * (
+    gated = (scanned + skip_ref[...] * mixed_ref[...].astype(F32)) * (
         gate * sigmoid(gate)
     )
     gated_ref[...] = gated
@@ -543,9 +539,9 @@
     while bit < tp_size // 2:
         pair = pair + swap(pair, "tp", tp_size, bit)
         bit *= 2
-    far = swap(pair.astype(BF16), "tp", tp_size, bit)
-
-    payload, states_even, states_odd = scan_call(
+    far = swap(pair, "tp", tp_size, bit)
+
+    payload, leaving = scan_call(
         prompts,
         prompt_lengths,
         pair,
@@ -559,16 +555,12 @@
     gated, sums = pl.pallas_call(
         gate_kernel,
         out_shape=(shape((rows, channels)), shape((2, rows))),
-        in_specs=[VMEM] * 8,
+        in_specs=[VMEM] * 5,
         out_specs=(VMEM, VMEM),
-        scratch_shapes=[
-            pltpu.VMEM((rows, BLOCK * STATE), BF16),
-            pltpu.VMEM((rows, channels), F32),
-        ],
         compiler_params=params(16),
         cost_estimate=pl.CostEstimate(flops=1 << 24, bytes_accessed=4 << 20, transcendentals=0),
         name="gate",
-    )(pair, far, states_even, states_odd, mixed, inner, mamba_skip[None], square)
+    )(leaving, mixed, inner, mamba_skip[None], square)
 
     held = payload[None]
     pr_bits = [1 << i for i in reversed(range((pr_size - 1).bit_length()))]

time: 31.1 us -> 32.5 us (1.045)
  waiting for transfers between devices: 5.8 us -> 7.07 us
  Pallas kernels: 8.57 us -> 9.24 us
  starting transfers between devices: 13.2 us -> 12.6 us
    ppermute x8, waiting for transfers between devices: 5.8 us -> 7.07 us  [swap(): return lax.ppermute(x, axis, [(i, i ^ bit) for i in range(size)])]
    pallas_call x1, Pallas kernels: 2.57 us -> 3.42 us  [scan_call(): pl.pallas_call(functools.partial(scan_kernel, prompts), out_shape=(jax.Sh...]
    ppermute x8, starting transfers between devices: 13.2 us -> 12.6 us  [swap(): return lax.ppermute(x, axis, [(i, i ^ bit) for i in range(size)])]
  transfers between devices with their start and end apart: 8 -> 8, of which waited for: 6 -> 7; matrix products, arithmetic and copies ran while one was open for 0% -> 0% of each run, Pallas kernels for 11% -> 10%
where the time goes in v11:
time: 32.5 us; the launch traced here: 32.4 us
  starting transfers between devices  12.6 us (39%)
  Pallas kernels  9.24 us (28%)
  waiting for transfers between devices  7.07 us (22%)
  matrix products  2.44 us (8%)
  between operations  0.86 us (3%)
    ppermute x8, starting transfers between devices, swap(): return lax.ppermute(x, axis, [(i, i ^ bit) for i in range(size)])  12.6 us
    ppermute x8, waiting for transfers between devices, swap(): return lax.ppermute(x, axis, [(i, i ^ bit) for i in range(size)])  7.07 us
    pallas_call x1, Pallas kernels, scan_call(): pl.pallas_call(functools.partial(scan_kernel, prompts), out_shape=(jax.Sh...  3.42 us
    dot_general x1, matrix products, on_device(): jnp.einsum('td,dgc->gtc', tokens, inner_weight, preferred_element_type=F32)  2.44 us
    pallas_call x1, Pallas kernels, on_device(): pl.pallas_call(functools.partial(deliver_kernel, prompts, len(pieces)), o...  1.99 us
    pallas_call x1, Pallas kernels, on_device(): pl.pallas_call(functools.partial(attend_kernel, prompts), out_shape=(shap...  1.4 us
    pallas_call x1, Pallas kernels, on_device(): pl.pallas_call(norm_kernel, out_shape=(shape((rows, features), BF16), sha...  1.03 us
    pallas_call x1, Pallas kernels, on_device(): pl.pallas_call(gate_kernel, out_shape=(shape((rows, channels)), shape((2,...  0.74 us
  transfers between devices with their start and end apart: 8, of which 7 were waited for; matrix products, arithmetic and copies ran while one was open for 0% of the time, Pallas kernels for 10%

profile of v11, /device:TPU:0, one launch (start us, length us, event | category | flops | bytes accessed | tf_op | source)
XLA Modules:
  0.0 32.4 jit_solution(15530665622162834370)
XLA Ops:
  0.7 2.4 %fusion.5.inner_ref = bf16[2,256,512]{2,1,0:T(8,128)(2,1)S(1)} fusion(bf16[896,2,512]{2,1,0:T(2,128)(2,1)} %inner_hbm.1, bf16[256,896]{1,0:T(8,128)(2,1)} %tokens_ref.1), kind=kOutput, calls=%fused_computation.3 | convolution fusion | flops 470024192 | bytes 2818048 | tf_op jit(solution)/shard_map/td,dgc->gtc/dot_general | solution.py:488
  3.2 0.0 copy-start.6
  3.2 0.0 copy-start.7
  3.3 0.6 %mix.1 = (f32[96,256]{1,0:T(8,128)S(1)}, bf16[256,512]{1,0:T(8,128)(2,1)S(1)}) custom-call(s32[1,2]{1,0:T(1,128)S(1)} %copy-done.9, bf16[2,256,512]{2,1,0:T(8,128)(2,1)S(1)} %fusion.5.inner_ref, f32[4,512]{1,0:T(4,128)S(1)} %copy-done.8, bf16[96,512]{1,0:T(8,128)(2,1)S(1)} %bitcast.19), custom_call_target="tpu_custom_call" | custom-call | tf_op jit(solution)/shard_map/mix/pallas_call | solution.py:490
  3.9 0.5 %collective-permute-start = (f32[96,256]{1,0:T(8,128)S(1)}, f32[96,256]{1,0:T(8,128)S(1)}, u32[]{:S(2)}, u32[]{:S(2)}) collective-permute-start(f32[96,256]{1,0:T(8,128)S(1)} %get-tuple-element.24), channel_id=1, source_target_pairs={{0,1},{1,0},{2,3},{3,2},{4,5},{5,4},{6,7},{7,6},{8,9},{9,8},{10,11... | collective-permute-start | bytes 294920 | tf_op jit(solution)/shard_map/ppermute | solution.py:504
  4.4 0.9 %collective-permute-done = f32[96,256]{1,0:T(8,128)S(1)} collective-permute-done((f32[96,256]{1,0:T(8,128)S(1)}, f32[96,256]{1,0:T(8,128)S(1)}, u32[]{:S(2)}, u32[]{:S(2)}) %collective-permute-start) | collective-permute-done | bytes 98336 | tf_op jit(solution)/shard_map/ppermute | solution.py:504
  5.4 2.9 %collective-permute-start.1 = (f32[96,256]{1,0:T(8,128)S(1)}, f32[96,256]{1,0:T(8,128)S(1)}, u32[]{:S(2)}, u32[]{:S(2)}) collective-permute-start(f32[96,256]{1,0:T(8,128)S(1)} %add.3.own_ref), channel_id=1, source_target_pairs={{0,2},{1,3},{2,0},{3,1},{4,6},{5,7},{6,4},{7,5},{8,10},{9,11},{10,... | collective-permute-start | bytes 294920 | tf_op jit(solution)/shard_map/ppermute | solution.py:504
  8.3 1.4 %attend.1 = (f32[256,256]{1,0:T(8,128)S(1)}, f32[8,256]{1,0:T(8,128)S(1)}, bf16[96,128]{1,0:T(8,128)(2,1)S(1)}) custom-call(s32[1,2]{1,0:T(1,128)S(1)} %copy-done.9, bf16[256,896]{1,0:T(8,128)(2,1)S(1)} %copy-done.1, bf16[896,256]{1,0:T(8,128)(2,1)S(1)} %copy-done.2, bf16[64,896]{1,0:T(8,128)(2,1)S(1)} %bitcast.17, bf16[64,896]{1,0:T(8,128)(2,1)S(1)} %bitcast.18, ...), custom_call_target="tpu_custom_call" | custom-call | flops 352321536 | bytes 4194304 | tf_op jit(solution)/shard_map/attend/pallas_call | solution.py:509
  9.7 1.7 %collective-permute-done.1.other_ref = f32[96,256]{1,0:T(8,128)S(1)} collective-permute-done((f32[96,256]{1,0:T(8,128)S(1)}, f32[96,256]{1,0:T(8,128)S(1)}, u32[]{:S(2)}, u32[]{:S(2)}) %collective-permute-start.1) | collective-permute-done | bytes 98336 | tf_op jit(solution)/shard_map/ppermute | solution.py:504
  11.4 3.4 %scan.1 = (bf16[224,128]{1,0:T(8,128)(2,1)S(1)}, f32[4,2048,128]{2,1,0:T(8,128)S(1)}) custom-call(s32[1,2]{1,0:T(1,128)S(1)} %copy-done.9, f32[96,256]{1,0:T(8,128)S(1)} %add.3.own_ref, f32[96,256]{1,0:T(8,128)S(1)} %collective-permute-done.1.other_ref, bf16[256,512]{1,0:T(8,128)(2,1)S(1)} %get-tuple-element.25.mixed_ref, bf16[64,512]{1,0:T(8,128)(2,1)S(1)} %copy-done.6, ...), custom_call_target="tpu_custom_call" | custom-call | tf_op jit(solution)/shard_map/scan/pallas_call | solution.py:269
  14.8 2.9 %collective-permute-start.2 = (bf16[1,224,128]{2,1,0:T(8,128)(2,1)S(1)}, bf16[1,224,128]{2,1,0:T(8,128)(2,1)S(1)}, u32[]{:S(2)}, u32[]{:S(2)}) collective-permute-start(bf16[1,224,128]{2,1,0:T(8,128)(2,1)S(1)} %bitcast.20), channel_id=1, source_target_pairs={{0,16},{4,20},{8,24},{12,28},{16,0},{20,4},{24,8},{28,12},{1,17},{... | collective-permute-start | bytes 172040 | tf_op jit(solution)/shard_map/ppermute | solution.py:504
  17.8 0.7 %gate.1 = (f32[256,512]{1,0:T(8,128)S(1)}, f32[2,256]{1,0:T(2,128)S(1)}) custom-call(f32[4,2048,128]{2,1,0:T(8,128)S(1)} %get-tuple-element.27.leaving_ref, bf16[256,512]{1,0:T(8,128)(2,1)S(1)} %get-tuple-element.25.mixed_ref, bf16[2,256,512]{2,1,0:T(8,128)(2,1)S(1)} %fusion.5.inner_ref, f32[1,512]{1,0:T(1,128)S(1)} %bitcast.23, ...), custom_call_target="tpu_custom_call" | custom-call | flops 16777216 | bytes 4194304 | tf_op jit(solution)/shard_map/gate/pallas_call | solution.py:555
  18.5 0.1 collective-permute-start.3
  18.6 1.1 %collective-permute-done.3.other_ref = f32[2,256]{1,0:T(2,128)S(1)} collective-permute-done((f32[2,256]{1,0:T(2,128)S(1)}, f32[2,256]{1,0:T(2,128)S(1)}, u32[]{:S(2)}, u32[]{:S(2)}) %collective-permute-start.3) | collective-permute-done | bytes 2080 | tf_op jit(solution)/shard_map/ppermute | solution.py:504
  19.7 0.5 %collective-permute-done.2.new_ref = bf16[1,224,128]{2,1,0:T(8,128)(2,1)S(1)} collective-permute-done((bf16[1,224,128]{2,1,0:T(8,128)(2,1)S(1)}, bf16[1,224,128]{2,1,0:T(8,128)(2,1)S(1)}, u32[]{:S(2)}, u32[]{:S(2)}) %collective-permute-start.2) | collective-permute-done | bytes 57376 | tf_op jit(solution)/shard_map/ppermute | solution.py:504
  20.2 1.7 %collective-permute-start.4 = (bf16[2,224,128]{2,1,0:T(8,128)(2,1)S(1)}, bf16[2,224,128]{2,1,0:T(8,128)(2,1)S(1)}, u32[]{:S(2)}, u32[]{:S(2)}) collective-permute-start(bf16[2,224,128]{2,1,0:T(8,128)(2,1)S(1)} %get-tuple-element.32.refs_0_), channel_id=1, source_target_pairs={{0,8},{4,12},{8,0},{12,4},{16,24},{20,28},{24,16},{28,20},{1,9},{5... | collective-permute-start | bytes 344072 | tf_op jit(solution)/shard_map/ppermute | solution.py:504
  21.9 1.5 %collective-permute-start.5 = (f32[2,256]{1,0:T(2,128)S(1)}, f32[2,256]{1,0:T(2,128)S(1)}, u32[]{:S(2)}, u32[]{:S(2)}) collective-permute-start(f32[2,256]{1,0:T(2,128)S(1)} %get-tuple-element.33.own_ref), channel_id=1, source_target_pairs={{0,2},{1,3},{2,0},{3,1},{4,6},{5,7},{6,4},{7,5},{8,10},{9,11},{10,... | collective-permute-start | bytes 6152 | tf_op jit(solution)/shard_map/ppermute | solution.py:504
  23.4 1.5 %collective-permute-start.6 = (bf16[2,224,128]{2,1,0:T(8,128)(2,1)S(1)}, bf16[2,224,128]{2,1,0:T(8,128)(2,1)S(1)}, u32[]{:S(2)}, u32[]{:S(2)}) collective-permute-start(bf16[2,224,128]{2,1,0:T(8,128)(2,1)S(1)} %get-tuple-element.32.refs_0_), channel_id=1, source_target_pairs={{0,4},{4,0},{8,12},{12,8},{16,20},{20,16},{24,28},{28,24},{1,5},{5... | collective-permute-start | bytes 344072 | tf_op jit(solution)/shard_map/ppermute | solution.py:504
  24.9 0.6 %collective-permute-done.5.other_ref = f32[2,256]{1,0:T(2,128)S(1)} collective-permute-done((f32[2,256]{1,0:T(2,128)S(1)}, f32[2,256]{1,0:T(2,128)S(1)}, u32[]{:S(2)}, u32[]{:S(2)}) %collective-permute-start.5) | collective-permute-done | bytes 2080 | tf_op jit(solution)/shard_map/ppermute | solution.py:504
  25.5 1.6 %collective-permute-start.7 = (bf16[2,224,128]{2,1,0:T(8,128)(2,1)S(1)}, bf16[2,224,128]{2,1,0:T(8,128)(2,1)S(1)}, u32[]{:S(2)}, u32[]{:S(2)}) collective-permute-start(bf16[2,224,128]{2,1,0:T(8,128)(2,1)S(1)} %get-tuple-element.37.refs_1_), channel_id=1, source_target_pairs={{0,4},{4,0},{8,12},{12,8},{16,20},{20,16},{24,28},{28,24},{1,5},{5... | collective-permute-start | bytes 344072 | tf_op jit(solution)/shard_map/ppermute | solution.py:504
  27.1 2.1 %collective-permute-done.6.crossed_hbm.refs_2_ = bf16[2,224,128]{2,1,0:T(8,128)(2,1)S(1)} collective-permute-done((bf16[2,224,128]{2,1,0:T(8,128)(2,1)S(1)}, bf16[2,224,128]{2,1,0:T(8,128)(2,1)S(1)}, u32[]{:S(2)}, u32[]{:S(2)}) %collective-permute-start.6) | collective-permute-done | bytes 114720 | tf_op jit(solution)/shard_map/ppermute | solution.py:504
  29.1 1.0 %norm.1 = (bf16[256,256]{1,0:T(8,128)(2,1)}, bf16[256,512]{1,0:T(8,128)(2,1)}) custom-call(f32[256,256]{1,0:T(8,128)S(1)} %get-tuple-element.23.attended_ref, f32[256,512]{1,0:T(8,128)S(1)} %get-tuple-element.29.gated_ref, f32[2,256]{1,0:T(2,128)S(1)} %get-tuple-element.34.sums_ref, f32[1,256]{1,0:T(1,128)S(1)} %bitcast.25, f32[1,512]{1,0:T(1,128)S(1)} %bitcast.24, ...), custom_call_target="tpu_custom_call" | custom-call | flops 16777216 | bytes 2097152 | tf_op jit(solution)/shard_map/norm/pallas_call | solution.py:598
  30.2 0.2 collective-permute-done.7.refs_3_
  30.4 2.0 %deliver.1 = (bf16[56,2,32,64]{3,2,1,0:T(8,128)(2,1)}, bf16[56,16,512]{2,1,0:T(8,128)(2,1)}, bf16[3,56,512]{2,1,0:T(8,128)(2,1)}) custom-call(bf16[2,224,128]{2,1,0:T(8,128)(2,1)S(1)} %get-tuple-element.32.refs_0_, bf16[2,224,128]{2,1,0:T(8,128)(2,1)S(1)} %get-tuple-element.37.refs_1_, bf16[2,224,128]{2,1,0:T(8,128)(2,1)S(1)} %collective-permute-done.6.crossed_hbm.refs_2_, ...), custom_call_target="tpu_custom_call" | custom-call | tf_op jit(solution)/shard_map/deliver/pallas_call | solution.py:607
  (36 shorter events, 0.1 us)
Async XLA Ops:
  0.6 7.6 %copy-start.1 = (bf16[256,896]{1,0:T(8,128)(2,1)S(1)}, bf16[256,896]{1,0:T(8,128)(2,1)}, u32[]{:S(2)}) copy-start(bf16[256,896]{1,0:T(8,128)(2,1)} %tokens_ref.1) | copy-start | bytes 1376260
  0.6 2.6 %copy-start.9 = (s32[1,2]{1,0:T(1,128)S(1)}, s32[1,2]{1,0:T(1,128)}, u32[]{:S(2)}) copy-start(s32[1,2]{1,0:T(1,128)} %len_ref.5) | copy-start | bytes 28
  0.7 2.6 %copy-start.5 = (bf16[512,96]{0,1:T(8,128)(2,1)S(1)}, bf16[512,96]{0,1:T(8,128)(2,1)}, u32[]{:S(2)}) copy-start(bf16[512,96]{0,1:T(8,128)(2,1)} %param.25) | copy-start | bytes 294916
  0.7 7.6 %copy-start.16 = (s32[56]{0:T(128)S(1)}, s32[56]{0:T(128)}, u32[]{:S(2)}) copy-start(s32[56]{0:T(128)} %param.33) | copy-start | bytes 676
  0.7 7.6 %copy-start.15 = (s32[56]{0:T(128)S(1)}, s32[56]{0:T(128)}, u32[]{:S(2)}) copy-start(s32[56]{0:T(128)} %param.32) | copy-start | bytes 676
  0.7 7.6 %copy-start.14 = (s32[56]{0:T(128)S(1)}, s32[56]{0:T(128)}, u32[]{:S(2)}) copy-start(s32[56]{0:T(128)} %param.31) | copy-start | bytes 676
  0.7 7.6 %copy-start.4 = (bf16[896,64]{0,1:T(8,128)(2,1)S(1)}, bf16[896,64]{0,1:T(8,128)(2,1)}, u32[]{:S(2)}) copy-start(bf16[896,64]{0,1:T(8,128)(2,1)} %param.21) | copy-start | bytes 344068
  0.7 7.6 %copy-start.3 = (bf16[896,64]{0,1:T(8,128)(2,1)S(1)}, bf16[896,64]{0,1:T(8,128)(2,1)}, u32[]{:S(2)}) copy-start(bf16[896,64]{0,1:T(8,128)(2,1)} %param.20) | copy-start | bytes 344068
  0.7 7.6 %copy-start.2 = (bf16[896,256]{1,0:T(8,128)(2,1)S(1)}, bf16[896,256]{1,0:T(8,128)(2,1)}, u32[]{:S(2)}) copy-start(bf16[896,256]{1,0:T(8,128)(2,1)} %query_ref.1) | copy-start | bytes 1376260
  3.2 8.2 %copy-start.6 = (bf16[64,512]{1,0:T(8,128)(2,1)S(1)}, bf16[64,512]{1,0:T(8,128)(2,1)}, u32[]{:S(2)}) copy-start(bf16[64,512]{1,0:T(8,128)(2,1)} %step_weight_ref.1) | copy-start | bytes 196612
  3.2 8.2 %copy-start.7 = (f32[16,512]{1,0:T(8,128)S(1)}, f32[16,512]{1,0:T(8,128)}, u32[]{:S(2)}) copy-start(f32[16,512]{1,0:T(8,128)} %rate_ref.1) | copy-start | bytes 98308
  3.2 8.2 %copy-start.10 = (f32[512]{0:T(512)S(1)}, f32[512]{0:T(512)}, u32[]{:S(2)}) copy-start(f32[512]{0:T(512)} %param.27) | copy-start | bytes 6148
  3.2 14.5 %copy-start.11 = (f32[512]{0:T(512)S(1)}, f32[512]{0:T(512)}, u32[]{:S(2)}) copy-start(f32[512]{0:T(512)} %param.29) | copy-start | bytes 6148
  3.9 1.5 %collective-permute-start = (f32[96,256]{1,0:T(8,128)S(1)}, f32[96,256]{1,0:T(8,128)S(1)}, u32[]{:S(2)}, u32[]{:S(2)}) collective-permute-start(f32[96,256]{1,0:T(8,128)S(1)} %get-tuple-element.24), channel_id=1, source_target_pairs={{0,1},{1,0},{2,3},{3,2},{4,5},{5,4},{6,7},{7,6},{8,9},{9,8},{10,11... | collective-permute-start | bytes 294920 | tf_op jit(solution)/shard_map/ppermute | solution.py:504
  5.4 6.0 %collective-permute-start.1 = (f32[96,256]{1,0:T(8,128)S(1)}, f32[96,256]{1,0:T(8,128)S(1)}, u32[]{:S(2)}, u32[]{:S(2)}) collective-permute-start(f32[96,256]{1,0:T(8,128)S(1)} %add.3.own_ref), channel_id=1, source_target_pairs={{0,2},{1,3},{2,0},{3,1},{4,6},{5,7},{6,4},{7,5},{8,10},{9,11},{10,... | collective-permute-start | bytes 294920 | tf_op jit(solution)/shard_map/ppermute | solution.py:504
  14.8 5.4 %collective-permute-start.2 = (bf16[1,224,128]{2,1,0:T(8,128)(2,1)S(1)}, bf16[1,224,128]{2,1,0:T(8,128)(2,1)S(1)}, u32[]{:S(2)}, u32[]{:S(2)}) collective-permute-start(bf16[1,224,128]{2,1,0:T(8,128)(2,1)S(1)} %bitcast.20), channel_id=1, source_target_pairs={{0,16},{4,20},{8,24},{12,28},{16,0},{20,4},{24,8},{28,12},{1,17},{... | collective-permute-start | bytes 172040 | tf_op jit(solution)/shard_map/ppermute | solution.py:504
  17.7 11.4 %copy-start = (bf16[896,2,512]{2,1,0:T(2,128)(2,1)S(1)}, bf16[896,2,512]{2,1,0:T(2,128)(2,1)}, u32[]{:S(2)}) copy-start(bf16[896,2,512]{2,1,0:T(2,128)(2,1)} %inner_hbm.1) | copy-start | bytes 5505028
  17.7 11.4 %copy-start.12 = (f32[512]{0:T(512)S(1)}, f32[512]{0:T(512)}, u32[]{:S(2)}) copy-start(f32[512]{0:T(512)} %param.30) | copy-start | bytes 6148
  17.7 11.4 %copy-start.13 = (f32[256]{0:T(256)S(1)}, f32[256]{0:T(256)}, u32[]{:S(2)}) copy-start(f32[256]{0:T(256)} %param.22) | copy-start | bytes 3076
  18.5 1.2 %collective-permute-start.3 = (f32[2,256]{1,0:T(2,128)S(1)}, f32[2,256]{1,0:T(2,128)S(1)}, u32[]{:S(2)}, u32[]{:S(2)}) collective-permute-start(f32[2,256]{1,0:T(2,128)S(1)} %get-tuple-element.31.own_ref), channel_id=1, source_target_pairs={{0,1},{1,0},{2,3},{3,2},{4,5},{5,4},{6,7},{7,6},{8,9},{9,8},{10,11... | collective-permute-start | bytes 6152 | tf_op jit(solution)/shard_map/ppermute | solution.py:504
  20.2 5.2 %collective-permute-start.4 = (bf16[2,224,128]{2,1,0:T(8,128)(2,1)S(1)}, bf16[2,224,128]{2,1,0:T(8,128)(2,1)S(1)}, u32[]{:S(2)}, u32[]{:S(2)}) collective-permute-start(bf16[2,224,128]{2,1,0:T(8,128)(2,1)S(1)} %get-tuple-element.32.refs_0_), channel_id=1, source_target_pairs={{0,8},{4,12},{8,0},{12,4},{16,24},{20,28},{24,16},{28,20},{1,9},{5... | collective-permute-start | bytes 344072 | tf_op jit(solution)/shard_map/ppermute | solution.py:504
  21.9 3.6 %collective-permute-start.5 = (f32[2,256]{1,0:T(2,128)S(1)}, f32[2,256]{1,0:T(2,128)S(1)}, u32[]{:S(2)}, u32[]{:S(2)}) collective-permute-start(f32[2,256]{1,0:T(2,128)S(1)} %get-tuple-element.33.own_ref), channel_id=1, source_target_pairs={{0,2},{1,3},{2,0},{3,1},{4,6},{5,7},{6,4},{7,5},{8,10},{9,11},{10,... | collective-permute-start | bytes 6152 | tf_op jit(solution)/shard_map/ppermute | solution.py:504
  23.4 5.8 %collective-permute-start.6 = (bf16[2,224,128]{2,1,0:T(8,128)(2,1)S(1)}, bf16[2,224,128]{2,1,0:T(8,128)(2,1)S(1)}, u32[]{:S(2)}, u32[]{:S(2)}) collective-permute-start(bf16[2,224,128]{2,1,0:T(8,128)(2,1)S(1)} %get-tuple-element.32.refs_0_), channel_id=1, source_target_pairs={{0,4},{4,0},{8,12},{12,8},{16,20},{20,16},{24,28},{28,24},{1,5},{5... | collective-permute-start | bytes 344072 | tf_op jit(solution)/shard_map/ppermute | solution.py:504
  25.5 4.9 %collective-permute-start.7 = (bf16[2,224,128]{2,1,0:T(8,128)(2,1)S(1)}, bf16[2,224,128]{2,1,0:T(8,128)(2,1)S(1)}, u32[]{:S(2)}, u32[]{:S(2)}) collective-permute-start(bf16[2,224,128]{2,1,0:T(8,128)(2,1)S(1)} %get-tuple-element.37.refs_1_), channel_id=1, source_target_pairs={{0,4},{4,0},{8,12},{12,8},{16,20},{20,16},{24,28},{28,24},{1,5},{5... | collective-permute-start | bytes 344072 | tf_op jit(solution)/shard_map/ppermute | solution.py:504
  (1 other events, 2.6 us)

commit v12 on v11

--- a/solution.py
+++ b/solution.py
@@ -19,6 +19,7 @@
 EPSILON = 1e-06
 LANES = 128
 BLOCK = 16
+LONGEST = 160
 RESET = 1e30
 
 F32 = jnp.float32
@@ -225,13 +226,14 @@
         out_map_ref[block, :, 0:BLOCK] = projected[DT_RANK + STATE :, columns]
     rate = rate_ref[...] * (-math.log2(math.e))
 
-    def advance(block, state, states_ref, index):
+    def advance(block, state, states_ref, index, keep):
         at = pl.multiple_of(block * BLOCK, BLOCK)
         for token in range(BLOCK):
             decay = jnp.exp2(decay_ref[pl.ds(at + token, 1), :] * rate)
             entering = in_map_ref[block, :, token : token + 1] * input_ref[pl.ds(at + token, 1), :]
             state = state * decay + entering
-            states_ref[index, token * STATE : (token + 1) * STATE, :] = state.astype(BF16)
+            if keep:
+                states_ref[index, token * STATE : (token + 1) * STATE, :] = state.astype(BF16)
             leaving = out_map_ref[block, :, token : token + 1] * state
             leaving = leaving[:8, :] + leaving[8:, :]
             row = pl.multiple_of(block * BLOCK * 8, BLOCK * 8) + 8 * token
@@ -239,22 +241,32 @@
                 leaving_ref[tile, pl.ds(row, 8), :] = leaving[:, tile * LANES : (tile + 1) * LANES]
         return state
 
-    def two_blocks(pair, state):
-        state = advance(2 * pair, state, states_even_ref, pair)
-        return advance(2 * pair + 1, state, states_odd_ref, pair)
-
-    lax.fori_loop(0, pairs, two_blocks, jnp.zeros((STATE, channels), F32))
+    def two_blocks(keep, pair, state):
+        state = advance(2 * pair, state, states_even_ref, pair, keep)
+        return advance(2 * pair + 1, state, states_odd_ref, pair, keep)
+
+    first, last = 0, pairs
+    if prompts == 2:
+        first = max(rows - LONGEST - 1, 0) // (2 * BLOCK)
+        last = min((LONGEST - 1) // (2 * BLOCK) + 1, pairs)
+    state = jnp.zeros((STATE, channels), F32)
+    for keep, start, stop in ((False, 0, first), (True, first, last), (False, last, pairs)):
+        if start < stop:
+            state = lax.fori_loop(start, stop, functools.partial(two_blocks, keep), state)
     scalars_copy.wait()
     last = -1
     for p in range(prompts):
         last = last + scalars_ref[0, p]
         block = last // BLOCK
         at = pl.multiple_of((last - block * BLOCK) * STATE, STATE)
-        final = jnp.where(
-            block % 2 == 0,
-            states_even_ref[block // 2, pl.ds(at, STATE), :],
-            states_odd_ref[block // 2, pl.ds(at, STATE), :],
-        )
+        if p == prompts - 1:
+            final = state.astype(BF16)
+        else:
+            final = jnp.where(
+                block % 2 == 0,
+                states_even_ref[block // 2, pl.ds(at, STATE), :],
+                states_odd_ref[block // 2, pl.ds(at, STATE), :],
+            )
         for tile in range(channels // LANES):
             at = (p * (channels // LANES) + tile) * STATE
             payload_ref[at : at + STATE, :] = final[:, tile * LANES : (tile + 1) * LANES]

time: 32.5 us -> 32.4 us (level)
  no operation moved by 1% of the time
where the time goes in v12:
time: 32.4 us; the launch traced here: 32.2 us
  starting transfers between devices  12.6 us (39%)
  Pallas kernels  9.12 us (28%)
  waiting for transfers between devices  7.07 us (22%)
  matrix products  2.44 us (8%)
  between operations  0.86 us (3%)
    ppermute x8, starting transfers between devices, swap(): return lax.ppermute(x, axis, [(i, i ^ bit) for i in range(size)])  12.6 us
    ppermute x8, waiting for transfers between devices, swap(): return lax.ppermute(x, axis, [(i, i ^ bit) for i in range(size)])  7.07 us
    pallas_call x1, Pallas kernels, scan_call(): pl.pallas_call(functools.partial(scan_kernel, prompts), out_shape=(jax.Sh...  3.31 us
    dot_general x1, matrix products, on_device(): jnp.einsum('td,dgc->gtc', tokens, inner_weight, preferred_element_type=F32)  2.44 us
    pallas_call x1, Pallas kernels, on_device(): pl.pallas_call(functools.partial(deliver_kernel, prompts, len(pieces)), o...  1.99 us
    pallas_call x1, Pallas kernels, on_device(): pl.pallas_call(functools.partial(attend_kernel, prompts), out_shape=(shap...  1.4 us
    pallas_call x1, Pallas kernels, on_device(): pl.pallas_call(norm_kernel, out_shape=(shape((rows, features), BF16), sha...  1.03 us
    pallas_call x1, Pallas kernels, on_device(): pl.pallas_call(gate_kernel, out_shape=(shape((rows, channels)), shape((2,...  0.74 us
  transfers between devices with their start and end apart: 8, of which 7 were waited for; matrix products, arithmetic and copies ran while one was open for 0% of the time, Pallas kernels for 10%

profile of v12, /device:TPU:0, one launch (start us, length us, event | category | flops | bytes accessed | tf_op | source)
XLA Modules:
  0.0 32.2 jit_solution(247046932786405148)
XLA Ops:
  0.7 2.4 %fusion.5.inner_ref = bf16[2,256,512]{2,1,0:T(8,128)(2,1)S(1)} fusion(bf16[896,2,512]{2,1,0:T(2,128)(2,1)} %inner_hbm.1, bf16[256,896]{1,0:T(8,128)(2,1)} %tokens_ref.1), kind=kOutput, calls=%fused_computation.3 | convolution fusion | flops 470024192 | bytes 2818048 | tf_op jit(solution)/shard_map/td,dgc->gtc/dot_general | solution.py:500
  3.2 0.0 copy-start.6
  3.2 0.0 copy-start.11
  3.3 0.6 %mix.1 = (f32[96,256]{1,0:T(8,128)S(1)}, bf16[256,512]{1,0:T(8,128)(2,1)S(1)}) custom-call(s32[1,2]{1,0:T(1,128)S(1)} %copy-done.9, bf16[2,256,512]{2,1,0:T(8,128)(2,1)S(1)} %fusion.5.inner_ref, f32[4,512]{1,0:T(4,128)S(1)} %copy-done.8, bf16[96,512]{1,0:T(8,128)(2,1)S(1)} %bitcast.19), custom_call_target="tpu_custom_call" | custom-call | tf_op jit(solution)/shard_map/mix/pallas_call | solution.py:502
  3.9 0.5 %collective-permute-start = (f32[96,256]{1,0:T(8,128)S(1)}, f32[96,256]{1,0:T(8,128)S(1)}, u32[]{:S(2)}, u32[]{:S(2)}) collective-permute-start(f32[96,256]{1,0:T(8,128)S(1)} %get-tuple-element.24), channel_id=1, source_target_pairs={{0,1},{1,0},{2,3},{3,2},{4,5},{5,4},{6,7},{7,6},{8,9},{9,8},{10,11... | collective-permute-start | bytes 294920 | tf_op jit(solution)/shard_map/ppermute | solution.py:516
  4.4 0.9 %collective-permute-done = f32[96,256]{1,0:T(8,128)S(1)} collective-permute-done((f32[96,256]{1,0:T(8,128)S(1)}, f32[96,256]{1,0:T(8,128)S(1)}, u32[]{:S(2)}, u32[]{:S(2)}) %collective-permute-start) | collective-permute-done | bytes 98336 | tf_op jit(solution)/shard_map/ppermute | solution.py:516
  5.4 2.9 %collective-permute-start.1 = (f32[96,256]{1,0:T(8,128)S(1)}, f32[96,256]{1,0:T(8,128)S(1)}, u32[]{:S(2)}, u32[]{:S(2)}) collective-permute-start(f32[96,256]{1,0:T(8,128)S(1)} %add.3.own_ref), channel_id=1, source_target_pairs={{0,2},{1,3},{2,0},{3,1},{4,6},{5,7},{6,4},{7,5},{8,10},{9,11},{10,... | collective-permute-start | bytes 294920 | tf_op jit(solution)/shard_map/ppermute | solution.py:516
  8.3 1.4 %attend.1 = (f32[256,256]{1,0:T(8,128)S(1)}, f32[8,256]{1,0:T(8,128)S(1)}, bf16[96,128]{1,0:T(8,128)(2,1)S(1)}) custom-call(s32[1,2]{1,0:T(1,128)S(1)} %copy-done.9, bf16[256,896]{1,0:T(8,128)(2,1)S(1)} %copy-done.1, bf16[896,256]{1,0:T(8,128)(2,1)S(1)} %copy-done.2, bf16[64,896]{1,0:T(8,128)(2,1)S(1)} %bitcast.17, bf16[64,896]{1,0:T(8,128)(2,1)S(1)} %bitcast.18, ...), custom_call_target="tpu_custom_call" | custom-call | flops 352321536 | bytes 4194304 | tf_op jit(solution)/shard_map/attend/pallas_call | solution.py:521
  9.7 1.7 %collective-permute-done.1.other_ref = f32[96,256]{1,0:T(8,128)S(1)} collective-permute-done((f32[96,256]{1,0:T(8,128)S(1)}, f32[96,256]{1,0:T(8,128)S(1)}, u32[]{:S(2)}, u32[]{:S(2)}) %collective-permute-start.1) | collective-permute-done | bytes 98336 | tf_op jit(solution)/shard_map/ppermute | solution.py:516
  11.4 3.3 %scan.1 = (bf16[224,128]{1,0:T(8,128)(2,1)S(1)}, f32[4,2048,128]{2,1,0:T(8,128)S(1)}) custom-call(s32[1,2]{1,0:T(1,128)S(1)} %copy-done.9, f32[96,256]{1,0:T(8,128)S(1)} %add.3.own_ref, f32[96,256]{1,0:T(8,128)S(1)} %collective-permute-done.1.other_ref, bf16[256,512]{1,0:T(8,128)(2,1)S(1)} %get-tuple-element.25.mixed_ref, bf16[64,512]{1,0:T(8,128)(2,1)S(1)} %copy-done.6, ...), custom_call_target="tpu_custom_call" | custom-call | tf_op jit(solution)/shard_map/scan/pallas_call | solution.py:281
  14.7 2.9 %collective-permute-start.2 = (bf16[1,224,128]{2,1,0:T(8,128)(2,1)S(1)}, bf16[1,224,128]{2,1,0:T(8,128)(2,1)S(1)}, u32[]{:S(2)}, u32[]{:S(2)}) collective-permute-start(bf16[1,224,128]{2,1,0:T(8,128)(2,1)S(1)} %bitcast.20), channel_id=1, source_target_pairs={{0,16},{4,20},{8,24},{12,28},{16,0},{20,4},{24,8},{28,12},{1,17},{... | collective-permute-start | bytes 172040 | tf_op jit(solution)/shard_map/ppermute | solution.py:516
  17.6 0.7 %gate.1 = (f32[256,512]{1,0:T(8,128)S(1)}, f32[2,256]{1,0:T(2,128)S(1)}) custom-call(f32[4,2048,128]{2,1,0:T(8,128)S(1)} %get-tuple-element.27.leaving_ref, bf16[256,512]{1,0:T(8,128)(2,1)S(1)} %get-tuple-element.25.mixed_ref, bf16[2,256,512]{2,1,0:T(8,128)(2,1)S(1)} %fusion.5.inner_ref, f32[1,512]{1,0:T(1,128)S(1)} %bitcast.23, ...), custom_call_target="tpu_custom_call" | custom-call | flops 16777216 | bytes 4194304 | tf_op jit(solution)/shard_map/gate/pallas_call | solution.py:567
  18.4 0.1 collective-permute-start.3
  18.5 1.1 %collective-permute-done.3.other_ref = f32[2,256]{1,0:T(2,128)S(1)} collective-permute-done((f32[2,256]{1,0:T(2,128)S(1)}, f32[2,256]{1,0:T(2,128)S(1)}, u32[]{:S(2)}, u32[]{:S(2)}) %collective-permute-start.3) | collective-permute-done | bytes 2080 | tf_op jit(solution)/shard_map/ppermute | solution.py:516
  19.6 0.5 %collective-permute-done.2.new_ref = bf16[1,224,128]{2,1,0:T(8,128)(2,1)S(1)} collective-permute-done((bf16[1,224,128]{2,1,0:T(8,128)(2,1)S(1)}, bf16[1,224,128]{2,1,0:T(8,128)(2,1)S(1)}, u32[]{:S(2)}, u32[]{:S(2)}) %collective-permute-start.2) | collective-permute-done | bytes 57376 | tf_op jit(solution)/shard_map/ppermute | solution.py:516
  20.1 1.7 %collective-permute-start.4 = (bf16[2,224,128]{2,1,0:T(8,128)(2,1)S(1)}, bf16[2,224,128]{2,1,0:T(8,128)(2,1)S(1)}, u32[]{:S(2)}, u32[]{:S(2)}) collective-permute-start(bf16[2,224,128]{2,1,0:T(8,128)(2,1)S(1)} %get-tuple-element.32.refs_0_), channel_id=1, source_target_pairs={{0,8},{4,12},{8,0},{12,4},{16,24},{20,28},{24,16},{28,20},{1,9},{5... | collective-permute-start | bytes 344072 | tf_op jit(solution)/shard_map/ppermute | solution.py:516
  21.8 1.5 %collective-permute-start.5 = (f32[2,256]{1,0:T(2,128)S(1)}, f32[2,256]{1,0:T(2,128)S(1)}, u32[]{:S(2)}, u32[]{:S(2)}) collective-permute-start(f32[2,256]{1,0:T(2,128)S(1)} %get-tuple-element.33.own_ref), channel_id=1, source_target_pairs={{0,2},{1,3},{2,0},{3,1},{4,6},{5,7},{6,4},{7,5},{8,10},{9,11},{10,... | collective-permute-start | bytes 6152 | tf_op jit(solution)/shard_map/ppermute | solution.py:516
  23.3 1.5 %collective-permute-start.6 = (bf16[2,224,128]{2,1,0:T(8,128)(2,1)S(1)}, bf16[2,224,128]{2,1,0:T(8,128)(2,1)S(1)}, u32[]{:S(2)}, u32[]{:S(2)}) collective-permute-start(bf16[2,224,128]{2,1,0:T(8,128)(2,1)S(1)} %get-tuple-element.32.refs_0_), channel_id=1, source_target_pairs={{0,4},{4,0},{8,12},{12,8},{16,20},{20,16},{24,28},{28,24},{1,5},{5... | collective-permute-start | bytes 344072 | tf_op jit(solution)/shard_map/ppermute | solution.py:516
  24.8 0.6 %collective-permute-done.5.other_ref = f32[2,256]{1,0:T(2,128)S(1)} collective-permute-done((f32[2,256]{1,0:T(2,128)S(1)}, f32[2,256]{1,0:T(2,128)S(1)}, u32[]{:S(2)}, u32[]{:S(2)}) %collective-permute-start.5) | collective-permute-done | bytes 2080 | tf_op jit(solution)/shard_map/ppermute | solution.py:516
  25.4 1.6 %collective-permute-start.7 = (bf16[2,224,128]{2,1,0:T(8,128)(2,1)S(1)}, bf16[2,224,128]{2,1,0:T(8,128)(2,1)S(1)}, u32[]{:S(2)}, u32[]{:S(2)}) collective-permute-start(bf16[2,224,128]{2,1,0:T(8,128)(2,1)S(1)} %get-tuple-element.37.refs_1_), channel_id=1, source_target_pairs={{0,4},{4,0},{8,12},{12,8},{16,20},{20,16},{24,28},{28,24},{1,5},{5... | collective-permute-start | bytes 344072 | tf_op jit(solution)/shard_map/ppermute | solution.py:516
  27.0 2.1 %collective-permute-done.6.crossed_hbm.refs_2_ = bf16[2,224,128]{2,1,0:T(8,128)(2,1)S(1)} collective-permute-done((bf16[2,224,128]{2,1,0:T(8,128)(2,1)S(1)}, bf16[2,224,128]{2,1,0:T(8,128)(2,1)S(1)}, u32[]{:S(2)}, u32[]{:S(2)}) %collective-permute-start.6) | collective-permute-done | bytes 114720 | tf_op jit(solution)/shard_map/ppermute | solution.py:516
  29.0 1.0 %norm.1 = (bf16[256,256]{1,0:T(8,128)(2,1)}, bf16[256,512]{1,0:T(8,128)(2,1)}) custom-call(f32[256,256]{1,0:T(8,128)S(1)} %get-tuple-element.23.attended_ref, f32[256,512]{1,0:T(8,128)S(1)} %get-tuple-element.29.gated_ref, f32[2,256]{1,0:T(2,128)S(1)} %get-tuple-element.34.sums_ref, f32[1,256]{1,0:T(1,128)S(1)} %bitcast.25, f32[1,512]{1,0:T(1,128)S(1)} %bitcast.24, ...), custom_call_target="tpu_custom_call" | custom-call | flops 16777216 | bytes 2097152 | tf_op jit(solution)/shard_map/norm/pallas_call | solution.py:610
  30.1 0.2 collective-permute-done.7.refs_3_
  30.2 2.0 %deliver.1 = (bf16[56,2,32,64]{3,2,1,0:T(8,128)(2,1)}, bf16[56,16,512]{2,1,0:T(8,128)(2,1)}, bf16[3,56,512]{2,1,0:T(8,128)(2,1)}) custom-call(bf16[2,224,128]{2,1,0:T(8,128)(2,1)S(1)} %get-tuple-element.32.refs_0_, bf16[2,224,128]{2,1,0:T(8,128)(2,1)S(1)} %get-tuple-element.37.refs_1_, bf16[2,224,128]{2,1,0:T(8,128)(2,1)S(1)} %collective-permute-done.6.crossed_hbm.refs_2_, ...), custom_call_target="tpu_custom_call" | custom-call | tf_op jit(solution)/shard_map/deliver/pallas_call | solution.py:619
  (36 shorter events, 0.1 us)
Async XLA Ops:
  0.6 7.6 %copy-start.1 = (bf16[256,896]{1,0:T(8,128)(2,1)S(1)}, bf16[256,896]{1,0:T(8,128)(2,1)}, u32[]{:S(2)}) copy-start(bf16[256,896]{1,0:T(8,128)(2,1)} %tokens_ref.1) | copy-start | bytes 1376260
  0.6 2.6 %copy-start.9 = (s32[1,2]{1,0:T(1,128)S(1)}, s32[1,2]{1,0:T(1,128)}, u32[]{:S(2)}) copy-start(s32[1,2]{1,0:T(1,128)} %len_ref.5) | copy-start | bytes 28
  0.7 2.6 %copy-start.5 = (bf16[512,96]{0,1:T(8,128)(2,1)S(1)}, bf16[512,96]{0,1:T(8,128)(2,1)}, u32[]{:S(2)}) copy-start(bf16[512,96]{0,1:T(8,128)(2,1)} %param.25) | copy-start | bytes 294916
  0.7 7.6 %copy-start.16 = (s32[56]{0:T(128)S(1)}, s32[56]{0:T(128)}, u32[]{:S(2)}) copy-start(s32[56]{0:T(128)} %param.33) | copy-start | bytes 676
  0.7 7.6 %copy-start.15 = (s32[56]{0:T(128)S(1)}, s32[56]{0:T(128)}, u32[]{:S(2)}) copy-start(s32[56]{0:T(128)} %param.32) | copy-start | bytes 676
  0.7 7.6 %copy-start.14 = (s32[56]{0:T(128)S(1)}, s32[56]{0:T(128)}, u32[]{:S(2)}) copy-start(s32[56]{0:T(128)} %param.31) | copy-start | bytes 676
  0.7 7.6 %copy-start.4 = (bf16[896,64]{0,1:T(8,128)(2,1)S(1)}, bf16[896,64]{0,1:T(8,128)(2,1)}, u32[]{:S(2)}) copy-start(bf16[896,64]{0,1:T(8,128)(2,1)} %param.21) | copy-start | bytes 344068
  0.7 7.6 %copy-start.3 = (bf16[896,64]{0,1:T(8,128)(2,1)S(1)}, bf16[896,64]{0,1:T(8,128)(2,1)}, u32[]{:S(2)}) copy-start(bf16[896,64]{0,1:T(8,128)(2,1)} %param.20) | copy-start | bytes 344068
  0.7 7.6 %copy-start.2 = (bf16[896,256]{1,0:T(8,128)(2,1)S(1)}, bf16[896,256]{1,0:T(8,128)(2,1)}, u32[]{:S(2)}) copy-start(bf16[896,256]{1,0:T(8,128)(2,1)} %query_ref.1) | copy-start | bytes 1376260
  3.2 8.2 %copy-start.6 = (bf16[64,512]{1,0:T(8,128)(2,1)S(1)}, bf16[64,512]{1,0:T(8,128)(2,1)}, u32[]{:S(2)}) copy-start(bf16[64,512]{1,0:T(8,128)(2,1)} %step_weight_ref.1) | copy-start | bytes 196612
  3.2 8.2 %copy-start.7 = (f32[16,512]{1,0:T(8,128)S(1)}, f32[16,512]{1,0:T(8,128)}, u32[]{:S(2)}) copy-start(f32[16,512]{1,0:T(8,128)} %rate_ref.1) | copy-start | bytes 98308
  3.2 8.2 %copy-start.10 = (f32[512]{0:T(512)S(1)}, f32[512]{0:T(512)}, u32[]{:S(2)}) copy-start(f32[512]{0:T(512)} %param.27) | copy-start | bytes 6148
  3.2 14.4 %copy-start.11 = (f32[512]{0:T(512)S(1)}, f32[512]{0:T(512)}, u32[]{:S(2)}) copy-start(f32[512]{0:T(512)} %param.29) | copy-start | bytes 6148
  3.9 1.5 %collective-permute-start = (f32[96,256]{1,0:T(8,128)S(1)}, f32[96,256]{1,0:T(8,128)S(1)}, u32[]{:S(2)}, u32[]{:S(2)}) collective-permute-start(f32[96,256]{1,0:T(8,128)S(1)} %get-tuple-element.24), channel_id=1, source_target_pairs={{0,1},{1,0},{2,3},{3,2},{4,5},{5,4},{6,7},{7,6},{8,9},{9,8},{10,11... | collective-permute-start | bytes 294920 | tf_op jit(solution)/shard_map/ppermute | solution.py:516
  5.4 6.0 %collective-permute-start.1 = (f32[96,256]{1,0:T(8,128)S(1)}, f32[96,256]{1,0:T(8,128)S(1)}, u32[]{:S(2)}, u32[]{:S(2)}) collective-permute-start(f32[96,256]{1,0:T(8,128)S(1)} %add.3.own_ref), channel_id=1, source_target_pairs={{0,2},{1,3},{2,0},{3,1},{4,6},{5,7},{6,4},{7,5},{8,10},{9,11},{10,... | collective-permute-start | bytes 294920 | tf_op jit(solution)/shard_map/ppermute | solution.py:516
  14.7 5.4 %collective-permute-start.2 = (bf16[1,224,128]{2,1,0:T(8,128)(2,1)S(1)}, bf16[1,224,128]{2,1,0:T(8,128)(2,1)S(1)}, u32[]{:S(2)}, u32[]{:S(2)}) collective-permute-start(bf16[1,224,128]{2,1,0:T(8,128)(2,1)S(1)} %bitcast.20), channel_id=1, source_target_pairs={{0,16},{4,20},{8,24},{12,28},{16,0},{20,4},{24,8},{28,12},{1,17},{... | collective-permute-start | bytes 172040 | tf_op jit(solution)/shard_map/ppermute | solution.py:516
  17.6 11.4 %copy-start = (bf16[896,2,512]{2,1,0:T(2,128)(2,1)S(1)}, bf16[896,2,512]{2,1,0:T(2,128)(2,1)}, u32[]{:S(2)}) copy-start(bf16[896,2,512]{2,1,0:T(2,128)(2,1)} %inner_hbm.1) | copy-start | bytes 5505028
  17.6 11.4 %copy-start.12 = (f32[512]{0:T(512)S(1)}, f32[512]{0:T(512)}, u32[]{:S(2)}) copy-start(f32[512]{0:T(512)} %param.30) | copy-start | bytes 6148
  17.6 11.4 %copy-start.13 = (f32[256]{0:T(256)S(1)}, f32[256]{0:T(256)}, u32[]{:S(2)}) copy-start(f32[256]{0:T(256)} %param.22) | copy-start | bytes 3076
  18.4 1.2 %collective-permute-start.3 = (f32[2,256]{1,0:T(2,128)S(1)}, f32[2,256]{1,0:T(2,128)S(1)}, u32[]{:S(2)}, u32[]{:S(2)}) collective-permute-start(f32[2,256]{1,0:T(2,128)S(1)} %get-tuple-element.31.own_ref), channel_id=1, source_target_pairs={{0,1},{1,0},{2,3},{3,2},{4,5},{5,4},{6,7},{7,6},{8,9},{9,8},{10,11... | collective-permute-start | bytes 6152 | tf_op jit(solution)/shard_map/ppermute | solution.py:516
  20.1 5.2 %collective-permute-start.4 = (bf16[2,224,128]{2,1,0:T(8,128)(2,1)S(1)}, bf16[2,224,128]{2,1,0:T(8,128)(2,1)S(1)}, u32[]{:S(2)}, u32[]{:S(2)}) collective-permute-start(bf16[2,224,128]{2,1,0:T(8,128)(2,1)S(1)} %get-tuple-element.32.refs_0_), channel_id=1, source_target_pairs={{0,8},{4,12},{8,0},{12,4},{16,24},{20,28},{24,16},{28,20},{1,9},{5... | collective-permute-start | bytes 344072 | tf_op jit(solution)/shard_map/ppermute | solution.py:516
  21.8 3.6 %collective-permute-start.5 = (f32[2,256]{1,0:T(2,128)S(1)}, f32[2,256]{1,0:T(2,128)S(1)}, u32[]{:S(2)}, u32[]{:S(2)}) collective-permute-start(f32[2,256]{1,0:T(2,128)S(1)} %get-tuple-element.33.own_ref), channel_id=1, source_target_pairs={{0,2},{1,3},{2,0},{3,1},{4,6},{5,7},{6,4},{7,5},{8,10},{9,11},{10,... | collective-permute-start | bytes 6152 | tf_op jit(solution)/shard_map/ppermute | solution.py:516
  23.3 5.8 %collective-permute-start.6 = (bf16[2,224,128]{2,1,0:T(8,128)(2,1)S(1)}, bf16[2,224,128]{2,1,0:T(8,128)(2,1)S(1)}, u32[]{:S(2)}, u32[]{:S(2)}) collective-permute-start(bf16[2,224,128]{2,1,0:T(8,128)(2,1)S(1)} %get-tuple-element.32.refs_0_), channel_id=1, source_target_pairs={{0,4},{4,0},{8,12},{12,8},{16,20},{20,16},{24,28},{28,24},{1,5},{5... | collective-permute-start | bytes 344072 | tf_op jit(solution)/shard_map/ppermute | solution.py:516
  25.4 4.9 %collective-permute-start.7 = (bf16[2,224,128]{2,1,0:T(8,128)(2,1)S(1)}, bf16[2,224,128]{2,1,0:T(8,128)(2,1)S(1)}, u32[]{:S(2)}, u32[]{:S(2)}) collective-permute-start(bf16[2,224,128]{2,1,0:T(8,128)(2,1)S(1)} %get-tuple-element.37.refs_1_), channel_id=1, source_target_pairs={{0,4},{4,0},{8,12},{12,8},{16,20},{20,16},{24,28},{28,24},{1,5},{5... | collective-permute-start | bytes 344072 | tf_op jit(solution)/shard_map/ppermute | solution.py:516
  (1 other events, 2.6 us)
